TPU v7x, 32 devices: a whole 2x2x4 slice. The times are simulated.
32 devices in a mesh: dp: 4 (over z), ctx: 4 (over y, core), tensor: 2 (over x).
Axes of the slice: x: 2, y: 2, z: 4, core: 2. Of those that a mesh axis runs over, the one named last changes fastest.
Arguments:
- block_input: bfloat16 [4, 1024, 2560], P('dp', ('ctx', 'tensor')), may hold values from -6 to 6
- segment_ids: int32 [4, 1024], P('dp', 'ctx'), may hold values from 0 to 2, as said below
- output_grad: bfloat16 [4, 1024, 2560], P('dp', ('ctx', 'tensor')), may hold values from -6 to 6
- attention_gain: bfloat16 [2560], P(('dp', 'ctx')), may hold values from 0.25 to 1.75
- query_weight: bfloat16 [2560, 2560], P(('dp', 'ctx'), 'tensor'), may hold values from -0.125 to 0.125
- keyvalue_weight: bfloat16 [2560, 512], P(('dp', 'ctx'), 'tensor'), may hold values from -0.125 to 0.125
- output_weight: bfloat16 [2560, 2560], P('tensor', ('dp', 'ctx')), may hold values from -1 to 1
- output_bias: bfloat16 [2560], P(('dp', 'ctx')), may hold values from -1.796875 to 1.796875
- channel_gain: bfloat16 [2560], P(('dp', 'ctx')), may hold values from 0.25 to 1.75
- gate_weight: bfloat16 [2560, 7680], P(('dp', 'ctx'), 'tensor'), may hold values from -0.125 to 0.125
- up_weight: bfloat16 [2560, 7680], P(('dp', 'ctx'), 'tensor'), may hold values from -0.125 to 0.125
- down_weight: bfloat16 [7680, 2560], P('tensor', ('dp', 'ctx')), may hold values from -0.0625 to 0.0625
- gate_bias: bfloat16 [7680], P('tensor'), may hold values from -1.796875 to 1.796875
- up_bias: bfloat16 [7680], P('tensor'), may hold values from -1.796875 to 1.796875
- down_bias: bfloat16 [2560], P(('dp', 'ctx')), may hold values from -1.796875 to 1.796875
Outputs:
- block_output: bfloat16 [4, 1024, 2560], P('dp', ('ctx', 'tensor'))
- input_grad: float32 [4, 1024, 2560], P('dp', ('ctx', 'tensor'))
- attention_gain_grad: float32 [2560], P(('dp', 'ctx'))
- query_weight_grad: float32 [2560, 2560], P(('dp', 'ctx'), 'tensor')
- keyvalue_weight_grad: float32 [2560, 512], P(('dp', 'ctx'), 'tensor')
- output_weight_grad: float32 [2560, 2560], P('tensor', ('dp', 'ctx'))
- output_bias_grad: float32 [2560], P(('dp', 'ctx'))
- channel_gain_grad: float32 [2560], P(('dp', 'ctx'))
- gate_weight_grad: float32 [2560, 7680], P(('dp', 'ctx'), 'tensor')
- up_weight_grad: float32 [2560, 7680], P(('dp', 'ctx'), 'tensor')
- down_weight_grad: float32 [7680, 2560], P('tensor', ('dp', 'ctx'))
- gate_bias_grad: float32 [7680], P('tensor')
- up_bias_grad: float32 [7680], P('tensor')
- down_bias_grad: float32 [2560], P(('dp', 'ctx'))
Inputs may be any that keep to these rules, and one draw needn't show every extreme that they name: `segment_ids`: within each sequence the numbers start at 0 and rise by 0 or 1 from one token to the next; every sequence holds exactly three documents. The first and the last have 256 // 4 to 255 tokens each (at least one), so that the middle one begins among the first 256 tokens and ends among the last 256 tokens.
All inputs are finite; a program needn't handle non-finite values.
Results may differ from a plain program's by a relative error of at most 0.014.
Values may be sent and summed in bfloat16 or wider, within the bound.
No kernel may reach another device: no remote copies, remote signals or barrier semaphores. Data moves between devices by JAX's collectives and lax.ppermute only.
A program may use at most 256 MiB of HBM per device.

v0:
```python
from functools import partial
import math

import jax
import jax.numpy as jnp
from jax import lax
from jax.sharding import PartitionSpec as P

HD = 256
WINDOW = 2048


def norm_scale(vectors, scale_gain):
    return (
        vectors
        * lax.rsqrt(jnp.mean(vectors * vectors, axis=-1, keepdims=True) + 1e-06)
        * scale_gain
    )


def rotary_tables(positions, head_size):
    quarter = head_size // 4
    frequency = jnp.exp(jnp.arange(quarter, dtype=jnp.float32) * (-math.log(10000.0) / quarter))
    angles = positions.astype(jnp.float32)[:, None] * frequency[None, :]
    return (jnp.cos(angles), jnp.sin(angles))


def rotate(vectors, cosine_table, sine_table, direction):
    quarter = cosine_table.shape[-1]
    lead_part = vectors[..., :quarter]
    trail_part = vectors[..., quarter : 2 * quarter]
    cosine_wide = cosine_table[:, None, :]
    sine_wide = direction * sine_table[:, None, :]
    return jnp.concatenate(
        [
            lead_part * cosine_wide - trail_part * sine_wide,
            trail_part * cosine_wide + lead_part * sine_wide,
            vectors[..., 2 * quarter :],
        ],
        axis=-1,
    )


def gather_rows(values_low):
    return lax.all_gather(values_low, "tensor", axis=0, tiled=True)


def sum_rows(partial_rows):
    return lax.psum_scatter(partial_rows, "tensor", scatter_dimension=0, tiled=True)


def fetch_set(first_item, second_item, third_item, fourth_item, fifth_item):
    return (
        lax.all_gather(first_item, ("dp", "ctx"), axis=0, tiled=True),
        lax.all_gather(second_item, ("dp", "ctx"), axis=0, tiled=True),
        lax.all_gather(third_item, ("dp", "ctx"), axis=1, tiled=True),
        lax.all_gather(fourth_item, ("dp", "ctx"), axis=0, tiled=True),
        lax.all_gather(fifth_item, ("dp", "ctx"), axis=0, tiled=True),
    )


def refetch_set(first_item, second_item, third_item):
    return (
        lax.all_gather(first_item, ("dp", "ctx"), axis=0, tiled=True),
        lax.all_gather(second_item, ("dp", "ctx"), axis=0, tiled=True),
        lax.all_gather(third_item, ("dp", "ctx"), axis=1, tiled=True),
    )


def local(
    block_input,
    segment_ids,
    output_grad,
    attention_gain,
    query_weight,
    keyvalue_weight,
    output_weight,
    output_bias,
    channel_gain,
    gate_weight,
    up_weight,
    down_weight,
    gate_bias,
    up_bias,
    down_bias,
):
    f32 = jnp.float32
    bf16 = jnp.bfloat16
    local_in = block_input[0].astype(f32)
    tensor_index = lax.axis_index("tensor")
    ctx_index = lax.axis_index("ctx")
    full_query, full_keyvalue, full_output, gain_one, full_obias = fetch_set(
        query_weight, keyvalue_weight, output_weight, attention_gain, output_bias
    )
    normed_local, norm_one_pull = jax.vjp(norm_scale, local_in, gain_one.astype(f32))
    normed = gather_rows(normed_local.astype(bf16))
    row_count = normed.shape[0]
    all_segments = lax.all_gather(segment_ids, "ctx", axis=1, tiled=True)[0]
    length = all_segments.shape[0]
    group_count = length // row_count
    own_segments = lax.dynamic_slice_in_dim(all_segments, ctx_index * row_count, row_count)
    query_index = ctx_index * row_count + jnp.arange(row_count, dtype=jnp.int32)
    earlier = jnp.sum((all_segments[None, :] < own_segments[:, None]).astype(jnp.int32), axis=1)
    positions = query_index - earlier
    cosine_table, sine_table = rotary_tables(positions, HD)
    head_count = full_query.shape[1] // HD
    query_proj = jnp.dot(normed, full_query, preferred_element_type=f32)
    queries = (
        rotate(query_proj.reshape(row_count, head_count, HD), cosine_table, sine_table, 1.0)
        * HD ** (-0.5)
    ).astype(bf16)
    half_proj = jnp.dot(normed, full_keyvalue, preferred_element_type=f32)
    is_key = tensor_index == 0
    half_low = jnp.where(
        is_key, rotate(half_proj[:, None, :], cosine_table, sine_table, 1.0)[:, 0], half_proj
    ).astype(bf16)
    gathered = lax.all_gather(half_low[None], ("ctx", "tensor"), axis=0, tiled=True)
    gathered = gathered.reshape(group_count, 2, row_count, HD)
    all_keys = gathered[:, 0].reshape(length, HD)
    all_values = gathered[:, 1].reshape(length, HD)
    key_index = jnp.arange(length, dtype=jnp.int32)
    allowed = (
        (own_segments[:, None] == all_segments[None, :])
        & (key_index[None, :] <= query_index[:, None])
        & (query_index[:, None] - key_index[None, :] < WINDOW)
    )
    scores = jnp.einsum("qhd,kd->hqk", queries, all_keys, preferred_element_type=f32)
    scores = jnp.where(allowed[None], scores, -1e30)
    score_peak = jnp.max(scores, axis=-1, keepdims=True)
    exp_scores = jnp.exp(scores - score_peak)
    exp_total = jnp.sum(exp_scores, axis=-1, keepdims=True)
    log_total = score_peak + jnp.log(exp_total)
    probs_low = (exp_scores / exp_total).astype(bf16)
    context = jnp.einsum("hqk,kd->qhd", probs_low, all_values, preferred_element_type=f32).astype(
        bf16
    )
    context = context.reshape(row_count, head_count * HD)
    mixed = (
        local_in + sum_rows(jnp.dot(context, full_output, preferred_element_type=f32)) + full_obias
    )
    full_gate, full_up, full_down, gain_two, full_dbias = fetch_set(
        gate_weight, up_weight, down_weight, channel_gain, down_bias
    )
    normed_two_local, norm_two_pull = jax.vjp(norm_scale, mixed, gain_two.astype(f32))
    normed_two = gather_rows(normed_two_local.astype(bf16))
    gate_pre = jnp.dot(normed_two, full_gate, preferred_element_type=f32) + gate_bias
    up_pre = jnp.dot(normed_two, full_up, preferred_element_type=f32) + up_bias
    activated, gelu_pull = jax.vjp(partial(jax.nn.gelu, approximate=True), gate_pre)
    hidden = (activated * up_pre).astype(bf16)
    block_output = (
        mixed + sum_rows(jnp.dot(hidden, full_down, preferred_element_type=f32)) + full_dbias
    ).astype(bf16)
    back_gate, back_up, back_down = refetch_set(gate_weight, up_weight, down_weight)
    grad_local = output_grad[0]
    grad_full = grad_local.astype(f32)
    dbias_part = jnp.sum(grad_full, axis=0)
    grad_rows = gather_rows(grad_local)
    down_wgrad = jnp.einsum("rf,rd->fd", hidden, grad_rows, preferred_element_type=f32)
    hidden_grad = jnp.einsum("rd,fd->rf", grad_rows, back_down, preferred_element_type=f32)
    gate_grad_full = gelu_pull(hidden_grad * up_pre)[0]
    up_grad_full = hidden_grad * activated
    gbias_part = jnp.sum(gate_grad_full, axis=0)
    ubias_part = jnp.sum(up_grad_full, axis=0)
    gate_grad = gate_grad_full.astype(bf16)
    up_grad = up_grad_full.astype(bf16)
    gate_wgrad = jnp.einsum("rd,rf->df", normed_two, gate_grad, preferred_element_type=f32)
    up_wgrad = jnp.einsum("rd,rf->df", normed_two, up_grad, preferred_element_type=f32)
    two_part = jnp.einsum(
        "rf,df->rd", gate_grad, back_gate, preferred_element_type=f32
    ) + jnp.einsum("rf,df->rd", up_grad, back_up, preferred_element_type=f32)
    mixed_part, gain_two_part = norm_two_pull(sum_rows(two_part))
    mixed_grad = grad_full + mixed_part
    back_query, back_keyvalue, back_output = refetch_set(
        query_weight, keyvalue_weight, output_weight
    )
    obias_part = jnp.sum(mixed_grad, axis=0)
    attn_rows = gather_rows(mixed_grad.astype(bf16))
    output_wgrad = jnp.einsum("rc,rd->cd", context, attn_rows, preferred_element_type=f32)
    context_grad = jnp.einsum(
        "rd,cd->rc", attn_rows, back_output, preferred_element_type=f32
    ).astype(bf16)
    context_grad = context_grad.reshape(row_count, head_count, HD)
    scores_again = jnp.einsum("qhd,kd->hqk", queries, all_keys, preferred_element_type=f32)
    probs_again = jnp.exp(jnp.where(allowed[None], scores_again, -1e30) - log_total)
    probs_grad = jnp.einsum("qhd,kd->hqk", context_grad, all_values, preferred_element_type=f32)
    values_grad = jnp.einsum(
        "hqk,qhd->kd", probs_again.astype(bf16), context_grad, preferred_element_type=f32
    )
    prob_dot = jnp.sum(probs_again * probs_grad, axis=-1, keepdims=True)
    score_grad = (probs_again * (probs_grad - prob_dot)).astype(bf16)
    query_grad = jnp.einsum("hqk,kd->qhd", score_grad, all_keys, preferred_element_type=f32)
    keys_grad = jnp.einsum("hqk,qhd->kd", score_grad, queries, preferred_element_type=f32)
    stacked = jnp.stack(
        [
            keys_grad.reshape(group_count, row_count, HD),
            values_grad.reshape(group_count, row_count, HD),
        ],
        axis=1,
    )
    stacked = stacked.reshape(2 * group_count, row_count, HD)
    half_grad = lax.psum_scatter(stacked, ("ctx", "tensor"), scatter_dimension=0, tiled=True)[0]
    half_grad = jnp.where(
        is_key, rotate(half_grad[:, None, :], cosine_table, sine_table, -1.0)[:, 0], half_grad
    ).astype(bf16)
    query_proj_grad = rotate(query_grad * HD ** (-0.5), cosine_table, sine_table, -1.0)
    query_proj_grad = query_proj_grad.reshape(row_count, head_count * HD).astype(bf16)
    query_wgrad = jnp.einsum("rd,rc->dc", normed, query_proj_grad, preferred_element_type=f32)
    keyvalue_wgrad = jnp.einsum("rd,rc->dc", normed, half_grad, preferred_element_type=f32)
    one_part = jnp.einsum(
        "rc,dc->rd", query_proj_grad, back_query, preferred_element_type=f32
    ) + jnp.einsum("rc,dc->rd", half_grad, back_keyvalue, preferred_element_type=f32)
    input_part, gain_one_part = norm_one_pull(sum_rows(one_part))
    input_grad = mixed_grad + input_part
    query_out, keyvalue_out, proj_out, gate_out, up_out, down_out = (
        lax.psum_scatter(query_wgrad, ("dp", "ctx"), scatter_dimension=0, tiled=True),
        lax.psum_scatter(keyvalue_wgrad, ("dp", "ctx"), scatter_dimension=0, tiled=True),
        lax.psum_scatter(output_wgrad, ("dp", "ctx"), scatter_dimension=1, tiled=True),
        lax.psum_scatter(gate_wgrad, ("dp", "ctx"), scatter_dimension=0, tiled=True),
        lax.psum_scatter(up_wgrad, ("dp", "ctx"), scatter_dimension=0, tiled=True),
        lax.psum_scatter(down_wgrad, ("dp", "ctx"), scatter_dimension=1, tiled=True),
    )
    ff_half = gbias_part.shape[0]
    slice_start = tensor_index * ff_half
    gate_full = lax.dynamic_update_slice(jnp.zeros((2 * ff_half,), f32), gbias_part, (slice_start,))
    up_full = lax.dynamic_update_slice(jnp.zeros((2 * ff_half,), f32), ubias_part, (slice_start,))
    gain_one_sum, gain_two_sum, obias_sum, dbias_sum, gbias_sum, ubias_sum = lax.psum(
        (gain_one_part, gain_two_part, obias_part, dbias_part, gate_full, up_full),
        ("dp", "ctx", "tensor"),
    )
    shard_rows = attention_gain.shape[0]
    fsdp_index = lax.axis_index("dp") * lax.axis_size("ctx") + ctx_index
    shard_start = fsdp_index * shard_rows
    return (
        block_output[None],
        input_grad[None],
        lax.dynamic_slice_in_dim(gain_one_sum, shard_start, shard_rows),
        query_out,
        keyvalue_out,
        proj_out,
        lax.dynamic_slice_in_dim(obias_sum, shard_start, shard_rows),
        lax.dynamic_slice_in_dim(gain_two_sum, shard_start, shard_rows),
        gate_out,
        up_out,
        down_out,
        lax.dynamic_slice_in_dim(gbias_sum, slice_start, ff_half),
        lax.dynamic_slice_in_dim(ubias_sum, slice_start, ff_half),
        lax.dynamic_slice_in_dim(dbias_sum, shard_start, shard_rows),
    )


def solution(mesh):
    placed = (
        P("dp", ("ctx", "tensor"), None),
        P("dp", "ctx"),
        P("dp", ("ctx", "tensor"), None),
        P(("dp", "ctx")),
        P(("dp", "ctx"), "tensor"),
        P(("dp", "ctx"), "tensor"),
        P("tensor", ("dp", "ctx")),
        P(("dp", "ctx")),
        P(("dp", "ctx")),
        P(("dp", "ctx"), "tensor"),
        P(("dp", "ctx"), "tensor"),
        P("tensor", ("dp", "ctx")),
        P("tensor"),
        P("tensor"),
        P(("dp", "ctx")),
    )
    return jax.shard_map(
        local,
        mesh=mesh,
        in_specs=placed,
        out_specs=(
            P("dp", ("ctx", "tensor"), None),
            P("dp", ("ctx", "tensor"), None),
            P(("dp", "ctx")),
            P(("dp", "ctx"), "tensor"),
            P(("dp", "ctx"), "tensor"),
            P("tensor", ("dp", "ctx")),
            P(("dp", "ctx")),
            P(("dp", "ctx")),
            P(("dp", "ctx"), "tensor"),
            P(("dp", "ctx"), "tensor"),
            P("tensor", ("dp", "ctx")),
            P("tensor"),
            P("tensor"),
            P(("dp", "ctx")),
        ),
        check_vma=False,
    )
```

profile of v0, /device:TPU:0, one launch (start us, length us, event | category | flops | bytes accessed | tf_op | source)
XLA Modules:
  0.0 2606.0 jit_solution(2581289209805932169)
XLA Ops:
  12.6 62.9 %all-reduce.5 = (bf16[2560]{0:T(1024)(128)(2,1)S(1)}, bf16[2560]{0:T(1024)(128)(2,1)}, bf16[2560]{0:T(1024)(128)(2,1)}, bf16[2560]{0:T(1024)(128)(2,1)}) all-reduce(bf16[2560]{0:T(1024)(128)(2,1)S(1)} %dynamic-update-slice, bf16[2560]{0:T(1024)(128)(2,1)S(1)} %dynamic-update-slice.1, ...), channel_id=1, replica_groups=mesh['dp'=4,'ctx'=4,'tensor'=2] {'dp','ctx'}, use_global_device_ids=true, to_apply=%add | all-reduce | flops 10240 | bytes 40960
  76.8 2.1 fusion.19
  79.8 5.1 all_gather.57
  85.2 15.5 all-gather.14.cloned.1.call-done
  100.7 41.1 %all-gather.16.cloned.1.call-done = bf16[2560,256]{1,0:T(8,128)(2,1)} async-done(((bf16[160,256]{1,0:T(8,128)(2,1)}), bf16[2560,256]{1,0:T(8,128)(2,1)}) %all-gather.16.cloned.1.call-update) | async-done | bytes 1310736 | tf_op jit(solution)/shard_map/all_gather | solution.py:55
  141.8 2.3 fusion.76
  148.0 19.8 all-gather.32.cloned.1.call-done
  167.7 1.8 reshape.335
  169.6 2.3 fusion.75
  171.9 3.6 copy.70
  176.4 56.9 %all-gather.18.cloned.1.call-done = bf16[2560,1280]{1,0:T(8,128)(2,1)} async-done(((bf16[160,1280]{1,0:T(8,128)(2,1)}), bf16[2560,1280]{1,0:T(8,128)(2,1)}) %all-gather.18.cloned.1.call-update) | async-done | bytes 6553616 | tf_op jit(solution)/shard_map/all_gather | solution.py:54
  233.3 5.6 fusion.77
  240.3 2.2 multiply_subtract_fusion
  243.8 2.3 copy.47
  246.1 2.2 fusion.6
  249.2 1.3 copy-done
  250.6 1.6 fusion.18
  252.2 45.2 %all-gather.20.cloned.1.call-done = bf16[1280,2560]{0,1:T(8,128)(2,1)} async-done(((bf16[1280,160]{0,1:T(8,128)(2,1)}), bf16[1280,2560]{0,1:T(8,128)(2,1)}) %all-gather.20.cloned.1.call-update) | async-done | bytes 6553616 | tf_op jit(solution)/shard_map/all_gather | solution.py:56
  297.4 6.2 fusion.78
  305.0 35.0 %reduce-scatter.12.cloned.1.call-done = f32[128,2560]{1,0:T(8,128)} async-done(((f32[256,2560]{1,0:T(8,128)}), f32[128,2560]{1,0:T(8,128)}) %reduce-scatter.12.cloned.1.call-update) | async-done | bytes 1310736 | tf_op jit(solution)/shard_map/reduce_scatter | solution.py:49
  340.0 1.6 multiply_reduce_fusion.2
  349.6 18.6 all-gather.22.cloned.1.call-done
  368.1 104.4 %all-gather.24.cloned.1.call-done = bf16[2560,3840]{1,0:T(8,128)(2,1)} async-done(((bf16[160,3840]{1,0:T(8,128)(2,1)}), bf16[2560,3840]{1,0:T(8,128)(2,1)}) %all-gather.24.cloned.1.call-update) | async-done | bytes 19660816 | tf_op jit(solution)/shard_map/all_gather | solution.py:54
  472.5 13.6 convolution_add_fusion.1
  486.1 90.8 %all-gather.26.cloned.1.call-done = bf16[2560,3840]{1,0:T(8,128)(2,1)} async-done(((bf16[160,3840]{1,0:T(8,128)(2,1)}), bf16[2560,3840]{1,0:T(8,128)(2,1)}) %all-gather.26.cloned.1.call-update) | async-done | bytes 19660816 | tf_op jit(solution)/shard_map/all_gather | solution.py:55
  576.9 13.6 convolution_add_fusion
  590.5 12.1 all-gather.34.cloned.1.call-done
  602.6 104.4 %all-gather.28.cloned.1.call-done = bf16[3840,2560]{0,1:T(8,128)(2,1)} async-done(((bf16[3840,160]{0,1:T(8,128)(2,1)}), bf16[3840,2560]{0,1:T(8,128)(2,1)}) %all-gather.28.cloned.1.call-update) | async-done | bytes 19660816 | tf_op jit(solution)/shard_map/all_gather | solution.py:56
  707.0 15.8 fusion.68
  722.8 10.8 fusion.41
  733.6 11.7 convolution_add_fusion.2
  745.3 11.8 fusion.79
  758.5 24.5 reduce-scatter.16.cloned.1.call-done
  783.0 2.3 multiply_reduce_fusion
  785.9 37.0 %reduce-scatter.14.cloned.1.call-done = f32[128,2560]{1,0:T(8,128)} async-done(((f32[256,2560]{1,0:T(8,128)}), f32[128,2560]{1,0:T(8,128)}) %reduce-scatter.14.cloned.1.call-update) | async-done | bytes 1310736 | tf_op jit(solution)/shard_map/reduce_scatter | solution.py:49
  822.9 3.9 fusion.72
  829.4 4.8 fusion.1
  834.3 18.9 all-gather.30.cloned.1.call-done
  853.2 6.0 convolution_convert_fusion
  860.5 4.3 fusion.2
  869.9 1.5 pad_maximum_fusion
  871.3 2.9 copy.57
  875.3 2.6 fusion.17
  878.9 6.6 fusion.80
  885.5 30.1 %reduce-scatter.18.cloned.1.call-done = f32[1,256,256]{1,2,0:T(8,128)} async-done(((f32[8,256,256]{1,2,0:T(8,128)}), f32[1,256,256]{1,2,0:T(8,128)}) %reduce-scatter.18.cloned.1.call-update) | async-done | bytes 262160 | tf_op jit(solution)/shard_map/reduce_scatter | solution.py:201
  918.8 3.8 convolution_add_fusion.3
  925.2 35.2 %reduce-scatter.20.cloned.1.call-done = f32[128,2560]{1,0:T(8,128)} async-done(((f32[256,2560]{1,0:T(8,128)}), f32[128,2560]{1,0:T(8,128)}) %reduce-scatter.20.cloned.1.call-update) | async-done | bytes 1310736 | tf_op jit(solution)/shard_map/reduce_scatter | solution.py:49
  960.3 2.5 fusion.20
  962.9 2.1 fusion.82
  966.1 6.6 fusion.81
  974.3 6.7 fusion.83
  982.3 16.9 fusion.39
  999.3 16.9 fusion.36
  1017.5 16.9 fusion.28
  1036.1 1.5 fusion.23
  1037.6 54.4 %all-reduce.8.cloned.1.call-done = (f32[2560]{0:T(1024)}, f32[2560]{0:T(1024)}, f32[2560]{0:T(1024)}, f32[7680]{0:T(1024)}, f32[7680]{0:T(1024)}, /*index=5*/f32[2560]{0:T(1024)}) async-done(((f32[2560]{0:T(1024)}, f32[2560]{0:T(1024)}, f32[2560]{0:T(1024)}, f32[7680]{0:T(1024)}, f32[7680]{0:T(1024)}, /*index=5*/f32[2560]{0:T(1024)}), (f32[2560]{0:T(1024)}, f32[2560]{0:T(1024)}, f32[2560]{0:T(1024)}, ...) | async-done | bytes 102416 | tf_op jit(solution)/shard_map/psum | solution.py:226
  1096.0 1.4 dynamic_slice.25
  1097.4 1.4 dynamic_slice.26
  1100.1 61.2 %reduce-scatter.24.cloned.1.call-done = f32[160,256]{1,0:T(8,128)} async-done(((f32[2560,256]{1,0:T(8,128)}), f32[160,256]{1,0:T(8,128)}) %reduce-scatter.24.cloned.1.call-update) | async-done | bytes 163856 | tf_op jit(solution)/shard_map/reduce_scatter | solution.py:216
  1161.3 142.6 %reduce-scatter.22.cloned.1.call-done = f32[160,1280]{1,0:T(8,128)} async-done(((f32[2560,1280]{1,0:T(8,128)}), f32[160,1280]{1,0:T(8,128)}) %reduce-scatter.22.cloned.1.call-update) | async-done | bytes 819216 | tf_op jit(solution)/shard_map/reduce_scatter | solution.py:215
  1304.0 142.1 %reduce-scatter.26.cloned.1.call-done = f32[1280,160]{0,1:T(8,128)} async-done(((f32[1280,2560]{0,1:T(8,128)}), f32[1280,160]{0,1:T(8,128)}) %reduce-scatter.26.cloned.1.call-update) | async-done | bytes 819216 | tf_op jit(solution)/shard_map/reduce_scatter | solution.py:217
  1446.0 384.4 %reduce-scatter.28.cloned.1.call-done = f32[160,3840]{1,0:T(8,128)} async-done(((f32[2560,3840]{1,0:T(8,128)}), f32[160,3840]{1,0:T(8,128)}) %reduce-scatter.28.cloned.1.call-update) | async-done | bytes 2457616 | tf_op jit(solution)/shard_map/reduce_scatter | solution.py:218
  1830.4 384.4 %reduce-scatter.30.cloned.1.call-done = f32[160,3840]{1,0:T(8,128)} async-done(((f32[2560,3840]{1,0:T(8,128)}), f32[160,3840]{1,0:T(8,128)}) %reduce-scatter.30.cloned.1.call-update) | async-done | bytes 2457616 | tf_op jit(solution)/shard_map/reduce_scatter | solution.py:219
  2214.8 384.5 %reduce-scatter.32.cloned.1.call-done = f32[3840,160]{0,1:T(8,128)} async-done(((f32[3840,2560]{0,1:T(8,128)}), f32[3840,160]{0,1:T(8,128)}) %reduce-scatter.32.cloned.1.call-update) | async-done | bytes 2457616 | tf_op jit(solution)/shard_map/reduce_scatter | solution.py:220
  (230 shorter events, 55.2 us)
Async XLA Ops:
  7.2 72.6 %copy-start.56 = (s32[1,256]{1,0:T(1,128)S(1)}, s32[1,256]{1,0:T(1,128)}, u32[]{:S(2)}) copy-start(s32[1,256]{1,0:T(1,128)} %param.16) | copy-start | bytes 3076
  7.2 93.5 %all-gather.14.cloned.1.call-start = ((), (), s32[]{:S(2)}) async-start(), calls=%async_computation.11 | async-start | bytes 1966080 | tf_op jit(solution)/shard_map/all_gather | solution.py:45
  75.5 25.2 copy-start.33
  76.8 23.9 copy-start.57
  76.8 23.9 copy-start.49
  79.0 62.8 %all-gather.16.cloned.1.call-start = ((), (), s32[]{:S(2)}) async-start(), calls=%async_computation.12 | async-start | bytes 1392640 | tf_op jit(solution)/shard_map/all_gather | solution.py:55
  79.8 88.0 %all-gather.32.cloned.1.call-start = ((), (), s32[]{:S(2)}) async-start(), calls=%async_computation.31 | async-start | bytes 1179648 | tf_op jit(solution)/shard_map/all_gather | solution.py:117
  84.9 61.7 %copy-start.51 = (f32[64]{0:T(128)}, f32[64]{0:T(128)S(1)}, u32[]{:S(2)}) copy-start(f32[64]{0:T(128)S(1)} %multiply_exponential_fusion) | copy-start | bytes 772
  84.9 62.7 %copy-start.43 = (s32[1,256]{1,0:T(1,128)}, s32[1,256]{1,0:T(1,128)S(1)}, u32[]{:S(2)}) copy-start(s32[1,256]{1,0:T(1,128)S(1)} %constant_dynamic-slice_fusion) | copy-start | bytes 3076
  85.2 61.4 %copy-start.41 = (f32[256]{0:T(256)}, f32[256]{0:T(256)S(1)}, u32[]{:S(2)}) copy-start(f32[256]{0:T(256)S(1)} %subtract_convert_fusion.1) | copy-start | bytes 3076
  145.2 88.1 %all-gather.18.cloned.1.call-start = ((), (), s32[]{:S(2)}) async-start(), calls=%async_computation.13 | async-start | bytes 6963200 | tf_op jit(solution)/shard_map/all_gather | solution.py:54
  145.8 151.6 %all-gather.20.cloned.1.call-start = ((), (), s32[]{:S(2)}) async-start(), calls=%async_computation.14 | async-start | bytes 6963200 | tf_op jit(solution)/shard_map/all_gather | solution.py:56
  146.4 193.6 %reduce-scatter.12.cloned.1.call-start = ((), (), s32[]{:S(2)}) async-start(), calls=%async_computation.15 | async-start | bytes 3932160 | tf_op jit(solution)/shard_map/reduce_scatter | solution.py:49
  146.6 25.2 copy-start.54
  171.9 61.4 %copy-start.2 = (bf16[256,2560]{1,0:T(8,128)(2,1)S(1)}, bf16[256,2560]{1,0:T(8,128)(2,1)}, u32[]{:S(2)}) copy-start(bf16[256,2560]{1,0:T(8,128)(2,1)} %all-gather.14.cloned.1.call-done) | copy-start | bytes 3932164
  176.4 69.7 %copy-start.10 = (bf16[4,1,256,256]{3,2,0,1:T(8,128)(2,1)}, bf16[4,1,256,256]{3,2,0,1:T(8,128)(2,1)S(1)}, u32[]{:S(2)}) copy-start(bf16[4,1,256,256]{3,2,0,1:T(8,128)(2,1)S(1)} %copy.44) | copy-start | bytes 1572868
  240.2 8.0 copy-start.12
  243.7 4.5 copy-start.16
  248.3 2.3 copy-start
  248.3 2.3 copy-start.37
  248.3 2.3 copy-start.20
  249.2 2.9 copy-start.39
  252.2 51.5 %copy-start.27 = (bf16[256,5,256]{2,0,1:T(8,128)(2,1)}, bf16[256,5,256]{2,0,1:T(8,128)(2,1)S(1)}, u32[]{:S(2)}) copy-start(bf16[256,5,256]{2,0,1:T(8,128)(2,1)S(1)} %fusion.18) | copy-start | bytes 1966084
  303.7 36.3 %copy-start.1 = (bf16[1,128,2560]{2,1,0:T(8,128)(2,1)S(1)}, bf16[1,128,2560]{2,1,0:T(8,128)(2,1)}, u32[]{:S(2)}) copy-start(bf16[1,128,2560]{2,1,0:T(8,128)(2,1)} %param.15) | copy-start | bytes 1966084
  303.7 64.4 %all-gather.22.cloned.1.call-start = ((), (), s32[]{:S(2)}) async-start(), calls=%async_computation.16 | async-start | bytes 1966080 | tf_op jit(solution)/shard_map/all_gather | solution.py:45
  343.7 128.8 %all-gather.24.cloned.1.call-start = ((), (), s32[]{:S(2)}) async-start(), calls=%async_computation.17 | async-start | bytes 20889600 | tf_op jit(solution)/shard_map/all_gather | solution.py:54
  344.5 232.4 %all-gather.26.cloned.1.call-start = ((), (), s32[]{:S(2)}) async-start(), calls=%async_computation.18 | async-start | bytes 20889600 | tf_op jit(solution)/shard_map/all_gather | solution.py:55
  345.2 257.4 %all-gather.34.cloned.1.call-start = ((), (), s32[]{:S(2)}) async-start(), calls=%async_computation.32 | async-start | bytes 1966080 | tf_op jit(solution)/shard_map/all_gather | solution.py:45
  345.8 361.2 %all-gather.28.cloned.1.call-start = ((), (), s32[]{:S(2)}) async-start(), calls=%async_computation.19 | async-start | bytes 20889600 | tf_op jit(solution)/shard_map/all_gather | solution.py:56
  346.5 436.5 %reduce-scatter.16.cloned.1.call-start = ((), (), s32[]{:S(2)}) async-start(), calls=%async_computation.21 | async-start | bytes 3932160 | tf_op jit(solution)/shard_map/reduce_scatter | solution.py:49
  722.8 10.8 copy-start.23
  722.8 10.8 copy-start.22
  745.3 77.6 %reduce-scatter.14.cloned.1.call-start = ((), (), s32[]{:S(2)}) async-start(), calls=%async_computation.20 | async-start | bytes 3932160 | tf_op jit(solution)/shard_map/reduce_scatter | solution.py:49
  757.2 96.0 %all-gather.30.cloned.1.call-start = ((), (), s32[]{:S(2)}) async-start(), calls=%async_computation.22 | async-start | bytes 1966080 | tf_op jit(solution)/shard_map/all_gather | solution.py:45
  783.0 2.4 copy-start.60
  826.8 2.2 copy-start.44
  826.8 2.2 copy-start.55
  826.8 2.6 copy-start.38
  826.8 2.6 copy-start.40
  828.8 86.9 %reduce-scatter.18.cloned.1.call-start = ((), (), s32[]{:S(2)}) async-start(), calls=%async_computation.23 | async-start | bytes 2359296 | tf_op jit(solution)/shard_map/reduce_scatter | solution.py:201
  834.3 26.2 %copy-start.21 = (bf16[4,1,256,256]{3,2,0,1:T(8,128)(2,1)S(1)}, bf16[4,1,256,256]{3,2,0,1:T(8,128)(2,1)}, u32[]{:S(2)}) copy-start(bf16[4,1,256,256]{3,2,0,1:T(8,128)(2,1)} %copy.70) | copy-start | bytes 1572868
  860.5 4.3 slice-start
  860.5 4.3 slice-start.1
  866.3 2.7 copy-start.19
  874.3 3.7 copy-start.30
  874.3 3.7 copy-start.31
  874.3 86.1 %reduce-scatter.20.cloned.1.call-start = ((), (), s32[]{:S(2)}) async-start(), calls=%async_computation.24 | async-start | bytes 3932160 | tf_op jit(solution)/shard_map/reduce_scatter | solution.py:49
  878.9 37.6 %copy-start.42 = (f32[256]{0:T(256)S(1)}, f32[256]{0:T(256)}, u32[]{:S(2)}) copy-start(f32[256]{0:T(256)} %copy-done.41) | copy-start | bytes 3076
  878.9 37.7 %copy-start.52 = (f32[64]{0:T(128)S(1)}, f32[64]{0:T(128)}, u32[]{:S(2)}) copy-start(f32[64]{0:T(128)} %copy-done.51) | copy-start | bytes 772
  878.9 39.8 %copy-start.8 = (bf16[2560,256]{1,0:T(8,128)(2,1)S(1)}, bf16[2560,256]{1,0:T(8,128)(2,1)}, u32[]{:S(2)}) copy-start(bf16[2560,256]{1,0:T(8,128)(2,1)} %all-gather.16.cloned.1.call-done) | copy-start | bytes 3932164
  922.6 1.8 copy-start.46
  922.6 2.2 copy-start.45
  922.6 37.8 %copy-start.34 = (f32[2560]{0:T(1024)S(1)}, f32[2560]{0:T(1024)}, u32[]{:S(2)}) copy-start(f32[2560]{0:T(1024)} %copy-done.33) | copy-start | bytes 30724
  922.6 37.8 %copy-start.50 = (f32[128]{0:T(128)S(1)}, f32[128]{0:T(128)}, u32[]{:S(2)}) copy-start(f32[128]{0:T(128)} %copy-done.49) | copy-start | bytes 1540
  922.6 169.4 %all-reduce.8.cloned.1.call-start = ((), (), s32[]{:S(2)}) async-start(), calls=%async_computation.33 | async-start | bytes 229376 | tf_op jit(solution)/shard_map/psum | solution.py:226
  924.7 38.1 %copy-start.36 = (f32[7680]{0:T(1024)}, f32[7680]{0:T(1024)S(1)}, u32[]{:S(2)}) copy-start(f32[7680]{0:T(1024)S(1)} %dynamic_update_slice.6) | copy-start | bytes 92164
  925.2 37.7 %copy-start.35 = (f32[7680]{0:T(1024)}, f32[7680]{0:T(1024)S(1)}, u32[]{:S(2)}) copy-start(f32[7680]{0:T(1024)S(1)} %dynamic_update_slice.7) | copy-start | bytes 92164
  962.9 198.5 %reduce-scatter.24.cloned.1.call-start = ((), (), s32[]{:S(2)}) async-start(), calls=%async_computation.26 | async-start | bytes 2785280 | tf_op jit(solution)/shard_map/reduce_scatter | solution.py:216
  965.1 338.9 %reduce-scatter.22.cloned.1.call-start = ((), (), s32[]{:S(2)}) async-start(), calls=%async_computation.25 | async-start | bytes 13926400 | tf_op jit(solution)/shard_map/reduce_scatter | solution.py:215
  972.8 473.2 %reduce-scatter.26.cloned.1.call-start = ((), (), s32[]{:S(2)}) async-start(), calls=%async_computation.27 | async-start | bytes 13926400 | tf_op jit(solution)/shard_map/reduce_scatter | solution.py:217
  981.0 849.4 %reduce-scatter.28.cloned.1.call-start = ((), (), s32[]{:S(2)}) async-start(), calls=%async_computation.28 | async-start | bytes 41779200 | tf_op jit(solution)/shard_map/reduce_scatter | solution.py:218
  999.3 1215.5 %reduce-scatter.30.cloned.1.call-start = ((), (), s32[]{:S(2)}) async-start(), calls=%async_computation.29 | async-start | bytes 41779200 | tf_op jit(solution)/shard_map/reduce_scatter | solution.py:219
  1016.2 1583.0 %reduce-scatter.32.cloned.1.call-start = ((), (), s32[]{:S(2)}) async-start(), calls=%async_computation.30 | async-start | bytes 41779200 | tf_op jit(solution)/shard_map/reduce_scatter | solution.py:220
  1034.4 1.7 copy-start.9
  (22 other events, 25.0 us)
Sparse Core Ops, SparseCore 0:
  79.1 21.4 all-gather.13
  103.0 38.7 all-gather.15
  145.3 22.3 all-gather.31
  169.9 63.3 all-gather.17
  235.4 61.9 all-gather.19
  303.8 36.1 reduce-scatter.11
  343.8 24.2 all-gather.21
  369.8 102.6 all-gather.23
  474.2 102.6 all-gather.25
  578.3 24.2 all-gather.33
  604.3 102.6 all-gather.27
  745.4 37.5 reduce-scatter.15
  785.3 37.5 reduce-scatter.13
  828.9 24.2 all-gather.29
  874.4 41.2 reduce-scatter.17
  922.7 37.5 reduce-scatter.19
  968.3 123.5 all-reduce.7
  1096.6 64.6 reduce-scatter.23
  1166.5 137.3 reduce-scatter.21
  1308.5 137.4 reduce-scatter.25
  1451.5 378.8 reduce-scatter.27
  1835.8 378.8 reduce-scatter.29
  2220.2 378.9 reduce-scatter.31
where the time goes:
time: 2610 us
  waiting for transfers between devices  2250 us (86%)
  matrix products  186 us (7%)
  blocking collectives  68 us (3%)
  local copies, waits for them, and re-layouts  47.1 us (2%)
  other arithmetic  39 us (1%)
    reduce_scatter x1, waiting for transfers between devices, local(): lax.psum_scatter(down_wgrad, ('dp', 'ctx'), scatter_dimension=1, tiled=True)  384 us
    reduce_scatter x1, waiting for transfers between devices, local(): lax.psum_scatter(up_wgrad, ('dp', 'ctx'), scatter_dimension=0, tiled=True)  384 us
    reduce_scatter x1, waiting for transfers between devices, local(): lax.psum_scatter(gate_wgrad, ('dp', 'ctx'), scatter_dimension=0, tiled=True)  384 us
    all_gather x2, waiting for transfers between devices, fetch_set(): lax.all_gather(first_item, ('dp', 'ctx'), axis=0, tiled=True)  161 us
    all_gather x2, waiting for transfers between devices, fetch_set(): lax.all_gather(third_item, ('dp', 'ctx'), axis=1, tiled=True)  150 us
    reduce_scatter x1, waiting for transfers between devices, local(): lax.psum_scatter(query_wgrad, ('dp', 'ctx'), scatter_dimension=0, tiled=T...  143 us
    reduce_scatter x1, waiting for transfers between devices, local(): lax.psum_scatter(output_wgrad, ('dp', 'ctx'), scatter_dimension=1, tiled=...  142 us
    all_gather x2, waiting for transfers between devices, fetch_set(): lax.all_gather(second_item, ('dp', 'ctx'), axis=0, tiled=True)  132 us
  transfers between devices with their start and end apart: 23, of which 23 were waited for; matrix products, arithmetic and copies ran while one was open for 6% of the time, Pallas kernels for 0%

commit v1 on v0

v1 whole, which is shorter than its diff:
```python
from functools import partial
import math

import jax
import jax.numpy as jnp
from jax import lax
from jax.sharding import PartitionSpec as P

HD = 256
WINDOW = 2048
LANES = 128
f32 = jnp.float32
bf16 = jnp.bfloat16


def norm_scale(vectors, scale_gain):
    return (
        vectors
        * lax.rsqrt(jnp.mean(vectors * vectors, axis=-1, keepdims=True) + 1e-06)
        * scale_gain
    )


def rotary_tables(positions, head_size):
    quarter = head_size // 4
    frequency = jnp.exp(jnp.arange(quarter, dtype=jnp.float32) * (-math.log(10000.0) / quarter))
    angles = positions.astype(jnp.float32)[:, None] * frequency[None, :]
    return (jnp.cos(angles), jnp.sin(angles))


def rotate(vectors, cosine_table, sine_table, direction):
    quarter = cosine_table.shape[-1]
    lead_part = vectors[..., :quarter]
    trail_part = vectors[..., quarter : 2 * quarter]
    cosine_wide = cosine_table[:, None, :]
    sine_wide = direction * sine_table[:, None, :]
    return jnp.concatenate(
        [
            lead_part * cosine_wide - trail_part * sine_wide,
            trail_part * cosine_wide + lead_part * sine_wide,
            vectors[..., 2 * quarter :],
        ],
        axis=-1,
    )


def bits_of(axis, size):
    masks = []
    while size > 1:
        size //= 2
        masks.append((axis, size))
    return masks


def swap(values, bit):
    axis, mask = bit
    return lax.ppermute(values, axis, [(i, i ^ mask) for i in range(lax.axis_size(axis))])


def digit(bit):
    axis, mask = bit
    return (lax.axis_index(axis) // mask) % 2


def in_order(bit, mine, other):
    one = digit(bit) == 1
    return jnp.where(one, other, mine), jnp.where(one, mine, other)


def halves(values, bit, axis):
    size = values.shape[axis] // 2
    own = digit(bit)
    return (
        lax.dynamic_slice_in_dim(values, own * size, size, axis),
        lax.dynamic_slice_in_dim(values, (1 - own) * size, size, axis),
    )


class Plan:
    def __init__(self, sizes, shared):
        dp = bits_of("dp", sizes["dp"])
        ctx = bits_of("ctx", sizes["ctx"])
        self.sizes = sizes
        self.rows = dp + ctx
        self.ctx = ctx
        self.dp = dp
        self.tensor = bits_of("tensor", sizes["tensor"])[0]
        cut = len(dp) - shared
        self.repeat = dp[:cut]
        self.split = ctx + dp[cut:]
        self.core = ctx[-1]
        self.links = [self.tensor] + ctx[:-1] + dp[cut:]

    def where(self, bit, present):
        return sum(1 for other in self.rows[: self.rows.index(bit)] if other in present)


def spread_in(shard, plan):
    present = []
    for bit in plan.split:
        mine, theirs = halves(shard, bit, shard.ndim - 1)
        place = plan.where(bit, present)
        shard = jnp.stack(in_order(bit, mine, swap(theirs, bit)), axis=place)
        present.append(bit)
    for bit in plan.repeat:
        place = plan.where(bit, present)
        shard = jnp.stack(in_order(bit, shard, swap(shard, bit)), axis=place)
        present.append(bit)
    return shard.reshape(-1, shard.shape[-1])


def spread_out(grad, plan):
    columns = grad.shape[-1]
    grad = grad.reshape((2,) * len(plan.rows) + (-1, columns))
    present = list(plan.rows)
    for bit in plan.repeat:
        place = present.index(bit)
        present.remove(bit)
        mine, theirs = halves(grad, bit, place)
        grad = mine.astype(f32) + swap(theirs.astype(bf16), bit).astype(f32)
        grad = jnp.squeeze(grad, place).astype(bf16)
    for bit in reversed(plan.split):
        place = present.index(bit)
        present.remove(bit)
        mine, theirs = halves(grad, bit, place)
        grad = jnp.concatenate(in_order(bit, mine, swap(theirs, bit)), axis=-1)
        grad = jnp.squeeze(grad, place)
    return grad


def reduce_rows(grad, plan, order, kind=bf16):
    columns = grad.shape[-1]
    grad = grad.reshape((2,) * len(plan.rows) + (-1, columns))
    present = list(plan.rows)
    for bit in order:
        place = present.index(bit)
        present.remove(bit)
        mine, theirs = halves(grad, bit, place)
        grad = mine.astype(f32) + swap(theirs.astype(kind), bit).astype(f32)
        grad = jnp.squeeze(grad, place)
        if present:
            grad = grad.astype(kind)
    return grad


def token_parts(count, plan):
    links = len(plan.links)
    step = 16
    units = count // step
    sizes = [(units // links + (1 if i < units % links else 0)) * step for i in range(links)]
    parts = []
    start = 0
    for i, size in enumerate(sizes):
        if size:
            parts.append((start, size, plan.links[i:] + plan.links[:i]))
            start += size
    return parts


def gather_tokens(local_rows, plan):
    pieces = []
    for start, size, order in token_parts(local_rows.shape[0], plan):
        piece = local_rows[start : start + size]
        for bit in order:
            piece = jnp.concatenate([piece, swap(piece, bit)], axis=0)
        pieces.append(piece)
    chip = jnp.concatenate(pieces, axis=0)
    return jnp.concatenate([chip, swap(chip, plan.core)], axis=0)


def reduce_tokens(partial_rows, plan, count):
    size = partial_rows.shape[0] // 2
    chip = partial_rows[:size].astype(f32) + swap(
        partial_rows[size:].astype(bf16), plan.core
    ).astype(f32)
    chip = chip.astype(bf16)
    pieces = []
    copies = size // count
    for start, size, order in token_parts(count, plan):
        piece = chip[start * copies : (start + size) * copies]
        for bit in reversed(order):
            half = piece.shape[0] // 2
            piece = piece[:half].astype(f32) + swap(piece[half:].astype(bf16), bit).astype(f32)
            if half > size:
                piece = piece.astype(bf16)
        pieces.append(piece)
    return jnp.concatenate(pieces, axis=0)


def gather_rows(values_low, plan):
    return jnp.concatenate(in_order(plan.tensor, values_low, swap(values_low, plan.tensor)), axis=0)


def sum_rows(partial_rows, plan):
    mine, theirs = halves(partial_rows, plan.tensor, 0)
    return mine.astype(f32) + swap(theirs.astype(bf16), plan.tensor).astype(f32)


def local(
    plan,
    block_input,
    segment_ids,
    output_grad,
    attention_gain,
    query_weight,
    keyvalue_weight,
    output_weight,
    output_bias,
    channel_gain,
    gate_weight,
    up_weight,
    down_weight,
    gate_bias,
    up_bias,
    down_bias,
):
    local_in = block_input[0].astype(f32)
    grad_local = output_grad[0]
    tensor_index = lax.axis_index("tensor")
    ctx_index = lax.axis_index("ctx")
    is_key = tensor_index == 0
    shard_rows = attention_gain.shape[0]
    token_count, width = local_in.shape
    ff_half = gate_bias.shape[0]
    blocks = 2 ** len(plan.split)
    block = -(-ff_half // (blocks * LANES)) * LANES
    ff_pad = blocks * block - ff_half

    vectors = jnp.stack([attention_gain, output_bias, channel_gain, down_bias], axis=1)
    vectors = jnp.pad(vectors, ((0, 0), (0, LANES - 4)))
    first = lax.all_gather(
        jnp.concatenate([keyvalue_weight, vectors], axis=1), ("dp", "ctx"), axis=0, tiled=True
    )
    full_keyvalue = first[:, : keyvalue_weight.shape[1]]
    vectors = first[:, keyvalue_weight.shape[1] :].astype(f32)
    gain_one, full_obias, gain_two, full_dbias = (vectors[:, i] for i in range(4))
    full_query = lax.all_gather(query_weight, ("dp", "ctx"), axis=0, tiled=True)
    full_output = lax.all_gather(output_weight.T, ("dp", "ctx"), axis=0, tiled=True)

    pad = ((0, 0), (0, ff_pad))
    full_gate = spread_in(jnp.pad(gate_weight, pad), plan)
    full_up = spread_in(jnp.pad(up_weight, pad), plan)
    full_down = spread_in(jnp.pad(down_weight.T, pad), plan)
    block_index = 0
    for bit in plan.split:
        block_index = block_index * 2 + digit(bit)
    gate_bias_block, up_bias_block = (
        lax.dynamic_slice_in_dim(jnp.pad(item, (0, ff_pad)), block_index * block, block).astype(f32)
        for item in (gate_bias, up_bias)
    )

    normed_local, norm_one_pull = jax.vjp(norm_scale, local_in, gain_one)
    normed = gather_rows(normed_local.astype(bf16), plan)
    row_count = normed.shape[0]
    all_segments = lax.all_gather(segment_ids, "ctx", axis=1, tiled=True)[0]
    length = all_segments.shape[0]
    own_segments = lax.dynamic_slice_in_dim(all_segments, ctx_index * row_count, row_count)
    query_index = ctx_index * row_count + jnp.arange(row_count, dtype=jnp.int32)
    earlier = jnp.sum((all_segments[None, :] < own_segments[:, None]).astype(jnp.int32), axis=1)
    cosine_table, sine_table = rotary_tables(query_index - earlier, HD)
    head_count = full_query.shape[1] // HD
    half_proj = jnp.dot(normed, full_keyvalue, preferred_element_type=f32)
    half_low = jnp.where(
        is_key, rotate(half_proj[:, None, :], cosine_table, sine_table, 1.0)[:, 0], half_proj
    ).astype(bf16)
    keyvalue = jnp.concatenate(in_order(plan.tensor, half_low, swap(half_low, plan.tensor)), axis=1)
    masks = [0]
    for bit in plan.ctx:
        keyvalue = jnp.concatenate([keyvalue, swap(keyvalue, bit)], axis=0)
        masks = masks + [mask ^ bit[1] for mask in masks]
    all_keys = keyvalue[:, :HD]
    all_values = keyvalue[:, HD:]
    key_index = jnp.concatenate(
        [(ctx_index ^ mask) * row_count + jnp.arange(row_count, dtype=jnp.int32) for mask in masks]
    )
    key_segments = jnp.concatenate(
        [
            lax.dynamic_slice_in_dim(all_segments, (ctx_index ^ mask) * row_count, row_count)
            for mask in masks
        ]
    )
    query_proj = jnp.dot(normed, full_query, preferred_element_type=f32)
    queries = (
        rotate(query_proj.reshape(row_count, head_count, HD), cosine_table, sine_table, 1.0)
        * HD ** (-0.5)
    ).astype(bf16)
    allowed = (
        (own_segments[:, None] == key_segments[None, :])
        & (key_index[None, :] <= query_index[:, None])
        & (query_index[:, None] - key_index[None, :] < WINDOW)
    )
    scores = jnp.einsum("qhd,kd->hqk", queries, all_keys, preferred_element_type=f32)
    scores = jnp.where(allowed[None], scores, -1e30)
    score_peak = jnp.max(scores, axis=-1, keepdims=True)
    exp_scores = jnp.exp(scores - score_peak)
    exp_total = jnp.sum(exp_scores, axis=-1, keepdims=True)
    probs = exp_scores / exp_total
    probs_low = probs.astype(bf16)
    context = jnp.einsum("hqk,kd->qhd", probs_low, all_values, preferred_element_type=f32)
    context = context.astype(bf16).reshape(row_count, head_count * HD)
    attended = jnp.einsum("rc,dc->rd", context, full_output, preferred_element_type=f32)
    mixed = local_in + sum_rows(attended, plan) + full_obias

    grad_full = grad_local.astype(f32)
    dbias_part = jnp.sum(grad_full, axis=0)
    grad_rows = gather_tokens(grad_local, plan)
    hidden_grad = jnp.dot(grad_rows, full_down, preferred_element_type=f32)
    normed_two_local, norm_two_pull = jax.vjp(norm_scale, mixed, gain_two)
    normed_two = gather_tokens(normed_two_local.astype(bf16), plan)
    gate_pre = jnp.dot(normed_two, full_gate, preferred_element_type=f32) + gate_bias_block
    up_pre = jnp.dot(normed_two, full_up, preferred_element_type=f32) + up_bias_block
    activated, gelu_pull = jax.vjp(partial(jax.nn.gelu, approximate=True), gate_pre)
    hidden = (activated * up_pre).astype(bf16)
    gate_grad_full = gelu_pull(hidden_grad * up_pre)[0]
    up_grad_full = hidden_grad * activated
    gbias_part = jnp.sum(gate_grad_full, axis=0)
    ubias_part = jnp.sum(up_grad_full, axis=0)
    gate_grad = gate_grad_full.astype(bf16)
    up_grad = up_grad_full.astype(bf16)
    two_part = jnp.einsum(
        "rf,df->rd", gate_grad, full_gate, preferred_element_type=f32
    ) + jnp.einsum("rf,df->rd", up_grad, full_up, preferred_element_type=f32)
    two_grad = reduce_tokens(two_part.astype(bf16), plan, token_count)
    out_part = jnp.einsum("rf,df->rd", hidden, full_down, preferred_element_type=f32)
    block_output = (
        mixed + reduce_tokens(out_part.astype(bf16), plan, token_count) + full_dbias
    ).astype(bf16)
    ff_grads = []
    for rows, branch in ((grad_rows, hidden), (normed_two, gate_grad), (normed_two, up_grad)):
        weight_grad = jnp.einsum("rd,rf->df", rows, branch, preferred_element_type=f32)
        ff_grads.append(spread_out(weight_grad.astype(bf16), plan)[:, :ff_half].astype(f32))
    down_out, gate_out, up_out = ff_grads

    mixed_part, gain_two_part = norm_two_pull(two_grad)
    mixed_grad = grad_full + mixed_part
    obias_part = jnp.sum(mixed_grad, axis=0)
    attn_rows = gather_rows(mixed_grad.astype(bf16), plan)
    order = plan.ctx[::-1] + plan.dp[::-1]
    output_wgrad = jnp.einsum("rd,rc->dc", attn_rows, context, preferred_element_type=f32)
    proj_out = reduce_rows(output_wgrad.astype(bf16), plan, order)
    context_grad = jnp.dot(attn_rows, full_output, preferred_element_type=f32).astype(bf16)
    context_grad = context_grad.reshape(row_count, head_count, HD)
    probs_grad = jnp.einsum("qhd,kd->hqk", context_grad, all_values, preferred_element_type=f32)
    values_grad = jnp.einsum("hqk,qhd->kd", probs_low, context_grad, preferred_element_type=f32)
    prob_dot = jnp.sum(probs * probs_grad, axis=-1, keepdims=True)
    score_grad = (probs * (probs_grad - prob_dot)).astype(bf16)
    query_grad = jnp.einsum("hqk,kd->qhd", score_grad, all_keys, preferred_element_type=f32)
    keys_grad = jnp.einsum("hqk,qhd->kd", score_grad, queries, preferred_element_type=f32)
    stacked = jnp.concatenate([keys_grad, values_grad], axis=1)
    for bit in reversed(plan.ctx):
        half = stacked.shape[0] // 2
        stacked = stacked[:half] + swap(stacked[half:].astype(bf16), bit).astype(f32)
    mine, theirs = halves(stacked, plan.tensor, 1)
    half_grad = mine + swap(theirs.astype(bf16), plan.tensor).astype(f32)
    half_grad = jnp.where(
        is_key, rotate(half_grad[:, None, :], cosine_table, sine_table, -1.0)[:, 0], half_grad
    ).astype(bf16)
    query_proj_grad = rotate(query_grad * HD ** (-0.5), cosine_table, sine_table, -1.0)
    query_proj_grad = query_proj_grad.reshape(row_count, head_count * HD).astype(bf16)
    query_wgrad = jnp.einsum("rd,rc->dc", normed, query_proj_grad, preferred_element_type=f32)
    query_out = reduce_rows(query_wgrad.astype(bf16), plan, order)
    keyvalue_wgrad = jnp.einsum("rd,rc->dc", normed, half_grad, preferred_element_type=f32)
    keyvalue_out = reduce_rows(keyvalue_wgrad.astype(bf16), plan, order)
    one_part = jnp.einsum(
        "rc,dc->rd", query_proj_grad, full_query, preferred_element_type=f32
    ) + jnp.einsum("rc,dc->rd", half_grad, full_keyvalue, preferred_element_type=f32)
    input_part, gain_one_part = norm_one_pull(sum_rows(one_part, plan))
    input_grad = mixed_grad + input_part

    small = jnp.stack([gain_one_part, gain_two_part, obias_part, dbias_part], axis=0)
    small = small.reshape(4, -1, shard_rows).transpose(1, 0, 2)
    small = small + swap(small, plan.tensor)
    small = reduce_rows(small.reshape(-1, shard_rows), plan, order, f32)
    ff_small = jnp.stack([gbias_part, ubias_part], axis=0)
    for bit in plan.repeat:
        ff_small = ff_small + swap(ff_small, bit)
    for bit in reversed(plan.split):
        ff_small = jnp.concatenate(in_order(bit, ff_small, swap(ff_small, bit)), axis=1)
    return (
        block_output[None],
        input_grad[None],
        small[0],
        query_out,
        keyvalue_out,
        proj_out.T,
        small[2],
        small[1],
        gate_out,
        up_out,
        down_out.T,
        ff_small[0, :ff_half],
        ff_small[1, :ff_half],
        small[3],
    )


SHARED = 1


def solution(mesh):
    plan = Plan(dict(mesh.shape), SHARED)
    rows = P("dp", ("ctx", "tensor"), None)
    vector = P(("dp", "ctx"))
    wide = P(("dp", "ctx"), "tensor")
    tall = P("tensor", ("dp", "ctx"))
    units = P("tensor")
    return jax.shard_map(
        partial(local, plan),
        mesh=mesh,
        in_specs=(
            rows,
            P("dp", "ctx"),
            rows,
            vector,
            wide,
            wide,
            tall,
            vector,
            vector,
            wide,
            wide,
            tall,
            units,
            units,
            vector,
        ),
        out_specs=(
            rows,
            rows,
            vector,
            wide,
            wide,
            tall,
            vector,
            vector,
            wide,
            wide,
            tall,
            units,
            units,
            vector,
        ),
        check_vma=False,
    )
```

time: 2610 us -> 1260 us (0.48)
  waiting for transfers between devices: 2250 us -> 809 us
  starting transfers between devices: 2.15 us -> 85.2 us
  matrix products: 186 us -> 131 us
  other arithmetic: 39 us -> 84.4 us
  local copies, waits for them, and re-layouts: 47.1 us -> 86.6 us
  blocking collectives: 68 us -> 34.9 us
    reduce_scatter x11 -> x0, waiting for transfers between devices: 1660 us -> none  [the longest x1 384 us: local(): lax.psum_scatter(down_wgrad, ('dp', 'ctx'), scatter_dimension=1, tiled=True)]
    ppermute x0 -> x95, waiting for transfers between devices: none -> 767 us  [swap(): lax.ppermute(values, axis, [(i, i ^ mask) for i in range(lax.axis_size(ax...]
    all_gather x11 -> x3, waiting for transfers between devices: 528 us -> 41.4 us  [the longest x1 40.4 us: local(): lax.all_gather(output_weight.T, ('dp', 'ctx'), axis=0, tiled=True)]
    ppermute x0 -> x95, starting transfers between devices: none -> 85.1 us  [swap(): lax.ppermute(values, axis, [(i, i ^ mask) for i in range(lax.axis_size(ax...]
    unnamed x1 -> x0, blocking collectives: 62.9 us -> none
    psum x1 -> x0, waiting for transfers between devices: 54.4 us -> none  [local(): lax.psum((gain_one_part, gain_two_part, obias_part, dbias_part, gate_full...]
    dot_general x15, matrix products: 158 us -> 109 us  [the longest x3 29.5 us: local(): jnp.einsum('rd,rf->df', rows, branch, preferred_element_type=f32)]
    all_gather x1, blocking collectives: 5.07 us -> 34.9 us  [local(): all_segments = lax.all_gather(segment_ids, 'ctx', axis=1, tiled=True)[0]]
  transfers between devices with their start and end apart: 23 -> 98, of which waited for: 23 -> 59; matrix products, arithmetic and copies ran while one was open for 6% -> 16% of each run, Pallas kernels for 0% -> 0%
where the time goes in v1:
time: 1260 us; the launch traced here: 1250 us
  waiting for transfers between devices  809 us (64%)
  matrix products  131 us (10%)
  local copies, waits for them, and re-layouts  86.6 us (7%)
  starting transfers between devices  85.2 us (7%)
  other arithmetic  84.4 us (7%)
  blocking collectives  34.9 us (3%)
  between operations  16.6 us (1%)
    ppermute x95, waiting for transfers between devices, swap(): lax.ppermute(values, axis, [(i, i ^ mask) for i in range(lax.axis_size(ax...  767 us
    ppermute x95, starting transfers between devices, swap(): lax.ppermute(values, axis, [(i, i ^ mask) for i in range(lax.axis_size(ax...  85.1 us
    all_gather x1, waiting for transfers between devices, local(): lax.all_gather(output_weight.T, ('dp', 'ctx'), axis=0, tiled=True)  40.4 us
    unnamed x215, local copies, waits for them, and re-layouts  38.9 us
    all_gather x1, blocking collectives, local(): all_segments = lax.all_gather(segment_ids, 'ctx', axis=1, tiled=True)[0]  34.9 us
    dot_general x3, matrix products, local(): jnp.einsum('rd,rf->df', rows, branch, preferred_element_type=f32)  29.5 us
  transfers between devices with their start and end apart: 98, of which 59 were waited for; matrix products, arithmetic and copies ran while one was open for 16% of the time, Pallas kernels for 0%

profile of v1, /device:TPU:0, one launch (start us, length us, event | category | flops | bytes accessed | tf_op | source)
XLA Modules:
  0.0 1247.1 jit_solution(13728609105828788429)
XLA Ops:
  24.4 34.9 %all_gather.13 = s32[1,1024]{1,0:T(1,128)S(1)} all-gather(s32[1,256]{1,0:T(1,128)S(1)} %copy-done.81), channel_id=1, replica_groups=mesh['dp'=4,'ctx'=4,'tensor'=2] {'ctx'}, dimensions={1}, use_global_device_ids=true | all-gather | bytes 5120 | tf_op jit(solution)/shard_map/all_gather | solution.py:255
  76.0 15.4 %collective-permute-done = bf16[128,2560]{1,0:T(8,128)(2,1)S(1)} collective-permute-done((bf16[128,2560]{1,0:T(8,128)(2,1)S(1)}, bf16[128,2560]{1,0:T(8,128)(2,1)S(1)}, u32[]{:S(2)}, u32[]{:S(2)}) %collective-permute-start) | collective-permute-done | bytes 655392 | tf_op jit(solution)/shard_map/ppermute | solution.py:57
  104.4 36.7 %collective-permute-done.2 = bf16[256,512]{0,1:T(8,128)(2,1)S(1)} collective-permute-done((bf16[256,512]{0,1:T(8,128)(2,1)S(1)}, bf16[256,512]{0,1:T(8,128)(2,1)S(1)}, u32[]{:S(2)}, u32[]{:S(2)}) %collective-permute-start.2) | collective-permute-done | bytes 262176 | tf_op jit(solution)/shard_map/ppermute | solution.py:57
  146.7 6.0 fusion.120
  170.6 40.4 %all-gather.8.cloned.1.call-done = bf16[2560,1280]{1,0:T(8,128)(2,1)} async-done(((bf16[160,1280]{1,0:T(8,128)(2,1)}), bf16[2560,1280]{1,0:T(8,128)(2,1)}) %all-gather.8.cloned.1.call-update) | async-done | bytes 6553616 | tf_op jit(solution)/shard_map/all_gather | solution.py:238
  211.0 5.0 fusion.132
  219.9 13.3 %collective-permute-done.4 = bf16[128,2560]{1,0:T(8,128)(2,1)S(1)} collective-permute-done((bf16[128,2560]{1,0:T(8,128)(2,1)S(1)}, bf16[128,2560]{1,0:T(8,128)(2,1)S(1)}, u32[]{:S(2)}, u32[]{:S(2)}) %collective-permute-start.4) | collective-permute-done | bytes 655392 | tf_op jit(solution)/shard_map/ppermute | solution.py:57
  236.4 19.8 %collective-permute-done.39 = bf16[192,2560]{1,0:T(8,128)(2,1)S(1)} collective-permute-done((bf16[192,2560]{1,0:T(8,128)(2,1)S(1)}, bf16[192,2560]{1,0:T(8,128)(2,1)S(1)}, u32[]{:S(2)}, u32[]{:S(2)}) %collective-permute-start.39) | collective-permute-done | bytes 983072 | tf_op jit(solution)/shard_map/ppermute | solution.py:57
  265.0 8.5 collective-permute-done.6
  278.7 15.2 %collective-permute-done.7 = bf16[192,2560]{1,0:T(8,128)(2,1)S(1)} collective-permute-done((bf16[192,2560]{1,0:T(8,128)(2,1)S(1)}, bf16[192,2560]{1,0:T(8,128)(2,1)S(1)}, u32[]{:S(2)}, u32[]{:S(2)}) %collective-permute-start.7) | collective-permute-done | bytes 983072 | tf_op jit(solution)/shard_map/ppermute | solution.py:57
  297.2 16.1 %collective-permute-done.42 = bf16[192,2560]{1,0:T(8,128)(2,1)S(1)} collective-permute-done((bf16[192,2560]{1,0:T(8,128)(2,1)S(1)}, bf16[192,2560]{1,0:T(8,128)(2,1)S(1)}, u32[]{:S(2)}, u32[]{:S(2)}) %collective-permute-start.42) | collective-permute-done | bytes 983072 | tf_op jit(solution)/shard_map/ppermute | solution.py:57
  315.4 4.2 collective-permute-done.8
  321.8 6.7 collective-permute-done.9
  333.4 11.7 collective-permute-done.10
  361.5 11.9 collective-permute-done.13
  385.8 11.7 collective-permute-done.25
  400.8 35.3 %collective-permute-done.21 = bf16[2,2,160,512]{3,2,0,1:T(8,128)(2,1)S(1)} collective-permute-done((bf16[2,2,160,512]{3,2,0,1:T(8,128)(2,1)S(1)}, bf16[2,2,160,512]{3,2,0,1:T(8,128)(2,1)S(1)}, u32[]{:S(2)}, u32[]{:S(2)}) %collective-permute-start.21) | collective-permute-done | bytes 655392 | tf_op jit(solution)/shard_map/ppermute | solution.py:57
  437.6 12.1 collective-permute-done.17
  452.9 63.2 %collective-permute-done.26 = bf16[2,2,2,160,512]{4,3,1,2,0:T(8,128)(2,1)} collective-permute-done((bf16[2,2,2,160,512]{4,3,1,2,0:T(8,128)(2,1)}, bf16[2,2,2,160,512]{4,3,1,2,0:T(8,128)(2,1)}, u32[]{:S(2)}, u32[]{:S(2)}) %collective-permute-start.26) | collective-permute-done | bytes 1310752 | tf_op jit(solution)/shard_map/ppermute | solution.py:57
  518.0 26.2 %collective-permute-done.22 = bf16[2,2,2,160,512]{4,3,1,2,0:T(8,128)(2,1)} collective-permute-done((bf16[2,2,2,160,512]{4,3,1,2,0:T(8,128)(2,1)}, bf16[2,2,2,160,512]{4,3,1,2,0:T(8,128)(2,1)}, u32[]{:S(2)}, u32[]{:S(2)}) %collective-permute-start.22) | collective-permute-done | bytes 1310752 | tf_op jit(solution)/shard_map/ppermute | solution.py:57
  546.1 24.4 %collective-permute-done.18 = bf16[2,2,2,160,512]{4,3,2,1,0:T(8,128)(2,1)} collective-permute-done((bf16[2,2,2,160,512]{4,3,2,1,0:T(8,128)(2,1)}, bf16[2,2,2,160,512]{4,3,2,1,0:T(8,128)(2,1)}, u32[]{:S(2)}, u32[]{:S(2)}) %collective-permute-start.18) | collective-permute-done | bytes 1310752 | tf_op jit(solution)/shard_map/ppermute | solution.py:57
  572.3 5.2 constant_dynamic-update-slice_fusion.37
  577.5 5.3 constant_dynamic-update-slice_fusion.12
  582.9 9.3 fusion.134
  592.3 7.1 fusion.133
  599.3 12.4 multiply_reduce_fusion
  611.7 9.1 convolution_convert_fusion.3
  620.8 5.9 convolution_convert_fusion.2
  626.7 12.1 convolution_convert_fusion.5
  638.8 10.0 fusion.40
  648.9 8.3 convolution_convert_fusion.4
  665.2 25.9 %collective-permute-done.92 = f32[2,512]{1,0:T(2,128)S(1)} collective-permute-done((f32[2,512]{1,0:T(2,128)S(1)}, f32[2,512]{1,0:T(2,128)S(1)}, u32[]{:S(2)}, u32[]{:S(2)}) %collective-permute-start.92) | collective-permute-done | bytes 4128 | tf_op jit(solution)/shard_map/ppermute | solution.py:57
  696.6 13.9 %add_convert_fusion = bf16[2048,2560]{1,0:T(8,128)(2,1)} fusion(f32[2048,2560]{1,0:T(8,128)} %fusion.40, bf16[2048,512]{1,0:T(8,128)(2,1)} %copy-done.86, bf16[2560,512]{1,0:T(8,128)(2,1)} %bitcast.360), kind=kOutput, calls=%fused_computation.1 | convolution fusion | flops 5379194880 | bytes 36175872 | tf_op jit(solution)/shard_map/rf,df->rd/dot_general | solution.py:322
  714.3 60.6 %collective-permute-done.87 = bf16[1,2,2,2,160,512]{5,4,3,2,1,0:T(8,128)(2,1)} collective-permute-done((bf16[1,2,2,2,160,512]{5,4,3,2,1,0:T(8,128)(2,1)}, bf16[1,2,2,2,160,512]{5,4,3,2,1,0:T(8,128)(2,1)}, u32[]{:S(2)}, u32[]{:S(2)}) %collective-permute-start.87) | collective-permute-done | bytes 1310752 | tf_op jit(solution)/shard_map/ppermute | solution.py:57
  776.7 26.4 %collective-permute-done.83 = bf16[1,2,2,2,160,512]{5,4,3,2,1,0:T(8,128)(2,1)} collective-permute-done((bf16[1,2,2,2,160,512]{5,4,3,2,1,0:T(8,128)(2,1)}, bf16[1,2,2,2,160,512]{5,4,3,2,1,0:T(8,128)(2,1)}, u32[]{:S(2)}, u32[]{:S(2)}) %collective-permute-start.83) | collective-permute-done | bytes 1310752 | tf_op jit(solution)/shard_map/ppermute | solution.py:57
  804.9 24.5 %collective-permute-done.79 = bf16[1,2,2,2,160,512]{5,4,3,2,1,0:T(8,128)(2,1)} collective-permute-done((bf16[1,2,2,2,160,512]{5,4,3,2,1,0:T(8,128)(2,1)}, bf16[1,2,2,2,160,512]{5,4,3,2,1,0:T(8,128)(2,1)}, u32[]{:S(2)}, u32[]{:S(2)}) %collective-permute-start.79) | collective-permute-done | bytes 1310752 | tf_op jit(solution)/shard_map/ppermute | solution.py:57
  831.3 12.1 collective-permute-done.88
  843.6 13.8 %collective-permute-done.84 = bf16[1,2,2,160,512]{4,3,2,1,0:T(8,128)(2,1)S(1)} collective-permute-done((bf16[1,2,2,160,512]{4,3,2,1,0:T(8,128)(2,1)S(1)}, bf16[1,2,2,160,512]{4,3,2,1,0:T(8,128)(2,1)S(1)}, u32[]{:S(2)}, u32[]{:S(2)}) %collective-permute-start.84) | collective-permute-done | bytes 655392 | tf_op jit(solution)/shard_map/ppermute | solution.py:57
  857.7 13.7 %collective-permute-done.80 = bf16[1,2,2,160,512]{4,3,2,1,0:T(8,128)(2,1)S(1)} collective-permute-done((bf16[1,2,2,160,512]{4,3,2,1,0:T(8,128)(2,1)S(1)}, bf16[1,2,2,160,512]{4,3,2,1,0:T(8,128)(2,1)S(1)}, u32[]{:S(2)}, u32[]{:S(2)}) %collective-permute-start.80) | collective-permute-done | bytes 655392 | tf_op jit(solution)/shard_map/ppermute | solution.py:57
  875.6 14.0 %collective-permute-done.90 = bf16[1,160,2048]{2,1,0:T(8,128)(2,1)S(1)} collective-permute-done((bf16[1,160,2048]{2,1,0:T(8,128)(2,1)S(1)}, bf16[1,160,2048]{2,1,0:T(8,128)(2,1)S(1)}, u32[]{:S(2)}, u32[]{:S(2)}) %collective-permute-start.90) | collective-permute-done | bytes 655392 | tf_op jit(solution)/shard_map/ppermute | solution.py:57
  890.0 13.7 %collective-permute-done.86 = bf16[1,160,2048]{2,1,0:T(8,128)(2,1)S(1)} collective-permute-done((bf16[1,160,2048]{2,1,0:T(8,128)(2,1)S(1)}, bf16[1,160,2048]{2,1,0:T(8,128)(2,1)S(1)}, u32[]{:S(2)}, u32[]{:S(2)}) %collective-permute-start.86) | collective-permute-done | bytes 655392 | tf_op jit(solution)/shard_map/ppermute | solution.py:57
  904.2 13.1 %collective-permute-done.82 = bf16[1,160,2048]{2,1,0:T(8,128)(2,1)S(1)} collective-permute-done((bf16[1,160,2048]{2,1,0:T(8,128)(2,1)S(1)}, bf16[1,160,2048]{2,1,0:T(8,128)(2,1)S(1)}, u32[]{:S(2)}, u32[]{:S(2)}) %collective-permute-start.82) | collective-permute-done | bytes 655392 | tf_op jit(solution)/shard_map/ppermute | solution.py:57
  922.0 5.4 add_convert_fusion.2
  929.7 5.5 add_convert_fusion.1
  938.9 6.4 collective-permute-done.34
  947.1 13.3 %collective-permute-done.54 = bf16[128,2560]{1,0:T(8,128)(2,1)S(1)} collective-permute-done((bf16[128,2560]{1,0:T(8,128)(2,1)S(1)}, bf16[128,2560]{1,0:T(8,128)(2,1)S(1)}, u32[]{:S(2)}, u32[]{:S(2)}) %collective-permute-start.54) | collective-permute-done | bytes 655392 | tf_op jit(solution)/shard_map/ppermute | solution.py:57
  962.1 17.9 %collective-permute-done.35 = bf16[64,2560]{1,0:T(8,128)(2,1)S(1)} collective-permute-done((bf16[64,2560]{1,0:T(8,128)(2,1)S(1)}, bf16[64,2560]{1,0:T(8,128)(2,1)S(1)}, u32[]{:S(2)}, u32[]{:S(2)}) %collective-permute-start.35) | collective-permute-done | bytes 327712 | tf_op jit(solution)/shard_map/ppermute | solution.py:57
  980.7 7.8 collective-permute-done.55
  999.1 6.3 collective-permute-done.29
  1010.4 4.4 collective-permute-done.49
  1029.2 10.5 collective-permute-done.57
  1039.8 4.7 convolution_convert_fusion
  1044.5 4.7 convolution_convert_fusion.7
  1049.5 3.5 convolution_bitcast_fusion
  1053.0 3.5 fusion.1
  1066.5 7.6 collective-permute-done.59
  1081.2 4.7 convolution_convert_fusion.1
  1087.5 8.6 collective-permute-done.61
  1097.3 5.1 constant_dynamic-slice_fusion.8
  1132.4 4.5 collective-permute-done.73
  1138.5 25.7 %collective-permute-done.76 = bf16[2,2,1,160,1280]{4,3,0,2,1:T(8,128)(2,1)S(1)} collective-permute-done((bf16[2,2,1,160,1280]{4,3,0,2,1:T(8,128)(2,1)S(1)}, bf16[2,2,1,160,1280]{4,3,0,2,1:T(8,128)(2,1)S(1)}, u32[]{:S(2)}, u32[]{:S(2)}) %collective-permute-start.76) | collective-permute-done | bytes 1638432 | tf_op jit(solution)/shard_map/ppermute | solution.py:57
  1165.8 29.5 %collective-permute-done.68 = bf16[2,2,1,160,1280]{4,3,0,2,1:T(8,128)(2,1)S(1)} collective-permute-done((bf16[2,2,1,160,1280]{4,3,0,2,1:T(8,128)(2,1)S(1)}, bf16[2,2,1,160,1280]{4,3,0,2,1:T(8,128)(2,1)S(1)}, u32[]{:S(2)}, u32[]{:S(2)}) %collective-permute-start.68) | collective-permute-done | bytes 1638432 | tf_op jit(solution)/shard_map/ppermute | solution.py:57
  1199.3 21.6 %collective-permute-done.69 = bf16[2,1,160,1280]{3,2,1,0:T(8,128)(2,1)S(1)} collective-permute-done((bf16[2,1,160,1280]{3,2,1,0:T(8,128)(2,1)S(1)}, bf16[2,1,160,1280]{3,2,1,0:T(8,128)(2,1)S(1)}, u32[]{:S(2)}, u32[]{:S(2)}) %collective-permute-start.69) | collective-permute-done | bytes 819232 | tf_op jit(solution)/shard_map/ppermute | solution.py:57
  1222.3 17.1 %collective-permute-done.70 = bf16[1,160,1280]{2,1,0:T(8,128)(2,1)S(1)} collective-permute-done((bf16[1,160,1280]{2,1,0:T(8,128)(2,1)S(1)}, bf16[1,160,1280]{2,1,0:T(8,128)(2,1)S(1)}, u32[]{:S(2)}, u32[]{:S(2)}) %collective-permute-start.70) | collective-permute-done | bytes 409632 | tf_op jit(solution)/shard_map/ppermute | solution.py:57
  (602 shorter events, 277.3 us)
Async XLA Ops:
  7.2 62.6 %all-gather.4.cloned.1.call-start = ((), (), s32[]{:S(2)}) async-start(), calls=%async_computation | async-start | bytes 2088960 | tf_op jit(solution)/shard_map/all_gather | solution.py:231
  11.7 135.0 %all-gather.6.cloned.1.call-start = ((), (), s32[]{:S(2)}) async-start(), calls=%async_computation.1 | async-start | bytes 6963200 | tf_op jit(solution)/shard_map/all_gather | solution.py:237
  12.5 198.6 %all-gather.8.cloned.1.call-start = ((), (), s32[]{:S(2)}) async-start(), calls=%async_computation.2 | async-start | bytes 6963200 | tf_op jit(solution)/shard_map/all_gather | solution.py:238
  14.6 85.9 %collective-permute-start.19 = (bf16[160,2048]{1,0:T(8,128)(2,1)}, bf16[160,2048]{1,0:T(8,128)(2,1)}, u32[]{:S(2)}, u32[]{:S(2)}) collective-permute-start(bf16[160,2048]{1,0:T(8,128)(2,1)} %pad_dynamic-slice_fusion.51), channel_id=1, source_target_pairs={{0,4},{2,6},{4,0},{6,2},{1,5},{3,7},{5,1},{7,3},{8,12},{10,14},{12... | collective-permute-start | bytes 1966088 | tf_op jit(solution)/shard_map/ppermute | solution.py:57
  18.5 83.6 %collective-permute-start.23 = (bf16[160,2048]{1,0:T(8,128)(2,1)}, bf16[160,2048]{1,0:T(8,128)(2,1)}, u32[]{:S(2)}, u32[]{:S(2)}) collective-permute-start(bf16[160,2048]{1,0:T(8,128)(2,1)} %pad_dynamic-slice_fusion.49), channel_id=1, source_target_pairs={{0,4},{2,6},{4,0},{6,2},{1,5},{3,7},{5,1},{7,3},{8,12},{10,14},{12... | collective-permute-start | bytes 1966088 | tf_op jit(solution)/shard_map/ppermute | solution.py:57
  18.6 48.9 %collective-permute-start.37 = (bf16[48,2560]{1,0:T(8,128)(2,1)S(1)}, bf16[48,2560]{1,0:T(8,128)(2,1)S(1)}, u32[]{:S(2)}, u32[]{:S(2)}) collective-permute-start(bf16[48,2560]{1,0:T(8,128)(2,1)S(1)} %get-tuple-element.118), channel_id=1, source_target_pairs={{0,1},{1,0},{2,3},{3,2},{4,5},{5,4},{6,7},{7,6},{8,9},{9,8},{10,11... | collective-permute-start | bytes 737288 | tf_op jit(solution)/shard_map/ppermute | solution.py:57
  20.6 53.2 %collective-permute-start.40 = (bf16[48,2560]{1,0:T(8,128)(2,1)S(1)}, bf16[48,2560]{1,0:T(8,128)(2,1)S(1)}, u32[]{:S(2)}, u32[]{:S(2)}) collective-permute-start(bf16[48,2560]{1,0:T(8,128)(2,1)S(1)} %get-tuple-element.117), channel_id=1, source_target_pairs={{0,4},{2,6},{4,0},{6,2},{1,5},{3,7},{5,1},{7,3},{8,12},{10,14},{12... | collective-permute-start | bytes 737288 | tf_op jit(solution)/shard_map/ppermute | solution.py:57
  22.8 41.1 %collective-permute-start.43 = (bf16[32,2560]{1,0:T(8,128)(2,1)}, bf16[32,2560]{1,0:T(8,128)(2,1)}, u32[]{:S(2)}, u32[]{:S(2)}) collective-permute-start(bf16[32,2560]{1,0:T(8,128)(2,1)} %slice_bitcast_fusion.8), channel_id=1, source_target_pairs={{0,8},{8,0},{16,24},{24,16},{1,9},{9,1},{17,25},{25,17},{2,10},{10... | collective-permute-start | bytes 491528 | tf_op jit(solution)/shard_map/ppermute | solution.py:57
  64.0 310.3 %collective-permute-start.15 = (bf16[160,2048]{1,0:T(8,128)(2,1)}, bf16[160,2048]{1,0:T(8,128)(2,1)}, u32[]{:S(2)}, u32[]{:S(2)}) collective-permute-start(bf16[160,2048]{1,0:T(8,128)(2,1)} %pad_dynamic-slice_fusion.53), channel_id=1, source_target_pairs={{0,4},{2,6},{4,0},{6,2},{1,5},{3,7},{5,1},{7,3},{8,12},{10,14},{12... | collective-permute-start | bytes 1966088 | tf_op jit(solution)/shard_map/ppermute | solution.py:57
  67.5 26.1 %collective-permute-start.44 = (bf16[64,2560]{1,0:T(8,128)(2,1)}, bf16[64,2560]{1,0:T(8,128)(2,1)S(1)}, u32[]{:S(2)}, u32[]{:S(2)}) collective-permute-start(bf16[64,2560]{1,0:T(8,128)(2,1)} %pad_maximum_fusion.26), channel_id=1, source_target_pairs={{0,1},{1,0},{2,3},{3,2},{4,5},{5,4},{6,7},{7,6},{8,9},{9,8},{10,11... | collective-permute-start | bytes 983048 | tf_op jit(solution)/shard_map/ppermute | solution.py:57
  73.8 17.7 %collective-permute-start = (bf16[128,2560]{1,0:T(8,128)(2,1)S(1)}, bf16[128,2560]{1,0:T(8,128)(2,1)S(1)}, u32[]{:S(2)}, u32[]{:S(2)}) collective-permute-start(bf16[128,2560]{1,0:T(8,128)(2,1)S(1)} %fusion.20), channel_id=1, source_target_pairs={{0,1},{1,0},{2,3},{3,2},{4,5},{5,4},{6,7},{7,6},{8,9},{9,8},{10,11... | collective-permute-start | bytes 1966088 | tf_op jit(solution)/shard_map/ppermute | solution.py:57
  91.4 51.6 %collective-permute-start.38 = (bf16[96,2560]{1,0:T(8,128)(2,1)S(1)}, bf16[96,2560]{1,0:T(8,128)(2,1)S(1)}, u32[]{:S(2)}, u32[]{:S(2)}) collective-permute-start(bf16[96,2560]{1,0:T(8,128)(2,1)S(1)} %copy-done.58), channel_id=1, source_target_pairs={{0,4},{2,6},{4,0},{6,2},{1,5},{3,7},{5,1},{7,3},{8,12},{10,14},{12... | collective-permute-start | bytes 1474568 | tf_op jit(solution)/shard_map/ppermute | solution.py:57
  98.7 117.5 %collective-permute-start.41 = (bf16[96,2560]{1,0:T(8,128)(2,1)}, bf16[96,2560]{1,0:T(8,128)(2,1)}, u32[]{:S(2)}, u32[]{:S(2)}) collective-permute-start(bf16[96,2560]{1,0:T(8,128)(2,1)} %pad_maximum_fusion.24), channel_id=1, source_target_pairs={{0,8},{8,0},{16,24},{24,16},{1,9},{9,1},{17,25},{25,17},{2,10},{10... | collective-permute-start | bytes 1474568 | tf_op jit(solution)/shard_map/ppermute | solution.py:57
  100.5 253.3 %collective-permute-start.45 = (bf16[128,2560]{1,0:T(8,128)(2,1)}, bf16[128,2560]{1,0:T(8,128)(2,1)}, u32[]{:S(2)}, u32[]{:S(2)}) collective-permute-start(bf16[128,2560]{1,0:T(8,128)(2,1)} %pad_maximum_fusion.18), channel_id=1, source_target_pairs={{0,4},{2,6},{4,0},{6,2},{1,5},{3,7},{5,1},{7,3},{8,12},{10,14},{12... | collective-permute-start | bytes 1966088 | tf_op jit(solution)/shard_map/ppermute | solution.py:57
  102.1 39.0 %collective-permute-start.2 = (bf16[256,512]{0,1:T(8,128)(2,1)S(1)}, bf16[256,512]{0,1:T(8,128)(2,1)S(1)}, u32[]{:S(2)}, u32[]{:S(2)}) collective-permute-start(bf16[256,512]{0,1:T(8,128)(2,1)S(1)} %pad_maximum_fusion.27), channel_id=1, source_target_pairs={{0,4},{2,6},{4,0},{6,2},{1,5},{3,7},{5,1},{7,3},{8,12},{10,14},{12... | collective-permute-start | bytes 786440 | tf_op jit(solution)/shard_map/ppermute | solution.py:57
  143.0 235.3 %collective-permute-start.24 = (bf16[2,160,1024]{2,1,0:T(8,128)(2,1)}, bf16[2,160,1024]{2,1,0:T(8,128)(2,1)}, u32[]{:S(2)}, u32[]{:S(2)}) collective-permute-start(bf16[2,160,1024]{2,1,0:T(8,128)(2,1)} %fusion.73), channel_id=1, source_target_pairs={{0,2},{2,0},{4,6},{6,4},{1,3},{3,1},{5,7},{7,5},{8,10},{10,8},{12,... | collective-permute-start | bytes 1966088 | tf_op jit(solution)/shard_map/ppermute | solution.py:57
  144.6 236.7 %collective-permute-start.20 = (bf16[2,160,1024]{2,1,0:T(8,128)(2,1)}, bf16[2,160,1024]{2,1,0:T(8,128)(2,1)}, u32[]{:S(2)}, u32[]{:S(2)}) collective-permute-start(bf16[2,160,1024]{2,1,0:T(8,128)(2,1)} %fusion.77), channel_id=1, source_target_pairs={{0,2},{2,0},{4,6},{6,4},{1,3},{3,1},{5,7},{7,5},{8,10},{10,8},{12,... | collective-permute-start | bytes 1966088 | tf_op jit(solution)/shard_map/ppermute | solution.py:57
  216.2 17.0 %collective-permute-start.4 = (bf16[128,2560]{1,0:T(8,128)(2,1)S(1)}, bf16[128,2560]{1,0:T(8,128)(2,1)S(1)}, u32[]{:S(2)}, u32[]{:S(2)}) collective-permute-start(bf16[128,2560]{1,0:T(8,128)(2,1)S(1)} %dynamic-slice_convert_fusion.1), channel_id=1, source_target_pairs={{0,1},{1,0},{2,3},{3,2},{4,5},{5,4},{6,7},{7,6},{8,9},{9,8},{10,11... | collective-permute-start | bytes 1966088 | tf_op jit(solution)/shard_map/ppermute | solution.py:57
  233.2 23.1 %collective-permute-start.39 = (bf16[192,2560]{1,0:T(8,128)(2,1)S(1)}, bf16[192,2560]{1,0:T(8,128)(2,1)S(1)}, u32[]{:S(2)}, u32[]{:S(2)}) collective-permute-start(bf16[192,2560]{1,0:T(8,128)(2,1)S(1)} %copy-done.54), channel_id=1, source_target_pairs={{0,8},{8,0},{16,24},{24,16},{1,9},{9,1},{17,25},{25,17},{2,10},{10... | collective-permute-start | bytes 2949128 | tf_op jit(solution)/shard_map/ppermute | solution.py:57
  273.5 20.4 %collective-permute-start.7 = (bf16[192,2560]{1,0:T(8,128)(2,1)S(1)}, bf16[192,2560]{1,0:T(8,128)(2,1)S(1)}, u32[]{:S(2)}, u32[]{:S(2)}) collective-permute-start(bf16[192,2560]{1,0:T(8,128)(2,1)S(1)} %pad_maximum_fusion.11), channel_id=1, source_target_pairs={{0,8},{8,0},{16,24},{24,16},{1,9},{9,1},{17,25},{25,17},{2,10},{10... | collective-permute-start | bytes 2949128 | tf_op jit(solution)/shard_map/ppermute | solution.py:57
  294.0 19.4 %collective-permute-start.42 = (bf16[192,2560]{1,0:T(8,128)(2,1)S(1)}, bf16[192,2560]{1,0:T(8,128)(2,1)S(1)}, u32[]{:S(2)}, u32[]{:S(2)}) collective-permute-start(bf16[192,2560]{1,0:T(8,128)(2,1)S(1)} %pad_maximum_fusion.14), channel_id=1, source_target_pairs={{0,1},{1,0},{2,3},{3,2},{4,5},{5,4},{6,7},{7,6},{8,9},{9,8},{10,11... | collective-permute-start | bytes 2949128 | tf_op jit(solution)/shard_map/ppermute | solution.py:57
  328.6 16.5 %collective-permute-start.10 = (bf16[192,2560]{1,0:T(8,128)(2,1)S(1)}, bf16[192,2560]{1,0:T(8,128)(2,1)S(1)}, u32[]{:S(2)}, u32[]{:S(2)}) collective-permute-start(bf16[192,2560]{1,0:T(8,128)(2,1)S(1)} %pad_maximum_fusion.12), channel_id=1, source_target_pairs={{0,1},{1,0},{2,3},{3,2},{4,5},{5,4},{6,7},{7,6},{8,9},{9,8},{10,11... | collective-permute-start | bytes 2949128 | tf_op jit(solution)/shard_map/ppermute | solution.py:57
  356.0 216.3 %collective-permute-start.46 = (bf16[1024,2560]{1,0:T(8,128)(2,1)}, bf16[1024,2560]{1,0:T(8,128)(2,1)}, u32[]{:S(2)}, u32[]{:S(2)}) collective-permute-start(bf16[1024,2560]{1,0:T(8,128)(2,1)} %get-tuple-element.109), channel_id=1, source_target_pairs={{0,2},{2,0},{4,6},{6,4},{1,3},{3,1},{5,7},{7,5},{8,10},{10,8},{12,... | collective-permute-start | bytes 15728648 | tf_op jit(solution)/shard_map/ppermute | solution.py:57
  374.2 203.3 %collective-permute-start.14 = (bf16[1024,2560]{1,0:T(8,128)(2,1)}, bf16[1024,2560]{1,0:T(8,128)(2,1)}, u32[]{:S(2)}, u32[]{:S(2)}) collective-permute-start(bf16[1024,2560]{1,0:T(8,128)(2,1)} %get-tuple-element.119), channel_id=1, source_target_pairs={{0,2},{2,0},{4,6},{6,4},{1,3},{3,1},{5,7},{7,5},{8,10},{10,8},{12,... | collective-permute-start | bytes 15728648 | tf_op jit(solution)/shard_map/ppermute | solution.py:57
  379.8 17.6 %collective-permute-start.25 = (bf16[2,2,160,512]{3,2,0,1:T(8,128)(2,1)S(1)}, bf16[2,2,160,512]{3,2,0,1:T(8,128)(2,1)S(1)}, u32[]{:S(2)}, u32[]{:S(2)}) collective-permute-start(bf16[2,2,160,512]{3,2,0,1:T(8,128)(2,1)S(1)} %fusion.71), channel_id=1, source_target_pairs={{0,8},{8,0},{16,24},{24,16},{1,9},{9,1},{17,25},{25,17},{2,10},{10... | collective-permute-start | bytes 1966088 | tf_op jit(solution)/shard_map/ppermute | solution.py:57
  382.8 53.3 %collective-permute-start.21 = (bf16[2,2,160,512]{3,2,0,1:T(8,128)(2,1)S(1)}, bf16[2,2,160,512]{3,2,0,1:T(8,128)(2,1)S(1)}, u32[]{:S(2)}, u32[]{:S(2)}) collective-permute-start(bf16[2,2,160,512]{3,2,0,1:T(8,128)(2,1)S(1)} %fusion.75), channel_id=1, source_target_pairs={{0,8},{8,0},{16,24},{24,16},{1,9},{9,1},{17,25},{25,17},{2,10},{10... | collective-permute-start | bytes 1966088 | tf_op jit(solution)/shard_map/ppermute | solution.py:57
  384.3 65.4 %collective-permute-start.17 = (bf16[2,2,160,512]{3,2,1,0:T(8,128)(2,1)S(1)}, bf16[2,2,160,512]{3,2,1,0:T(8,128)(2,1)S(1)}, u32[]{:S(2)}, u32[]{:S(2)}) collective-permute-start(bf16[2,2,160,512]{3,2,1,0:T(8,128)(2,1)S(1)} %fusion.79), channel_id=1, source_target_pairs={{0,8},{8,0},{16,24},{24,16},{1,9},{9,1},{17,25},{25,17},{2,10},{10... | collective-permute-start | bytes 1966088 | tf_op jit(solution)/shard_map/ppermute | solution.py:57
  398.9 117.2 %collective-permute-start.26 = (bf16[2,2,2,160,512]{4,3,1,2,0:T(8,128)(2,1)}, bf16[2,2,2,160,512]{4,3,1,2,0:T(8,128)(2,1)}, u32[]{:S(2)}, u32[]{:S(2)}) collective-permute-start(bf16[2,2,2,160,512]{4,3,1,2,0:T(8,128)(2,1)} %pad_maximum_fusion.6), channel_id=1, source_target_pairs={{0,16},{8,24},{16,0},{24,8},{1,17},{9,25},{17,1},{25,9},{2,18},{10... | collective-permute-start | bytes 3932168 | tf_op jit(solution)/shard_map/ppermute | solution.py:57
  437.6 106.6 %collective-permute-start.22 = (bf16[2,2,2,160,512]{4,3,1,2,0:T(8,128)(2,1)}, bf16[2,2,2,160,512]{4,3,1,2,0:T(8,128)(2,1)}, u32[]{:S(2)}, u32[]{:S(2)}) collective-permute-start(bf16[2,2,2,160,512]{4,3,1,2,0:T(8,128)(2,1)} %pad_maximum_fusion.5), channel_id=1, source_target_pairs={{0,16},{8,24},{16,0},{24,8},{1,17},{9,25},{17,1},{25,9},{2,18},{10... | collective-permute-start | bytes 3932168 | tf_op jit(solution)/shard_map/ppermute | solution.py:57
  452.0 118.5 %collective-permute-start.18 = (bf16[2,2,2,160,512]{4,3,2,1,0:T(8,128)(2,1)}, bf16[2,2,2,160,512]{4,3,2,1,0:T(8,128)(2,1)}, u32[]{:S(2)}, u32[]{:S(2)}) collective-permute-start(bf16[2,2,2,160,512]{4,3,2,1,0:T(8,128)(2,1)} %pad_maximum_fusion.4), channel_id=1, source_target_pairs={{0,16},{8,24},{16,0},{24,8},{1,17},{9,25},{17,1},{25,9},{2,18},{10... | collective-permute-start | bytes 3932168 | tf_op jit(solution)/shard_map/ppermute | solution.py:57
  658.6 116.3 %collective-permute-start.87 = (bf16[1,2,2,2,160,512]{5,4,3,2,1,0:T(8,128)(2,1)}, bf16[1,2,2,2,160,512]{5,4,3,2,1,0:T(8,128)(2,1)}, u32[]{:S(2)}, u32[]{:S(2)}) collective-permute-start(bf16[1,2,2,2,160,512]{5,4,3,2,1,0:T(8,128)(2,1)} %constant_dynamic-slice_fusion), channel_id=1, source_target_pairs={{0,16},{8,24},{16,0},{24,8},{1,17},{9,25},{17,1},{25,9},{2,18},{10... | collective-permute-start | bytes 3932168 | tf_op jit(solution)/shard_map/ppermute | solution.py:57
  661.5 29.5 %collective-permute-start.92 = (f32[2,512]{1,0:T(2,128)S(1)}, f32[2,512]{1,0:T(2,128)S(1)}, u32[]{:S(2)}, u32[]{:S(2)}) collective-permute-start(f32[2,512]{1,0:T(2,128)S(1)} %fusion.118), channel_id=1, source_target_pairs={{0,8},{8,0},{16,24},{24,16},{1,9},{9,1},{17,25},{25,17},{2,10},{10... | collective-permute-start | bytes 12296 | tf_op jit(solution)/shard_map/ppermute | solution.py:57
  662.7 140.3 %collective-permute-start.83 = (bf16[1,2,2,2,160,512]{5,4,3,2,1,0:T(8,128)(2,1)}, bf16[1,2,2,2,160,512]{5,4,3,2,1,0:T(8,128)(2,1)}, u32[]{:S(2)}, u32[]{:S(2)}) collective-permute-start(bf16[1,2,2,2,160,512]{5,4,3,2,1,0:T(8,128)(2,1)} %constant_dynamic-slice_fusion.1), channel_id=1, source_target_pairs={{0,16},{8,24},{16,0},{24,8},{1,17},{9,25},{17,1},{25,9},{2,18},{10... | collective-permute-start | bytes 3932168 | tf_op jit(solution)/shard_map/ppermute | solution.py:57
  692.4 137.1 %collective-permute-start.79 = (bf16[1,2,2,2,160,512]{5,4,3,2,1,0:T(8,128)(2,1)}, bf16[1,2,2,2,160,512]{5,4,3,2,1,0:T(8,128)(2,1)}, u32[]{:S(2)}, u32[]{:S(2)}) collective-permute-start(bf16[1,2,2,2,160,512]{5,4,3,2,1,0:T(8,128)(2,1)} %constant_dynamic-slice_fusion.2), channel_id=1, source_target_pairs={{0,16},{8,24},{16,0},{24,8},{1,17},{9,25},{17,1},{25,9},{2,18},{10... | collective-permute-start | bytes 3932168 | tf_op jit(solution)/shard_map/ppermute | solution.py:57
  695.6 226.4 %collective-permute-start.27 = (bf16[1024,2560]{1,0:T(8,128)(2,1)S(1)}, bf16[1024,2560]{1,0:T(8,128)(2,1)}, u32[]{:S(2)}, u32[]{:S(2)}) collective-permute-start(bf16[1024,2560]{1,0:T(8,128)(2,1)S(1)} %slice.370), channel_id=1, source_target_pairs={{0,2},{2,0},{4,6},{6,4},{1,3},{3,1},{5,7},{7,5},{8,10},{10,8},{12,... | collective-permute-start | bytes 15728648 | tf_op jit(solution)/shard_map/ppermute | solution.py:57
  695.9 17.5 %collective-permute-start.94 = (f32[2,2048]{1,0:T(2,128)S(1)}, f32[2,2048]{1,0:T(2,128)S(1)}, u32[]{:S(2)}, u32[]{:S(2)}) collective-permute-start(f32[2,2048]{1,0:T(2,128)S(1)} %pad_maximum_fusion.28), channel_id=1, source_target_pairs={{0,4},{2,6},{4,0},{6,2},{1,5},{3,7},{5,1},{7,3},{8,12},{10,14},{12... | collective-permute-start | bytes 49160 | tf_op jit(solution)/shard_map/ppermute | solution.py:57
  713.5 216.2 %collective-permute-start.47 = (bf16[1024,2560]{1,0:T(8,128)(2,1)S(1)}, bf16[1024,2560]{1,0:T(8,128)(2,1)}, u32[]{:S(2)}, u32[]{:S(2)}) collective-permute-start(bf16[1024,2560]{1,0:T(8,128)(2,1)S(1)} %slice.391), channel_id=1, source_target_pairs={{0,2},{2,0},{4,6},{6,4},{1,3},{3,1},{5,7},{7,5},{8,10},{10,8},{12,... | collective-permute-start | bytes 15728648 | tf_op jit(solution)/shard_map/ppermute | solution.py:57
  776.6 66.7 %collective-permute-start.88 = (bf16[1,2,2,160,512]{4,3,2,1,0:T(8,128)(2,1)S(1)}, bf16[1,2,2,160,512]{4,3,2,1,0:T(8,128)(2,1)S(1)}, u32[]{:S(2)}, u32[]{:S(2)}) collective-permute-start(bf16[1,2,2,160,512]{4,3,2,1,0:T(8,128)(2,1)S(1)} %dynamic-slice_bitcast_fusion.4), channel_id=1, source_target_pairs={{0,8},{8,0},{16,24},{24,16},{1,9},{9,1},{17,25},{25,17},{2,10},{10... | collective-permute-start | bytes 1966088 | tf_op jit(solution)/shard_map/ppermute | solution.py:57
  804.8 52.6 %collective-permute-start.84 = (bf16[1,2,2,160,512]{4,3,2,1,0:T(8,128)(2,1)S(1)}, bf16[1,2,2,160,512]{4,3,2,1,0:T(8,128)(2,1)S(1)}, u32[]{:S(2)}, u32[]{:S(2)}) collective-permute-start(bf16[1,2,2,160,512]{4,3,2,1,0:T(8,128)(2,1)S(1)} %dynamic-slice_bitcast_fusion.5), channel_id=1, source_target_pairs={{0,8},{8,0},{16,24},{24,16},{1,9},{9,1},{17,25},{25,17},{2,10},{10... | collective-permute-start | bytes 1966088 | tf_op jit(solution)/shard_map/ppermute | solution.py:57
  831.2 40.1 %collective-permute-start.80 = (bf16[1,2,2,160,512]{4,3,2,1,0:T(8,128)(2,1)S(1)}, bf16[1,2,2,160,512]{4,3,2,1,0:T(8,128)(2,1)S(1)}, u32[]{:S(2)}, u32[]{:S(2)}) collective-permute-start(bf16[1,2,2,160,512]{4,3,2,1,0:T(8,128)(2,1)S(1)} %dynamic-slice_bitcast_fusion.6), channel_id=1, source_target_pairs={{0,8},{8,0},{16,24},{24,16},{1,9},{9,1},{17,25},{25,17},{2,10},{10... | collective-permute-start | bytes 1966088 | tf_op jit(solution)/shard_map/ppermute | solution.py:57
  843.6 28.1 %collective-permute-start.89 = (bf16[2,1,160,1024]{3,2,1,0:T(8,128)(2,1)S(1)}, bf16[2,1,160,1024]{3,2,1,0:T(8,128)(2,1)S(1)}, u32[]{:S(2)}, u32[]{:S(2)}) collective-permute-start(bf16[2,1,160,1024]{3,2,1,0:T(8,128)(2,1)S(1)} %fusion.53), channel_id=1, source_target_pairs={{0,2},{2,0},{4,6},{6,4},{1,3},{3,1},{5,7},{7,5},{8,10},{10,8},{12,... | collective-permute-start | bytes 1966088 | tf_op jit(solution)/shard_map/ppermute | solution.py:57
  872.0 17.6 %collective-permute-start.90 = (bf16[1,160,2048]{2,1,0:T(8,128)(2,1)S(1)}, bf16[1,160,2048]{2,1,0:T(8,128)(2,1)S(1)}, u32[]{:S(2)}, u32[]{:S(2)}) collective-permute-start(bf16[1,160,2048]{2,1,0:T(8,128)(2,1)S(1)} %fusion.49), channel_id=1, source_target_pairs={{0,4},{2,6},{4,0},{6,2},{1,5},{3,7},{5,1},{7,3},{8,12},{10,14},{12... | collective-permute-start | bytes 1966088 | tf_op jit(solution)/shard_map/ppermute | solution.py:57
  873.1 30.6 %collective-permute-start.86 = (bf16[1,160,2048]{2,1,0:T(8,128)(2,1)S(1)}, bf16[1,160,2048]{2,1,0:T(8,128)(2,1)S(1)}, u32[]{:S(2)}, u32[]{:S(2)}) collective-permute-start(bf16[1,160,2048]{2,1,0:T(8,128)(2,1)S(1)} %fusion.57), channel_id=1, source_target_pairs={{0,4},{2,6},{4,0},{6,2},{1,5},{3,7},{5,1},{7,3},{8,12},{10,14},{12... | collective-permute-start | bytes 1966088 | tf_op jit(solution)/shard_map/ppermute | solution.py:57
  875.0 42.3 %collective-permute-start.82 = (bf16[1,160,2048]{2,1,0:T(8,128)(2,1)S(1)}, bf16[1,160,2048]{2,1,0:T(8,128)(2,1)S(1)}, u32[]{:S(2)}, u32[]{:S(2)}) collective-permute-start(bf16[1,160,2048]{2,1,0:T(8,128)(2,1)S(1)} %fusion.65), channel_id=1, source_target_pairs={{0,4},{2,6},{4,0},{6,2},{1,5},{3,7},{5,1},{7,3},{8,12},{10,14},{12... | collective-permute-start | bytes 1966088 | tf_op jit(solution)/shard_map/ppermute | solution.py:57
  928.6 61.4 %collective-permute-start.28 = (bf16[192,2560]{1,0:T(8,128)(2,1)}, bf16[192,2560]{1,0:T(8,128)(2,1)S(1)}, u32[]{:S(2)}, u32[]{:S(2)}) collective-permute-start(bf16[192,2560]{1,0:T(8,128)(2,1)} %get-tuple-element.46), channel_id=1, source_target_pairs={{0,8},{8,0},{16,24},{24,16},{1,9},{9,1},{17,25},{25,17},{2,10},{10... | collective-permute-start | bytes 2949128 | tf_op jit(solution)/shard_map/ppermute | solution.py:57
  928.6 62.1 %collective-permute-start.31 = (bf16[192,2560]{1,0:T(8,128)(2,1)S(1)}, bf16[192,2560]{1,0:T(8,128)(2,1)S(1)}, u32[]{:S(2)}, u32[]{:S(2)}) collective-permute-start(bf16[192,2560]{1,0:T(8,128)(2,1)S(1)} %get-tuple-element.47), channel_id=1, source_target_pairs={{0,1},{1,0},{2,3},{3,2},{4,5},{5,4},{6,7},{7,6},{8,9},{9,8},{10,11... | collective-permute-start | bytes 2949128 | tf_op jit(solution)/shard_map/ppermute | solution.py:57
  929.1 16.2 %collective-permute-start.34 = (bf16[128,2560]{1,0:T(8,128)(2,1)S(1)}, bf16[128,2560]{1,0:T(8,128)(2,1)}, u32[]{:S(2)}, u32[]{:S(2)}) collective-permute-start(bf16[128,2560]{1,0:T(8,128)(2,1)S(1)} %slice.384), channel_id=1, source_target_pairs={{0,4},{2,6},{4,0},{6,2},{1,5},{3,7},{5,1},{7,3},{8,12},{10,14},{12... | collective-permute-start | bytes 1966088 | tf_op jit(solution)/shard_map/ppermute | solution.py:57
  935.4 56.5 %collective-permute-start.48 = (bf16[192,2560]{1,0:T(8,128)(2,1)S(1)}, bf16[192,2560]{1,0:T(8,128)(2,1)S(1)}, u32[]{:S(2)}, u32[]{:S(2)}) collective-permute-start(bf16[192,2560]{1,0:T(8,128)(2,1)S(1)} %get-tuple-element.42), channel_id=1, source_target_pairs={{0,8},{8,0},{16,24},{24,16},{1,9},{9,1},{17,25},{25,17},{2,10},{10... | collective-permute-start | bytes 2949128 | tf_op jit(solution)/shard_map/ppermute | solution.py:57
  937.4 55.9 %collective-permute-start.51 = (bf16[192,2560]{1,0:T(8,128)(2,1)S(1)}, bf16[192,2560]{1,0:T(8,128)(2,1)S(1)}, u32[]{:S(2)}, u32[]{:S(2)}) collective-permute-start(bf16[192,2560]{1,0:T(8,128)(2,1)S(1)} %get-tuple-element.43), channel_id=1, source_target_pairs={{0,1},{1,0},{2,3},{3,2},{4,5},{5,4},{6,7},{7,6},{8,9},{9,8},{10,11... | collective-permute-start | bytes 2949128 | tf_op jit(solution)/shard_map/ppermute | solution.py:57
  960.4 19.6 %collective-permute-start.35 = (bf16[64,2560]{1,0:T(8,128)(2,1)S(1)}, bf16[64,2560]{1,0:T(8,128)(2,1)S(1)}, u32[]{:S(2)}, u32[]{:S(2)}) collective-permute-start(bf16[64,2560]{1,0:T(8,128)(2,1)S(1)} %slice.386), channel_id=1, source_target_pairs={{0,1},{1,0},{2,3},{3,2},{4,5},{5,4},{6,7},{7,6},{8,9},{9,8},{10,11... | collective-permute-start | bytes 983048 | tf_op jit(solution)/shard_map/ppermute | solution.py:57
  991.9 17.8 %collective-permute-start.32 = (bf16[96,2560]{1,0:T(8,128)(2,1)S(1)}, bf16[96,2560]{1,0:T(8,128)(2,1)S(1)}, u32[]{:S(2)}, u32[]{:S(2)}) collective-permute-start(bf16[96,2560]{1,0:T(8,128)(2,1)S(1)} %slice.380), channel_id=1, source_target_pairs={{0,8},{8,0},{16,24},{24,16},{1,9},{9,1},{17,25},{25,17},{2,10},{10... | collective-permute-start | bytes 1474568 | tf_op jit(solution)/shard_map/ppermute | solution.py:57
  993.9 21.0 %collective-permute-start.49 = (bf16[96,2560]{1,0:T(8,128)(2,1)S(1)}, bf16[96,2560]{1,0:T(8,128)(2,1)S(1)}, u32[]{:S(2)}, u32[]{:S(2)}) collective-permute-start(bf16[96,2560]{1,0:T(8,128)(2,1)S(1)} %slice.395), channel_id=1, source_target_pairs={{0,4},{2,6},{4,0},{6,2},{1,5},{3,7},{5,1},{7,3},{8,12},{10,14},{12... | collective-permute-start | bytes 1474568 | tf_op jit(solution)/shard_map/ppermute | solution.py:57
  995.6 21.4 %collective-permute-start.52 = (bf16[96,2560]{1,0:T(8,128)(2,1)S(1)}, bf16[96,2560]{1,0:T(8,128)(2,1)S(1)}, u32[]{:S(2)}, u32[]{:S(2)}) collective-permute-start(bf16[96,2560]{1,0:T(8,128)(2,1)S(1)} %slice.401), channel_id=1, source_target_pairs={{0,8},{8,0},{16,24},{24,16},{1,9},{9,1},{17,25},{25,17},{2,10},{10... | collective-permute-start | bytes 1474568 | tf_op jit(solution)/shard_map/ppermute | solution.py:57
  1064.2 58.2 %collective-permute-start.75 = (bf16[2,2,2,1,160,1280]{5,4,0,1,3,2:T(8,128)(2,1)}, bf16[2,2,2,1,160,1280]{5,4,0,1,3,2:T(8,128)(2,1)}, u32[]{:S(2)}, u32[]{:S(2)}) collective-permute-start(bf16[2,2,2,1,160,1280]{5,4,0,1,3,2:T(8,128)(2,1)} %copy.97), channel_id=1, source_target_pairs={{0,2},{2,0},{4,6},{6,4},{1,3},{3,1},{5,7},{7,5},{8,10},{10,8},{12,... | collective-permute-start | bytes 9830408 | tf_op jit(solution)/shard_map/ppermute | solution.py:57
  1087.5 17.7 %collective-permute-start.71 = (bf16[2,2,2,1,160,256]{5,4,0,1,3,2:T(8,128)(2,1)}, bf16[2,2,2,1,160,256]{5,4,0,1,3,2:T(8,128)(2,1)}, u32[]{:S(2)}, u32[]{:S(2)}) collective-permute-start(bf16[2,2,2,1,160,256]{5,4,0,1,3,2:T(8,128)(2,1)} %copy.95), channel_id=1, source_target_pairs={{0,2},{2,0},{4,6},{6,4},{1,3},{3,1},{5,7},{7,5},{8,10},{10,8},{12,... | collective-permute-start | bytes 1966088 | tf_op jit(solution)/shard_map/ppermute | solution.py:57
  1104.4 21.4 %collective-permute-start.67 = (bf16[2,2,2,1,160,1280]{5,4,0,1,3,2:T(8,128)(2,1)}, bf16[2,2,2,1,160,1280]{5,4,0,1,3,2:T(8,128)(2,1)}, u32[]{:S(2)}, u32[]{:S(2)}) collective-permute-start(bf16[2,2,2,1,160,1280]{5,4,0,1,3,2:T(8,128)(2,1)} %copy.93), channel_id=1, source_target_pairs={{0,2},{2,0},{4,6},{6,4},{1,3},{3,1},{5,7},{7,5},{8,10},{10,8},{12,... | collective-permute-start | bytes 9830408 | tf_op jit(solution)/shard_map/ppermute | solution.py:57
  1110.7 19.9 %collective-permute-start.72 = (bf16[2,2,1,160,256]{4,3,0,2,1:T(8,128)(2,1)S(1)}, bf16[2,2,1,160,256]{4,3,0,2,1:T(8,128)(2,1)S(1)}, u32[]{:S(2)}, u32[]{:S(2)}) collective-permute-start(bf16[2,2,1,160,256]{4,3,0,2,1:T(8,128)(2,1)S(1)} %dynamic-slice_bitcast_fusion.9), channel_id=1, source_target_pairs={{0,4},{2,6},{4,0},{6,2},{1,5},{3,7},{5,1},{7,3},{8,12},{10,14},{12... | collective-permute-start | bytes 983048 | tf_op jit(solution)/shard_map/ppermute | solution.py:57
  1125.4 38.8 %collective-permute-start.76 = (bf16[2,2,1,160,1280]{4,3,0,2,1:T(8,128)(2,1)S(1)}, bf16[2,2,1,160,1280]{4,3,0,2,1:T(8,128)(2,1)S(1)}, u32[]{:S(2)}, u32[]{:S(2)}) collective-permute-start(bf16[2,2,1,160,1280]{4,3,0,2,1:T(8,128)(2,1)S(1)} %dynamic-slice_bitcast_fusion), channel_id=1, source_target_pairs={{0,4},{2,6},{4,0},{6,2},{1,5},{3,7},{5,1},{7,3},{8,12},{10,14},{12... | collective-permute-start | bytes 4915208 | tf_op jit(solution)/shard_map/ppermute | solution.py:57
  1130.1 65.2 %collective-permute-start.68 = (bf16[2,2,1,160,1280]{4,3,0,2,1:T(8,128)(2,1)S(1)}, bf16[2,2,1,160,1280]{4,3,0,2,1:T(8,128)(2,1)S(1)}, u32[]{:S(2)}, u32[]{:S(2)}) collective-permute-start(bf16[2,2,1,160,1280]{4,3,0,2,1:T(8,128)(2,1)S(1)} %dynamic-slice_bitcast_fusion.1), channel_id=1, source_target_pairs={{0,4},{2,6},{4,0},{6,2},{1,5},{3,7},{5,1},{7,3},{8,12},{10,14},{12... | collective-permute-start | bytes 4915208 | tf_op jit(solution)/shard_map/ppermute | solution.py:57
  1137.0 60.0 %collective-permute-start.74 = (bf16[1,160,256]{2,1,0:T(8,128)(2,1)S(1)}, bf16[1,160,256]{2,1,0:T(8,128)(2,1)S(1)}, u32[]{:S(2)}, u32[]{:S(2)}) collective-permute-start(bf16[1,160,256]{2,1,0:T(8,128)(2,1)S(1)} %dynamic-slice_bitcast_fusion.11), channel_id=1, source_target_pairs={{0,16},{8,24},{16,0},{24,8},{1,17},{9,25},{17,1},{25,9},{2,18},{10... | collective-permute-start | bytes 245768 | tf_op jit(solution)/shard_map/ppermute | solution.py:57
  1164.7 33.0 %collective-permute-start.77 = (bf16[2,1,160,1280]{3,2,1,0:T(8,128)(2,1)S(1)}, bf16[2,1,160,1280]{3,2,1,0:T(8,128)(2,1)S(1)}, u32[]{:S(2)}, u32[]{:S(2)}) collective-permute-start(bf16[2,1,160,1280]{3,2,1,0:T(8,128)(2,1)S(1)} %dynamic-slice_bitcast_fusion.2), channel_id=1, source_target_pairs={{0,8},{8,0},{16,24},{24,16},{1,9},{9,1},{17,25},{25,17},{2,10},{10... | collective-permute-start | bytes 2457608 | tf_op jit(solution)/shard_map/ppermute | solution.py:57
  1195.8 25.1 %collective-permute-start.69 = (bf16[2,1,160,1280]{3,2,1,0:T(8,128)(2,1)S(1)}, bf16[2,1,160,1280]{3,2,1,0:T(8,128)(2,1)S(1)}, u32[]{:S(2)}, u32[]{:S(2)}) collective-permute-start(bf16[2,1,160,1280]{3,2,1,0:T(8,128)(2,1)S(1)} %dynamic-slice_bitcast_fusion.3), channel_id=1, source_target_pairs={{0,8},{8,0},{16,24},{24,16},{1,9},{9,1},{17,25},{25,17},{2,10},{10... | collective-permute-start | bytes 2457608 | tf_op jit(solution)/shard_map/ppermute | solution.py:57
  1197.9 23.4 %collective-permute-start.78 = (bf16[1,160,1280]{2,1,0:T(8,128)(2,1)S(1)}, bf16[1,160,1280]{2,1,0:T(8,128)(2,1)S(1)}, u32[]{:S(2)}, u32[]{:S(2)}) collective-permute-start(bf16[1,160,1280]{2,1,0:T(8,128)(2,1)S(1)} %dynamic-slice_bitcast_fusion.7), channel_id=1, source_target_pairs={{0,16},{8,24},{16,0},{24,8},{1,17},{9,25},{17,1},{25,9},{2,18},{10... | collective-permute-start | bytes 1228808 | tf_op jit(solution)/shard_map/ppermute | solution.py:57
  1221.2 18.2 %collective-permute-start.70 = (bf16[1,160,1280]{2,1,0:T(8,128)(2,1)S(1)}, bf16[1,160,1280]{2,1,0:T(8,128)(2,1)S(1)}, u32[]{:S(2)}, u32[]{:S(2)}) collective-permute-start(bf16[1,160,1280]{2,1,0:T(8,128)(2,1)S(1)} %dynamic-slice_bitcast_fusion.8), channel_id=1, source_target_pairs={{0,16},{8,24},{16,0},{24,8},{1,17},{9,25},{17,1},{25,9},{2,18},{10... | collective-permute-start | bytes 1228808 | tf_op jit(solution)/shard_map/ppermute | solution.py:57
  (127 other events, 1747.3 us)
Sparse Core Ops, SparseCore 0:
  11.8 48.6 all-gather.3
  62.7 83.9 all-gather.5
  149.0 61.9 all-gather.7

commit v2 on v1

v2 whole, which is shorter than its diff:
```python
from functools import partial
import math

import jax
import jax.numpy as jnp
from jax import lax
from jax.sharding import Mesh
from jax.sharding import PartitionSpec as P

HD = 256
WINDOW = 2048
LANES = 128
DP = ("far", "near")
CTX = ("y", "core")
DP_CTX = DP + CTX
f32 = jnp.float32
bf16 = jnp.bfloat16


def norm_scale(vectors, scale_gain):
    return (
        vectors
        * lax.rsqrt(jnp.mean(vectors * vectors, axis=-1, keepdims=True) + 1e-06)
        * scale_gain
    )


def rotary_tables(positions, head_size):
    quarter = head_size // 4
    frequency = jnp.exp(jnp.arange(quarter, dtype=jnp.float32) * (-math.log(10000.0) / quarter))
    angles = positions.astype(jnp.float32)[:, None] * frequency[None, :]
    return (jnp.cos(angles), jnp.sin(angles))


def rotate(vectors, cosine_table, sine_table, direction):
    quarter = cosine_table.shape[-1]
    lead_part = vectors[..., :quarter]
    trail_part = vectors[..., quarter : 2 * quarter]
    cosine_wide = cosine_table[:, None, :]
    sine_wide = direction * sine_table[:, None, :]
    return jnp.concatenate(
        [
            lead_part * cosine_wide - trail_part * sine_wide,
            trail_part * cosine_wide + lead_part * sine_wide,
            vectors[..., 2 * quarter :],
        ],
        axis=-1,
    )


def bits_of(axis, size):
    masks = []
    while size > 1:
        size //= 2
        masks.append((axis, size))
    return masks


def swap(values, bit):
    axis, mask = bit
    return lax.ppermute(values, axis, [(i, i ^ mask) for i in range(lax.axis_size(axis))])


def digit(bit):
    axis, mask = bit
    return (lax.axis_index(axis) // mask) % 2


def in_order(bit, mine, other):
    one = digit(bit) == 1
    return jnp.where(one, other, mine), jnp.where(one, mine, other)


def halves(values, bit, axis):
    size = values.shape[axis] // 2
    own = digit(bit)
    return (
        lax.dynamic_slice_in_dim(values, own * size, size, axis),
        lax.dynamic_slice_in_dim(values, (1 - own) * size, size, axis),
    )


def tie(*groups):
    return lax.optimization_barrier(groups)


def tie_to(values, hold):
    return (values, None) if hold is None else tie(values, hold)


class Plan:
    def __init__(self, sizes):
        self.far = bits_of("far", sizes["far"])
        self.near = bits_of("near", sizes["near"])
        self.y = bits_of("y", sizes["y"])
        self.core = ("core", 1)
        self.tensor = ("tensor", 1)
        self.ctx = self.y + [self.core]
        self.rows = self.far + self.near + self.ctx
        self.links = [self.tensor] + self.y + self.near
        self.chip = self.near + self.y + [self.tensor]
        self.blocks = sizes["near"] * sizes["y"] * 2


class Journey:
    def __init__(self, steps):
        self.steps = steps
        self.result = None
        next(steps)

    def step(self, hold):
        try:
            return self.steps.send(hold)
        except StopIteration as end:
            self.result, hold = end.value
            return hold

    def finish(self, hold):
        while self.result is None:
            hold = self.step(hold)
        return hold


def repeat_in(arrays, plan, cuts):
    hold, whole = None, []
    for rows in arrays:
        size = rows.shape[0] // cuts
        pieces = []
        for start in range(0, rows.shape[0], size):
            piece = rows[start : start + size]
            if hold is not None:
                piece, hold = tie(piece, hold)
            for bit in reversed(plan.far):
                other = swap(piece, bit)
                hold = yield hold
                other, hold = tie_to(other, hold)
                piece = jnp.concatenate(in_order(bit, piece, other), axis=0)
            pieces.append(piece.reshape(-1, size, rows.shape[1]))
        whole.append(jnp.concatenate(pieces, axis=1).reshape(-1, rows.shape[1]))
    return whole, hold


def spread_out(grad, plan):
    grad = lax.psum_scatter(grad, "far", scatter_dimension=0, tiled=True)
    hold = yield None
    grad, hold = tie_to(grad, hold)
    bits = plan.near + plan.ctx
    grad = grad.reshape((2,) * len(bits) + (-1, grad.shape[-1]))
    for bit in reversed(bits):
        place = grad.ndim - 3
        mine, theirs = halves(grad, bit, place)
        other = swap(theirs, bit)
        hold = yield hold
        other, hold = tie_to(other, hold)
        grad = jnp.squeeze(jnp.concatenate(in_order(bit, mine, other), axis=-1), place)
    return grad, hold


def reduce_rows(grads, plan, orders, kind=bf16):
    hold = None
    states = [
        (grad.reshape((2,) * len(plan.rows) + (-1, grad.shape[-1])), list(plan.rows))
        for grad in grads
    ]
    for step in range(len(plan.rows)):
        kept, others = [], []
        for (grad, present), order in zip(states, orders, strict=True):
            place = present.index(order[step])
            mine, theirs = halves(grad, order[step], place)
            kept.append((jnp.squeeze(mine, place), present[:place] + present[place + 1 :]))
            others.append(jnp.squeeze(swap(theirs.astype(kind), order[step]), place))
        hold = yield hold
        others, hold = tie_to(others, hold)
        states = []
        for (mine, present), other in zip(kept, others, strict=True):
            grad = mine.astype(f32) + other.astype(f32)
            states.append((grad.astype(kind) if present else grad, present))
    return [grad for grad, _ in states], hold


def spread_small(part, plan):
    hold = None
    for bit in plan.far:
        other = swap(part, bit)
        hold = yield hold
        other, hold = tie_to(other, hold)
        part = part + other
    for bit in reversed(plan.near + plan.ctx):
        other = swap(part, bit)
        hold = yield hold
        other, hold = tie_to(other, hold)
        part = jnp.concatenate(in_order(bit, part, other), axis=1)
    return part, hold


def token_parts(count, plan):
    links = len(plan.links)
    step = 16
    units = count // step
    sizes = [(units // links + (1 if i < units % links else 0)) * step for i in range(links)]
    parts = []
    start = 0
    for i, size in enumerate(sizes):
        if size:
            parts.append((start, size, plan.links[i:] + plan.links[:i]))
            start += size
    return parts


def gather_tokens(local_rows, plan):
    hold = None
    parts = token_parts(local_rows.shape[0], plan)
    pieces = [(local_rows[start : start + size], []) for start, size, _ in parts]
    for step in range(len(plan.links)):
        bits = [order[step] for _, _, order in parts]
        others = [swap(piece, bit) for (piece, _), bit in zip(pieces, bits, strict=True)]
        hold = yield hold
        others, hold = tie_to(others, hold)
        grown = []
        for (piece, present), bit, other in zip(pieces, bits, others, strict=True):
            place = sum(1 for done in present if plan.chip.index(done) < plan.chip.index(bit))
            grown.append((jnp.stack(in_order(bit, piece, other), axis=place), present + [bit]))
        pieces = grown
    chip = jnp.concatenate([piece for piece, _ in pieces], axis=-2).reshape(
        -1, local_rows.shape[1]
    )
    return [chip, swap(chip, plan.core)], hold


def reduce_tokens(own, other, plan, count):
    got = swap(other, plan.core)
    hold = yield None
    got, hold = tie_to(got, hold)
    chip = (own.astype(f32) + got.astype(f32)).astype(bf16)
    chip = chip.reshape((2,) * len(plan.chip) + (count, -1))
    parts = token_parts(count, plan)
    pieces = [
        (lax.slice_in_dim(chip, start, start + size, axis=chip.ndim - 2), list(plan.chip))
        for start, size, _ in parts
    ]
    for step in reversed(range(len(plan.links))):
        kept, others = [], []
        for (piece, present), (_, _, order) in zip(pieces, parts, strict=True):
            place = present.index(order[step])
            mine, theirs = halves(piece, order[step], place)
            kept.append((jnp.squeeze(mine, place), present[:place] + present[place + 1 :]))
            others.append(swap(jnp.squeeze(theirs, place), order[step]))
        hold = yield hold
        others, hold = tie_to(others, hold)
        pieces = []
        for (mine, present), got in zip(kept, others, strict=True):
            piece = mine.astype(f32) + got.astype(f32)
            pieces.append((piece.astype(bf16) if present else piece, present))
    return jnp.concatenate([piece for piece, _ in pieces], axis=0), hold


def gather_rows(values_low, plan):
    return jnp.concatenate(in_order(plan.tensor, values_low, swap(values_low, plan.tensor)), axis=0)


def sum_rows(partial_rows, plan):
    mine, theirs = halves(partial_rows, plan.tensor, 0)
    return mine.astype(f32) + swap(theirs.astype(bf16), plan.tensor).astype(f32)


def local(
    plan,
    block_input,
    segment_ids,
    output_grad,
    attention_gain,
    query_weight,
    keyvalue_weight,
    output_weight,
    output_bias,
    channel_gain,
    gate_weight,
    up_weight,
    down_weight,
    gate_bias,
    up_bias,
    down_bias,
):
    local_in = block_input[0].astype(f32)
    grad_local = output_grad[0]
    is_key = lax.axis_index("tensor") == 0
    ctx_index = lax.axis_index("y") * 2 + lax.axis_index("core")
    shard_rows = attention_gain.shape[0]
    token_count, width = local_in.shape
    ff_half = gate_bias.shape[0]
    blocks = plan.blocks
    block = -(-ff_half // (blocks * LANES)) * LANES
    ff_pad = blocks * block - ff_half

    segments = segment_ids[0]
    row_count = segments.shape[0]
    offsets = [0]
    for axis, mask in plan.ctx:
        segments = jnp.concatenate([segments, swap(segments, (axis, mask))])
        offsets = offsets + [item ^ (mask * 2 if axis == "y" else mask) for item in offsets]
    piece_index = jnp.arange(row_count, dtype=jnp.int32)
    key_index = jnp.concatenate([(ctx_index ^ item) * row_count + piece_index for item in offsets])
    own_segments = segments[:row_count]
    query_index = key_index[:row_count]
    earlier = jnp.sum((segments[None, :] < own_segments[:, None]).astype(jnp.int32), axis=1)
    cosine_table, sine_table = rotary_tables(query_index - earlier, HD)
    allowed = (
        (own_segments[:, None] == segments[None, :])
        & (key_index[None, :] <= query_index[:, None])
        & (query_index[:, None] - key_index[None, :] < WINDOW)
    )

    def by_block(item):
        return lax.all_to_all(
            jnp.pad(item, ((0, 0), (0, ff_pad))),
            ("near",) + CTX,
            split_axis=1,
            concat_axis=0,
            tiled=True,
        )

    raw = block_input[0]
    raw_other = swap(raw, plan.tensor)
    down_rows, gate_rows, up_rows = (
        by_block(item) for item in (down_weight.T, gate_weight, up_weight)
    )

    vectors = jnp.stack([attention_gain, output_bias, channel_gain, down_bias], axis=1)
    vectors = jnp.pad(vectors, ((0, 0), (0, LANES - 4)))
    first = lax.all_gather(
        jnp.concatenate([query_weight, keyvalue_weight, vectors], axis=1),
        DP_CTX,
        axis=0,
        tiled=True,
    )
    full_output = lax.all_gather(output_weight.T, DP_CTX, axis=0, tiled=True)

    first, raw_other, *ff_rows = tie(first, raw_other, down_rows, gate_rows, up_rows)
    ff_in = Journey(repeat_in(ff_rows, plan, 2))
    block_start = (lax.axis_index("near") * (blocks // 2) + ctx_index) * block
    pair_bias = jnp.concatenate(
        [
            lax.dynamic_slice_in_dim(jnp.pad(item, (0, ff_pad)), block_start, block)
            for item in (gate_bias, up_bias)
        ]
    ).astype(f32)

    query_columns, keyvalue_columns = query_weight.shape[1], keyvalue_weight.shape[1]
    full_query = first[:, :query_columns]
    full_keyvalue = first[:, query_columns : query_columns + keyvalue_columns]
    vectors = first[:, query_columns + keyvalue_columns :].astype(f32)
    gain_one, full_obias, gain_two, full_dbias = (vectors[:, i] for i in range(4))
    norm_one_pull = jax.vjp(norm_scale, local_in, gain_one)[1]
    raw_rows = jnp.concatenate(in_order(plan.tensor, raw, raw_other), axis=0)
    normed = norm_scale(raw_rows.astype(f32), gain_one).astype(bf16)
    length = segments.shape[0]
    head_count = full_query.shape[1] // HD
    half_proj = jnp.dot(normed, full_keyvalue, preferred_element_type=f32)
    half_low = jnp.where(
        is_key, rotate(half_proj[:, None, :], cosine_table, sine_table, 1.0)[:, 0], half_proj
    ).astype(bf16)
    keyvalue = jnp.concatenate(in_order(plan.tensor, half_low, swap(half_low, plan.tensor)), axis=1)
    for bit in plan.ctx:
        keyvalue = jnp.concatenate([keyvalue, swap(keyvalue, bit)], axis=0)
        if bit == plan.y[-1]:
            keyvalue = ff_in.step(keyvalue)
    keyvalue, grad_local = tie(keyvalue, grad_local)
    all_keys = keyvalue[:, :HD]
    all_values = keyvalue[:, HD:]
    all_grads = lax.all_gather(
        grad_local, ("core", "near", "y", "tensor"), axis=0, tiled=True
    ).reshape(2, -1, width)
    query_proj = jnp.dot(normed, full_query, preferred_element_type=f32)
    queries = (
        rotate(query_proj.reshape(row_count, head_count, HD), cosine_table, sine_table, 1.0)
        * HD ** (-0.5)
    ).astype(bf16)
    queries = ff_in.step(queries)
    scores = jnp.einsum("qhd,kd->hqk", queries, all_keys, preferred_element_type=f32)
    scores = jnp.where(allowed[None], scores, -1e30)
    score_peak = jnp.max(scores, axis=-1, keepdims=True)
    exp_scores = jnp.exp(scores - score_peak)
    exp_total = jnp.sum(exp_scores, axis=-1, keepdims=True)
    probs = exp_scores / exp_total
    probs_low = probs.astype(bf16)
    context = jnp.einsum("hqk,kd->qhd", probs_low, all_values, preferred_element_type=f32)
    context = context.astype(bf16).reshape(row_count, head_count * HD)
    attended = jnp.einsum("rc,dc->rd", context, full_output, preferred_element_type=f32)
    attended = ff_in.step(attended)
    mixed = local_in + sum_rows(attended, plan) + full_obias
    mixed = ff_in.step(mixed)

    normed_two_local, norm_two_pull = jax.vjp(norm_scale, mixed, gain_two)
    journey = Journey(gather_tokens(normed_two_local.astype(bf16), plan))
    mixed = ff_in.step(journey.step(mixed))
    mixed = ff_in.finish(journey.step(mixed))
    mixed = journey.finish(mixed)
    normed_two = journey.result
    full_down, full_gate, full_up = ff_in.result
    full_pair = jnp.concatenate([full_gate, full_up], axis=1)
    core = lax.axis_index("core")
    grad_rows = [
        lax.dynamic_index_in_dim(all_grads, item, 0, keepdims=False) for item in (core, 1 - core)
    ]
    hidden, pair_grad, pair_bias_grad = [], [], 0.0
    for rows_two, rows_grad in zip(normed_two, grad_rows, strict=True):
        hidden_grad = jnp.dot(rows_grad, full_down, preferred_element_type=f32)
        pair_pre = jnp.dot(rows_two, full_pair, preferred_element_type=f32) + pair_bias
        gate_pre, up_pre = pair_pre[:, :block], pair_pre[:, block:]
        activated, gelu_pull = jax.vjp(partial(jax.nn.gelu, approximate=True), gate_pre)
        hidden.append((activated * up_pre).astype(bf16))
        pair_full = jnp.concatenate(
            [gelu_pull(hidden_grad * up_pre)[0], hidden_grad * activated], axis=1
        )
        pair_bias_grad = pair_bias_grad + jnp.sum(pair_full, axis=0)
        pair_grad.append(pair_full.astype(bf16))

    def rows_out(rows, weight):
        return jnp.einsum("rf,df->rd", rows, weight, preferred_element_type=f32).astype(bf16)

    def weight_out(lefts, rights):
        return sum(
            jnp.einsum("rd,rf->df", left, right, preferred_element_type=f32)
            for left, right in zip(lefts, rights, strict=True)
        ).astype(bf16)

    two_other = rows_out(pair_grad[1], full_pair)
    two_other, pair_grad = tie(two_other, pair_grad)
    two_own = rows_out(pair_grad[0], full_pair)
    two_sum = Journey(reduce_tokens(two_own, two_other, plan, token_count))
    hidden = two_sum.step(hidden)
    down_wgrad = weight_out(grad_rows, hidden)
    down_wgrad, pair_grad = two_sum.step((down_wgrad, pair_grad))
    down_sum = Journey(spread_out(down_wgrad, plan))
    out_other = rows_out(hidden[1], full_down)
    out_other, hidden, pair_grad = two_sum.step((out_other, hidden, pair_grad))
    out_own = rows_out(hidden[0], full_down)
    out_own, out_other, pair_grad = two_sum.finish((out_own, out_other, pair_grad))
    two_grad = two_sum.result

    grad_full = grad_local.astype(f32)
    dbias_part = jnp.sum(grad_full, axis=0)
    mixed_part, gain_two_part = norm_two_pull(two_grad)
    mixed_grad = grad_full + mixed_part
    obias_part = jnp.sum(mixed_grad, axis=0)
    mixed_low = mixed_grad.astype(bf16)
    mixed_other = swap(mixed_low, plan.tensor)
    out_other, mixed_low = tie(out_other, mixed_low)
    out_sum = Journey(reduce_tokens(out_own, out_other, plan, token_count))
    pair_grad, mixed_low = out_sum.step((pair_grad, mixed_low))
    gate_wgrad = weight_out(normed_two, [item[:, :block] for item in pair_grad])
    mixed_other, gate_wgrad = tie(mixed_other, gate_wgrad)
    gate_sum = Journey(spread_out(gate_wgrad, plan))
    attn_rows = jnp.concatenate(in_order(plan.tensor, mixed_low, mixed_other), axis=0)
    context_grad = jnp.dot(attn_rows, full_output, preferred_element_type=f32).astype(bf16)
    context_grad = context_grad.reshape(row_count, head_count, HD)
    context_grad, attn_rows = tie(context_grad, attn_rows)
    order = plan.ctx[::-1] + plan.near + plan.far[::-1]
    output_wgrad = jnp.einsum("rd,rc->dc", attn_rows, context, preferred_element_type=f32)
    context_grad, output_wgrad = tie(context_grad, output_wgrad.astype(bf16))
    output_sum = Journey(reduce_rows([output_wgrad], plan, [order]))
    probs_grad = jnp.einsum("qhd,kd->hqk", context_grad, all_values, preferred_element_type=f32)
    values_grad = jnp.einsum("hqk,qhd->kd", probs_low, context_grad, preferred_element_type=f32)
    prob_dot = jnp.sum(probs * probs_grad, axis=-1, keepdims=True)
    score_grad = (probs * (probs_grad - prob_dot)).astype(bf16)
    score_grad = output_sum.step(score_grad)
    keys_grad = jnp.einsum("hqk,qhd->kd", score_grad, queries, preferred_element_type=f32)
    stacked = jnp.concatenate([keys_grad, values_grad], axis=1)
    query_grad = jnp.einsum("hqk,kd->qhd", score_grad, all_keys, preferred_element_type=f32)
    query_proj_grad = rotate(query_grad * HD ** (-0.5), cosine_table, sine_table, -1.0)
    query_proj_grad = query_proj_grad.reshape(row_count, head_count * HD).astype(bf16)
    query_proj_grad = out_sum.step(query_proj_grad)
    query_wgrad = jnp.einsum("rd,rc->dc", normed, query_proj_grad, preferred_element_type=f32)
    query_wgrad = query_wgrad.astype(bf16)
    for bit in reversed(plan.ctx):
        half = stacked.shape[0] // 2
        other = swap(stacked[half:].astype(bf16), bit)
        if bit == plan.core:
            pair_grad, query_wgrad = tie(pair_grad, query_wgrad)
            up_wgrad = weight_out(normed_two, [item[:, block:] for item in pair_grad])
            other, up_wgrad, query_wgrad = out_sum.step((other, up_wgrad, query_wgrad))
            other, up_wgrad, query_wgrad = down_sum.step((other, up_wgrad, query_wgrad))
            up_sum = Journey(spread_out(up_wgrad, plan))
            query_sum = Journey(reduce_rows([query_wgrad], plan, [order]))
        stacked = stacked[:half] + other.astype(f32)
    mine, theirs = halves(stacked, plan.tensor, 1)
    half_grad = mine + swap(theirs.astype(bf16), plan.tensor).astype(f32)
    half_grad = query_sum.step(half_grad)
    half_grad = jnp.where(
        is_key, rotate(half_grad[:, None, :], cosine_table, sine_table, -1.0)[:, 0], half_grad
    ).astype(bf16)
    one_part = jnp.einsum(
        "rc,dc->rd", query_proj_grad, full_query, preferred_element_type=f32
    ) + jnp.einsum("rc,dc->rd", half_grad, full_keyvalue, preferred_element_type=f32)
    mine, theirs = halves(one_part, plan.tensor, 0)
    theirs, half_grad = tie(theirs.astype(bf16), half_grad)
    other = swap(theirs, plan.tensor)
    keyvalue_wgrad = jnp.einsum("rd,rc->dc", normed, half_grad, preferred_element_type=f32)
    keyvalue_wgrad = out_sum.finish(keyvalue_wgrad.astype(bf16))
    keyvalue_wgrad = output_sum.step(keyvalue_wgrad)
    keyvalue_wgrad = down_sum.step(keyvalue_wgrad)
    keyvalue_sum = Journey(reduce_rows([keyvalue_wgrad], plan, [order]))
    block_output = (mixed + out_sum.result + full_dbias).astype(bf16)
    block_output = gate_sum.step(block_output)
    other, block_output = tie(other, block_output)
    input_part, gain_one_part = norm_one_pull(mine + other.astype(f32))
    input_grad = mixed_grad + input_part

    for item in (
        keyvalue_sum,
        gate_sum,
        down_sum,
        output_sum,
        query_sum,
        up_sum,
        gate_sum,
        down_sum,
        up_sum,
        keyvalue_sum,
        output_sum,
        query_sum,
    ):
        input_grad = item.step(input_grad)

    small = jnp.stack([gain_one_part, gain_two_part, obias_part, dbias_part], axis=0)
    small = small.reshape(4, -1, shard_rows).transpose(1, 0, 2)
    small, pair_bias_grad, input_grad = tie(small, pair_bias_grad, input_grad)
    small = small + swap(small, plan.tensor)
    small_sum = Journey(reduce_rows([small.reshape(-1, shard_rows)], plan, [order], f32))
    ff_small = Journey(spread_small(pair_bias_grad.reshape(2, block), plan))
    journeys = [query_sum, gate_sum, up_sum, output_sum, small_sum, ff_small, keyvalue_sum, down_sum]
    while any(item.result is None for item in journeys):
        for item in journeys:
            if item.result is None:
                input_grad = item.step(input_grad)
    proj_out = output_sum.result[0]
    query_out = query_sum.result[0]
    keyvalue_out = keyvalue_sum.result[0]
    small = small_sum.result[0].reshape(4, shard_rows)
    ff_small = ff_small.result
    down_out, gate_out, up_out = (
        item.result[:, :ff_half].astype(f32) for item in (down_sum, gate_sum, up_sum)
    )
    return (
        block_output[None],
        input_grad[None],
        small[0],
        query_out,
        keyvalue_out,
        proj_out.T,
        small[2],
        small[1],
        gate_out,
        up_out,
        down_out.T,
        ff_small[0, :ff_half],
        ff_small[1, :ff_half],
        small[3],
    )


def solution(mesh):
    near = 2
    shape = (mesh.shape["dp"] // near, near, mesh.shape["ctx"] // 2, 2, mesh.shape["tensor"])
    names = DP + CTX + ("tensor",)
    mesh = Mesh(mesh.devices.reshape(shape), names)
    plan = Plan(dict(zip(names, shape, strict=True)))
    rows = P(DP, CTX + ("tensor",), None)
    vector = P(DP_CTX)
    wide = P(DP_CTX, "tensor")
    tall = P("tensor", DP_CTX)
    units = P("tensor")
    return jax.shard_map(
        partial(local, plan),
        mesh=mesh,
        in_specs=(
            rows,
            P(DP, CTX),
            rows,
            vector,
            wide,
            wide,
            tall,
            vector,
            vector,
            wide,
            wide,
            tall,
            units,
            units,
            vector,
        ),
        out_specs=(
            rows,
            rows,
            vector,
            wide,
            wide,
            tall,
            vector,
            vector,
            wide,
            wide,
            tall,
            units,
            units,
            vector,
        ),
        check_vma=False,
    )
```

time: 1260 us -> 882 us (0.70)
  waiting for transfers between devices: 809 us -> 438 us
  blocking collectives: 34.9 us -> 0 us
  other arithmetic: 84.4 us -> 110 us
    ppermute x95 -> x78, waiting for transfers between devices: 767 us -> 364 us  [swap(): lax.ppermute(values, axis, [(i, i ^ mask) for i in range(lax.axis_size(ax...]
    all_to_all x0 -> x3, waiting for transfers between devices: none -> 73.7 us  [by_block(): lax.all_to_all(jnp.pad(item, ((0, 0), (0, ff_pad))), ('near',) + CTX, spl...]
    all_gather x3, waiting for transfers between devices: 41.4 us -> 0.01 us  [the longest x1 0.01 us: local(): lax.all_gather(jnp.concatenate([query_weight, keyvalue_weight, vectors],...]
    all_gather x1 -> x0, blocking collectives: 34.9 us -> none  [local(): all_segments = lax.all_gather(segment_ids, 'ctx', axis=1, tiled=True)[0]]
    ppermute x95 -> x78, starting transfers between devices: 85.1 us -> 68.5 us  [swap(): lax.ppermute(values, axis, [(i, i ^ mask) for i in range(lax.axis_size(ax...]
    another operation x26 -> x16, other arithmetic: 18.8 us -> 2.9 us  [the longest x14 1.94 us: gather_tokens(): jnp.stack(in_order(bit, piece, other), axis=place)]
    convert_element_type x32 -> x33, other arithmetic: 33.3 us -> 47.7 us  [the longest x9 15.1 us: reduce_rows(): states.append((grad.astype(kind) if present else grad, present))]
    select_n x15 -> x19, other arithmetic: 2.71 us -> 16 us  [in_order(): return (jnp.where(one, other, mine), jnp.where(one, mine, other))]
  transfers between devices with their start and end apart: 98 -> 87, of which waited for: 59 -> 42; matrix products, arithmetic and copies ran while one was open for 16% -> 32% of each run, Pallas kernels for 0% -> 0%
where the time goes in v2:
time: 882 us; the launch traced here: 871 us
  waiting for transfers between devices  438 us (50%)
  matrix products  141 us (16%)
  other arithmetic  110 us (12%)
  local copies, waits for them, and re-layouts  83.1 us (9%)
  starting transfers between devices  81.5 us (9%)
  between operations  17.2 us (2%)
    ppermute x78, waiting for transfers between devices, swap(): lax.ppermute(values, axis, [(i, i ^ mask) for i in range(lax.axis_size(ax...  364 us
    all_to_all x3, waiting for transfers between devices, by_block(): lax.all_to_all(jnp.pad(item, ((0, 0), (0, ff_pad))), ('near',) + CTX, spl...  73.7 us
    ppermute x78, starting transfers between devices, swap(): lax.ppermute(values, axis, [(i, i ^ mask) for i in range(lax.axis_size(ax...  68.5 us
    dot_general x6, matrix products, weight_out(): jnp.einsum('rd,rf->df', left, right, preferred_element_type=f32)  34.7 us
    unnamed x303, local copies, waits for them, and re-layouts  27.4 us
    dot_general x4, matrix products, rows_out(): jnp.einsum('rf,df->rd', rows, weight, preferred_element_type=f32)  25.5 us
    dot_general x2, matrix products, local(): jnp.dot(rows_two, full_pair, preferred_element_type=f32) + pair_bias  21.3 us
  transfers between devices with their start and end apart: 87, of which 42 were waited for; matrix products, arithmetic and copies ran while one was open for 32% of the time, Pallas kernels for 0%

profile of v2, /device:TPU:0, one launch (start us, length us, event | category | flops | bytes accessed | tf_op | source)
XLA Modules:
  0.0 871.0 jit_solution(17235467733753695985)
XLA Ops:
  14.1 5.3 all-to-all-start.1
  20.7 30.1 %all-to-all-done.1 = bf16[160,8,512]{2,0,1:T(8,128)(2,1)S(1)} async-done(((bf16[160,8,512]{2,0,1:T(8,128)(2,1)}), bf16[160,8,512]{2,0,1:T(8,128)(2,1)S(1)}, u32[]{:S(2)}, u32[]{:S(2)}) %all-to-all-start.1) | async-done | bytes 1310752 | tf_op jit(solution)/shard_map/all_to_all | solution.py:314
  50.8 4.0 all-to-all-start.2
  57.4 34.6 %all-to-all-done.2 = bf16[160,8,512]{2,0,1:T(8,128)(2,1)S(1)} async-done(((bf16[160,8,512]{2,0,1:T(8,128)(2,1)}), bf16[160,8,512]{2,0,1:T(8,128)(2,1)S(1)}, u32[]{:S(2)}, u32[]{:S(2)}) %all-to-all-start.2) | async-done | bytes 1310752 | tf_op jit(solution)/shard_map/all_to_all | solution.py:314
  92.0 3.6 all-to-all-start
  99.4 7.1 collective-permute-done.2
  108.7 5.5 collective-permute-done
  114.2 9.0 %all-to-all-done = bf16[160,8,512]{2,0,1:T(8,128)(2,1)S(1)} async-done(((bf16[160,8,512]{2,0,1:T(8,128)(2,1)}), bf16[160,8,512]{2,0,1:T(8,128)(2,1)S(1)}, u32[]{:S(2)}, u32[]{:S(2)}) %all-to-all-start) | async-done | bytes 1310752 | tf_op jit(solution)/shard_map/all_to_all | solution.py:314
  133.0 3.7 collective-permute-start.1
  137.5 2.9 fusion.6
  140.4 4.1 collective-permute-done.5
  145.3 32.4 %collective-permute-done.1 = bf16[640,512]{1,0:T(8,128)(2,1)S(1)} collective-permute-done((bf16[640,512]{1,0:T(8,128)(2,1)S(1)}, bf16[640,512]{1,0:T(8,128)(2,1)S(1)}, u32[]{:S(2)}, u32[]{:S(2)}) %collective-permute-start.1) | collective-permute-done | bytes 655392 | tf_op jit(solution)/shard_map/ppermute | solution.py:61
  190.7 39.4 %collective-permute-done.7 = bf16[640,512]{1,0:T(8,128)(2,1)} collective-permute-done((bf16[640,512]{1,0:T(8,128)(2,1)}, bf16[640,512]{1,0:T(8,128)(2,1)}, u32[]{:S(2)}, u32[]{:S(2)}) %collective-permute-start.7) | collective-permute-done | bytes 655392 | tf_op jit(solution)/shard_map/ppermute | solution.py:61
  238.9 5.1 fusion.171
  244.0 16.7 %collective-permute-done.8 = bf16[640,512]{1,0:T(8,128)(2,1)} collective-permute-done((bf16[640,512]{1,0:T(8,128)(2,1)}, bf16[640,512]{1,0:T(8,128)(2,1)}, u32[]{:S(2)}, u32[]{:S(2)}) %collective-permute-start.8) | collective-permute-done | bytes 655392 | tf_op jit(solution)/shard_map/ppermute | solution.py:61
  263.6 27.4 %collective-permute-done.10 = bf16[128,2560]{1,0:T(8,128)(2,1)S(1)} collective-permute-done((bf16[128,2560]{1,0:T(8,128)(2,1)S(1)}, bf16[128,2560]{1,0:T(8,128)(2,1)S(1)}, u32[]{:S(2)}, u32[]{:S(2)}) %collective-permute-start.10) | collective-permute-done | bytes 655392 | tf_op jit(solution)/shard_map/ppermute | solution.py:61
  298.5 3.0 collective-permute-start.17
  301.5 15.9 %collective-permute-done.13 = bf16[32,2560]{1,0:T(8,128)(2,1)} collective-permute-done((bf16[32,2560]{1,0:T(8,128)(2,1)S(1)}, bf16[32,2560]{1,0:T(8,128)(2,1)}, u32[]{:S(2)}, u32[]{:S(2)}) %collective-permute-start.13) | collective-permute-done | bytes 163872 | tf_op jit(solution)/shard_map/ppermute | solution.py:61
  318.9 10.3 %collective-permute-done.17 = bf16[640,512]{1,0:T(8,128)(2,1)S(1)} collective-permute-done((bf16[640,512]{1,0:T(8,128)(2,1)S(1)}, bf16[640,512]{1,0:T(8,128)(2,1)S(1)}, u32[]{:S(2)}, u32[]{:S(2)}) %collective-permute-start.17) | collective-permute-done | bytes 655392 | tf_op jit(solution)/shard_map/ppermute | solution.py:61
  330.0 21.5 %collective-permute-done.15 = bf16[2,48,2560]{2,1,0:T(8,128)(2,1)S(1)} collective-permute-done((bf16[2,48,2560]{2,1,0:T(8,128)(2,1)S(1)}, bf16[2,48,2560]{2,1,0:T(8,128)(2,1)S(1)}, u32[]{:S(2)}, u32[]{:S(2)}) %collective-permute-start.15) | collective-permute-done | bytes 491552 | tf_op jit(solution)/shard_map/ppermute | solution.py:61
  352.1 2.8 collective-permute-start.20
  357.2 12.1 %collective-permute-done.20 = bf16[2,2,32,2560]{3,2,0,1:T(8,128)(2,1)S(1)} collective-permute-done((bf16[2,2,32,2560]{3,2,0,1:T(8,128)(2,1)S(1)}, bf16[2,2,32,2560]{3,2,0,1:T(8,128)(2,1)S(1)}, u32[]{:S(2)}, u32[]{:S(2)}) %collective-permute-start.20) | collective-permute-done | bytes 655392 | tf_op jit(solution)/shard_map/ppermute | solution.py:61
  369.3 8.8 %collective-permute-done.18 = bf16[2,2,48,2560]{3,2,0,1:T(8,128)(2,1)S(1)} collective-permute-done((bf16[2,2,48,2560]{3,2,0,1:T(8,128)(2,1)S(1)}, bf16[2,2,48,2560]{3,2,0,1:T(8,128)(2,1)S(1)}, u32[]{:S(2)}, u32[]{:S(2)}) %collective-permute-start.18) | collective-permute-done | bytes 983072 | tf_op jit(solution)/shard_map/ppermute | solution.py:61
  379.2 2.9 copy.124
  389.3 11.1 %broadcast_add_fusion = f32[1024,1024]{0,1:T(8,128)} fusion(f32[1024]{0:T(1024)S(1)} %maximum_convert_fusion, bf16[1024,2560]{1,0:T(8,128)(2,1)} %bitcast.44, bf16[2560,512]{1,0:T(8,128)(2,1)S(1)} %bitcast.480, bf16[2560,512]{1,0:T(8,128)(2,1)S(1)} %bitcast.476), kind=kOutput, calls=%fused_computation.95 | convolution fusion | flops 5380243456 | bytes 14684160 | tf_op jit(solution)/shard_map/dot_general | solution.py:408
  400.5 10.2 %broadcast_add_fusion.1 = f32[1024,1024]{0,1:T(8,128)} fusion(f32[1024]{0:T(1024)S(1)} %maximum_convert_fusion, bf16[1024,2560]{1,0:T(8,128)(2,1)} %collective-permute-done.22, bf16[2560,512]{1,0:T(8,128)(2,1)S(1)} %bitcast.481, bf16[2560,512]{1,0:T(8,128)(2,1)S(1)} %bitcast.477), kind=kOutput, calls=%fused_computation.96 | convolution fusion | flops 5380243456 | bytes 14684160 | tf_op jit(solution)/shard_map/dot_general | solution.py:408
  410.7 9.7 %fusion.45 = (f32[1024,512]{0,1:T(8,128)S(1)}, f32[1024,512]{0,1:T(8,128)S(1)}, bf16[1024,512]{0,1:T(8,128)(2,1)}) fusion(f32[1024,1024]{0,1:T(8,128)} %broadcast_add_fusion.1, bf16[2560,512]{1,0:T(8,128)(2,1)} %bitcast.472, bf16[2,1024,2560]{2,1,0:T(8,128)(2,1)} %bitcast.524, s32[]{:T(128)S(6)} %select_n.704), kind=kOutput, calls=%fused_computation.84 | convolution fusion | flops 2696937472 | bytes 17301508 | tf_op jit(solution)/shard_map/dot_general | solution.py:407
  424.5 7.4 convolution_convert_fusion.5
  431.9 7.0 fusion.51
  441.4 8.7 convolution_convert_fusion.4
  450.2 3.9 add_convert_fusion.1
  460.3 5.5 fusion.14
  465.9 4.6 add_convert_fusion.4
  470.4 3.5 collective-permute-done.26
  473.9 9.6 %collective-permute-done.24 = bf16[2,2,48,2560]{3,2,1,0:T(8,128)(2,1)} collective-permute-done((bf16[2,2,48,2560]{3,2,1,0:T(8,128)(2,1)}, bf16[2,2,48,2560]{3,2,1,0:T(8,128)(2,1)}, u32[]{:S(2)}, u32[]{:S(2)}) %collective-permute-start.24) | collective-permute-done | bytes 983072 | tf_op jit(solution)/shard_map/ppermute | solution.py:61
  491.6 4.7 convolution_convert_fusion.3
  496.3 5.9 collective-permute-done.28
  506.2 4.7 convolution_convert_fusion.2
  522.9 6.0 add_convert_fusion
  532.0 5.5 fusion.84
  537.5 6.8 add_convert_fusion.3
  546.6 5.6 convolution_convert_fusion.7
  571.7 3.5 convolution_bitcast_fusion
  575.3 3.1 fusion.9
  583.1 21.5 %collective-permute-done.34 = bf16[2,2,48,2560]{3,2,1,0:T(8,128)(2,1)} collective-permute-done((bf16[2,2,48,2560]{3,2,1,0:T(8,128)(2,1)}, bf16[2,2,48,2560]{3,2,1,0:T(8,128)(2,1)}, u32[]{:S(2)}, u32[]{:S(2)}) %collective-permute-start.34) | collective-permute-done | bytes 983072 | tf_op jit(solution)/shard_map/ppermute | solution.py:61
  615.8 2.8 fusion.2
  620.9 4.8 convolution_convert_fusion
  625.7 5.1 fusion.82
  630.8 7.2 add_convert_fusion.2
  638.0 15.3 %collective-permute-done.40 = bf16[2,48,2560]{2,1,0:T(8,128)(2,1)} collective-permute-done((bf16[2,48,2560]{2,1,0:T(8,128)(2,1)}, bf16[2,48,2560]{2,1,0:T(8,128)(2,1)}, u32[]{:S(2)}, u32[]{:S(2)}) %collective-permute-start.40) | collective-permute-done | bytes 491552 | tf_op jit(solution)/shard_map/ppermute | solution.py:61
  653.3 5.2 constant_dynamic-slice_fusion.23
  667.6 4.9 collective-permute-done.44
  681.8 3.7 fusion.3
  689.1 4.9 fusion.25
  710.1 12.7 %collective-permute-done.46 = bf16[128,2560]{1,0:T(8,128)(2,1)S(1)} collective-permute-done((bf16[128,2560]{1,0:T(8,128)(2,1)S(1)}, bf16[128,2560]{1,0:T(8,128)(2,1)S(1)}, u32[]{:S(2)}, u32[]{:S(2)}) %collective-permute-start.46) | collective-permute-done | bytes 655392 | tf_op jit(solution)/shard_map/ppermute | solution.py:61
  726.9 22.5 %collective-permute-done.54 = bf16[2,1,160,1024]{3,2,1,0:T(8,128)(2,1)S(1)} collective-permute-done((bf16[2,1,160,1024]{3,2,1,0:T(8,128)(2,1)S(1)}, bf16[2,1,160,1024]{3,2,1,0:T(8,128)(2,1)S(1)}, u32[]{:S(2)}, u32[]{:S(2)}) %collective-permute-start.54) | collective-permute-done | bytes 655392 | tf_op jit(solution)/shard_map/ppermute | solution.py:61
  764.8 10.0 %collective-permute-done.62 = bf16[2,1,160,1024]{3,2,1,0:T(8,128)(2,1)} collective-permute-done((bf16[2,1,160,1024]{3,2,1,0:T(8,128)(2,1)}, bf16[2,1,160,1024]{3,2,1,0:T(8,128)(2,1)}, u32[]{:S(2)}, u32[]{:S(2)}) %collective-permute-start.62) | collective-permute-done | bytes 655392 | tf_op jit(solution)/shard_map/ppermute | solution.py:61
  776.7 5.5 collective-permute-done.61
  794.2 5.5 collective-permute-done.57
  810.1 13.2 %collective-permute-done.68 = bf16[1,160,1280]{2,1,0:T(8,128)(2,1)S(1)} collective-permute-done((bf16[1,160,1280]{2,1,0:T(8,128)(2,1)S(1)}, bf16[1,160,1280]{2,1,0:T(8,128)(2,1)S(1)}, u32[]{:S(2)}, u32[]{:S(2)}) %collective-permute-start.68) | collective-permute-done | bytes 409632 | tf_op jit(solution)/shard_map/ppermute | solution.py:61
  829.0 3.0 collective-permute-start.71
  835.9 13.3 %collective-permute-done.71 = bf16[1,160,2048]{2,1,0:T(8,128)(2,1)S(1)} collective-permute-done((bf16[1,160,2048]{2,1,0:T(8,128)(2,1)S(1)}, bf16[1,160,2048]{2,1,0:T(8,128)(2,1)S(1)}, u32[]{:S(2)}, u32[]{:S(2)}) %collective-permute-start.71) | collective-permute-done | bytes 655392 | tf_op jit(solution)/shard_map/ppermute | solution.py:61
  856.0 3.1 collective-permute-done.77
  860.2 2.8 collective-permute-done.76
  (680 shorter events, 251.9 us)
Async XLA Ops:
  7.2 116.0 %all-gather.4.cloned.1.call-start = ((), (), s32[]{:S(2)}) async-start(), calls=%async_computation.6 | async-start | bytes 9052160 | tf_op jit(solution)/shard_map/all_gather | solution.py:330
  12.0 226.8 %all-gather.8.cloned.1.call-start = ((), (), s32[]{:S(2)}) async-start(), calls=%async_computation.8 | async-start | bytes 6963200 | tf_op jit(solution)/shard_map/all_gather | solution.py:336
  14.1 36.7 %all-to-all-start.1 = ((bf16[160,8,512]{2,0,1:T(8,128)(2,1)}), bf16[160,8,512]{2,0,1:T(8,128)(2,1)S(1)}, u32[]{:S(2)}, u32[]{:S(2)}) async-start(bf16[160,8,512]{2,0,1:T(8,128)(2,1)} %bitcast.436), calls=%async_computation.1 | async-start | bytes 2621440 | tf_op jit(solution)/shard_map/all_to_all | solution.py:314
  50.8 41.2 %all-to-all-start.2 = ((bf16[160,8,512]{2,0,1:T(8,128)(2,1)}), bf16[160,8,512]{2,0,1:T(8,128)(2,1)S(1)}, u32[]{:S(2)}, u32[]{:S(2)}) async-start(bf16[160,8,512]{2,0,1:T(8,128)(2,1)} %bitcast.466), calls=%async_computation.2 | async-start | bytes 2621440 | tf_op jit(solution)/shard_map/all_to_all | solution.py:314
  92.0 31.1 %all-to-all-start = ((bf16[160,8,512]{2,0,1:T(8,128)(2,1)}), bf16[160,8,512]{2,0,1:T(8,128)(2,1)S(1)}, u32[]{:S(2)}, u32[]{:S(2)}) async-start(bf16[160,8,512]{2,0,1:T(8,128)(2,1)} %bitcast.465), calls=%async_computation | async-start | bytes 2621440 | tf_op jit(solution)/shard_map/all_to_all | solution.py:314
  95.6 315.1 %all-gather.6.cloned.1.call-start = ((), (), s32[]{:S(2)}) async-start(), calls=%async_computation.7 | async-start | bytes 11141120 | tf_op jit(solution)/shard_map/all_gather | solution.py:370
  97.8 16.4 %collective-permute-start = (bf16[128,2560]{1,0:T(8,128)(2,1)S(1)}, bf16[128,2560]{1,0:T(8,128)(2,1)}, u32[]{:S(2)}, u32[]{:S(2)}) collective-permute-start(bf16[128,2560]{1,0:T(8,128)(2,1)S(1)} %bitcast.451), channel_id=1, source_target_pairs={{0,1},{1,0},{2,3},{3,2},{4,5},{5,4},{6,7},{7,6},{8,9},{9,8},{10,11... | collective-permute-start | bytes 1966088 | tf_op jit(solution)/shard_map/ppermute | solution.py:61
  133.0 44.7 %collective-permute-start.1 = (bf16[640,512]{1,0:T(8,128)(2,1)S(1)}, bf16[640,512]{1,0:T(8,128)(2,1)S(1)}, u32[]{:S(2)}, u32[]{:S(2)}) collective-permute-start(bf16[640,512]{1,0:T(8,128)(2,1)S(1)} %slice.175), channel_id=1, source_target_pairs={{0,16},{16,0},{1,17},{17,1},{2,18},{18,2},{3,19},{19,3},{4,20},{20... | collective-permute-start | bytes 1966088 | tf_op jit(solution)/shard_map/ppermute | solution.py:61
  179.2 51.0 %collective-permute-start.7 = (bf16[640,512]{1,0:T(8,128)(2,1)}, bf16[640,512]{1,0:T(8,128)(2,1)}, u32[]{:S(2)}, u32[]{:S(2)}) collective-permute-start(bf16[640,512]{1,0:T(8,128)(2,1)} %get-tuple-element.190), channel_id=1, source_target_pairs={{0,16},{16,0},{1,17},{17,1},{2,18},{18,2},{3,19},{19,3},{4,20},{20... | collective-permute-start | bytes 1966088 | tf_op jit(solution)/shard_map/ppermute | solution.py:61
  190.7 462.6 %reduce-scatter.4.cloned.1.call-start = ((), (), s32[]{:S(2)}) async-start(), calls=%async_computation.9 | async-start | bytes 3932160 | tf_op jit(solution)/shard_map/reduce_scatter | solution.py:144
  230.2 30.6 %collective-permute-start.8 = (bf16[640,512]{1,0:T(8,128)(2,1)}, bf16[640,512]{1,0:T(8,128)(2,1)}, u32[]{:S(2)}, u32[]{:S(2)}) collective-permute-start(bf16[640,512]{1,0:T(8,128)(2,1)} %get-tuple-element.195), channel_id=1, source_target_pairs={{0,16},{16,0},{1,17},{17,1},{2,18},{18,2},{3,19},{19,3},{4,20},{20... | collective-permute-start | bytes 1966088 | tf_op jit(solution)/shard_map/ppermute | solution.py:61
  260.8 30.2 %collective-permute-start.10 = (bf16[128,2560]{1,0:T(8,128)(2,1)S(1)}, bf16[128,2560]{1,0:T(8,128)(2,1)S(1)}, u32[]{:S(2)}, u32[]{:S(2)}) collective-permute-start(bf16[128,2560]{1,0:T(8,128)(2,1)S(1)} %dynamic-slice_convert_fusion.1), channel_id=1, source_target_pairs={{0,1},{1,0},{2,3},{3,2},{4,5},{5,4},{6,7},{7,6},{8,9},{9,8},{10,11... | collective-permute-start | bytes 1966088 | tf_op jit(solution)/shard_map/ppermute | solution.py:61
  262.4 31.3 %collective-permute-start.9 = (bf16[640,512]{1,0:T(8,128)(2,1)}, bf16[640,512]{1,0:T(8,128)(2,1)}, u32[]{:S(2)}, u32[]{:S(2)}) collective-permute-start(bf16[640,512]{1,0:T(8,128)(2,1)} %get-tuple-element.199), channel_id=1, source_target_pairs={{0,16},{16,0},{1,17},{17,1},{2,18},{18,2},{3,19},{19,3},{4,20},{20... | collective-permute-start | bytes 1966088 | tf_op jit(solution)/shard_map/ppermute | solution.py:61
  294.8 22.6 %collective-permute-start.12 = (bf16[48,2560]{1,0:T(8,128)(2,1)}, bf16[48,2560]{1,0:T(8,128)(2,1)S(1)}, u32[]{:S(2)}, u32[]{:S(2)}) collective-permute-start(bf16[48,2560]{1,0:T(8,128)(2,1)} %get-tuple-element.450), channel_id=1, source_target_pairs={{0,4},{4,0},{1,5},{5,1},{2,6},{6,2},{3,7},{7,3},{8,12},{12,8},{9,1... | collective-permute-start | bytes 737288 | tf_op jit(solution)/shard_map/ppermute | solution.py:61
  296.4 21.0 %collective-permute-start.11 = (bf16[48,2560]{1,0:T(8,128)(2,1)S(1)}, bf16[48,2560]{1,0:T(8,128)(2,1)S(1)}, u32[]{:S(2)}, u32[]{:S(2)}) collective-permute-start(bf16[48,2560]{1,0:T(8,128)(2,1)S(1)} %get-tuple-element.451), channel_id=1, source_target_pairs={{0,1},{1,0},{2,3},{3,2},{4,5},{5,4},{6,7},{7,6},{8,9},{9,8},{10,11... | collective-permute-start | bytes 737288 | tf_op jit(solution)/shard_map/ppermute | solution.py:61
  298.4 19.0 %collective-permute-start.13 = (bf16[32,2560]{1,0:T(8,128)(2,1)S(1)}, bf16[32,2560]{1,0:T(8,128)(2,1)}, u32[]{:S(2)}, u32[]{:S(2)}) collective-permute-start(bf16[32,2560]{1,0:T(8,128)(2,1)S(1)} %slice.242), channel_id=1, source_target_pairs={{0,8},{8,0},{1,9},{9,1},{2,10},{10,2},{3,11},{11,3},{4,12},{12,4},... | collective-permute-start | bytes 491528 | tf_op jit(solution)/shard_map/ppermute | solution.py:61
  298.5 30.6 %collective-permute-start.17 = (bf16[640,512]{1,0:T(8,128)(2,1)S(1)}, bf16[640,512]{1,0:T(8,128)(2,1)S(1)}, u32[]{:S(2)}, u32[]{:S(2)}) collective-permute-start(bf16[640,512]{1,0:T(8,128)(2,1)S(1)} %copy-done.71), channel_id=1, source_target_pairs={{0,16},{16,0},{1,17},{17,1},{2,18},{18,2},{3,19},{19,3},{4,20},{20... | collective-permute-start | bytes 1966088 | tf_op jit(solution)/shard_map/ppermute | solution.py:61
  317.7 33.8 %collective-permute-start.15 = (bf16[2,48,2560]{2,1,0:T(8,128)(2,1)S(1)}, bf16[2,48,2560]{2,1,0:T(8,128)(2,1)S(1)}, u32[]{:S(2)}, u32[]{:S(2)}) collective-permute-start(bf16[2,48,2560]{2,1,0:T(8,128)(2,1)S(1)} %pad_maximum_fusion.25), channel_id=1, source_target_pairs={{0,8},{8,0},{1,9},{9,1},{2,10},{10,2},{3,11},{11,3},{4,12},{12,4},... | collective-permute-start | bytes 1474568 | tf_op jit(solution)/shard_map/ppermute | solution.py:61
  329.2 28.0 %collective-permute-start.21 = (bf16[640,512]{1,0:T(8,128)(2,1)S(1)}, bf16[640,512]{1,0:T(8,128)(2,1)S(1)}, u32[]{:S(2)}, u32[]{:S(2)}) collective-permute-start(bf16[640,512]{1,0:T(8,128)(2,1)S(1)} %copy-done.70), channel_id=1, source_target_pairs={{0,16},{16,0},{1,17},{17,1},{2,18},{18,2},{3,19},{19,3},{4,20},{20... | collective-permute-start | bytes 1966088 | tf_op jit(solution)/shard_map/ppermute | solution.py:61
  351.7 26.5 %collective-permute-start.18 = (bf16[2,2,48,2560]{3,2,0,1:T(8,128)(2,1)S(1)}, bf16[2,2,48,2560]{3,2,0,1:T(8,128)(2,1)S(1)}, u32[]{:S(2)}, u32[]{:S(2)}) collective-permute-start(bf16[2,2,48,2560]{3,2,0,1:T(8,128)(2,1)S(1)} %pad_maximum_fusion.19), channel_id=1, source_target_pairs={{0,8},{8,0},{1,9},{9,1},{2,10},{10,2},{3,11},{11,3},{4,12},{12,4},... | collective-permute-start | bytes 2949128 | tf_op jit(solution)/shard_map/ppermute | solution.py:61
  351.9 26.2 %collective-permute-start.19 = (bf16[2,2,48,2560]{3,2,1,0:T(8,128)(2,1)S(1)}, bf16[2,2,48,2560]{3,2,1,0:T(8,128)(2,1)S(1)}, u32[]{:S(2)}, u32[]{:S(2)}) collective-permute-start(bf16[2,2,48,2560]{3,2,1,0:T(8,128)(2,1)S(1)} %pad_maximum_fusion.20), channel_id=1, source_target_pairs={{0,1},{1,0},{2,3},{3,2},{4,5},{5,4},{6,7},{7,6},{8,9},{9,8},{10,11... | collective-permute-start | bytes 2949128 | tf_op jit(solution)/shard_map/ppermute | solution.py:61
  352.1 17.2 %collective-permute-start.20 = (bf16[2,2,32,2560]{3,2,0,1:T(8,128)(2,1)S(1)}, bf16[2,2,32,2560]{3,2,0,1:T(8,128)(2,1)S(1)}, u32[]{:S(2)}, u32[]{:S(2)}) collective-permute-start(bf16[2,2,32,2560]{3,2,0,1:T(8,128)(2,1)S(1)} %pad_maximum_fusion.21), channel_id=1, source_target_pairs={{0,4},{4,0},{1,5},{5,1},{2,6},{6,2},{3,7},{7,3},{8,12},{12,8},{9,1... | collective-permute-start | bytes 1966088 | tf_op jit(solution)/shard_map/ppermute | solution.py:61
  382.1 18.4 %collective-permute-start.22 = (bf16[1024,2560]{1,0:T(8,128)(2,1)}, bf16[1024,2560]{1,0:T(8,128)(2,1)}, u32[]{:S(2)}, u32[]{:S(2)}) collective-permute-start(bf16[1024,2560]{1,0:T(8,128)(2,1)} %bitcast.44), channel_id=1, source_target_pairs={{0,2},{2,0},{1,3},{3,1},{4,6},{6,4},{5,7},{7,5},{8,10},{10,8},{9,1... | collective-permute-start | bytes 15728648 | tf_op jit(solution)/shard_map/ppermute | solution.py:61
  456.3 17.6 %collective-permute-start.26 = (bf16[2,2,32,2560]{3,2,0,1:T(8,128)(2,1)}, bf16[2,2,32,2560]{3,2,0,1:T(8,128)(2,1)}, u32[]{:S(2)}, u32[]{:S(2)}) collective-permute-start(bf16[2,2,32,2560]{3,2,0,1:T(8,128)(2,1)} %bitcast.439), channel_id=1, source_target_pairs={{0,4},{4,0},{1,5},{5,1},{2,6},{6,2},{3,7},{7,3},{8,12},{12,8},{9,1... | collective-permute-start | bytes 1966088 | tf_op jit(solution)/shard_map/ppermute | solution.py:61
  459.2 24.2 %collective-permute-start.24 = (bf16[2,2,48,2560]{3,2,1,0:T(8,128)(2,1)}, bf16[2,2,48,2560]{3,2,1,0:T(8,128)(2,1)}, u32[]{:S(2)}, u32[]{:S(2)}) collective-permute-start(bf16[2,2,48,2560]{3,2,1,0:T(8,128)(2,1)} %dynamic-slice_bitcast_fusion.3), channel_id=1, source_target_pairs={{0,8},{8,0},{1,9},{9,1},{2,10},{10,2},{3,11},{11,3},{4,12},{12,4},... | collective-permute-start | bytes 2949128 | tf_op jit(solution)/shard_map/ppermute | solution.py:61
  460.3 24.2 %collective-permute-start.25 = (bf16[2,2,48,2560]{3,2,1,0:T(8,128)(2,1)}, bf16[2,2,48,2560]{3,2,1,0:T(8,128)(2,1)}, u32[]{:S(2)}, u32[]{:S(2)}) collective-permute-start(bf16[2,2,48,2560]{3,2,1,0:T(8,128)(2,1)} %dynamic-slice_bitcast_fusion.2), channel_id=1, source_target_pairs={{0,1},{1,0},{2,3},{3,2},{4,5},{5,4},{6,7},{7,6},{8,9},{9,8},{10,11... | collective-permute-start | bytes 2949128 | tf_op jit(solution)/shard_map/ppermute | solution.py:61
  489.5 12.7 %collective-permute-start.28 = (bf16[2,48,2560]{2,1,0:T(8,128)(2,1)S(1)}, bf16[2,48,2560]{2,1,0:T(8,128)(2,1)S(1)}, u32[]{:S(2)}, u32[]{:S(2)}) collective-permute-start(bf16[2,48,2560]{2,1,0:T(8,128)(2,1)S(1)} %dynamic-slice_bitcast_fusion.6), channel_id=1, source_target_pairs={{0,8},{8,0},{1,9},{9,1},{2,10},{10,2},{3,11},{11,3},{4,12},{12,4},... | collective-permute-start | bytes 1474568 | tf_op jit(solution)/shard_map/ppermute | solution.py:61
  491.3 12.0 %collective-permute-start.27 = (bf16[2,48,2560]{2,1,0:T(8,128)(2,1)S(1)}, bf16[2,48,2560]{2,1,0:T(8,128)(2,1)S(1)}, u32[]{:S(2)}, u32[]{:S(2)}) collective-permute-start(bf16[2,48,2560]{2,1,0:T(8,128)(2,1)S(1)} %dynamic-slice_bitcast_fusion.7), channel_id=1, source_target_pairs={{0,4},{4,0},{1,5},{5,1},{2,6},{6,2},{3,7},{7,3},{8,12},{12,8},{9,1... | collective-permute-start | bytes 1474568 | tf_op jit(solution)/shard_map/ppermute | solution.py:61
  518.8 182.6 %reduce-scatter.6.cloned.1.call-start = ((), (), s32[]{:S(2)}) async-start(), calls=%async_computation.10 | async-start | bytes 3932160 | tf_op jit(solution)/shard_map/reduce_scatter | solution.py:144
  518.9 25.5 %collective-permute-start.37 = (bf16[128,2560]{1,0:T(8,128)(2,1)S(1)}, bf16[128,2560]{1,0:T(8,128)(2,1)}, u32[]{:S(2)}, u32[]{:S(2)}) collective-permute-start(bf16[128,2560]{1,0:T(8,128)(2,1)S(1)} %convert_element_type.566), channel_id=1, source_target_pairs={{0,1},{1,0},{2,3},{3,2},{4,5},{5,4},{6,7},{7,6},{8,9},{9,8},{10,11... | collective-permute-start | bytes 1966088 | tf_op jit(solution)/shard_map/ppermute | solution.py:61
  560.9 17.4 %collective-permute-start.38 = (bf16[2,2,2,1,160,1280]{5,4,0,1,2,3:T(8,128)(2,1)}, bf16[2,2,2,1,160,1280]{5,4,0,1,2,3:T(8,128)(2,1)}, u32[]{:S(2)}, u32[]{:S(2)}) collective-permute-start(bf16[2,2,2,1,160,1280]{5,4,0,1,2,3:T(8,128)(2,1)} %copy.172), channel_id=1, source_target_pairs={{0,2},{2,0},{1,3},{3,1},{4,6},{6,4},{5,7},{7,5},{8,10},{10,8},{9,1... | collective-permute-start | bytes 9830408 | tf_op jit(solution)/shard_map/ppermute | solution.py:61
  564.5 18.6 %collective-permute-start.36 = (bf16[2,2,32,2560]{3,2,0,1:T(8,128)(2,1)}, bf16[2,2,32,2560]{3,2,0,1:T(8,128)(2,1)}, u32[]{:S(2)}, u32[]{:S(2)}) collective-permute-start(bf16[2,2,32,2560]{3,2,0,1:T(8,128)(2,1)} %bitcast.438), channel_id=1, source_target_pairs={{0,4},{4,0},{1,5},{5,1},{2,6},{6,2},{3,7},{7,3},{8,12},{12,8},{9,1... | collective-permute-start | bytes 1966088 | tf_op jit(solution)/shard_map/ppermute | solution.py:61
  566.5 38.2 %collective-permute-start.34 = (bf16[2,2,48,2560]{3,2,1,0:T(8,128)(2,1)}, bf16[2,2,48,2560]{3,2,1,0:T(8,128)(2,1)}, u32[]{:S(2)}, u32[]{:S(2)}) collective-permute-start(bf16[2,2,48,2560]{3,2,1,0:T(8,128)(2,1)} %dynamic-slice_bitcast_fusion.1), channel_id=1, source_target_pairs={{0,8},{8,0},{1,9},{9,1},{2,10},{10,2},{3,11},{11,3},{4,12},{12,4},... | collective-permute-start | bytes 2949128 | tf_op jit(solution)/shard_map/ppermute | solution.py:61
  568.9 35.7 %collective-permute-start.35 = (bf16[2,2,48,2560]{3,2,1,0:T(8,128)(2,1)}, bf16[2,2,48,2560]{3,2,1,0:T(8,128)(2,1)}, u32[]{:S(2)}, u32[]{:S(2)}) collective-permute-start(bf16[2,2,48,2560]{3,2,1,0:T(8,128)(2,1)} %dynamic-slice_bitcast_fusion), channel_id=1, source_target_pairs={{0,1},{1,0},{2,3},{3,2},{4,5},{5,4},{6,7},{7,6},{8,9},{9,8},{10,11... | collective-permute-start | bytes 2949128 | tf_op jit(solution)/shard_map/ppermute | solution.py:61
  569.6 195.2 %reduce-scatter.8.cloned.1.call-start = ((), (), s32[]{:S(2)}) async-start(), calls=%async_computation.11 | async-start | bytes 3932160 | tf_op jit(solution)/shard_map/reduce_scatter | solution.py:144
  610.3 27.6 %collective-permute-start.41 = (bf16[2,32,2560]{2,1,0:T(8,128)(2,1)}, bf16[2,32,2560]{2,1,0:T(8,128)(2,1)}, u32[]{:S(2)}, u32[]{:S(2)}) collective-permute-start(bf16[2,32,2560]{2,1,0:T(8,128)(2,1)} %dynamic-slice_bitcast_fusion.8), channel_id=1, source_target_pairs={{0,1},{1,0},{2,3},{3,2},{4,5},{5,4},{6,7},{7,6},{8,9},{9,8},{10,11... | collective-permute-start | bytes 983048 | tf_op jit(solution)/shard_map/ppermute | solution.py:61
  613.5 39.8 %collective-permute-start.40 = (bf16[2,48,2560]{2,1,0:T(8,128)(2,1)}, bf16[2,48,2560]{2,1,0:T(8,128)(2,1)}, u32[]{:S(2)}, u32[]{:S(2)}) collective-permute-start(bf16[2,48,2560]{2,1,0:T(8,128)(2,1)} %dynamic-slice_bitcast_fusion.4), channel_id=1, source_target_pairs={{0,8},{8,0},{1,9},{9,1},{2,10},{10,2},{3,11},{11,3},{4,12},{12,4},... | collective-permute-start | bytes 1474568 | tf_op jit(solution)/shard_map/ppermute | solution.py:61
  613.5 39.8 %collective-permute-start.39 = (bf16[2,48,2560]{2,1,0:T(8,128)(2,1)}, bf16[2,48,2560]{2,1,0:T(8,128)(2,1)}, u32[]{:S(2)}, u32[]{:S(2)}) collective-permute-start(bf16[2,48,2560]{2,1,0:T(8,128)(2,1)} %dynamic-slice_bitcast_fusion.5), channel_id=1, source_target_pairs={{0,4},{4,0},{1,5},{5,1},{2,6},{6,2},{3,7},{7,3},{8,12},{12,8},{9,1... | collective-permute-start | bytes 1474568 | tf_op jit(solution)/shard_map/ppermute | solution.py:61
  615.8 37.5 %collective-permute-start.42 = (bf16[512,512]{0,1:T(8,128)(2,1)}, bf16[512,512]{0,1:T(8,128)(2,1)}, u32[]{:S(2)}, u32[]{:S(2)}) collective-permute-start(bf16[512,512]{0,1:T(8,128)(2,1)} %fusion.79), channel_id=1, source_target_pairs={{0,2},{2,0},{1,3},{3,1},{4,6},{6,4},{5,7},{7,5},{8,10},{10,8},{9,1... | collective-permute-start | bytes 1572872 | tf_op jit(solution)/shard_map/ppermute | solution.py:61
  620.0 81.5 %collective-permute-start.51 = (bf16[2,2,1,160,1280]{4,3,0,1,2:T(8,128)(2,1)}, bf16[2,2,1,160,1280]{4,3,0,1,2:T(8,128)(2,1)}, u32[]{:S(2)}, u32[]{:S(2)}) collective-permute-start(bf16[2,2,1,160,1280]{4,3,0,1,2:T(8,128)(2,1)} %constant_dynamic-slice_fusion.20), channel_id=1, source_target_pairs={{0,4},{4,0},{1,5},{5,1},{2,6},{6,2},{3,7},{7,3},{8,12},{12,8},{9,1... | collective-permute-start | bytes 4915208 | tf_op jit(solution)/shard_map/ppermute | solution.py:61
  660.4 20.2 %collective-permute-start.43 = (bf16[2,2,2,1,160,1280]{5,4,0,1,2,3:T(8,128)(2,1)}, bf16[2,2,2,1,160,1280]{5,4,0,1,2,3:T(8,128)(2,1)}, u32[]{:S(2)}, u32[]{:S(2)}) collective-permute-start(bf16[2,2,2,1,160,1280]{5,4,0,1,2,3:T(8,128)(2,1)} %copy.175), channel_id=1, source_target_pairs={{0,2},{2,0},{1,3},{3,1},{4,6},{6,4},{5,7},{7,5},{8,10},{10,8},{9,1... | collective-permute-start | bytes 9830408 | tf_op jit(solution)/shard_map/ppermute | solution.py:61
  662.2 34.6 %collective-permute-start.49 = (bf16[32,2560]{1,0:T(8,128)(2,1)S(1)}, bf16[32,2560]{1,0:T(8,128)(2,1)}, u32[]{:S(2)}, u32[]{:S(2)}) collective-permute-start(bf16[32,2560]{1,0:T(8,128)(2,1)S(1)} %dynamic-slice_bitcast_fusion.14), channel_id=1, source_target_pairs={{0,8},{8,0},{1,9},{9,1},{2,10},{10,2},{3,11},{11,3},{4,12},{12,4},... | collective-permute-start | bytes 491528 | tf_op jit(solution)/shard_map/ppermute | solution.py:61
  674.6 23.8 %collective-permute-start.48 = (bf16[48,2560]{1,0:T(8,128)(2,1)}, bf16[48,2560]{1,0:T(8,128)(2,1)}, u32[]{:S(2)}, u32[]{:S(2)}) collective-permute-start(bf16[48,2560]{1,0:T(8,128)(2,1)} %dynamic-slice_bitcast_fusion.10), channel_id=1, source_target_pairs={{0,4},{4,0},{1,5},{5,1},{2,6},{6,2},{3,7},{7,3},{8,12},{12,8},{9,1... | collective-permute-start | bytes 737288 | tf_op jit(solution)/shard_map/ppermute | solution.py:61
  678.8 19.6 %collective-permute-start.47 = (bf16[48,2560]{1,0:T(8,128)(2,1)S(1)}, bf16[48,2560]{1,0:T(8,128)(2,1)S(1)}, u32[]{:S(2)}, u32[]{:S(2)}) collective-permute-start(bf16[48,2560]{1,0:T(8,128)(2,1)S(1)} %dynamic-slice_bitcast_fusion.11), channel_id=1, source_target_pairs={{0,1},{1,0},{2,3},{3,2},{4,5},{5,4},{6,7},{7,6},{8,9},{9,8},{10,11... | collective-permute-start | bytes 737288 | tf_op jit(solution)/shard_map/ppermute | solution.py:61
  680.7 20.8 %collective-permute-start.53 = (bf16[2,2,1,160,512]{4,3,2,1,0:T(8,128)(2,1)}, bf16[2,2,1,160,512]{4,3,2,1,0:T(8,128)(2,1)}, u32[]{:S(2)}, u32[]{:S(2)}) collective-permute-start(bf16[2,2,1,160,512]{4,3,2,1,0:T(8,128)(2,1)} %constant_dynamic-slice_fusion.18), channel_id=1, source_target_pairs={{0,2},{2,0},{1,3},{3,1},{4,6},{6,4},{5,7},{7,5},{8,10},{10,8},{9,1... | collective-permute-start | bytes 1966088 | tf_op jit(solution)/shard_map/ppermute | solution.py:61
  696.9 64.0 %collective-permute-start.50 = (bf16[2,2,1,160,1280]{4,3,0,1,2:T(8,128)(2,1)}, bf16[2,2,1,160,1280]{4,3,0,1,2:T(8,128)(2,1)}, u32[]{:S(2)}, u32[]{:S(2)}) collective-permute-start(bf16[2,2,1,160,1280]{4,3,0,1,2:T(8,128)(2,1)} %constant_dynamic-slice_fusion.22), channel_id=1, source_target_pairs={{0,4},{4,0},{1,5},{5,1},{2,6},{6,2},{3,7},{7,3},{8,12},{12,8},{9,1... | collective-permute-start | bytes 4915208 | tf_op jit(solution)/shard_map/ppermute | solution.py:61
  703.2 23.3 %collective-permute-start.55 = (bf16[2,2,1,160,512]{4,3,2,1,0:T(8,128)(2,1)S(1)}, bf16[2,2,1,160,512]{4,3,2,1,0:T(8,128)(2,1)S(1)}, u32[]{:S(2)}, u32[]{:S(2)}) collective-permute-start(bf16[2,2,1,160,512]{4,3,2,1,0:T(8,128)(2,1)S(1)} %constant_dynamic-slice_fusion.17), channel_id=1, source_target_pairs={{0,2},{2,0},{1,3},{3,1},{4,6},{6,4},{5,7},{7,5},{8,10},{10,8},{9,1... | collective-permute-start | bytes 1966088 | tf_op jit(solution)/shard_map/ppermute | solution.py:61
  705.0 44.3 %collective-permute-start.54 = (bf16[2,1,160,1024]{3,2,1,0:T(8,128)(2,1)S(1)}, bf16[2,1,160,1024]{3,2,1,0:T(8,128)(2,1)S(1)}, u32[]{:S(2)}, u32[]{:S(2)}) collective-permute-start(bf16[2,1,160,1024]{3,2,1,0:T(8,128)(2,1)S(1)} %fusion.118), channel_id=1, source_target_pairs={{0,4},{4,0},{1,5},{5,1},{2,6},{6,2},{3,7},{7,3},{8,12},{12,8},{9,1... | collective-permute-start | bytes 1966088 | tf_op jit(solution)/shard_map/ppermute | solution.py:61
  705.7 20.9 %collective-permute-start.56 = (bf16[2,2,2,1,160,256]{5,4,0,1,2,3:T(8,128)(2,1)S(1)}, bf16[2,2,2,1,160,256]{5,4,0,1,2,3:T(8,128)(2,1)S(1)}, u32[]{:S(2)}, u32[]{:S(2)}) collective-permute-start(bf16[2,2,2,1,160,256]{5,4,0,1,2,3:T(8,128)(2,1)S(1)} %copy.178), channel_id=1, source_target_pairs={{0,2},{2,0},{1,3},{3,1},{4,6},{6,4},{5,7},{7,5},{8,10},{10,8},{9,1... | collective-permute-start | bytes 1966088 | tf_op jit(solution)/shard_map/ppermute | solution.py:61
  705.7 17.1 %collective-permute-start.46 = (bf16[128,2560]{1,0:T(8,128)(2,1)S(1)}, bf16[128,2560]{1,0:T(8,128)(2,1)S(1)}, u32[]{:S(2)}, u32[]{:S(2)}) collective-permute-start(bf16[128,2560]{1,0:T(8,128)(2,1)S(1)} %copy-done.97), channel_id=1, source_target_pairs={{0,1},{1,0},{2,3},{3,2},{4,5},{5,4},{6,7},{7,6},{8,9},{9,8},{10,11... | collective-permute-start | bytes 1966088 | tf_op jit(solution)/shard_map/ppermute | solution.py:61
  722.8 35.0 %collective-permute-start.52 = (bf16[2,1,160,1280]{3,2,0,1:T(8,128)(2,1)}, bf16[2,1,160,1280]{3,2,0,1:T(8,128)(2,1)}, u32[]{:S(2)}, u32[]{:S(2)}) collective-permute-start(bf16[2,1,160,1280]{3,2,0,1:T(8,128)(2,1)} %constant_dynamic-slice_fusion.19), channel_id=1, source_target_pairs={{0,8},{8,0},{1,9},{9,1},{2,10},{10,2},{3,11},{11,3},{4,12},{12,4},... | collective-permute-start | bytes 2457608 | tf_op jit(solution)/shard_map/ppermute | solution.py:61
  751.0 36.0 %collective-permute-start.59 = (bf16[2,2,1,160,256]{4,3,0,1,2:T(8,128)(2,1)}, bf16[2,2,1,160,256]{4,3,0,1,2:T(8,128)(2,1)}, u32[]{:S(2)}, u32[]{:S(2)}) collective-permute-start(bf16[2,2,1,160,256]{4,3,0,1,2:T(8,128)(2,1)} %constant_dynamic-slice_fusion.12), channel_id=1, source_target_pairs={{0,4},{4,0},{1,5},{5,1},{2,6},{6,2},{3,7},{7,3},{8,12},{12,8},{9,1... | collective-permute-start | bytes 983048 | tf_op jit(solution)/shard_map/ppermute | solution.py:61
  753.3 21.5 %collective-permute-start.62 = (bf16[2,1,160,1024]{3,2,1,0:T(8,128)(2,1)}, bf16[2,1,160,1024]{3,2,1,0:T(8,128)(2,1)}, u32[]{:S(2)}, u32[]{:S(2)}) collective-permute-start(bf16[2,1,160,1024]{3,2,1,0:T(8,128)(2,1)} %fusion.110), channel_id=1, source_target_pairs={{0,4},{4,0},{1,5},{5,1},{2,6},{6,2},{3,7},{7,3},{8,12},{12,8},{9,1... | collective-permute-start | bytes 1966088 | tf_op jit(solution)/shard_map/ppermute | solution.py:61
  755.4 26.8 %collective-permute-start.61 = (bf16[1,160,2048]{2,1,0:T(8,128)(2,1)}, bf16[1,160,2048]{2,1,0:T(8,128)(2,1)}, u32[]{:S(2)}, u32[]{:S(2)}) collective-permute-start(bf16[1,160,2048]{2,1,0:T(8,128)(2,1)} %fusion.114), channel_id=1, source_target_pairs={{0,8},{8,0},{1,9},{9,1},{2,10},{10,2},{3,11},{11,3},{4,12},{12,4},... | collective-permute-start | bytes 1966088 | tf_op jit(solution)/shard_map/ppermute | solution.py:61
  760.0 27.0 %collective-permute-start.58 = (bf16[1,160,1280]{2,1,0:T(8,128)(2,1)}, bf16[1,160,1280]{2,1,0:T(8,128)(2,1)S(1)}, u32[]{:S(2)}, u32[]{:S(2)}) collective-permute-start(bf16[1,160,1280]{2,1,0:T(8,128)(2,1)} %constant_dynamic-slice_fusion.14), channel_id=1, source_target_pairs={{0,16},{16,0},{1,17},{17,1},{2,18},{18,2},{3,19},{19,3},{4,20},{20... | collective-permute-start | bytes 1228808 | tf_op jit(solution)/shard_map/ppermute | solution.py:61
  763.7 36.0 %collective-permute-start.57 = (bf16[2,1,160,1280]{3,2,0,1:T(8,128)(2,1)}, bf16[2,1,160,1280]{3,2,0,1:T(8,128)(2,1)}, u32[]{:S(2)}, u32[]{:S(2)}) collective-permute-start(bf16[2,1,160,1280]{3,2,0,1:T(8,128)(2,1)} %constant_dynamic-slice_fusion.15), channel_id=1, source_target_pairs={{0,8},{8,0},{1,9},{9,1},{2,10},{10,2},{3,11},{11,3},{4,12},{12,4},... | collective-permute-start | bytes 2457608 | tf_op jit(solution)/shard_map/ppermute | solution.py:61
  785.3 38.0 %collective-permute-start.67 = (bf16[1,160,2048]{2,1,0:T(8,128)(2,1)}, bf16[1,160,2048]{2,1,0:T(8,128)(2,1)}, u32[]{:S(2)}, u32[]{:S(2)}) collective-permute-start(bf16[1,160,2048]{2,1,0:T(8,128)(2,1)} %fusion.102), channel_id=1, source_target_pairs={{0,8},{8,0},{1,9},{9,1},{2,10},{10,2},{3,11},{11,3},{4,12},{12,4},... | collective-permute-start | bytes 1966088 | tf_op jit(solution)/shard_map/ppermute | solution.py:61
  789.6 39.2 %collective-permute-start.72 = (bf16[2,1,160,256]{3,2,0,1:T(8,128)(2,1)}, bf16[2,1,160,256]{3,2,0,1:T(8,128)(2,1)}, u32[]{:S(2)}, u32[]{:S(2)}) collective-permute-start(bf16[2,1,160,256]{3,2,0,1:T(8,128)(2,1)} %constant_dynamic-slice_fusion.6), channel_id=1, source_target_pairs={{0,8},{8,0},{1,9},{9,1},{2,10},{10,2},{3,11},{11,3},{4,12},{12,4},... | collective-permute-start | bytes 491528 | tf_op jit(solution)/shard_map/ppermute | solution.py:61
  792.8 34.6 %collective-permute-start.66 = (bf16[2,1,160,1024]{3,2,1,0:T(8,128)(2,1)}, bf16[2,1,160,1024]{3,2,1,0:T(8,128)(2,1)}, u32[]{:S(2)}, u32[]{:S(2)}) collective-permute-start(bf16[2,1,160,1024]{3,2,1,0:T(8,128)(2,1)} %fusion.106), channel_id=1, source_target_pairs={{0,4},{4,0},{1,5},{5,1},{2,6},{6,2},{3,7},{7,3},{8,12},{12,8},{9,1... | collective-permute-start | bytes 1966088 | tf_op jit(solution)/shard_map/ppermute | solution.py:61
  802.5 20.7 %collective-permute-start.68 = (bf16[1,160,1280]{2,1,0:T(8,128)(2,1)S(1)}, bf16[1,160,1280]{2,1,0:T(8,128)(2,1)S(1)}, u32[]{:S(2)}, u32[]{:S(2)}) collective-permute-start(bf16[1,160,1280]{2,1,0:T(8,128)(2,1)S(1)} %constant_dynamic-slice_fusion.9), channel_id=1, source_target_pairs={{0,16},{16,0},{1,17},{17,1},{2,18},{18,2},{3,19},{19,3},{4,20},{20... | collective-permute-start | bytes 1228808 | tf_op jit(solution)/shard_map/ppermute | solution.py:61
  807.7 19.7 %collective-permute-start.63 = (f32[2,512]{1,0:T(2,128)S(1)}, f32[2,512]{1,0:T(2,128)S(1)}, u32[]{:S(2)}, u32[]{:S(2)}) collective-permute-start(f32[2,512]{1,0:T(2,128)S(1)} %reshape.518), channel_id=1, source_target_pairs={{0,16},{16,0},{1,17},{17,1},{2,18},{18,2},{3,19},{19,3},{4,20},{20... | collective-permute-start | bytes 12296 | tf_op jit(solution)/shard_map/ppermute | solution.py:61
  828.9 20.6 %collective-permute-start.69 = (f32[2,512]{1,0:T(2,128)S(1)}, f32[2,512]{1,0:T(2,128)S(1)}, u32[]{:S(2)}, u32[]{:S(2)}) collective-permute-start(f32[2,512]{1,0:T(2,128)S(1)} %add.625), channel_id=1, source_target_pairs={{0,2},{2,0},{1,3},{3,1},{4,6},{6,4},{5,7},{7,5},{8,10},{10,8},{9,1... | collective-permute-start | bytes 12296 | tf_op jit(solution)/shard_map/ppermute | solution.py:61
  829.0 20.1 %collective-permute-start.71 = (bf16[1,160,2048]{2,1,0:T(8,128)(2,1)S(1)}, bf16[1,160,2048]{2,1,0:T(8,128)(2,1)S(1)}, u32[]{:S(2)}, u32[]{:S(2)}) collective-permute-start(bf16[1,160,2048]{2,1,0:T(8,128)(2,1)S(1)} %fusion.98), channel_id=1, source_target_pairs={{0,8},{8,0},{1,9},{9,1},{2,10},{10,2},{3,11},{11,3},{4,12},{12,4},... | collective-permute-start | bytes 1966088 | tf_op jit(solution)/shard_map/ppermute | solution.py:61
  834.4 18.6 %collective-permute-start.75 = (bf16[1,160,256]{2,1,0:T(8,128)(2,1)S(1)}, bf16[1,160,256]{2,1,0:T(8,128)(2,1)S(1)}, u32[]{:S(2)}, u32[]{:S(2)}) collective-permute-start(bf16[1,160,256]{2,1,0:T(8,128)(2,1)S(1)} %constant_dynamic-slice_fusion.3), channel_id=1, source_target_pairs={{0,16},{16,0},{1,17},{17,1},{2,18},{18,2},{3,19},{19,3},{4,20},{20... | collective-permute-start | bytes 245768 | tf_op jit(solution)/shard_map/ppermute | solution.py:61
  (169 other events, 1571.0 us)
Sparse Core Ops, SparseCore 0:
  12.2 106.4 all-gather.3
  120.9 106.7 all-gather.7
  229.3 122.2 all-gather.5
  518.9 65.0 reduce-scatter.3
  586.3 65.6 reduce-scatter.5
  676.3 65.3 reduce-scatter.7

commit v3 on v2

--- a/solution.py
+++ b/solution.py
@@ -4,12 +4,16 @@
 import jax
 import jax.numpy as jnp
 from jax import lax
+from jax.experimental import pallas as pl
+from jax.experimental.pallas import tpu as pltpu
 from jax.sharding import Mesh
 from jax.sharding import PartitionSpec as P
 
 HD = 256
 WINDOW = 2048
 LANES = 128
+GELU_SCALE = math.sqrt(2.0 / math.pi)
+GELU_CUBE = 0.044715
 DP = ("far", "near")
 CTX = ("y", "core")
 DP_CTX = DP + CTX
@@ -84,6 +88,14 @@
     return lax.optimization_barrier(groups)
 
 
+def finish_all(items, hold):
+    while any(item.result is None for item in items):
+        for item in items:
+            if item.result is None:
+                hold = item.step(hold)
+    return hold
+
+
 def tie_to(values, hold):
     return (values, None) if hold is None else tie(values, hold)
 
@@ -121,8 +133,8 @@
         return hold
 
 
-def repeat_in(arrays, plan, cuts):
-    hold, whole = None, []
+def repeat_in(arrays, plan, cuts, whole):
+    hold = None
     for rows in arrays:
         size = rows.shape[0] // cuts
         pieces = []
@@ -140,19 +152,24 @@
     return whole, hold
 
 
-def spread_out(grad, plan):
-    grad = lax.psum_scatter(grad, "far", scatter_dimension=0, tiled=True)
-    hold = yield None
-    grad, hold = tie_to(grad, hold)
-    bits = plan.near + plan.ctx
-    grad = grad.reshape((2,) * len(bits) + (-1, grad.shape[-1]))
-    for bit in reversed(bits):
-        place = grad.ndim - 3
+def spread_back(grad, plan, bits):
+    hold = None
+    columns = grad.shape[-1]
+    present = plan.near + plan.ctx
+    grad = grad.reshape((2,) * len(present) + (-1, columns))
+    for bit in bits:
+        place = present.index(bit)
+        present = present[:place] + present[place + 1 :]
         mine, theirs = halves(grad, bit, place)
-        other = swap(theirs, bit)
+        other = swap(jnp.squeeze(theirs, place), bit)
         hold = yield hold
         other, hold = tie_to(other, hold)
-        grad = jnp.squeeze(jnp.concatenate(in_order(bit, mine, other), axis=-1), place)
+        grad = jnp.concatenate(in_order(bit, jnp.squeeze(mine, place), other), axis=-1)
+    order = bits[::-1]
+    if order != plan.near + plan.ctx:
+        grad = grad.reshape((grad.shape[0],) + (2,) * len(bits) + (columns,))
+        axes = [1 + order.index(bit) for bit in plan.near + plan.ctx]
+        grad = grad.transpose([0] + axes + [len(bits) + 1]).reshape(grad.shape[0], -1)
     return grad, hold
 
 
@@ -197,7 +214,7 @@
     links = len(plan.links)
     step = 16
     units = count // step
-    sizes = [(units // links + (1 if i < units % links else 0)) * step for i in range(links)]
+    sizes = [(units + i) // links * step for i in range(links)]
     parts = []
     start = 0
     for i, size in enumerate(sizes):
@@ -261,6 +278,259 @@
 def sum_rows(partial_rows, plan):
     mine, theirs = halves(partial_rows, plan.tensor, 0)
     return mine.astype(f32) + swap(theirs.astype(bf16), plan.tensor).astype(f32)
+
+
+FREE = pl.CostEstimate(flops=0, bytes_accessed=0, transcendentals=0)
+PARAMS = pltpu.CompilerParams(vmem_limit_bytes=48 * 2**20)
+NN = (((1,), (0,)), ((), ()))
+NT = (((1,), (1,)), ((), ()))
+TN = (((0,), (0,)), ((), ()))
+
+
+def dot(left, right, dims):
+    return lax.dot_general(left, right, dims, preferred_element_type=f32)
+
+
+def tile_of(size, most):
+    return max(tile for tile in range(LANES, most + 1, LANES) if size % tile == 0)
+
+
+def hidden_kernel(
+    half_ref, rows_ref, grad_ref, gate_ref, up_ref, down_ref, bias_ref, hidden_ref, gate_grad_ref, up_grad_ref, sums_ref
+):
+    gate = dot(rows_ref[...], gate_ref[...], NN) + bias_ref[0:1]
+    up = dot(rows_ref[...], up_ref[...], NN) + bias_ref[1:2]
+    hidden_grad = dot(grad_ref[...], down_ref[...], NN)
+    square = gate * gate
+    bend = jnp.tanh(GELU_SCALE * gate * (1.0 + GELU_CUBE * square))
+    half = 0.5 * (1.0 + bend)
+    activated = gate * half
+    slope = half + 0.5 * gate * (1.0 - bend * bend) * (
+        GELU_SCALE * (1.0 + 3.0 * GELU_CUBE * square)
+    )
+    hidden_ref[...] = (activated * up).astype(bf16)
+    gate_grad = hidden_grad * up * slope
+    up_grad = hidden_grad * activated
+    gate_grad_ref[...] = gate_grad.astype(bf16)
+    up_grad_ref[...] = up_grad.astype(bf16)
+
+    @pl.when(pl.program_id(0) == 0)
+    def _():
+        sums_ref[...] = jnp.zeros_like(sums_ref)
+
+    sums_ref[0:1] += jnp.sum(gate_grad, axis=0, keepdims=True)
+    sums_ref[1:2] += jnp.sum(up_grad, axis=0, keepdims=True)
+
+
+def hidden_units(half, rows, grads, gate, up, down, bias):
+    count, width = rows.shape
+    block = gate.shape[1]
+    tile = tile_of(count, 256)
+    weight_spec = pl.BlockSpec((width, block), lambda i, half: (0, 0))
+    unit_spec = pl.BlockSpec((tile, block), lambda i, half: (i, 0))
+    pair_spec = pl.BlockSpec((2, block), lambda i, half: (0, 0))
+    return pl.pallas_call(
+        hidden_kernel,
+        grid_spec=pltpu.PrefetchScalarGridSpec(
+            num_scalar_prefetch=1,
+            grid=(count // tile,),
+            in_specs=[
+                pl.BlockSpec((tile, width), lambda i, half: (i, 0)),
+                pl.BlockSpec((tile, width), lambda i, half: (half[0] * (count // tile) + i, 0)),
+                weight_spec,
+                weight_spec,
+                weight_spec,
+                pair_spec,
+            ],
+            out_specs=[unit_spec, unit_spec, unit_spec, pair_spec],
+        ),
+        out_shape=[jax.ShapeDtypeStruct((count, block), bf16)] * 3
+        + [jax.ShapeDtypeStruct((2, block), f32)],
+        cost_estimate=FREE,
+        compiler_params=PARAMS,
+    )(half, rows, grads, gate, up, down, bias)
+
+
+def rows_kernel(*refs):
+    *pairs, out_ref = refs
+    half = len(pairs) // 2
+    out_ref[...] = sum(
+        dot(left[...], right[...], NT)
+        for left, right in zip(pairs[:half], pairs[half:], strict=True)
+    ).astype(out_ref.dtype)
+
+
+def rows_out(lefts, rights, kind=bf16, starts=None):
+    count = lefts[0].shape[0]
+    width = rights[0].shape[0]
+    tile = tile_of(count, 256)
+    depths = [item.shape[1] for item in lefts]
+    places = [start // depth for start, depth in zip(starts or [0] * len(lefts), depths, strict=True)]
+    return pl.pallas_call(
+        rows_kernel,
+        grid=(count // tile,),
+        in_specs=[pl.BlockSpec((tile, depth), lambda i: (i, 0)) for depth in depths]
+        + [
+            pl.BlockSpec((width, depth), partial(lambda place, i: (0, place), place))
+            for depth, place in zip(depths, places, strict=True)
+        ],
+        out_specs=pl.BlockSpec((tile, width), lambda i: (i, 0)),
+        out_shape=jax.ShapeDtypeStruct((count, width), kind),
+        cost_estimate=FREE,
+        compiler_params=PARAMS,
+    )(*lefts, *rights)
+
+
+def turn(vectors, cosine, sine):
+    lead = vectors[:, : HD // 2]
+    lead = lead * cosine + pltpu.roll(lead, HD // 4, 1) * sine
+    return jnp.concatenate([lead, vectors[:, HD // 2 :]], axis=1)
+
+
+def attend_kernel(
+    rows_ref, weight_ref, keys_ref, values_ref, allowed_ref, cosine_ref, sine_ref, queries_ref, context_ref, log_ref
+):
+    queries = dot(rows_ref[...], weight_ref[...], NN)
+    queries = (turn(queries, cosine_ref[...], sine_ref[...]) * HD ** (-0.5)).astype(bf16)
+    queries_ref[...] = queries
+    scores = jnp.where(allowed_ref[...] > 0, dot(queries, keys_ref[...], NT), -1e30)
+    peak = jnp.max(scores, axis=1, keepdims=True)
+    powers = jnp.exp(scores - peak)
+    total = jnp.sum(powers, axis=1, keepdims=True)
+    probs_low = (powers / total).astype(bf16)
+    context_ref[...] = dot(probs_low, values_ref[...], NN).astype(bf16)
+    log_ref[...] = jnp.broadcast_to(peak + jnp.log(total), log_ref.shape)
+
+
+def attend(rows, weights, keyvalue, allowed, cosine, sine, head_count):
+    count, width = rows.shape
+    length = keyvalue.shape[0]
+    head = pl.BlockSpec((count, HD), lambda h: (0, h))
+    table = pl.BlockSpec((count, HD // 2), lambda h: (0, 0))
+    return pl.pallas_call(
+        attend_kernel,
+        grid=(head_count,),
+        in_specs=[
+            pl.BlockSpec((count, width), lambda h: (0, 0)),
+            pl.BlockSpec((width, HD), lambda h: (0, h)),
+            pl.BlockSpec((length, HD), lambda h: (0, 0)),
+            pl.BlockSpec((length, HD), lambda h: (0, 1)),
+            pl.BlockSpec((count, length), lambda h: (0, 0)),
+            table,
+            table,
+        ],
+        out_specs=[head, head, pl.BlockSpec((count, LANES), lambda h: (0, h))],
+        out_shape=[jax.ShapeDtypeStruct((count, head_count * HD), bf16)] * 2
+        + [jax.ShapeDtypeStruct((count, head_count * LANES), f32)],
+        cost_estimate=FREE,
+        compiler_params=PARAMS,
+    )(rows, weights, keyvalue, keyvalue, allowed, cosine, sine)
+
+
+def attend_back_kernel(
+    rows_ref, weight_ref, queries_ref, log_ref, keys_ref, values_ref, allowed_ref, cosine_ref, sine_ref, query_ref, sums_ref
+):
+    context_grad = dot(rows_ref[...], weight_ref[...], NN).astype(bf16)
+    queries, keys = queries_ref[...], keys_ref[...]
+    scores = jnp.where(allowed_ref[...] > 0, dot(queries, keys, NT), -1e30)
+    probs = jnp.exp(scores - log_ref[:, :1])
+    probs_grad = dot(context_grad, values_ref[...], NT)
+    prob_dot = jnp.sum(probs * probs_grad, axis=1, keepdims=True)
+    score_grad = (probs * (probs_grad - prob_dot)).astype(bf16)
+    query_grad = dot(score_grad, keys, NN) * HD ** (-0.5)
+    query_ref[...] = turn(query_grad, cosine_ref[...], -sine_ref[...]).astype(bf16)
+
+    @pl.when(pl.program_id(0) == 0)
+    def _():
+        sums_ref[...] = jnp.zeros_like(sums_ref)
+
+    sums_ref[:, :HD] += dot(score_grad, queries, TN)
+    sums_ref[:, HD:] += dot(probs.astype(bf16), context_grad, TN)
+
+
+def attend_back(rows, weights, queries, logs, keyvalue, allowed, cosine, sine):
+    count, width = rows.shape
+    length = keyvalue.shape[0]
+    head = pl.BlockSpec((count, HD), lambda h: (0, h))
+    table = pl.BlockSpec((count, HD // 2), lambda h: (0, 0))
+    return pl.pallas_call(
+        attend_back_kernel,
+        grid=(queries.shape[1] // HD,),
+        in_specs=[
+            pl.BlockSpec((count, width), lambda h: (0, 0)),
+            pl.BlockSpec((width, HD), lambda h: (0, h)),
+            head,
+            pl.BlockSpec((count, LANES), lambda h: (0, h)),
+            pl.BlockSpec((length, HD), lambda h: (0, 0)),
+            pl.BlockSpec((length, HD), lambda h: (0, 1)),
+            pl.BlockSpec((count, length), lambda h: (0, 0)),
+            table,
+            table,
+        ],
+        out_specs=[head, pl.BlockSpec((length, 2 * HD), lambda h: (0, 0))],
+        out_shape=[
+            jax.ShapeDtypeStruct(queries.shape, bf16),
+            jax.ShapeDtypeStruct((length, 2 * HD), f32),
+        ],
+        cost_estimate=FREE,
+        compiler_params=PARAMS,
+    )(rows, weights, queries, logs, keyvalue, keyvalue, allowed, cosine, sine)
+
+
+def weight_kernel(groups, half_ref, *refs):
+    *pairs, out_ref = refs
+    start = 0
+    for lefts, rights in groups:
+        size = pairs[rights[0]].shape[1]
+        out_ref[:, start : start + size] = sum(
+            dot(pairs[left][...], pairs[right][...], TN)
+            for left, right in zip(lefts, rights, strict=True)
+        ).astype(out_ref.dtype)
+        start += size
+
+
+def weight_out(half, *products):
+    arrays, specs, groups, columns = [], [], [], 0
+    count = products[0][1][0].shape[0]
+    width = products[0][0][0].shape[1]
+    tile = tile_of(width, 512)
+    straight = pl.BlockSpec((count, tile), lambda i, half: (0, i))
+    first = pl.BlockSpec((count, tile), lambda i, half: (half[0], i))
+    second = pl.BlockSpec((count, tile), lambda i, half: (1 - half[0], i))
+    known = {}
+    for lefts, rights in products:
+        halved = len(lefts) < len(rights)
+        group = []
+        for items, item_specs in (
+            (lefts * 2 if halved else lefts, [first, second] if halved else [straight] * len(lefts)),
+            (
+                rights,
+                [pl.BlockSpec((count, item.shape[1]), lambda i, half: (0, 0)) for item in rights],
+            ),
+        ):
+            places = []
+            for item, spec in zip(items, item_specs, strict=True):
+                key = (id(item), id(spec) if halved else 0)
+                if key not in known:
+                    known[key] = len(arrays)
+                    arrays.append(item)
+                    specs.append(spec)
+                places.append(known[key])
+            group.append(places)
+        groups.append(group)
+        columns += rights[0].shape[1]
+    return pl.pallas_call(
+        partial(weight_kernel, groups),
+        grid_spec=pltpu.PrefetchScalarGridSpec(
+            num_scalar_prefetch=1,
+            grid=(width // tile,),
+            in_specs=specs,
+            out_specs=pl.BlockSpec((tile, columns), lambda i, half: (i, 0)),
+        ),
+        out_shape=jax.ShapeDtypeStruct((width, columns), bf16),
+        cost_estimate=FREE,
+        compiler_params=PARAMS,
+    )(half, *arrays)
 
 
 def local(
@@ -308,7 +578,9 @@
         (own_segments[:, None] == segments[None, :])
         & (key_index[None, :] <= query_index[:, None])
         & (query_index[:, None] - key_index[None, :] < WINDOW)
-    )
+    ).astype(f32)
+    cosine_both = jnp.concatenate([cosine_table, cosine_table], axis=1)
+    sine_both = jnp.concatenate([-sine_table, sine_table], axis=1)
 
     def by_block(item):
         return lax.all_to_all(
@@ -336,9 +608,10 @@
     full_output = lax.all_gather(output_weight.T, DP_CTX, axis=0, tiled=True)
 
     first, raw_other, *ff_rows = tie(first, raw_other, down_rows, gate_rows, up_rows)
-    ff_in = Journey(repeat_in(ff_rows, plan, 2))
+    full_ff = []
+    ff_in = Journey(repeat_in(ff_rows, plan, 2, full_ff))
     block_start = (lax.axis_index("near") * (blocks // 2) + ctx_index) * block
-    pair_bias = jnp.concatenate(
+    pair_bias = jnp.stack(
         [
             lax.dynamic_slice_in_dim(jnp.pad(item, (0, ff_pad)), block_start, block)
             for item in (gate_bias, up_bias)
@@ -346,15 +619,13 @@
     ).astype(f32)
 
     query_columns, keyvalue_columns = query_weight.shape[1], keyvalue_weight.shape[1]
-    full_query = first[:, :query_columns]
     full_keyvalue = first[:, query_columns : query_columns + keyvalue_columns]
     vectors = first[:, query_columns + keyvalue_columns :].astype(f32)
     gain_one, full_obias, gain_two, full_dbias = (vectors[:, i] for i in range(4))
     norm_one_pull = jax.vjp(norm_scale, local_in, gain_one)[1]
     raw_rows = jnp.concatenate(in_order(plan.tensor, raw, raw_other), axis=0)
     normed = norm_scale(raw_rows.astype(f32), gain_one).astype(bf16)
-    length = segments.shape[0]
-    head_count = full_query.shape[1] // HD
+    head_count = query_columns // HD
     half_proj = jnp.dot(normed, full_keyvalue, preferred_element_type=f32)
     half_low = jnp.where(
         is_key, rotate(half_proj[:, None, :], cosine_table, sine_table, 1.0)[:, 0], half_proj
@@ -365,27 +636,14 @@
         if bit == plan.y[-1]:
             keyvalue = ff_in.step(keyvalue)
     keyvalue, grad_local = tie(keyvalue, grad_local)
-    all_keys = keyvalue[:, :HD]
-    all_values = keyvalue[:, HD:]
     all_grads = lax.all_gather(
         grad_local, ("core", "near", "y", "tensor"), axis=0, tiled=True
-    ).reshape(2, -1, width)
-    query_proj = jnp.dot(normed, full_query, preferred_element_type=f32)
-    queries = (
-        rotate(query_proj.reshape(row_count, head_count, HD), cosine_table, sine_table, 1.0)
-        * HD ** (-0.5)
-    ).astype(bf16)
-    queries = ff_in.step(queries)
-    scores = jnp.einsum("qhd,kd->hqk", queries, all_keys, preferred_element_type=f32)
-    scores = jnp.where(allowed[None], scores, -1e30)
-    score_peak = jnp.max(scores, axis=-1, keepdims=True)
-    exp_scores = jnp.exp(scores - score_peak)
-    exp_total = jnp.sum(exp_scores, axis=-1, keepdims=True)
-    probs = exp_scores / exp_total
-    probs_low = probs.astype(bf16)
-    context = jnp.einsum("hqk,kd->qhd", probs_low, all_values, preferred_element_type=f32)
-    context = context.astype(bf16).reshape(row_count, head_count * HD)
-    attended = jnp.einsum("rc,dc->rd", context, full_output, preferred_element_type=f32)
+    )
+    keyvalue = ff_in.step(keyvalue)
+    queries, context, logs = attend(
+        normed, first, keyvalue, allowed, cosine_both, sine_both, head_count
+    )
+    attended = rows_out([context], [full_output], f32)
     attended = ff_in.step(attended)
     mixed = local_in + sum_rows(attended, plan) + full_obias
     mixed = ff_in.step(mixed)
@@ -394,48 +652,32 @@
     journey = Journey(gather_tokens(normed_two_local.astype(bf16), plan))
     mixed = ff_in.step(journey.step(mixed))
     mixed = ff_in.finish(journey.step(mixed))
+    mixed, full_ff = tie(mixed, full_ff)
     mixed = journey.finish(mixed)
     normed_two = journey.result
-    full_down, full_gate, full_up = ff_in.result
-    full_pair = jnp.concatenate([full_gate, full_up], axis=1)
+    full_down, full_gate, full_up = full_ff
     core = lax.axis_index("core")
-    grad_rows = [
-        lax.dynamic_index_in_dim(all_grads, item, 0, keepdims=False) for item in (core, 1 - core)
-    ]
-    hidden, pair_grad, pair_bias_grad = [], [], 0.0
-    for rows_two, rows_grad in zip(normed_two, grad_rows, strict=True):
-        hidden_grad = jnp.dot(rows_grad, full_down, preferred_element_type=f32)
-        pair_pre = jnp.dot(rows_two, full_pair, preferred_element_type=f32) + pair_bias
-        gate_pre, up_pre = pair_pre[:, :block], pair_pre[:, block:]
-        activated, gelu_pull = jax.vjp(partial(jax.nn.gelu, approximate=True), gate_pre)
-        hidden.append((activated * up_pre).astype(bf16))
-        pair_full = jnp.concatenate(
-            [gelu_pull(hidden_grad * up_pre)[0], hidden_grad * activated], axis=1
-        )
-        pair_bias_grad = pair_bias_grad + jnp.sum(pair_full, axis=0)
-        pair_grad.append(pair_full.astype(bf16))
-
-    def rows_out(rows, weight):
-        return jnp.einsum("rf,df->rd", rows, weight, preferred_element_type=f32).astype(bf16)
-
-    def weight_out(lefts, rights):
-        return sum(
-            jnp.einsum("rd,rf->df", left, right, preferred_element_type=f32)
-            for left, right in zip(lefts, rights, strict=True)
-        ).astype(bf16)
-
-    two_other = rows_out(pair_grad[1], full_pair)
-    two_other, pair_grad = tie(two_other, pair_grad)
-    two_own = rows_out(pair_grad[0], full_pair)
+    own_half, other_half = (jnp.full((1,), item, jnp.int32) for item in (core, 1 - core))
+    weights = (full_gate, full_up, full_down, pair_bias)
+    own_part = hidden_units(own_half, normed_two[0], all_grads, *weights)
+    normed_two[1], own_part = tie(normed_two[1], own_part)
+    parts = [own_part, hidden_units(other_half, normed_two[1], all_grads, *weights)]
+    hidden, gate_grad, up_grad, bias_sums = (list(item) for item in zip(*parts, strict=True))
+    pair_weights = [full_gate, full_up]
+    two_other = rows_out([gate_grad[1], up_grad[1]], pair_weights)
+    ff_small = Journey(spread_small(sum(bias_sums), plan))
+    two_other, gate_grad, up_grad = tie(two_other, gate_grad, up_grad)
+    two_own = rows_out([gate_grad[0], up_grad[0]], pair_weights)
+    two_own = ff_small.step(two_own)
     two_sum = Journey(reduce_tokens(two_own, two_other, plan, token_count))
-    hidden = two_sum.step(hidden)
-    down_wgrad = weight_out(grad_rows, hidden)
-    down_wgrad, pair_grad = two_sum.step((down_wgrad, pair_grad))
-    down_sum = Journey(spread_out(down_wgrad, plan))
-    out_other = rows_out(hidden[1], full_down)
-    out_other, hidden, pair_grad = two_sum.step((out_other, hidden, pair_grad))
-    out_own = rows_out(hidden[0], full_down)
-    out_own, out_other, pair_grad = two_sum.finish((out_own, out_other, pair_grad))
+    gate_grad, up_grad, hidden = two_sum.step((gate_grad, up_grad, hidden))
+    ff_wgrad = weight_out(
+        own_half, ([all_grads], hidden), (normed_two, gate_grad), (normed_two, up_grad)
+    )
+    ff_wgrad, hidden = ff_small.step(two_sum.step((ff_wgrad, hidden)))
+    ff_sum = lax.psum_scatter(ff_wgrad, "far", scatter_dimension=0, tiled=True)
+    hidden = ff_small.step(two_sum.step(hidden))
+    hidden = two_sum.finish(hidden)
     two_grad = two_sum.result
 
     grad_full = grad_local.astype(f32)
@@ -445,102 +687,79 @@
     obias_part = jnp.sum(mixed_grad, axis=0)
     mixed_low = mixed_grad.astype(bf16)
     mixed_other = swap(mixed_low, plan.tensor)
-    out_other, mixed_low = tie(out_other, mixed_low)
+    hidden, mixed_low = tie(hidden, mixed_low)
+    out_other = rows_out([hidden[1]], [full_down])
+    out_other, hidden = tie(out_other, hidden)
+    out_own = rows_out([hidden[0]], [full_down])
     out_sum = Journey(reduce_tokens(out_own, out_other, plan, token_count))
-    pair_grad, mixed_low = out_sum.step((pair_grad, mixed_low))
-    gate_wgrad = weight_out(normed_two, [item[:, :block] for item in pair_grad])
-    mixed_other, gate_wgrad = tie(mixed_other, gate_wgrad)
-    gate_sum = Journey(spread_out(gate_wgrad, plan))
+    mixed_other, out_own = tie(mixed_other, out_own)
     attn_rows = jnp.concatenate(in_order(plan.tensor, mixed_low, mixed_other), axis=0)
-    context_grad = jnp.dot(attn_rows, full_output, preferred_element_type=f32).astype(bf16)
-    context_grad = context_grad.reshape(row_count, head_count, HD)
-    context_grad, attn_rows = tie(context_grad, attn_rows)
-    order = plan.ctx[::-1] + plan.near + plan.far[::-1]
-    output_wgrad = jnp.einsum("rd,rc->dc", attn_rows, context, preferred_element_type=f32)
-    context_grad, output_wgrad = tie(context_grad, output_wgrad.astype(bf16))
-    output_sum = Journey(reduce_rows([output_wgrad], plan, [order]))
-    probs_grad = jnp.einsum("qhd,kd->hqk", context_grad, all_values, preferred_element_type=f32)
-    values_grad = jnp.einsum("hqk,qhd->kd", probs_low, context_grad, preferred_element_type=f32)
-    prob_dot = jnp.sum(probs * probs_grad, axis=-1, keepdims=True)
-    score_grad = (probs * (probs_grad - prob_dot)).astype(bf16)
-    score_grad = output_sum.step(score_grad)
-    keys_grad = jnp.einsum("hqk,qhd->kd", score_grad, queries, preferred_element_type=f32)
-    stacked = jnp.concatenate([keys_grad, values_grad], axis=1)
-    query_grad = jnp.einsum("hqk,kd->qhd", score_grad, all_keys, preferred_element_type=f32)
-    query_proj_grad = rotate(query_grad * HD ** (-0.5), cosine_table, sine_table, -1.0)
-    query_proj_grad = query_proj_grad.reshape(row_count, head_count * HD).astype(bf16)
-    query_proj_grad = out_sum.step(query_proj_grad)
-    query_wgrad = jnp.einsum("rd,rc->dc", normed, query_proj_grad, preferred_element_type=f32)
-    query_wgrad = query_wgrad.astype(bf16)
+    order_one = plan.ctx[::-1] + plan.near + plan.far[::-1]
+    order_two = [plan.core] + plan.near + plan.y[::-1] + plan.far[::-1]
+    attn_rows = ff_small.finish(out_sum.step(attn_rows))
+    query_proj_grad, stacked = attend_back(
+        attn_rows, full_output, queries, logs, keyvalue, allowed, cosine_both, sine_both
+    )
+    stacked, query_proj_grad, attn_rows = tie(stacked, query_proj_grad, attn_rows)
+    query_wgrad = weight_out(own_half, ([normed], [query_proj_grad]))
     for bit in reversed(plan.ctx):
         half = stacked.shape[0] // 2
         other = swap(stacked[half:].astype(bf16), bit)
         if bit == plan.core:
-            pair_grad, query_wgrad = tie(pair_grad, query_wgrad)
-            up_wgrad = weight_out(normed_two, [item[:, block:] for item in pair_grad])
-            other, up_wgrad, query_wgrad = out_sum.step((other, up_wgrad, query_wgrad))
-            other, up_wgrad, query_wgrad = down_sum.step((other, up_wgrad, query_wgrad))
-            up_sum = Journey(spread_out(up_wgrad, plan))
-            query_sum = Journey(reduce_rows([query_wgrad], plan, [order]))
+            other, query_wgrad, attn_rows = tie(other, query_wgrad, attn_rows)
+            query_sum = Journey(reduce_rows([query_wgrad], plan, [order_one]))
+            output_wgrad = weight_out(own_half, ([attn_rows], [context]))
+        elif bit == plan.y[-1]:
+            other, output_wgrad = query_sum.step(out_sum.step((other, output_wgrad)))
         stacked = stacked[:half] + other.astype(f32)
     mine, theirs = halves(stacked, plan.tensor, 1)
     half_grad = mine + swap(theirs.astype(bf16), plan.tensor).astype(f32)
-    half_grad = query_sum.step(half_grad)
     half_grad = jnp.where(
         is_key, rotate(half_grad[:, None, :], cosine_table, sine_table, -1.0)[:, 0], half_grad
     ).astype(bf16)
-    one_part = jnp.einsum(
-        "rc,dc->rd", query_proj_grad, full_query, preferred_element_type=f32
-    ) + jnp.einsum("rc,dc->rd", half_grad, full_keyvalue, preferred_element_type=f32)
+    one_part = rows_out([query_proj_grad, half_grad], [first, first], f32, [0, query_columns])
     mine, theirs = halves(one_part, plan.tensor, 0)
-    theirs, half_grad = tie(theirs.astype(bf16), half_grad)
+    theirs, half_grad, output_wgrad = tie(theirs.astype(bf16), half_grad, output_wgrad)
     other = swap(theirs, plan.tensor)
-    keyvalue_wgrad = jnp.einsum("rd,rc->dc", normed, half_grad, preferred_element_type=f32)
-    keyvalue_wgrad = out_sum.finish(keyvalue_wgrad.astype(bf16))
-    keyvalue_wgrad = output_sum.step(keyvalue_wgrad)
-    keyvalue_wgrad = down_sum.step(keyvalue_wgrad)
-    keyvalue_sum = Journey(reduce_rows([keyvalue_wgrad], plan, [order]))
-    block_output = (mixed + out_sum.result + full_dbias).astype(bf16)
-    block_output = gate_sum.step(block_output)
-    other, block_output = tie(other, block_output)
+    keyvalue_wgrad = weight_out(own_half, ([normed], [half_grad]))
+    other, keyvalue_wgrad, output_wgrad = out_sum.step((other, keyvalue_wgrad, output_wgrad))
     input_part, gain_one_part = norm_one_pull(mine + other.astype(f32))
     input_grad = mixed_grad + input_part
-
-    for item in (
-        keyvalue_sum,
-        gate_sum,
-        down_sum,
-        output_sum,
-        query_sum,
-        up_sum,
-        gate_sum,
-        down_sum,
-        up_sum,
-        keyvalue_sum,
-        output_sum,
-        query_sum,
-    ):
-        input_grad = item.step(input_grad)
+    input_grad, output_wgrad, keyvalue_wgrad = out_sum.finish(
+        (input_grad, output_wgrad, keyvalue_wgrad)
+    )
+    block_output = (mixed + out_sum.result + full_dbias).astype(bf16)
 
     small = jnp.stack([gain_one_part, gain_two_part, obias_part, dbias_part], axis=0)
     small = small.reshape(4, -1, shard_rows).transpose(1, 0, 2)
-    small, pair_bias_grad, input_grad = tie(small, pair_bias_grad, input_grad)
     small = small + swap(small, plan.tensor)
-    small_sum = Journey(reduce_rows([small.reshape(-1, shard_rows)], plan, [order], f32))
-    ff_small = Journey(spread_small(pair_bias_grad.reshape(2, block), plan))
-    journeys = [query_sum, gate_sum, up_sum, output_sum, small_sum, ff_small, keyvalue_sum, down_sum]
-    while any(item.result is None for item in journeys):
-        for item in journeys:
-            if item.result is None:
-                input_grad = item.step(input_grad)
+    small_sum = Journey(reduce_rows([small.reshape(-1, shard_rows)], plan, [order_one], f32))
+    keyvalue_sum = Journey(reduce_rows([keyvalue_wgrad], plan, [order_one]))
+    for item in (small_sum, keyvalue_sum, query_sum):
+        input_grad = item.step(input_grad)
+    output_wgrad, input_grad = tie(output_wgrad, input_grad)
+    output_sum = Journey(reduce_rows([output_wgrad], plan, [order_one]))
+    for item in (small_sum, keyvalue_sum, output_sum):
+        input_grad = item.step(input_grad)
+    ff_sum, input_grad = tie(ff_sum, input_grad)
+    y_first = [plan.core] + plan.y[::-1] + plan.near[::-1]
+    near_first = [plan.core] + plan.near[::-1] + plan.y[::-1]
+    backs = [
+        Journey(spread_back(ff_sum[:, i * block : (i + 1) * block], plan, bits))
+        for i, bits in enumerate((y_first, near_first, y_first))
+    ]
+    for item in (small_sum, keyvalue_sum, query_sum, *backs, small_sum, keyvalue_sum):
+        if item.result is None:
+            input_grad = item.step(input_grad)
+    input_grad = finish_all(
+        [output_sum, *backs, keyvalue_sum, small_sum, query_sum], input_grad
+    )
     proj_out = output_sum.result[0]
     query_out = query_sum.result[0]
     keyvalue_out = keyvalue_sum.result[0]
     small = small_sum.result[0].reshape(4, shard_rows)
     ff_small = ff_small.result
-    down_out, gate_out, up_out = (
-        item.result[:, :ff_half].astype(f32) for item in (down_sum, gate_sum, up_sum)
-    )
+    down_out, gate_out, up_out = (item.result[:, :ff_half].astype(f32) for item in backs)
     return (
         block_output[None],
         input_grad[None],

time: 882 us -> 855 us (0.969)
  matrix products: 141 us -> 2.36 us
  Pallas kernels: 0 us -> 122 us
  other arithmetic: 110 us -> 79.2 us
  waiting for transfers between devices: 438 us -> 459 us
    dot_general x28 -> x0, matrix products: 140 us -> none  [the longest x6 34.7 us: weight_out(): jnp.einsum('rd,rf->df', left, right, preferred_element_type=f32)]
    pallas_call x0 -> x14, Pallas kernels: none -> 122 us  [the longest x6 38.8 us: rows_out(): pl.pallas_call(rows_kernel, grid=(count // tile,), in_specs=[pl.BlockSpec...]
    ppermute x78, waiting for transfers between devices: 364 us -> 386 us  [swap(): lax.ppermute(values, axis, [(i, i ^ mask) for i in range(lax.axis_size(ax...]
    reshape x1 -> x2, local copies, waits for them, and re-layouts: 0.01 us -> 8.96 us  [the longest x1 4.61 us: spread_back(): grad = grad.reshape((grad.shape[0],) + (2,) * len(bits) + (columns,))]
    unnamed x303 -> x175, local copies, waits for them, and re-layouts: 27.4 us -> 28.5 us
  transfers between devices with their start and end apart: 87 -> 85, of which waited for: 42 -> 38; matrix products, arithmetic and copies ran while one was open for 32% -> 13% of each run, Pallas kernels for 0% -> 11%
where the time goes in v3:
time: 855 us; the launch traced here: 847 us
  waiting for transfers between devices  459 us (54%)
  Pallas kernels  122 us (14%)
  local copies, waits for them, and re-layouts  87.2 us (10%)
  starting transfers between devices  80.9 us (9%)
  other arithmetic  79.2 us (9%)
  between operations  16.1 us (2%)
    ppermute x78, waiting for transfers between devices, swap(): lax.ppermute(values, axis, [(i, i ^ mask) for i in range(lax.axis_size(ax...  386 us
    all_to_all x3, waiting for transfers between devices, by_block(): lax.all_to_all(jnp.pad(item, ((0, 0), (0, ff_pad))), ('near',) + CTX, spl...  72.2 us
    ppermute x78, starting transfers between devices, swap(): lax.ppermute(values, axis, [(i, i ^ mask) for i in range(lax.axis_size(ax...  66.5 us
    pallas_call x6, Pallas kernels, rows_out(): pl.pallas_call(rows_kernel, grid=(count // tile,), in_specs=[pl.BlockSpec...  38.8 us
    pallas_call x4, Pallas kernels, weight_out(): pl.pallas_call(partial(weight_kernel, groups), grid_spec=pltpu.PrefetchSc...  33.2 us
    unnamed x175, local copies, waits for them, and re-layouts  28.5 us
    pallas_call x2, Pallas kernels, hidden_units(): pl.pallas_call(hidden_kernel, grid_spec=pltpu.PrefetchScalarGridSpec(num_...  25.7 us
  transfers between devices with their start and end apart: 85, of which 38 were waited for; matrix products, arithmetic and copies ran while one was open for 13% of the time, Pallas kernels for 11%

profile of v3, /device:TPU:0, one launch (start us, length us, event | category | flops | bytes accessed | tf_op | source)
XLA Modules:
  0.0 847.2 jit_solution(9201862325510489553)
XLA Ops:
  13.4 5.4 all-to-all-start
  20.8 28.8 %all-to-all-done = bf16[160,8,512]{2,0,1:T(8,128)(2,1)S(1)} async-done(((bf16[160,8,512]{2,0,1:T(8,128)(2,1)}), bf16[160,8,512]{2,0,1:T(8,128)(2,1)S(1)}, u32[]{:S(2)}, u32[]{:S(2)}) %all-to-all-start) | async-done | bytes 1310752 | tf_op jit(solution)/shard_map/all_to_all | solution.py:586
  49.6 4.2 all-to-all-start.1
  56.5 34.6 %all-to-all-done.1 = bf16[160,8,512]{2,0,1:T(8,128)(2,1)S(1)} async-done(((bf16[160,8,512]{2,0,1:T(8,128)(2,1)}), bf16[160,8,512]{2,0,1:T(8,128)(2,1)S(1)}, u32[]{:S(2)}, u32[]{:S(2)}) %all-to-all-start.1) | async-done | bytes 1310752 | tf_op jit(solution)/shard_map/all_to_all | solution.py:586
  92.2 4.4 all-to-all-start.2
  100.1 7.4 collective-permute-done.2
  108.9 4.8 collective-permute-done
  113.7 8.7 %all-to-all-done.2 = bf16[160,8,512]{2,0,1:T(8,128)(2,1)} async-done(((bf16[160,8,512]{2,0,1:T(8,128)(2,1)}), bf16[160,8,512]{2,0,1:T(8,128)(2,1)}, u32[]{:S(2)}, u32[]{:S(2)}) %all-to-all-start.2) | async-done | bytes 1310752 | tf_op jit(solution)/shard_map/all_to_all | solution.py:586
  124.0 2.7 slice_reduce_fusion
  131.8 4.0 collective-permute-start.1
  138.4 5.1 collective-permute-done.5
  143.6 33.7 %collective-permute-done.1 = bf16[640,512]{1,0:T(8,128)(2,1)S(1)} collective-permute-done((bf16[640,512]{1,0:T(8,128)(2,1)S(1)}, bf16[640,512]{1,0:T(8,128)(2,1)S(1)}, u32[]{:S(2)}, u32[]{:S(2)}) %collective-permute-start.1) | collective-permute-done | bytes 655392 | tf_op jit(solution)/shard_map/ppermute | solution.py:65
  180.7 47.6 %collective-permute-done.6 = bf16[640,512]{1,0:T(8,128)(2,1)} collective-permute-done((bf16[640,512]{1,0:T(8,128)(2,1)}, bf16[640,512]{1,0:T(8,128)(2,1)}, u32[]{:S(2)}, u32[]{:S(2)}) %collective-permute-start.6) | collective-permute-done | bytes 655392 | tf_op jit(solution)/shard_map/ppermute | solution.py:65
  229.4 2.5 fusion.92
  234.3 10.4 %shard_map.254 = (bf16[256,1280]{1,0:T(8,128)(2,1)S(1)}, bf16[256,1280]{1,0:T(8,128)(2,1)S(1)}, f32[256,640]{1,0:T(8,128)S(1)}) custom-call(bf16[256,2560]{1,0:T(8,128)(2,1)S(1)} %fusion.6.rows_ref.refs_0_, bf16[2560,1664]{1,0:T(8,128)(2,1)} %all-gather.4.cloned.1.call-done.weight_ref.refs_2_.refs_3_, ...), custom_call_target="tpu_custom_call" | custom-call | tf_op jit(solution)/shard_map/pallas_call | solution.py:410
  248.3 4.7 shard_map.255
  253.1 5.6 collective-permute-done.8
  264.9 24.0 %collective-permute-done.10 = bf16[128,2560]{1,0:T(8,128)(2,1)S(1)} collective-permute-done((bf16[128,2560]{1,0:T(8,128)(2,1)S(1)}, bf16[128,2560]{1,0:T(8,128)(2,1)S(1)}, u32[]{:S(2)}, u32[]{:S(2)}) %collective-permute-start.10) | collective-permute-done | bytes 655392 | tf_op jit(solution)/shard_map/ppermute | solution.py:65
  289.3 3.7 collective-permute-done.9
  299.2 4.2 collective-permute-done.11
  303.3 17.8 %collective-permute-done.13 = bf16[48,2560]{1,0:T(8,128)(2,1)S(1)} collective-permute-done((bf16[48,2560]{1,0:T(8,128)(2,1)S(1)}, bf16[48,2560]{1,0:T(8,128)(2,1)S(1)}, u32[]{:S(2)}, u32[]{:S(2)}) %collective-permute-start.13) | collective-permute-done | bytes 245792 | tf_op jit(solution)/shard_map/ppermute | solution.py:65
  321.9 4.5 collective-permute-done.17
  326.4 3.4 collective-permute-start.21
  329.8 30.6 %collective-permute-done.15 = bf16[2,48,2560]{2,1,0:T(8,128)(2,1)S(1)} collective-permute-done((bf16[2,48,2560]{2,1,0:T(8,128)(2,1)S(1)}, bf16[2,48,2560]{2,1,0:T(8,128)(2,1)S(1)}, u32[]{:S(2)}, u32[]{:S(2)}) %collective-permute-start.15) | collective-permute-done | bytes 491552 | tf_op jit(solution)/shard_map/ppermute | solution.py:65
  363.3 14.0 %collective-permute-done.18 = bf16[2,2,32,2560]{3,2,1,0:T(8,128)(2,1)S(1)} collective-permute-done((bf16[2,2,32,2560]{3,2,1,0:T(8,128)(2,1)S(1)}, bf16[2,2,32,2560]{3,2,1,0:T(8,128)(2,1)S(1)}, u32[]{:S(2)}, u32[]{:S(2)}) %collective-permute-start.18) | collective-permute-done | bytes 655392 | tf_op jit(solution)/shard_map/ppermute | solution.py:65
  377.4 5.5 collective-permute-done.19
  384.3 2.8 copy.93
  387.2 12.9 %shard_map.256 = (bf16[1024,512]{1,0:T(8,128)(2,1)S(1)}, bf16[1024,512]{1,0:T(8,128)(2,1)S(1)}, bf16[1024,512]{1,0:T(8,128)(2,1)S(1)}, f32[2,512]{1,0:T(2,128)S(1)}) custom-call(s32[1]{0:T(128)} %bitcast.44.half_ref, bf16[1024,2560]{1,0:T(8,128)(2,1)} %bitcast.43.rows_ref.refs_4_, bf16[2048,2560]{1,0:T(8,128)(2,1)} %all-gather.8.cloned.1.call-done.grad_ref.refs_0_.refs_1_, ...), custom_call_target="tpu_custom_call" | custom-call | tf_op jit(solution)/shard_map/pallas_call | solution.py:332
  403.0 12.8 %shard_map.257 = (bf16[1024,512]{1,0:T(8,128)(2,1)S(1)}, bf16[1024,512]{1,0:T(8,128)(2,1)S(1)}, bf16[1024,512]{1,0:T(8,128)(2,1)S(1)}, f32[2,512]{1,0:T(2,128)S(1)}) custom-call(s32[1]{0:T(128)} %bitcast.45.half_ref, bf16[1024,2560]{1,0:T(8,128)(2,1)} %collective-permute-done.22.rows_ref.refs_5_, ...), custom_call_target="tpu_custom_call" | custom-call | tf_op jit(solution)/shard_map/pallas_call | solution.py:332
  416.8 9.8 %shard_map.258 = bf16[1024,2560]{1,0:T(8,128)(2,1)} custom-call(bf16[1024,512]{1,0:T(8,128)(2,1)S(1)} %get-tuple-element.274.refs_0_.refs_7_, bf16[1024,512]{1,0:T(8,128)(2,1)S(1)} %get-tuple-element.276.refs_1_.refs_9_, bf16[2560,512]{1,0:T(8,128)(2,1)S(1)} %bitcast.376, bf16[2560,512]{1,0:T(8,128)(2,1)} %bitcast.381), custom_call_target="tpu_custom_call" | custom-call | tf_op jit(solution)/shard_map/pallas_call | solution.py:369
  430.5 9.1 %shard_map.259 = bf16[1024,2560]{1,0:T(8,128)(2,1)} custom-call(bf16[1024,512]{1,0:T(8,128)(2,1)S(1)} %copy-done.16, bf16[1024,512]{1,0:T(8,128)(2,1)S(1)} %copy-done.19, bf16[2560,512]{1,0:T(8,128)(2,1)S(1)} %bitcast.377, bf16[2560,512]{1,0:T(8,128)(2,1)} %bitcast.382), custom_call_target="tpu_custom_call" | custom-call | tf_op jit(solution)/shard_map/pallas_call | solution.py:369
  439.6 5.4 add_convert_fusion.1
  455.9 21.4 %shard_map.260 = bf16[2560,1536]{1,0:T(8,128)(2,1)} custom-call(s32[1]{0:T(128)} %bitcast.44.half_ref, bf16[2048,2560]{1,0:T(8,128)(2,1)} %all-gather.8.cloned.1.call-done.grad_ref.refs_0_.refs_1_, bf16[2048,2560]{1,0:T(8,128)(2,1)} %all-gather.8.cloned.1.call-done.grad_ref.refs_0_.refs_1_, bf16[1024,512]{1,0:T(8,128)(2,1)S(1)} %copy-done.10, ...), custom_call_target="tpu_custom_call" | custom-call | tf_op jit(solution)/shard_map/pallas_call | solution.py:522
  487.3 6.5 collective-permute-done.28
  502.2 2.6 collective-permute-done.35
  509.8 4.8 shard_map.261
  518.9 4.9 shard_map.262
  524.0 7.9 collective-permute-done.37
  533.2 5.4 add_convert_fusion
  542.3 14.0 %shard_map.263 = (bf16[256,1280]{1,0:T(8,128)(2,1)S(1)}, f32[1024,512]{1,0:T(8,128)}) custom-call(bf16[256,2560]{1,0:T(8,128)(2,1)S(1)} %pad_maximum_fusion.11.rows_ref.refs_0_, bf16[2560,1280]{1,0:T(8,128)(2,1)} %all-gather.6.cloned.1.call-done.refs_1_.weight_ref, bf16[256,1280]{1,0:T(8,128)(2,1)S(1)} %copy-done.30, f32[256,640]{1,0:T(8,128)S(1)} %copy-done.32, ...), custom_call_target="tpu_custom_call" | custom-call | tf_op jit(solution)/shard_map/pallas_call | solution.py:456
  562.9 5.0 shard_map.264
  569.1 3.4 constant_dynamic-slice_fusion.21
  575.2 5.0 shard_map.265
  580.2 11.3 %collective-permute-done.43 = bf16[256,512]{1,0:T(8,128)(2,1)S(1)} collective-permute-done((bf16[256,512]{1,0:T(8,128)(2,1)S(1)}, bf16[256,512]{1,0:T(8,128)(2,1)S(1)}, u32[]{:S(2)}, u32[]{:S(2)}) %collective-permute-start.43) | collective-permute-done | bytes 262176 | tf_op jit(solution)/shard_map/ppermute | solution.py:65
  600.9 4.3 collective-permute-done.48
  606.0 5.4 shard_map.266
  611.7 2.7 fusion.1
  620.9 6.8 collective-permute-done.49
  638.1 2.7 collective-permute-done.55
  641.0 3.1 fusion.13
  644.1 12.4 %collective-permute-done.51 = bf16[48,2560]{1,0:T(8,128)(2,1)} collective-permute-done((bf16[48,2560]{1,0:T(8,128)(2,1)}, bf16[48,2560]{1,0:T(8,128)(2,1)}, u32[]{:S(2)}, u32[]{:S(2)}) %collective-permute-start.51) | collective-permute-done | bytes 245792 | tf_op jit(solution)/shard_map/ppermute | solution.py:65
  659.7 3.5 constant_dynamic-slice_fusion.17
  672.9 20.9 %collective-permute-done.62 = f32[2,1,4,160]{3,1,0,2:T(1,128)S(1)} collective-permute-done((f32[2,1,4,160]{3,1,0,2:T(1,128)S(1)}, f32[2,1,4,160]{3,1,0,2:T(1,128)S(1)}, u32[]{:S(2)}, u32[]{:S(2)}) %collective-permute-start.62) | collective-permute-done | bytes 5152 | tf_op jit(solution)/shard_map/ppermute | solution.py:65
  698.3 16.4 %collective-permute-done.61 = bf16[2,1,160,256]{3,2,0,1:T(8,128)(2,1)S(1)} collective-permute-done((bf16[2,1,160,256]{3,2,0,1:T(8,128)(2,1)}, bf16[2,1,160,256]{3,2,0,1:T(8,128)(2,1)S(1)}, u32[]{:S(2)}, u32[]{:S(2)}) %collective-permute-start.61) | collective-permute-done | bytes 163872 | tf_op jit(solution)/shard_map/ppermute | solution.py:65
  714.9 2.4 fusion.91
  720.4 2.9 collective-permute-start.63
  724.3 13.0 %collective-permute-done.63 = bf16[1,160,256]{2,1,0:T(8,128)(2,1)S(1)} collective-permute-done((bf16[1,160,256]{2,1,0:T(8,128)(2,1)S(1)}, bf16[1,160,256]{2,1,0:T(8,128)(2,1)S(1)}, u32[]{:S(2)}, u32[]{:S(2)}) %collective-permute-start.63) | collective-permute-done | bytes 81952 | tf_op jit(solution)/shard_map/ppermute | solution.py:65
  745.3 24.3 %collective-permute-done.73 = bf16[2,160,1024]{2,1,0:T(8,128)(2,1)S(1)} collective-permute-done((bf16[2,160,1024]{2,1,0:T(8,128)(2,1)S(1)}, bf16[2,160,1024]{2,1,0:T(8,128)(2,1)S(1)}, u32[]{:S(2)}, u32[]{:S(2)}) %collective-permute-start.73) | collective-permute-done | bytes 655392 | tf_op jit(solution)/shard_map/ppermute | solution.py:65
  769.6 7.7 collective-permute-done.72
  783.5 33.7 %collective-permute-done.77 = bf16[160,2048]{1,0:T(8,128)(2,1)S(1)} collective-permute-done((bf16[160,2048]{1,0:T(8,128)(2,1)S(1)}, bf16[160,2048]{1,0:T(8,128)(2,1)S(1)}, u32[]{:S(2)}, u32[]{:S(2)}) %collective-permute-start.77) | collective-permute-done | bytes 655392 | tf_op jit(solution)/shard_map/ppermute | solution.py:65
  820.5 4.6 reshape.373
  825.1 3.3 copy.104
  828.4 4.3 reshape.374
  832.7 2.9 slice_convert_fusion
  (520 shorter events, 186.2 us)
Async XLA Ops:
  7.2 115.2 %all-gather.4.cloned.1.call-start = ((), (), s32[]{:S(2)}) async-start(), calls=%async_computation.4 | async-start | bytes 9052160 | tf_op jit(solution)/shard_map/all_gather | solution.py:602
  13.4 36.3 %all-to-all-start = ((bf16[160,8,512]{2,0,1:T(8,128)(2,1)}), bf16[160,8,512]{2,0,1:T(8,128)(2,1)S(1)}, u32[]{:S(2)}, u32[]{:S(2)}) async-start(bf16[160,8,512]{2,0,1:T(8,128)(2,1)} %bitcast.363), calls=%async_computation | async-start | bytes 2621440 | tf_op jit(solution)/shard_map/all_to_all | solution.py:586
  18.7 228.5 %all-gather.6.cloned.1.call-start = ((), (), s32[]{:S(2)}) async-start(), calls=%async_computation.5 | async-start | bytes 6963200 | tf_op jit(solution)/shard_map/all_gather | solution.py:608
  49.6 41.5 %all-to-all-start.1 = ((bf16[160,8,512]{2,0,1:T(8,128)(2,1)}), bf16[160,8,512]{2,0,1:T(8,128)(2,1)S(1)}, u32[]{:S(2)}, u32[]{:S(2)}) async-start(bf16[160,8,512]{2,0,1:T(8,128)(2,1)} %bitcast.400), calls=%async_computation.1 | async-start | bytes 2621440 | tf_op jit(solution)/shard_map/all_to_all | solution.py:586
  92.2 30.2 %all-to-all-start.2 = ((bf16[160,8,512]{2,0,1:T(8,128)(2,1)}), bf16[160,8,512]{2,0,1:T(8,128)(2,1)}, u32[]{:S(2)}, u32[]{:S(2)}) async-start(bf16[160,8,512]{2,0,1:T(8,128)(2,1)} %bitcast.399), calls=%async_computation.2 | async-start | bytes 2621440 | tf_op jit(solution)/shard_map/all_to_all | solution.py:586
  96.6 290.6 %all-gather.8.cloned.1.call-start = ((), (), s32[]{:S(2)}) async-start(), calls=%async_computation.6 | async-start | bytes 11141120 | tf_op jit(solution)/shard_map/all_gather | solution.py:639
  96.6 17.0 %collective-permute-start = (bf16[128,2560]{1,0:T(8,128)(2,1)S(1)}, bf16[128,2560]{1,0:T(8,128)(2,1)S(1)}, u32[]{:S(2)}, u32[]{:S(2)}) collective-permute-start(bf16[128,2560]{1,0:T(8,128)(2,1)S(1)} %bitcast.389), channel_id=1, source_target_pairs={{0,1},{1,0},{2,3},{3,2},{4,5},{5,4},{6,7},{7,6},{8,9},{9,8},{10,11... | collective-permute-start | bytes 1966088 | tf_op jit(solution)/shard_map/ppermute | solution.py:65
  131.8 45.4 %collective-permute-start.1 = (bf16[640,512]{1,0:T(8,128)(2,1)S(1)}, bf16[640,512]{1,0:T(8,128)(2,1)S(1)}, u32[]{:S(2)}, u32[]{:S(2)}) collective-permute-start(bf16[640,512]{1,0:T(8,128)(2,1)S(1)} %slice.135), channel_id=1, source_target_pairs={{0,16},{16,0},{1,17},{17,1},{2,18},{18,2},{3,19},{19,3},{4,20},{20... | collective-permute-start | bytes 1966088 | tf_op jit(solution)/shard_map/ppermute | solution.py:65
  178.7 49.6 %collective-permute-start.6 = (bf16[640,512]{1,0:T(8,128)(2,1)}, bf16[640,512]{1,0:T(8,128)(2,1)}, u32[]{:S(2)}, u32[]{:S(2)}) collective-permute-start(bf16[640,512]{1,0:T(8,128)(2,1)} %get-tuple-element.211), channel_id=1, source_target_pairs={{0,16},{16,0},{1,17},{17,1},{2,18},{18,2},{3,19},{19,3},{4,20},{20... | collective-permute-start | bytes 1966088 | tf_op jit(solution)/shard_map/ppermute | solution.py:65
  228.3 30.4 %collective-permute-start.8 = (bf16[640,512]{1,0:T(8,128)(2,1)}, bf16[640,512]{1,0:T(8,128)(2,1)}, u32[]{:S(2)}, u32[]{:S(2)}) collective-permute-start(bf16[640,512]{1,0:T(8,128)(2,1)} %get-tuple-element.215), channel_id=1, source_target_pairs={{0,16},{16,0},{1,17},{17,1},{2,18},{18,2},{3,19},{19,3},{4,20},{20... | collective-permute-start | bytes 1966088 | tf_op jit(solution)/shard_map/ppermute | solution.py:65
  233.1 465.3 %reduce-scatter.2.cloned.1.call-start = ((), (), s32[]{:S(2)}) async-start(), calls=%async_computation.7 | async-start | bytes 11796480 | tf_op jit(solution)/shard_map/reduce_scatter | solution.py:678
  258.8 30.1 %collective-permute-start.10 = (bf16[128,2560]{1,0:T(8,128)(2,1)S(1)}, bf16[128,2560]{1,0:T(8,128)(2,1)S(1)}, u32[]{:S(2)}, u32[]{:S(2)}) collective-permute-start(bf16[128,2560]{1,0:T(8,128)(2,1)S(1)} %dynamic-slice_convert_fusion.1), channel_id=1, source_target_pairs={{0,1},{1,0},{2,3},{3,2},{4,5},{5,4},{6,7},{7,6},{8,9},{9,8},{10,11... | collective-permute-start | bytes 1966088 | tf_op jit(solution)/shard_map/ppermute | solution.py:65
  261.7 31.2 %collective-permute-start.9 = (bf16[640,512]{1,0:T(8,128)(2,1)S(1)}, bf16[640,512]{1,0:T(8,128)(2,1)S(1)}, u32[]{:S(2)}, u32[]{:S(2)}) collective-permute-start(bf16[640,512]{1,0:T(8,128)(2,1)S(1)} %copy-done.57), channel_id=1, source_target_pairs={{0,16},{16,0},{1,17},{17,1},{2,18},{18,2},{3,19},{19,3},{4,20},{20... | collective-permute-start | bytes 1966088 | tf_op jit(solution)/shard_map/ppermute | solution.py:65
  293.4 9.9 %collective-permute-start.11 = (bf16[32,2560]{1,0:T(8,128)(2,1)S(1)}, bf16[32,2560]{1,0:T(8,128)(2,1)S(1)}, u32[]{:S(2)}, u32[]{:S(2)}) collective-permute-start(bf16[32,2560]{1,0:T(8,128)(2,1)S(1)} %slice.180), channel_id=1, source_target_pairs={{0,1},{1,0},{2,3},{3,2},{4,5},{5,4},{6,7},{7,6},{8,9},{9,8},{10,11... | collective-permute-start | bytes 491528 | tf_op jit(solution)/shard_map/ppermute | solution.py:65
  295.6 25.5 %collective-permute-start.13 = (bf16[48,2560]{1,0:T(8,128)(2,1)S(1)}, bf16[48,2560]{1,0:T(8,128)(2,1)S(1)}, u32[]{:S(2)}, u32[]{:S(2)}) collective-permute-start(bf16[48,2560]{1,0:T(8,128)(2,1)S(1)} %get-tuple-element.487), channel_id=1, source_target_pairs={{0,8},{8,0},{1,9},{9,1},{2,10},{10,2},{3,11},{11,3},{4,12},{12,4},... | collective-permute-start | bytes 737288 | tf_op jit(solution)/shard_map/ppermute | solution.py:65
  296.1 30.3 %collective-permute-start.17 = (bf16[640,512]{1,0:T(8,128)(2,1)S(1)}, bf16[640,512]{1,0:T(8,128)(2,1)S(1)}, u32[]{:S(2)}, u32[]{:S(2)}) collective-permute-start(bf16[640,512]{1,0:T(8,128)(2,1)S(1)} %copy-done.55), channel_id=1, source_target_pairs={{0,16},{16,0},{1,17},{17,1},{2,18},{18,2},{3,19},{19,3},{4,20},{20... | collective-permute-start | bytes 1966088 | tf_op jit(solution)/shard_map/ppermute | solution.py:65
  321.3 39.1 %collective-permute-start.15 = (bf16[2,48,2560]{2,1,0:T(8,128)(2,1)S(1)}, bf16[2,48,2560]{2,1,0:T(8,128)(2,1)S(1)}, u32[]{:S(2)}, u32[]{:S(2)}) collective-permute-start(bf16[2,48,2560]{2,1,0:T(8,128)(2,1)S(1)} %pad_maximum_fusion.20), channel_id=1, source_target_pairs={{0,8},{8,0},{1,9},{9,1},{2,10},{10,2},{3,11},{11,3},{4,12},{12,4},... | collective-permute-start | bytes 1474568 | tf_op jit(solution)/shard_map/ppermute | solution.py:65
  321.4 38.9 %collective-permute-start.16 = (bf16[2,48,2560]{2,1,0:T(8,128)(2,1)S(1)}, bf16[2,48,2560]{2,1,0:T(8,128)(2,1)S(1)}, u32[]{:S(2)}, u32[]{:S(2)}) collective-permute-start(bf16[2,48,2560]{2,1,0:T(8,128)(2,1)S(1)} %pad_maximum_fusion.21), channel_id=1, source_target_pairs={{0,1},{1,0},{2,3},{3,2},{4,5},{5,4},{6,7},{7,6},{8,9},{9,8},{10,11... | collective-permute-start | bytes 1474568 | tf_op jit(solution)/shard_map/ppermute | solution.py:65
  326.4 34.9 %collective-permute-start.21 = (bf16[640,512]{1,0:T(8,128)(2,1)S(1)}, bf16[640,512]{1,0:T(8,128)(2,1)S(1)}, u32[]{:S(2)}, u32[]{:S(2)}) collective-permute-start(bf16[640,512]{1,0:T(8,128)(2,1)S(1)} %copy-done.54), channel_id=1, source_target_pairs={{0,16},{16,0},{1,17},{17,1},{2,18},{18,2},{3,19},{19,3},{4,20},{20... | collective-permute-start | bytes 1966088 | tf_op jit(solution)/shard_map/ppermute | solution.py:65
  360.5 16.9 %collective-permute-start.18 = (bf16[2,2,32,2560]{3,2,1,0:T(8,128)(2,1)S(1)}, bf16[2,2,32,2560]{3,2,1,0:T(8,128)(2,1)S(1)}, u32[]{:S(2)}, u32[]{:S(2)}) collective-permute-start(bf16[2,2,32,2560]{3,2,1,0:T(8,128)(2,1)S(1)} %pad_maximum_fusion.18), channel_id=1, source_target_pairs={{0,8},{8,0},{1,9},{9,1},{2,10},{10,2},{3,11},{11,3},{4,12},{12,4},... | collective-permute-start | bytes 1966088 | tf_op jit(solution)/shard_map/ppermute | solution.py:65
  360.8 22.1 %collective-permute-start.19 = (bf16[2,2,48,2560]{3,2,0,1:T(8,128)(2,1)S(1)}, bf16[2,2,48,2560]{3,2,0,1:T(8,128)(2,1)S(1)}, u32[]{:S(2)}, u32[]{:S(2)}) collective-permute-start(bf16[2,2,48,2560]{3,2,0,1:T(8,128)(2,1)S(1)} %pad_maximum_fusion.16), channel_id=1, source_target_pairs={{0,1},{1,0},{2,3},{3,2},{4,5},{5,4},{6,7},{7,6},{8,9},{9,8},{10,11... | collective-permute-start | bytes 2949128 | tf_op jit(solution)/shard_map/ppermute | solution.py:65
  361.0 22.1 %collective-permute-start.20 = (bf16[2,2,48,2560]{3,2,0,1:T(8,128)(2,1)S(1)}, bf16[2,2,48,2560]{3,2,0,1:T(8,128)(2,1)S(1)}, u32[]{:S(2)}, u32[]{:S(2)}) collective-permute-start(bf16[2,2,48,2560]{3,2,0,1:T(8,128)(2,1)S(1)} %pad_maximum_fusion.17), channel_id=1, source_target_pairs={{0,4},{4,0},{1,5},{5,1},{2,6},{6,2},{3,7},{7,3},{8,12},{12,8},{9,1... | collective-permute-start | bytes 2949128 | tf_op jit(solution)/shard_map/ppermute | solution.py:65
  387.1 15.9 %collective-permute-start.22 = (bf16[1024,2560]{1,0:T(8,128)(2,1)}, bf16[1024,2560]{1,0:T(8,128)(2,1)}, u32[]{:S(2)}, u32[]{:S(2)}) collective-permute-start(bf16[1024,2560]{1,0:T(8,128)(2,1)} %bitcast.43.rows_ref.refs_4_), channel_id=1, source_target_pairs={{0,2},{2,0},{1,3},{3,1},{4,6},{6,4},{5,7},{7,5},{8,10},{10,8},{9,1... | collective-permute-start | bytes 15728648 | tf_op jit(solution)/shard_map/ppermute | solution.py:65
  426.6 13.0 %collective-permute-start.24 = (bf16[1024,2560]{1,0:T(8,128)(2,1)}, bf16[1024,2560]{1,0:T(8,128)(2,1)}, u32[]{:S(2)}, u32[]{:S(2)}) collective-permute-start(bf16[1024,2560]{1,0:T(8,128)(2,1)} %shard_map.258), channel_id=1, source_target_pairs={{0,2},{2,0},{1,3},{3,1},{4,6},{6,4},{5,7},{7,5},{8,10},{10,8},{9,1... | collective-permute-start | bytes 15728648 | tf_op jit(solution)/shard_map/ppermute | solution.py:65
  427.1 12.5 %collective-permute-start.23 = (f32[2,512]{1,0:T(2,128)S(1)}, f32[2,512]{1,0:T(2,128)S(1)}, u32[]{:S(2)}, u32[]{:S(2)}) collective-permute-start(f32[2,512]{1,0:T(2,128)S(1)} %add.499), channel_id=1, source_target_pairs={{0,16},{16,0},{1,17},{17,1},{2,18},{18,2},{3,19},{19,3},{4,20},{20... | collective-permute-start | bytes 12296 | tf_op jit(solution)/shard_map/ppermute | solution.py:65
  446.7 30.6 %collective-permute-start.26 = (bf16[2,2,48,2560]{3,2,1,0:T(8,128)(2,1)}, bf16[2,2,48,2560]{3,2,1,0:T(8,128)(2,1)}, u32[]{:S(2)}, u32[]{:S(2)}) collective-permute-start(bf16[2,2,48,2560]{3,2,1,0:T(8,128)(2,1)} %dynamic-slice_bitcast_fusion.1), channel_id=1, source_target_pairs={{0,1},{1,0},{2,3},{3,2},{4,5},{5,4},{6,7},{7,6},{8,9},{9,8},{10,11... | collective-permute-start | bytes 2949128 | tf_op jit(solution)/shard_map/ppermute | solution.py:65
  450.7 26.7 %collective-permute-start.27 = (bf16[2,2,48,2560]{3,2,0,1:T(8,128)(2,1)}, bf16[2,2,48,2560]{3,2,0,1:T(8,128)(2,1)}, u32[]{:S(2)}, u32[]{:S(2)}) collective-permute-start(bf16[2,2,48,2560]{3,2,0,1:T(8,128)(2,1)} %bitcast.365), channel_id=1, source_target_pairs={{0,4},{4,0},{1,5},{5,1},{2,6},{6,2},{3,7},{7,3},{8,12},{12,8},{9,1... | collective-permute-start | bytes 2949128 | tf_op jit(solution)/shard_map/ppermute | solution.py:65
  452.9 24.5 %collective-permute-start.25 = (bf16[2,2,32,2560]{3,2,1,0:T(8,128)(2,1)}, bf16[2,2,32,2560]{3,2,1,0:T(8,128)(2,1)}, u32[]{:S(2)}, u32[]{:S(2)}) collective-permute-start(bf16[2,2,32,2560]{3,2,1,0:T(8,128)(2,1)} %dynamic-slice_bitcast_fusion.6), channel_id=1, source_target_pairs={{0,8},{8,0},{1,9},{9,1},{2,10},{10,2},{3,11},{11,3},{4,12},{12,4},... | collective-permute-start | bytes 1966088 | tf_op jit(solution)/shard_map/ppermute | solution.py:65
  479.2 14.5 %collective-permute-start.29 = (bf16[2,48,2560]{2,1,0:T(8,128)(2,1)S(1)}, bf16[2,48,2560]{2,1,0:T(8,128)(2,1)}, u32[]{:S(2)}, u32[]{:S(2)}) collective-permute-start(bf16[2,48,2560]{2,1,0:T(8,128)(2,1)S(1)} %dynamic-slice_bitcast_fusion.10), channel_id=1, source_target_pairs={{0,8},{8,0},{1,9},{9,1},{2,10},{10,2},{3,11},{11,3},{4,12},{12,4},... | collective-permute-start | bytes 1474568 | tf_op jit(solution)/shard_map/ppermute | solution.py:65
  483.1 12.1 %collective-permute-start.30 = (bf16[2,48,2560]{2,1,0:T(8,128)(2,1)}, bf16[2,48,2560]{2,1,0:T(8,128)(2,1)}, u32[]{:S(2)}, u32[]{:S(2)}) collective-permute-start(bf16[2,48,2560]{2,1,0:T(8,128)(2,1)} %dynamic-slice_bitcast_fusion.9), channel_id=1, source_target_pairs={{0,1},{1,0},{2,3},{3,2},{4,5},{5,4},{6,7},{7,6},{8,9},{9,8},{10,11... | collective-permute-start | bytes 1474568 | tf_op jit(solution)/shard_map/ppermute | solution.py:65
  514.6 18.5 %collective-permute-start.36 = (bf16[1024,2560]{1,0:T(8,128)(2,1)}, bf16[1024,2560]{1,0:T(8,128)(2,1)}, u32[]{:S(2)}, u32[]{:S(2)}) collective-permute-start(bf16[1024,2560]{1,0:T(8,128)(2,1)} %shard_map.261), channel_id=1, source_target_pairs={{0,2},{2,0},{1,3},{3,1},{4,6},{6,4},{5,7},{7,5},{8,10},{10,8},{9,1... | collective-permute-start | bytes 15728648 | tf_op jit(solution)/shard_map/ppermute | solution.py:65
  514.6 17.3 %collective-permute-start.37 = (bf16[128,2560]{1,0:T(8,128)(2,1)S(1)}, bf16[128,2560]{1,0:T(8,128)(2,1)}, u32[]{:S(2)}, u32[]{:S(2)}) collective-permute-start(bf16[128,2560]{1,0:T(8,128)(2,1)S(1)} %convert_element_type.488), channel_id=1, source_target_pairs={{0,1},{1,0},{2,3},{3,2},{4,5},{5,4},{6,7},{7,6},{8,9},{9,8},{10,11... | collective-permute-start | bytes 1966088 | tf_op jit(solution)/shard_map/ppermute | solution.py:65
  516.4 25.8 %collective-permute-start.41 = (f32[2,2048]{1,0:T(2,128)S(1)}, f32[2,2048]{1,0:T(2,128)S(1)}, u32[]{:S(2)}, u32[]{:S(2)}) collective-permute-start(f32[2,2048]{1,0:T(2,128)S(1)} %pad_maximum_fusion.26), channel_id=1, source_target_pairs={{0,8},{8,0},{1,9},{9,1},{2,10},{10,2},{3,11},{11,3},{4,12},{12,4},... | collective-permute-start | bytes 49160 | tf_op jit(solution)/shard_map/ppermute | solution.py:65
  541.2 39.1 %collective-permute-start.38 = (bf16[2,2,32,2560]{3,2,1,0:T(8,128)(2,1)}, bf16[2,2,32,2560]{3,2,1,0:T(8,128)(2,1)}, u32[]{:S(2)}, u32[]{:S(2)}) collective-permute-start(bf16[2,2,32,2560]{3,2,1,0:T(8,128)(2,1)} %dynamic-slice_bitcast_fusion.5), channel_id=1, source_target_pairs={{0,8},{8,0},{1,9},{9,1},{2,10},{10,2},{3,11},{11,3},{4,12},{12,4},... | collective-permute-start | bytes 1966088 | tf_op jit(solution)/shard_map/ppermute | solution.py:65
  557.8 10.1 %collective-permute-start.42 = (bf16[512,512]{1,0:T(8,128)(2,1)S(1)}, bf16[512,512]{1,0:T(8,128)(2,1)S(1)}, u32[]{:S(2)}, u32[]{:S(2)}) collective-permute-start(bf16[512,512]{1,0:T(8,128)(2,1)S(1)} %slice.229), channel_id=1, source_target_pairs={{0,2},{2,0},{1,3},{3,1},{4,6},{6,4},{5,7},{7,5},{8,10},{10,8},{9,1... | collective-permute-start | bytes 1572872 | tf_op jit(solution)/shard_map/ppermute | solution.py:65
  558.9 32.6 %collective-permute-start.39 = (bf16[2,2,48,2560]{3,2,1,0:T(8,128)(2,1)}, bf16[2,2,48,2560]{3,2,1,0:T(8,128)(2,1)S(1)}, u32[]{:S(2)}, u32[]{:S(2)}) collective-permute-start(bf16[2,2,48,2560]{3,2,1,0:T(8,128)(2,1)} %dynamic-slice_bitcast_fusion), channel_id=1, source_target_pairs={{0,1},{1,0},{2,3},{3,2},{4,5},{5,4},{6,7},{7,6},{8,9},{9,8},{10,11... | collective-permute-start | bytes 2949128 | tf_op jit(solution)/shard_map/ppermute | solution.py:65
  561.8 30.6 %collective-permute-start.40 = (bf16[2,2,48,2560]{3,2,0,1:T(8,128)(2,1)}, bf16[2,2,48,2560]{3,2,0,1:T(8,128)(2,1)}, u32[]{:S(2)}, u32[]{:S(2)}) collective-permute-start(bf16[2,2,48,2560]{3,2,0,1:T(8,128)(2,1)} %bitcast.364), channel_id=1, source_target_pairs={{0,4},{4,0},{1,5},{5,1},{2,6},{6,2},{3,7},{7,3},{8,12},{12,8},{9,1... | collective-permute-start | bytes 2949128 | tf_op jit(solution)/shard_map/ppermute | solution.py:65
  568.1 23.3 %collective-permute-start.43 = (bf16[256,512]{1,0:T(8,128)(2,1)S(1)}, bf16[256,512]{1,0:T(8,128)(2,1)S(1)}, u32[]{:S(2)}, u32[]{:S(2)}) collective-permute-start(bf16[256,512]{1,0:T(8,128)(2,1)S(1)} %slice.230), channel_id=1, source_target_pairs={{0,4},{4,0},{1,5},{5,1},{2,6},{6,2},{3,7},{7,3},{8,12},{12,8},{9,1... | collective-permute-start | bytes 786440 | tf_op jit(solution)/shard_map/ppermute | solution.py:65
  574.5 24.1 %collective-permute-start.47 = (bf16[2,2,2,1,160,1280]{5,4,0,1,2,3:T(8,128)(2,1)}, bf16[2,2,2,1,160,1280]{5,4,0,1,2,3:T(8,128)(2,1)}, u32[]{:S(2)}, u32[]{:S(2)}) collective-permute-start(bf16[2,2,2,1,160,1280]{5,4,0,1,2,3:T(8,128)(2,1)} %copy.126), channel_id=1, source_target_pairs={{0,2},{2,0},{1,3},{3,1},{4,6},{6,4},{5,7},{7,5},{8,10},{10,8},{9,1... | collective-permute-start | bytes 9830408 | tf_op jit(solution)/shard_map/ppermute | solution.py:65
  594.5 24.5 %collective-permute-start.44 = (bf16[2,32,2560]{2,1,0:T(8,128)(2,1)}, bf16[2,32,2560]{2,1,0:T(8,128)(2,1)}, u32[]{:S(2)}, u32[]{:S(2)}) collective-permute-start(bf16[2,32,2560]{2,1,0:T(8,128)(2,1)} %dynamic-slice_bitcast_fusion.11), channel_id=1, source_target_pairs={{0,4},{4,0},{1,5},{5,1},{2,6},{6,2},{3,7},{7,3},{8,12},{12,8},{9,1... | collective-permute-start | bytes 983048 | tf_op jit(solution)/shard_map/ppermute | solution.py:65
  595.9 24.9 %collective-permute-start.45 = (bf16[2,48,2560]{2,1,0:T(8,128)(2,1)S(1)}, bf16[2,48,2560]{2,1,0:T(8,128)(2,1)}, u32[]{:S(2)}, u32[]{:S(2)}) collective-permute-start(bf16[2,48,2560]{2,1,0:T(8,128)(2,1)S(1)} %dynamic-slice_bitcast_fusion.8), channel_id=1, source_target_pairs={{0,8},{8,0},{1,9},{9,1},{2,10},{10,2},{3,11},{11,3},{4,12},{12,4},... | collective-permute-start | bytes 1474568 | tf_op jit(solution)/shard_map/ppermute | solution.py:65
  599.1 21.7 %collective-permute-start.46 = (bf16[2,48,2560]{2,1,0:T(8,128)(2,1)S(1)}, bf16[2,48,2560]{2,1,0:T(8,128)(2,1)}, u32[]{:S(2)}, u32[]{:S(2)}) collective-permute-start(bf16[2,48,2560]{2,1,0:T(8,128)(2,1)S(1)} %dynamic-slice_bitcast_fusion.7), channel_id=1, source_target_pairs={{0,1},{1,0},{2,3},{3,2},{4,5},{5,4},{6,7},{7,6},{8,9},{9,8},{10,11... | collective-permute-start | bytes 1474568 | tf_op jit(solution)/shard_map/ppermute | solution.py:65
  611.5 16.2 %collective-permute-start.49 = (bf16[128,2560]{1,0:T(8,128)(2,1)S(1)}, bf16[128,2560]{1,0:T(8,128)(2,1)S(1)}, u32[]{:S(2)}, u32[]{:S(2)}) collective-permute-start(bf16[128,2560]{1,0:T(8,128)(2,1)S(1)} %dynamic-slice_convert_fusion), channel_id=1, source_target_pairs={{0,1},{1,0},{2,3},{3,2},{4,5},{5,4},{6,7},{7,6},{8,9},{9,8},{10,11... | collective-permute-start | bytes 1966088 | tf_op jit(solution)/shard_map/ppermute | solution.py:65
  616.7 43.1 %collective-permute-start.53 = (bf16[2,2,1,160,1280]{4,3,0,1,2:T(8,128)(2,1)}, bf16[2,2,1,160,1280]{4,3,0,1,2:T(8,128)(2,1)}, u32[]{:S(2)}, u32[]{:S(2)}) collective-permute-start(bf16[2,2,1,160,1280]{4,3,0,1,2:T(8,128)(2,1)} %constant_dynamic-slice_fusion.20), channel_id=1, source_target_pairs={{0,4},{4,0},{1,5},{5,1},{2,6},{6,2},{3,7},{7,3},{8,12},{12,8},{9,1... | collective-permute-start | bytes 4915208 | tf_op jit(solution)/shard_map/ppermute | solution.py:65
  629.7 14.4 %collective-permute-start.50 = (bf16[32,2560]{1,0:T(8,128)(2,1)}, bf16[32,2560]{1,0:T(8,128)(2,1)}, u32[]{:S(2)}, u32[]{:S(2)}) collective-permute-start(bf16[32,2560]{1,0:T(8,128)(2,1)} %dynamic-slice_bitcast_fusion.17), channel_id=1, source_target_pairs={{0,1},{1,0},{2,3},{3,2},{4,5},{5,4},{6,7},{7,6},{8,9},{9,8},{10,11... | collective-permute-start | bytes 491528 | tf_op jit(solution)/shard_map/ppermute | solution.py:65
  632.1 24.5 %collective-permute-start.51 = (bf16[48,2560]{1,0:T(8,128)(2,1)}, bf16[48,2560]{1,0:T(8,128)(2,1)}, u32[]{:S(2)}, u32[]{:S(2)}) collective-permute-start(bf16[48,2560]{1,0:T(8,128)(2,1)} %dynamic-slice_bitcast_fusion.14), channel_id=1, source_target_pairs={{0,4},{4,0},{1,5},{5,1},{2,6},{6,2},{3,7},{7,3},{8,12},{12,8},{9,1... | collective-permute-start | bytes 737288 | tf_op jit(solution)/shard_map/ppermute | solution.py:65
  634.7 21.8 %collective-permute-start.52 = (bf16[48,2560]{1,0:T(8,128)(2,1)}, bf16[48,2560]{1,0:T(8,128)(2,1)}, u32[]{:S(2)}, u32[]{:S(2)}) collective-permute-start(bf16[48,2560]{1,0:T(8,128)(2,1)} %dynamic-slice_bitcast_fusion.13), channel_id=1, source_target_pairs={{0,8},{8,0},{1,9},{9,1},{2,10},{10,2},{3,11},{11,3},{4,12},{12,4},... | collective-permute-start | bytes 737288 | tf_op jit(solution)/shard_map/ppermute | solution.py:65
  656.9 9.3 %collective-permute-start.59 = (f32[2,2,1,4,160]{4,2,1,0,3:T(1,128)S(1)}, f32[2,2,1,4,160]{4,2,1,0,3:T(1,128)S(1)}, u32[]{:S(2)}, u32[]{:S(2)}) collective-permute-start(f32[2,2,1,4,160]{4,2,1,0,3:T(1,128)S(1)} %get-tuple-element.500), channel_id=1, source_target_pairs={{0,4},{4,0},{1,5},{5,1},{2,6},{6,2},{3,7},{7,3},{8,12},{12,8},{9,1... | collective-permute-start | bytes 30728 | tf_op jit(solution)/shard_map/ppermute | solution.py:65
  663.5 31.2 %collective-permute-start.57 = (bf16[2,2,2,1,160,1280]{5,4,0,1,2,3:T(8,128)(2,1)S(1)}, bf16[2,2,2,1,160,1280]{5,4,0,1,2,3:T(8,128)(2,1)S(1)}, u32[]{:S(2)}, u32[]{:S(2)}) collective-permute-start(bf16[2,2,2,1,160,1280]{5,4,0,1,2,3:T(8,128)(2,1)S(1)} %copy.130), channel_id=1, source_target_pairs={{0,2},{2,0},{1,3},{3,1},{4,6},{6,4},{5,7},{7,5},{8,10},{10,8},{9,1... | collective-permute-start | bytes 9830408 | tf_op jit(solution)/shard_map/ppermute | solution.py:65
  666.4 27.4 %collective-permute-start.58 = (bf16[2,2,1,160,256]{4,3,0,1,2:T(8,128)(2,1)S(1)}, bf16[2,2,1,160,256]{4,3,0,1,2:T(8,128)(2,1)S(1)}, u32[]{:S(2)}, u32[]{:S(2)}) collective-permute-start(bf16[2,2,1,160,256]{4,3,0,1,2:T(8,128)(2,1)S(1)} %constant_dynamic-slice_fusion.14), channel_id=1, source_target_pairs={{0,4},{4,0},{1,5},{5,1},{2,6},{6,2},{3,7},{7,3},{8,12},{12,8},{9,1... | collective-permute-start | bytes 983048 | tf_op jit(solution)/shard_map/ppermute | solution.py:65
  667.8 25.9 %collective-permute-start.62 = (f32[2,1,4,160]{3,1,0,2:T(1,128)S(1)}, f32[2,1,4,160]{3,1,0,2:T(1,128)S(1)}, u32[]{:S(2)}, u32[]{:S(2)}) collective-permute-start(f32[2,1,4,160]{3,1,0,2:T(1,128)S(1)} %get-tuple-element.502), channel_id=1, source_target_pairs={{0,8},{8,0},{1,9},{9,1},{2,10},{10,2},{3,11},{11,3},{4,12},{12,4},... | collective-permute-start | bytes 15368 | tf_op jit(solution)/shard_map/ppermute | solution.py:65
  671.7 46.4 %collective-permute-start.68 = (bf16[2,1,160,1280]{3,2,0,1:T(8,128)(2,1)}, bf16[2,1,160,1280]{3,2,0,1:T(8,128)(2,1)}, u32[]{:S(2)}, u32[]{:S(2)}) collective-permute-start(bf16[2,1,160,1280]{3,2,0,1:T(8,128)(2,1)} %constant_dynamic-slice_fusion.4), channel_id=1, source_target_pairs={{0,8},{8,0},{1,9},{9,1},{2,10},{10,2},{3,11},{11,3},{4,12},{12,4},... | collective-permute-start | bytes 2457608 | tf_op jit(solution)/shard_map/ppermute | solution.py:65
  694.6 20.1 %collective-permute-start.61 = (bf16[2,1,160,256]{3,2,0,1:T(8,128)(2,1)}, bf16[2,1,160,256]{3,2,0,1:T(8,128)(2,1)S(1)}, u32[]{:S(2)}, u32[]{:S(2)}) collective-permute-start(bf16[2,1,160,256]{3,2,0,1:T(8,128)(2,1)} %constant_dynamic-slice_fusion.10), channel_id=1, source_target_pairs={{0,8},{8,0},{1,9},{9,1},{2,10},{10,2},{3,11},{11,3},{4,12},{12,4},... | collective-permute-start | bytes 491528 | tf_op jit(solution)/shard_map/ppermute | solution.py:65
  696.9 40.4 %collective-permute-start.60 = (bf16[2,2,1,160,1280]{4,3,0,1,2:T(8,128)(2,1)}, bf16[2,2,1,160,1280]{4,3,0,1,2:T(8,128)(2,1)}, u32[]{:S(2)}, u32[]{:S(2)}) collective-permute-start(bf16[2,2,1,160,1280]{4,3,0,1,2:T(8,128)(2,1)} %constant_dynamic-slice_fusion.11), channel_id=1, source_target_pairs={{0,4},{4,0},{1,5},{5,1},{2,6},{6,2},{3,7},{7,3},{8,12},{12,8},{9,1... | collective-permute-start | bytes 4915208 | tf_op jit(solution)/shard_map/ppermute | solution.py:65
  720.4 16.8 %collective-permute-start.63 = (bf16[1,160,256]{2,1,0:T(8,128)(2,1)S(1)}, bf16[1,160,256]{2,1,0:T(8,128)(2,1)S(1)}, u32[]{:S(2)}, u32[]{:S(2)}) collective-permute-start(bf16[1,160,256]{2,1,0:T(8,128)(2,1)S(1)} %constant_dynamic-slice_fusion.7), channel_id=1, source_target_pairs={{0,16},{16,0},{1,17},{17,1},{2,18},{18,2},{3,19},{19,3},{4,20},{20... | collective-permute-start | bytes 245768 | tf_op jit(solution)/shard_map/ppermute | solution.py:65
  723.3 54.0 %collective-permute-start.70 = (bf16[1,160,1280]{2,1,0:T(8,128)(2,1)S(1)}, bf16[1,160,1280]{2,1,0:T(8,128)(2,1)S(1)}, u32[]{:S(2)}, u32[]{:S(2)}) collective-permute-start(bf16[1,160,1280]{2,1,0:T(8,128)(2,1)S(1)} %constant_dynamic-slice_fusion.2), channel_id=1, source_target_pairs={{0,16},{16,0},{1,17},{17,1},{2,18},{18,2},{3,19},{19,3},{4,20},{20... | collective-permute-start | bytes 1228808 | tf_op jit(solution)/shard_map/ppermute | solution.py:65
  739.1 43.0 %collective-permute-start.69 = (bf16[2,1,160,1280]{3,2,0,1:T(8,128)(2,1)S(1)}, bf16[2,1,160,1280]{3,2,0,1:T(8,128)(2,1)S(1)}, u32[]{:S(2)}, u32[]{:S(2)}) collective-permute-start(bf16[2,1,160,1280]{3,2,0,1:T(8,128)(2,1)S(1)} %constant_dynamic-slice_fusion.3), channel_id=1, source_target_pairs={{0,8},{8,0},{1,9},{9,1},{2,10},{10,2},{3,11},{11,3},{4,12},{12,4},... | collective-permute-start | bytes 2457608 | tf_op jit(solution)/shard_map/ppermute | solution.py:65
  739.4 37.9 %collective-permute-start.71 = (bf16[2,160,1024]{2,1,0:T(8,128)(2,1)S(1)}, bf16[2,160,1024]{2,1,0:T(8,128)(2,1)S(1)}, u32[]{:S(2)}, u32[]{:S(2)}) collective-permute-start(bf16[2,160,1024]{2,1,0:T(8,128)(2,1)S(1)} %fusion.59), channel_id=1, source_target_pairs={{0,4},{4,0},{1,5},{5,1},{2,6},{6,2},{3,7},{7,3},{8,12},{12,8},{9,1... | collective-permute-start | bytes 1966088 | tf_op jit(solution)/shard_map/ppermute | solution.py:65
  741.1 36.1 %collective-permute-start.72 = (bf16[2,160,1024]{2,1,0:T(8,128)(2,1)S(1)}, bf16[2,160,1024]{2,1,0:T(8,128)(2,1)S(1)}, u32[]{:S(2)}, u32[]{:S(2)}) collective-permute-start(bf16[2,160,1024]{2,1,0:T(8,128)(2,1)S(1)} %fusion.55), channel_id=1, source_target_pairs={{0,8},{8,0},{1,9},{9,1},{2,10},{10,2},{3,11},{11,3},{4,12},{12,4},... | collective-permute-start | bytes 1966088 | tf_op jit(solution)/shard_map/ppermute | solution.py:65
  743.4 26.2 %collective-permute-start.73 = (bf16[2,160,1024]{2,1,0:T(8,128)(2,1)S(1)}, bf16[2,160,1024]{2,1,0:T(8,128)(2,1)S(1)}, u32[]{:S(2)}, u32[]{:S(2)}) collective-permute-start(bf16[2,160,1024]{2,1,0:T(8,128)(2,1)S(1)} %fusion.51), channel_id=1, source_target_pairs={{0,4},{4,0},{1,5},{5,1},{2,6},{6,2},{3,7},{7,3},{8,12},{12,8},{9,1... | collective-permute-start | bytes 1966088 | tf_op jit(solution)/shard_map/ppermute | solution.py:65
  777.7 39.5 %collective-permute-start.75 = (bf16[160,2048]{1,0:T(8,128)(2,1)S(1)}, bf16[160,2048]{1,0:T(8,128)(2,1)S(1)}, u32[]{:S(2)}, u32[]{:S(2)}) collective-permute-start(bf16[160,2048]{1,0:T(8,128)(2,1)S(1)} %fusion.47), channel_id=1, source_target_pairs={{0,8},{8,0},{1,9},{9,1},{2,10},{10,2},{3,11},{11,3},{4,12},{12,4},... | collective-permute-start | bytes 1966088 | tf_op jit(solution)/shard_map/ppermute | solution.py:65
  778.2 39.1 %collective-permute-start.76 = (bf16[160,2048]{1,0:T(8,128)(2,1)S(1)}, bf16[160,2048]{1,0:T(8,128)(2,1)S(1)}, u32[]{:S(2)}, u32[]{:S(2)}) collective-permute-start(bf16[160,2048]{1,0:T(8,128)(2,1)S(1)} %fusion.43), channel_id=1, source_target_pairs={{0,4},{4,0},{1,5},{5,1},{2,6},{6,2},{3,7},{7,3},{8,12},{12,8},{9,1... | collective-permute-start | bytes 1966088 | tf_op jit(solution)/shard_map/ppermute | solution.py:65
  780.1 37.1 %collective-permute-start.77 = (bf16[160,2048]{1,0:T(8,128)(2,1)S(1)}, bf16[160,2048]{1,0:T(8,128)(2,1)S(1)}, u32[]{:S(2)}, u32[]{:S(2)}) collective-permute-start(bf16[160,2048]{1,0:T(8,128)(2,1)S(1)} %fusion.39), channel_id=1, source_target_pairs={{0,8},{8,0},{1,9},{9,1},{2,10},{10,2},{3,11},{11,3},{4,12},{12,4},... | collective-permute-start | bytes 1966088 | tf_op jit(solution)/shard_map/ppermute | solution.py:65
  782.4 34.8 %collective-permute-start.74 = (bf16[1,160,1280]{2,1,0:T(8,128)(2,1)S(1)}, bf16[1,160,1280]{2,1,0:T(8,128)(2,1)S(1)}, u32[]{:S(2)}, u32[]{:S(2)}) collective-permute-start(bf16[1,160,1280]{2,1,0:T(8,128)(2,1)S(1)} %constant_dynamic-slice_fusion.1), channel_id=1, source_target_pairs={{0,16},{16,0},{1,17},{17,1},{2,18},{18,2},{3,19},{19,3},{4,20},{20... | collective-permute-start | bytes 1228808 | tf_op jit(solution)/shard_map/ppermute | solution.py:65
  (104 other events, 686.3 us)
Sparse Core Ops, SparseCore 0:
  12.2 103.2 all-gather.3
  117.8 107.8 all-gather.5
  233.2 132.9 all-gather.7
  516.5 178.9 reduce-scatter.1

commit v4 on v3

--- a/solution.py
+++ b/solution.py
@@ -635,7 +635,6 @@
         keyvalue = jnp.concatenate([keyvalue, swap(keyvalue, bit)], axis=0)
         if bit == plan.y[-1]:
             keyvalue = ff_in.step(keyvalue)
-    keyvalue, grad_local = tie(keyvalue, grad_local)
     all_grads = lax.all_gather(
         grad_local, ("core", "near", "y", "tensor"), axis=0, tiled=True
     )
@@ -644,7 +643,7 @@
         normed, first, keyvalue, allowed, cosine_both, sine_both, head_count
     )
     attended = rows_out([context], [full_output], f32)
-    attended = ff_in.step(attended)
+    attended, grad_low = ff_in.step((attended, grad_local))
     mixed = local_in + sum_rows(attended, plan) + full_obias
     mixed = ff_in.step(mixed)
 
@@ -731,33 +730,32 @@
     block_output = (mixed + out_sum.result + full_dbias).astype(bf16)
 
     small = jnp.stack([gain_one_part, gain_two_part, obias_part, dbias_part], axis=0)
-    small = small.reshape(4, -1, shard_rows).transpose(1, 0, 2)
     small = small + swap(small, plan.tensor)
-    small_sum = Journey(reduce_rows([small.reshape(-1, shard_rows)], plan, [order_one], f32))
+    small = jnp.pad(small.T.astype(bf16), ((0, 0), (0, LANES - 4)))
+    keyvalue_wgrad = jnp.concatenate([keyvalue_wgrad, small], axis=1)
     keyvalue_sum = Journey(reduce_rows([keyvalue_wgrad], plan, [order_one]))
-    for item in (small_sum, keyvalue_sum, query_sum):
-        input_grad = item.step(input_grad)
+    input_grad = query_sum.step(input_grad)
     output_wgrad, input_grad = tie(output_wgrad, input_grad)
     output_sum = Journey(reduce_rows([output_wgrad], plan, [order_one]))
-    for item in (small_sum, keyvalue_sum, output_sum):
-        input_grad = item.step(input_grad)
+    input_grad = output_sum.step(input_grad)
+    input_grad = keyvalue_sum.step(input_grad)
     ff_sum, input_grad = tie(ff_sum, input_grad)
     y_first = [plan.core] + plan.y[::-1] + plan.near[::-1]
     near_first = [plan.core] + plan.near[::-1] + plan.y[::-1]
     backs = [
         Journey(spread_back(ff_sum[:, i * block : (i + 1) * block], plan, bits))
-        for i, bits in enumerate((y_first, near_first, y_first))
+        for i, bits in enumerate((y_first, y_first, near_first))
     ]
-    for item in (small_sum, keyvalue_sum, query_sum, *backs, small_sum, keyvalue_sum):
-        if item.result is None:
-            input_grad = item.step(input_grad)
-    input_grad = finish_all(
-        [output_sum, *backs, keyvalue_sum, small_sum, query_sum], input_grad
-    )
+    input_grad = backs[0].step(input_grad)
+    input_grad = backs[1].step(input_grad)
+    input_grad = backs[2].step(input_grad)
+    input_grad = query_sum.step(input_grad)
+    input_grad = keyvalue_sum.step(input_grad)
+    input_grad = finish_all([output_sum, *backs, query_sum, keyvalue_sum], input_grad)
     proj_out = output_sum.result[0]
     query_out = query_sum.result[0]
-    keyvalue_out = keyvalue_sum.result[0]
-    small = small_sum.result[0].reshape(4, shard_rows)
+    keyvalue_out = keyvalue_sum.result[0][:, :keyvalue_columns]
+    small = keyvalue_sum.result[0][:, keyvalue_columns : keyvalue_columns + 4].T
     ff_small = ff_small.result
     down_out, gate_out, up_out = (item.result[:, :ff_half].astype(f32) for item in backs)
     return (

time: 855 us -> 844 us (0.987)
  local copies, waits for them, and re-layouts: 87.2 us -> 77.3 us
  waiting for transfers between devices: 459 us -> 450 us
    ppermute x78 -> x74, waiting for transfers between devices: 386 us -> 353 us  [swap(): lax.ppermute(values, axis, [(i, i ^ mask) for i in range(lax.axis_size(ax...]
    reduce_scatter x1, waiting for transfers between devices: 0.01 us -> 22.7 us  [local(): ff_sum = lax.psum_scatter(ff_wgrad, 'far', scatter_dimension=0, tiled=True)]
    ppermute x78 -> x74, starting transfers between devices: 66.5 us -> 70 us  [swap(): lax.ppermute(values, axis, [(i, i ^ mask) for i in range(lax.axis_size(ax...]
    unnamed x175 -> x195, local copies, waits for them, and re-layouts: 28.5 us -> 25.9 us
  transfers between devices with their start and end apart: 85 -> 81, of which waited for: 38 -> 38; matrix products, arithmetic and copies ran while one was open for 13% -> 12% of each run, Pallas kernels for 11% -> 11%
where the time goes in v4:
time: 844 us; the launch traced here: 835 us
  waiting for transfers between devices  450 us (53%)
  Pallas kernels  123 us (15%)
  other arithmetic  83.3 us (10%)
  starting transfers between devices  83.2 us (10%)
  local copies, waits for them, and re-layouts  77.3 us (9%)
  between operations  15.8 us (2%)
    ppermute x74, waiting for transfers between devices, swap(): lax.ppermute(values, axis, [(i, i ^ mask) for i in range(lax.axis_size(ax...  353 us
    all_to_all x3, waiting for transfers between devices, by_block(): lax.all_to_all(jnp.pad(item, ((0, 0), (0, ff_pad))), ('near',) + CTX, spl...  74 us
    ppermute x74, starting transfers between devices, swap(): lax.ppermute(values, axis, [(i, i ^ mask) for i in range(lax.axis_size(ax...  70 us
    pallas_call x6, Pallas kernels, rows_out(): pl.pallas_call(rows_kernel, grid=(count // tile,), in_specs=[pl.BlockSpec...  39.6 us
    pallas_call x4, Pallas kernels, weight_out(): pl.pallas_call(partial(weight_kernel, groups), grid_spec=pltpu.PrefetchSc...  33.1 us
    unnamed x195, local copies, waits for them, and re-layouts  25.9 us
    pallas_call x2, Pallas kernels, hidden_units(): pl.pallas_call(hidden_kernel, grid_spec=pltpu.PrefetchScalarGridSpec(num_...  25.7 us
    reduce_scatter x1, waiting for transfers between devices, local(): ff_sum = lax.psum_scatter(ff_wgrad, 'far', scatter_dimension=0, tiled=True)  22.7 us
  transfers between devices with their start and end apart: 81, of which 38 were waited for; matrix products, arithmetic and copies ran while one was open for 12% of the time, Pallas kernels for 11%

profile of v4, /device:TPU:0, one launch (start us, length us, event | category | flops | bytes accessed | tf_op | source)
XLA Modules:
  0.0 835.4 jit_solution(14641296521086443837)
XLA Ops:
  14.1 5.4 all-to-all-start
  20.8 30.1 %all-to-all-done = bf16[160,8,512]{2,0,1:T(8,128)(2,1)S(1)} async-done(((bf16[160,8,512]{2,0,1:T(8,128)(2,1)}), bf16[160,8,512]{2,0,1:T(8,128)(2,1)S(1)}, u32[]{:S(2)}, u32[]{:S(2)}) %all-to-all-start) | async-done | bytes 1310752 | tf_op jit(solution)/shard_map/all_to_all | solution.py:586
  50.9 4.1 all-to-all-start.1
  57.6 34.6 %all-to-all-done.1 = bf16[160,8,512]{2,0,1:T(8,128)(2,1)S(1)} async-done(((bf16[160,8,512]{2,0,1:T(8,128)(2,1)}), bf16[160,8,512]{2,0,1:T(8,128)(2,1)S(1)}, u32[]{:S(2)}, u32[]{:S(2)}) %all-to-all-start.1) | async-done | bytes 1310752 | tf_op jit(solution)/shard_map/all_to_all | solution.py:586
  93.3 3.6 all-to-all-start.2
  98.5 2.1 collective-permute-start.2
  102.4 5.3 collective-permute-done.2
  109.8 4.3 collective-permute-done
  114.1 9.3 %all-to-all-done.2 = bf16[160,8,512]{2,0,1:T(8,128)(2,1)S(1)} async-done(((bf16[160,8,512]{2,0,1:T(8,128)(2,1)}), bf16[160,8,512]{2,0,1:T(8,128)(2,1)S(1)}, u32[]{:S(2)}, u32[]{:S(2)}) %all-to-all-start.2) | async-done | bytes 1310752 | tf_op jit(solution)/shard_map/all_to_all | solution.py:586
  125.0 2.7 slice_reduce_fusion
  129.7 2.3 fusion.26
  135.1 3.6 collective-permute-start.1
  141.7 5.7 collective-permute-done.5
  147.5 33.8 %collective-permute-done.1 = bf16[640,512]{1,0:T(8,128)(2,1)S(1)} collective-permute-done((bf16[640,512]{1,0:T(8,128)(2,1)S(1)}, bf16[640,512]{1,0:T(8,128)(2,1)S(1)}, u32[]{:S(2)}, u32[]{:S(2)}) %collective-permute-start.1) | collective-permute-done | bytes 655392 | tf_op jit(solution)/shard_map/ppermute | solution.py:65
  184.2 45.0 %collective-permute-done.6 = bf16[640,512]{1,0:T(8,128)(2,1)S(1)} collective-permute-done((bf16[640,512]{1,0:T(8,128)(2,1)S(1)}, bf16[640,512]{1,0:T(8,128)(2,1)S(1)}, u32[]{:S(2)}, u32[]{:S(2)}) %collective-permute-start.6) | collective-permute-done | bytes 655392 | tf_op jit(solution)/shard_map/ppermute | solution.py:65
  231.6 10.9 %shard_map.254 = (bf16[256,1280]{1,0:T(8,128)(2,1)S(1)}, bf16[256,1280]{1,0:T(8,128)(2,1)S(1)}, f32[256,640]{1,0:T(8,128)S(1)}) custom-call(bf16[256,2560]{1,0:T(8,128)(2,1)S(1)} %fusion.7.rows_ref.refs_0_, bf16[2560,1664]{1,0:T(8,128)(2,1)} %all-gather.5.cloned.1.call-done.weight_ref.refs_2_.refs_3_, ...), custom_call_target="tpu_custom_call" | custom-call | tf_op jit(solution)/shard_map/pallas_call | solution.py:410
  243.4 5.3 shard_map.255
  248.7 10.9 %collective-permute-done.8 = bf16[640,512]{1,0:T(8,128)(2,1)} collective-permute-done((bf16[640,512]{1,0:T(8,128)(2,1)}, bf16[640,512]{1,0:T(8,128)(2,1)}, u32[]{:S(2)}, u32[]{:S(2)}) %collective-permute-start.8) | collective-permute-done | bytes 655392 | tf_op jit(solution)/shard_map/ppermute | solution.py:65
  264.5 25.3 %collective-permute-done.10 = bf16[128,2560]{1,0:T(8,128)(2,1)S(1)} collective-permute-done((bf16[128,2560]{1,0:T(8,128)(2,1)S(1)}, bf16[128,2560]{1,0:T(8,128)(2,1)S(1)}, u32[]{:S(2)}, u32[]{:S(2)}) %collective-permute-start.10) | collective-permute-done | bytes 655392 | tf_op jit(solution)/shard_map/ppermute | solution.py:65
  296.0 2.8 collective-permute-start.17
  300.4 2.4 collective-permute-done.11
  302.8 18.8 %collective-permute-done.13 = bf16[48,2560]{1,0:T(8,128)(2,1)S(1)} collective-permute-done((bf16[48,2560]{1,0:T(8,128)(2,1)S(1)}, bf16[48,2560]{1,0:T(8,128)(2,1)S(1)}, u32[]{:S(2)}, u32[]{:S(2)}) %collective-permute-start.13) | collective-permute-done | bytes 245792 | tf_op jit(solution)/shard_map/ppermute | solution.py:65
  323.1 3.2 collective-permute-done.17
  326.3 3.4 collective-permute-start.21
  330.9 22.6 %collective-permute-done.15 = bf16[2,48,2560]{2,1,0:T(8,128)(2,1)S(1)} collective-permute-done((bf16[2,48,2560]{2,1,0:T(8,128)(2,1)S(1)}, bf16[2,48,2560]{2,1,0:T(8,128)(2,1)S(1)}, u32[]{:S(2)}, u32[]{:S(2)}) %collective-permute-start.15) | collective-permute-done | bytes 491552 | tf_op jit(solution)/shard_map/ppermute | solution.py:65
  354.1 3.2 collective-permute-start.20
  359.4 11.4 %collective-permute-done.18 = bf16[2,2,32,2560]{3,2,1,0:T(8,128)(2,1)S(1)} collective-permute-done((bf16[2,2,32,2560]{3,2,1,0:T(8,128)(2,1)S(1)}, bf16[2,2,32,2560]{3,2,1,0:T(8,128)(2,1)S(1)}, u32[]{:S(2)}, u32[]{:S(2)}) %collective-permute-start.18) | collective-permute-done | bytes 655392 | tf_op jit(solution)/shard_map/ppermute | solution.py:65
  370.8 6.6 collective-permute-done.19
  379.8 2.8 copy.124
  382.7 12.9 %shard_map.256 = (bf16[1024,512]{1,0:T(8,128)(2,1)S(1)}, bf16[1024,512]{1,0:T(8,128)(2,1)S(1)}, bf16[1024,512]{1,0:T(8,128)(2,1)S(1)}, f32[2,512]{1,0:T(2,128)S(1)}) custom-call(s32[1]{0:T(128)} %bitcast.44.half_ref, bf16[1024,2560]{1,0:T(8,128)(2,1)} %bitcast.43.rows_ref.refs_4_, bf16[2048,2560]{1,0:T(8,128)(2,1)} %bitcast.355, ...), custom_call_target="tpu_custom_call" | custom-call | tf_op jit(solution)/shard_map/pallas_call | solution.py:332
  398.6 12.8 %shard_map.257 = (bf16[1024,512]{1,0:T(8,128)(2,1)S(1)}, bf16[1024,512]{1,0:T(8,128)(2,1)S(1)}, bf16[1024,512]{1,0:T(8,128)(2,1)S(1)}, f32[2,512]{1,0:T(2,128)S(1)}) custom-call(s32[1]{0:T(128)} %bitcast.46.half_ref, bf16[1024,2560]{1,0:T(8,128)(2,1)} %collective-permute-done.22.rows_ref.refs_5_, bf16[2048,2560]{1,0:T(8,128)(2,1)} %bitcast.356, ...), custom_call_target="tpu_custom_call" | custom-call | tf_op jit(solution)/shard_map/pallas_call | solution.py:332
  412.4 9.8 %shard_map.258 = bf16[1024,2560]{1,0:T(8,128)(2,1)} custom-call(bf16[1024,512]{1,0:T(8,128)(2,1)S(1)} %get-tuple-element.262.refs_0_.refs_7_, bf16[1024,512]{1,0:T(8,128)(2,1)S(1)} %get-tuple-element.264.refs_1_.refs_9_, bf16[2560,512]{1,0:T(8,128)(2,1)S(1)} %bitcast.353, bf16[2560,512]{1,0:T(8,128)(2,1)} %bitcast.361), custom_call_target="tpu_custom_call" | custom-call | tf_op jit(solution)/shard_map/pallas_call | solution.py:369
  422.7 4.8 collective-permute-start.23
  430.0 9.1 %shard_map.259 = bf16[1024,2560]{1,0:T(8,128)(2,1)} custom-call(bf16[1024,512]{1,0:T(8,128)(2,1)S(1)} %copy-done.14, bf16[1024,512]{1,0:T(8,128)(2,1)S(1)} %copy-done.17, bf16[2560,512]{1,0:T(8,128)(2,1)S(1)} %bitcast.354, bf16[2560,512]{1,0:T(8,128)(2,1)} %bitcast.362), custom_call_target="tpu_custom_call" | custom-call | tf_op jit(solution)/shard_map/pallas_call | solution.py:369
  439.1 5.4 add_convert_fusion.1
  455.2 21.4 %shard_map.260 = bf16[2560,1536]{1,0:T(8,128)(2,1)} custom-call(s32[1]{0:T(128)} %bitcast.44.half_ref, bf16[2048,2560]{1,0:T(8,128)(2,1)} %bitcast.357, bf16[2048,2560]{1,0:T(8,128)(2,1)} %bitcast.358, bf16[1024,512]{1,0:T(8,128)(2,1)S(1)} %copy-done.8, bf16[1024,512]{1,0:T(8,128)(2,1)S(1)} %copy-done.11, bf16[1024,2560]{1,0:T(8,128)(2,1)} %bitcast.43.rows_ref.refs_4_, ...), custom_call_target="tpu_custom_call" | custom-call | tf_op jit(solution)/shard_map/pallas_call | solution.py:522
  486.8 6.5 collective-permute-done.28
  501.2 2.6 collective-permute-done.35
  510.0 4.8 shard_map.261
  520.5 5.2 shard_map.262
  527.5 4.5 collective-permute-done.37
  533.3 5.4 add_convert_fusion
  541.1 14.0 %shard_map.263 = (bf16[256,1280]{1,0:T(8,128)(2,1)S(1)}, f32[1024,512]{1,0:T(8,128)}) custom-call(bf16[256,2560]{1,0:T(8,128)(2,1)S(1)} %pad_maximum_fusion.11.rows_ref.refs_0_, bf16[2560,1280]{1,0:T(8,128)(2,1)} %all-gather.7.cloned.1.call-done.refs_1_.weight_ref, bf16[256,1280]{1,0:T(8,128)(2,1)S(1)} %copy-done.25, f32[256,640]{1,0:T(8,128)S(1)} %copy-done.27, ...), custom_call_target="tpu_custom_call" | custom-call | tf_op jit(solution)/shard_map/pallas_call | solution.py:456
  560.9 5.0 shard_map.264
  567.3 3.4 constant_dynamic-slice_fusion.13
  573.4 5.0 shard_map.265
  578.5 10.6 %collective-permute-done.43 = bf16[256,512]{1,0:T(8,128)(2,1)S(1)} collective-permute-done((bf16[256,512]{1,0:T(8,128)(2,1)S(1)}, bf16[256,512]{1,0:T(8,128)(2,1)S(1)}, u32[]{:S(2)}, u32[]{:S(2)}) %collective-permute-start.43) | collective-permute-done | bytes 262176 | tf_op jit(solution)/shard_map/ppermute | solution.py:65
  597.7 4.3 collective-permute-done.48
  602.8 5.4 shard_map.266
  608.6 2.7 fusion.1
  615.9 8.6 %collective-permute-done.49 = bf16[128,2560]{1,0:T(8,128)(2,1)S(1)} collective-permute-done((bf16[128,2560]{1,0:T(8,128)(2,1)S(1)}, bf16[128,2560]{1,0:T(8,128)(2,1)S(1)}, u32[]{:S(2)}, u32[]{:S(2)}) %collective-permute-start.49) | collective-permute-done | bytes 655392 | tf_op jit(solution)/shard_map/ppermute | solution.py:65
  633.7 20.1 %collective-permute-done.51 = bf16[48,2560]{1,0:T(8,128)(2,1)} collective-permute-done((bf16[48,2560]{1,0:T(8,128)(2,1)S(1)}, bf16[48,2560]{1,0:T(8,128)(2,1)}, u32[]{:S(2)}, u32[]{:S(2)}) %collective-permute-start.51) | collective-permute-done | bytes 245792 | tf_op jit(solution)/shard_map/ppermute | solution.py:65
  653.8 3.5 constant_dynamic-slice_fusion.11
  659.8 2.0 convert_add_fusion.31
  671.7 22.7 %reduce-scatter.2.cloned.1.call-done = bf16[1280,1536]{1,0:T(8,128)(2,1)} async-done(((bf16[2560,1536]{1,0:T(8,128)(2,1)}), bf16[1280,1536]{1,0:T(8,128)(2,1)}) %reduce-scatter.2.cloned.1.call-update) | async-done | bytes 3932176 | tf_op jit(solution)/shard_map/reduce_scatter | solution.py:677
  694.4 2.4 fusion.92
  704.2 5.8 collective-permute-done.59
  710.0 9.1 %collective-permute-done.58 = bf16[2,2,1,160,384]{4,3,0,1,2:T(8,128)(2,1)S(1)} collective-permute-done((bf16[2,2,1,160,384]{4,3,0,1,2:T(8,128)(2,1)S(1)}, bf16[2,2,1,160,384]{4,3,0,1,2:T(8,128)(2,1)S(1)}, u32[]{:S(2)}, u32[]{:S(2)}) %collective-permute-start.58) | collective-permute-done | bytes 491552 | tf_op jit(solution)/shard_map/ppermute | solution.py:65
  719.1 1.9 fusion.4
  728.7 24.6 %collective-permute-done.68 = bf16[2,160,1024]{2,1,0:T(8,128)(2,1)S(1)} collective-permute-done((bf16[2,160,1024]{2,1,0:T(8,128)(2,1)S(1)}, bf16[2,160,1024]{2,1,0:T(8,128)(2,1)S(1)}, u32[]{:S(2)}, u32[]{:S(2)}) %collective-permute-start.68) | collective-permute-done | bytes 655392 | tf_op jit(solution)/shard_map/ppermute | solution.py:65
  760.3 16.2 %collective-permute-done.63 = bf16[2,1,160,1280]{3,2,0,1:T(8,128)(2,1)S(1)} collective-permute-done((bf16[2,1,160,1280]{3,2,0,1:T(8,128)(2,1)S(1)}, bf16[2,1,160,1280]{3,2,0,1:T(8,128)(2,1)S(1)}, u32[]{:S(2)}, u32[]{:S(2)}) %collective-permute-start.63) | collective-permute-done | bytes 819232 | tf_op jit(solution)/shard_map/ppermute | solution.py:65
  776.8 33.7 %collective-permute-done.73 = bf16[160,2048]{1,0:T(8,128)(2,1)S(1)} collective-permute-done((bf16[160,2048]{1,0:T(8,128)(2,1)S(1)}, bf16[160,2048]{1,0:T(8,128)(2,1)S(1)}, u32[]{:S(2)}, u32[]{:S(2)}) %collective-permute-start.73) | collective-permute-done | bytes 655392 | tf_op jit(solution)/shard_map/ppermute | solution.py:65
  817.4 2.2 copy.136
  821.4 2.9 slice_convert_fusion
  (527 shorter events, 186.4 us)
Async XLA Ops:
  7.2 116.2 %all-gather.5.cloned.1.call-start = ((), (), s32[]{:S(2)}) async-start(), calls=%async_computation.4 | async-start | bytes 9052160 | tf_op jit(solution)/shard_map/all_gather | solution.py:602
  12.0 231.3 %all-gather.7.cloned.1.call-start = ((), (), s32[]{:S(2)}) async-start(), calls=%async_computation.5 | async-start | bytes 6963200 | tf_op jit(solution)/shard_map/all_gather | solution.py:608
  14.1 36.8 %all-to-all-start = ((bf16[160,8,512]{2,0,1:T(8,128)(2,1)}), bf16[160,8,512]{2,0,1:T(8,128)(2,1)S(1)}, u32[]{:S(2)}, u32[]{:S(2)}) async-start(bf16[160,8,512]{2,0,1:T(8,128)(2,1)} %bitcast.344), calls=%async_computation | async-start | bytes 2621440 | tf_op jit(solution)/shard_map/all_to_all | solution.py:586
  50.9 41.3 %all-to-all-start.1 = ((bf16[160,8,512]{2,0,1:T(8,128)(2,1)}), bf16[160,8,512]{2,0,1:T(8,128)(2,1)S(1)}, u32[]{:S(2)}, u32[]{:S(2)}) async-start(bf16[160,8,512]{2,0,1:T(8,128)(2,1)} %bitcast.382), calls=%async_computation.1 | async-start | bytes 2621440 | tf_op jit(solution)/shard_map/all_to_all | solution.py:586
  93.3 30.1 %all-to-all-start.2 = ((bf16[160,8,512]{2,0,1:T(8,128)(2,1)}), bf16[160,8,512]{2,0,1:T(8,128)(2,1)S(1)}, u32[]{:S(2)}, u32[]{:S(2)}) async-start(bf16[160,8,512]{2,0,1:T(8,128)(2,1)} %bitcast.381), calls=%async_computation.2 | async-start | bytes 2621440 | tf_op jit(solution)/shard_map/all_to_all | solution.py:586
  96.9 285.9 %all-gather.9.cloned.1.call-start = ((), (), s32[]{:S(2)}) async-start(), calls=%async_computation.7 | async-start | bytes 11141120 | tf_op jit(solution)/shard_map/all_gather | solution.py:638
  96.9 17.2 %collective-permute-start = (bf16[128,2560]{1,0:T(8,128)(2,1)S(1)}, bf16[128,2560]{1,0:T(8,128)(2,1)}, u32[]{:S(2)}, u32[]{:S(2)}) collective-permute-start(bf16[128,2560]{1,0:T(8,128)(2,1)S(1)} %bitcast.369), channel_id=1, source_target_pairs={{0,1},{1,0},{2,3},{3,2},{4,5},{5,4},{6,7},{7,6},{8,9},{9,8},{10,11... | collective-permute-start | bytes 1966088 | tf_op jit(solution)/shard_map/ppermute | solution.py:65
  98.5 9.3 %collective-permute-start.2 = (s32[256]{0:T(256)S(1)}, s32[256]{0:T(256)S(1)}, u32[]{:S(2)}, u32[]{:S(2)}) collective-permute-start(s32[256]{0:T(256)S(1)} %bitcast.407), channel_id=1, source_target_pairs={{0,4},{4,0},{1,5},{5,1},{2,6},{6,2},{3,7},{7,3},{8,12},{12,8},{9,1... | collective-permute-start | bytes 3080 | tf_op jit(solution)/shard_map/ppermute | solution.py:65
  100.7 593.7 %reduce-scatter.2.cloned.1.call-start = ((), (), s32[]{:S(2)}) async-start(), calls=%async_computation.6 | async-start | bytes 11796480 | tf_op jit(solution)/shard_map/reduce_scatter | solution.py:677
  135.1 46.2 %collective-permute-start.1 = (bf16[640,512]{1,0:T(8,128)(2,1)S(1)}, bf16[640,512]{1,0:T(8,128)(2,1)S(1)}, u32[]{:S(2)}, u32[]{:S(2)}) collective-permute-start(bf16[640,512]{1,0:T(8,128)(2,1)S(1)} %slice.141), channel_id=1, source_target_pairs={{0,16},{16,0},{1,17},{17,1},{2,18},{18,2},{3,19},{19,3},{4,20},{20... | collective-permute-start | bytes 1966088 | tf_op jit(solution)/shard_map/ppermute | solution.py:65
  181.4 47.7 %collective-permute-start.6 = (bf16[640,512]{1,0:T(8,128)(2,1)S(1)}, bf16[640,512]{1,0:T(8,128)(2,1)S(1)}, u32[]{:S(2)}, u32[]{:S(2)}) collective-permute-start(bf16[640,512]{1,0:T(8,128)(2,1)S(1)} %get-tuple-element.201), channel_id=1, source_target_pairs={{0,16},{16,0},{1,17},{17,1},{2,18},{18,2},{3,19},{19,3},{4,20},{20... | collective-permute-start | bytes 1966088 | tf_op jit(solution)/shard_map/ppermute | solution.py:65
  229.2 30.5 %collective-permute-start.8 = (bf16[640,512]{1,0:T(8,128)(2,1)}, bf16[640,512]{1,0:T(8,128)(2,1)}, u32[]{:S(2)}, u32[]{:S(2)}) collective-permute-start(bf16[640,512]{1,0:T(8,128)(2,1)} %get-tuple-element.204), channel_id=1, source_target_pairs={{0,16},{16,0},{1,17},{17,1},{2,18},{18,2},{3,19},{19,3},{4,20},{20... | collective-permute-start | bytes 1966088 | tf_op jit(solution)/shard_map/ppermute | solution.py:65
  259.8 30.1 %collective-permute-start.10 = (bf16[128,2560]{1,0:T(8,128)(2,1)S(1)}, bf16[128,2560]{1,0:T(8,128)(2,1)S(1)}, u32[]{:S(2)}, u32[]{:S(2)}) collective-permute-start(bf16[128,2560]{1,0:T(8,128)(2,1)S(1)} %dynamic-slice_convert_fusion.1), channel_id=1, source_target_pairs={{0,1},{1,0},{2,3},{3,2},{4,5},{5,4},{6,7},{7,6},{8,9},{9,8},{10,11... | collective-permute-start | bytes 1966088 | tf_op jit(solution)/shard_map/ppermute | solution.py:65
  261.4 31.1 %collective-permute-start.9 = (bf16[640,512]{1,0:T(8,128)(2,1)S(1)}, bf16[640,512]{1,0:T(8,128)(2,1)S(1)}, u32[]{:S(2)}, u32[]{:S(2)}) collective-permute-start(bf16[640,512]{1,0:T(8,128)(2,1)S(1)} %copy-done.52), channel_id=1, source_target_pairs={{0,16},{16,0},{1,17},{17,1},{2,18},{18,2},{3,19},{19,3},{4,20},{20... | collective-permute-start | bytes 1966088 | tf_op jit(solution)/shard_map/ppermute | solution.py:65
  292.9 9.8 %collective-permute-start.11 = (bf16[32,2560]{1,0:T(8,128)(2,1)S(1)}, bf16[32,2560]{1,0:T(8,128)(2,1)S(1)}, u32[]{:S(2)}, u32[]{:S(2)}) collective-permute-start(bf16[32,2560]{1,0:T(8,128)(2,1)S(1)} %slice.188), channel_id=1, source_target_pairs={{0,1},{1,0},{2,3},{3,2},{4,5},{5,4},{6,7},{7,6},{8,9},{9,8},{10,11... | collective-permute-start | bytes 491528 | tf_op jit(solution)/shard_map/ppermute | solution.py:65
  295.9 25.6 %collective-permute-start.13 = (bf16[48,2560]{1,0:T(8,128)(2,1)S(1)}, bf16[48,2560]{1,0:T(8,128)(2,1)S(1)}, u32[]{:S(2)}, u32[]{:S(2)}) collective-permute-start(bf16[48,2560]{1,0:T(8,128)(2,1)S(1)} %get-tuple-element.471), channel_id=1, source_target_pairs={{0,8},{8,0},{1,9},{9,1},{2,10},{10,2},{3,11},{11,3},{4,12},{12,4},... | collective-permute-start | bytes 737288 | tf_op jit(solution)/shard_map/ppermute | solution.py:65
  296.0 30.3 %collective-permute-start.17 = (bf16[640,512]{1,0:T(8,128)(2,1)S(1)}, bf16[640,512]{1,0:T(8,128)(2,1)S(1)}, u32[]{:S(2)}, u32[]{:S(2)}) collective-permute-start(bf16[640,512]{1,0:T(8,128)(2,1)S(1)} %copy-done.51), channel_id=1, source_target_pairs={{0,16},{16,0},{1,17},{17,1},{2,18},{18,2},{3,19},{19,3},{4,20},{20... | collective-permute-start | bytes 1966088 | tf_op jit(solution)/shard_map/ppermute | solution.py:65
  321.7 31.8 %collective-permute-start.15 = (bf16[2,48,2560]{2,1,0:T(8,128)(2,1)S(1)}, bf16[2,48,2560]{2,1,0:T(8,128)(2,1)S(1)}, u32[]{:S(2)}, u32[]{:S(2)}) collective-permute-start(bf16[2,48,2560]{2,1,0:T(8,128)(2,1)S(1)} %pad_maximum_fusion.20), channel_id=1, source_target_pairs={{0,8},{8,0},{1,9},{9,1},{2,10},{10,2},{3,11},{11,3},{4,12},{12,4},... | collective-permute-start | bytes 1474568 | tf_op jit(solution)/shard_map/ppermute | solution.py:65
  321.8 31.7 %collective-permute-start.16 = (bf16[2,48,2560]{2,1,0:T(8,128)(2,1)S(1)}, bf16[2,48,2560]{2,1,0:T(8,128)(2,1)S(1)}, u32[]{:S(2)}, u32[]{:S(2)}) collective-permute-start(bf16[2,48,2560]{2,1,0:T(8,128)(2,1)S(1)} %pad_maximum_fusion.21), channel_id=1, source_target_pairs={{0,1},{1,0},{2,3},{3,2},{4,5},{5,4},{6,7},{7,6},{8,9},{9,8},{10,11... | collective-permute-start | bytes 1474568 | tf_op jit(solution)/shard_map/ppermute | solution.py:65
  322.0 8.9 %collective-permute-start.14 = (bf16[2,32,2560]{2,1,0:T(8,128)(2,1)S(1)}, bf16[2,32,2560]{2,1,0:T(8,128)(2,1)S(1)}, u32[]{:S(2)}, u32[]{:S(2)}) collective-permute-start(bf16[2,32,2560]{2,1,0:T(8,128)(2,1)S(1)} %pad_maximum_fusion.22), channel_id=1, source_target_pairs={{0,4},{4,0},{1,5},{5,1},{2,6},{6,2},{3,7},{7,3},{8,12},{12,8},{9,1... | collective-permute-start | bytes 983048 | tf_op jit(solution)/shard_map/ppermute | solution.py:65
  326.3 31.1 %collective-permute-start.21 = (bf16[640,512]{1,0:T(8,128)(2,1)S(1)}, bf16[640,512]{1,0:T(8,128)(2,1)S(1)}, u32[]{:S(2)}, u32[]{:S(2)}) collective-permute-start(bf16[640,512]{1,0:T(8,128)(2,1)S(1)} %copy-done.50), channel_id=1, source_target_pairs={{0,16},{16,0},{1,17},{17,1},{2,18},{18,2},{3,19},{19,3},{4,20},{20... | collective-permute-start | bytes 1966088 | tf_op jit(solution)/shard_map/ppermute | solution.py:65
  353.6 17.2 %collective-permute-start.18 = (bf16[2,2,32,2560]{3,2,1,0:T(8,128)(2,1)S(1)}, bf16[2,2,32,2560]{3,2,1,0:T(8,128)(2,1)S(1)}, u32[]{:S(2)}, u32[]{:S(2)}) collective-permute-start(bf16[2,2,32,2560]{3,2,1,0:T(8,128)(2,1)S(1)} %pad_maximum_fusion.18), channel_id=1, source_target_pairs={{0,8},{8,0},{1,9},{9,1},{2,10},{10,2},{3,11},{11,3},{4,12},{12,4},... | collective-permute-start | bytes 1966088 | tf_op jit(solution)/shard_map/ppermute | solution.py:65
  353.9 23.6 %collective-permute-start.19 = (bf16[2,2,48,2560]{3,2,0,1:T(8,128)(2,1)S(1)}, bf16[2,2,48,2560]{3,2,0,1:T(8,128)(2,1)S(1)}, u32[]{:S(2)}, u32[]{:S(2)}) collective-permute-start(bf16[2,2,48,2560]{3,2,0,1:T(8,128)(2,1)S(1)} %pad_maximum_fusion.16), channel_id=1, source_target_pairs={{0,1},{1,0},{2,3},{3,2},{4,5},{5,4},{6,7},{7,6},{8,9},{9,8},{10,11... | collective-permute-start | bytes 2949128 | tf_op jit(solution)/shard_map/ppermute | solution.py:65
  354.1 24.5 %collective-permute-start.20 = (bf16[2,2,48,2560]{3,2,0,1:T(8,128)(2,1)S(1)}, bf16[2,2,48,2560]{3,2,0,1:T(8,128)(2,1)S(1)}, u32[]{:S(2)}, u32[]{:S(2)}) collective-permute-start(bf16[2,2,48,2560]{3,2,0,1:T(8,128)(2,1)S(1)} %pad_maximum_fusion.17), channel_id=1, source_target_pairs={{0,4},{4,0},{1,5},{5,1},{2,6},{6,2},{3,7},{7,3},{8,12},{12,8},{9,1... | collective-permute-start | bytes 2949128 | tf_op jit(solution)/shard_map/ppermute | solution.py:65
  382.6 16.0 %collective-permute-start.22 = (bf16[1024,2560]{1,0:T(8,128)(2,1)}, bf16[1024,2560]{1,0:T(8,128)(2,1)}, u32[]{:S(2)}, u32[]{:S(2)}) collective-permute-start(bf16[1024,2560]{1,0:T(8,128)(2,1)} %bitcast.43.rows_ref.refs_4_), channel_id=1, source_target_pairs={{0,2},{2,0},{1,3},{3,1},{4,6},{6,4},{5,7},{7,5},{8,10},{10,8},{9,1... | collective-permute-start | bytes 15728648 | tf_op jit(solution)/shard_map/ppermute | solution.py:65
  422.2 16.9 %collective-permute-start.24 = (bf16[1024,2560]{1,0:T(8,128)(2,1)}, bf16[1024,2560]{1,0:T(8,128)(2,1)}, u32[]{:S(2)}, u32[]{:S(2)}) collective-permute-start(bf16[1024,2560]{1,0:T(8,128)(2,1)} %shard_map.258), channel_id=1, source_target_pairs={{0,2},{2,0},{1,3},{3,1},{4,6},{6,4},{5,7},{7,5},{8,10},{10,8},{9,1... | collective-permute-start | bytes 15728648 | tf_op jit(solution)/shard_map/ppermute | solution.py:65
  422.7 16.4 %collective-permute-start.23 = (f32[2,512]{1,0:T(2,128)S(1)}, f32[2,512]{1,0:T(2,128)S(1)}, u32[]{:S(2)}, u32[]{:S(2)}) collective-permute-start(f32[2,512]{1,0:T(2,128)S(1)} %add.477), channel_id=1, source_target_pairs={{0,16},{16,0},{1,17},{17,1},{2,18},{18,2},{3,19},{19,3},{4,20},{20... | collective-permute-start | bytes 12296 | tf_op jit(solution)/shard_map/ppermute | solution.py:65
  446.2 30.4 %collective-permute-start.26 = (bf16[2,2,48,2560]{3,2,1,0:T(8,128)(2,1)}, bf16[2,2,48,2560]{3,2,1,0:T(8,128)(2,1)}, u32[]{:S(2)}, u32[]{:S(2)}) collective-permute-start(bf16[2,2,48,2560]{3,2,1,0:T(8,128)(2,1)} %dynamic-slice_bitcast_fusion.1), channel_id=1, source_target_pairs={{0,1},{1,0},{2,3},{3,2},{4,5},{5,4},{6,7},{7,6},{8,9},{9,8},{10,11... | collective-permute-start | bytes 2949128 | tf_op jit(solution)/shard_map/ppermute | solution.py:65
  450.2 26.4 %collective-permute-start.27 = (bf16[2,2,48,2560]{3,2,0,1:T(8,128)(2,1)}, bf16[2,2,48,2560]{3,2,0,1:T(8,128)(2,1)}, u32[]{:S(2)}, u32[]{:S(2)}) collective-permute-start(bf16[2,2,48,2560]{3,2,0,1:T(8,128)(2,1)} %bitcast.346), channel_id=1, source_target_pairs={{0,4},{4,0},{1,5},{5,1},{2,6},{6,2},{3,7},{7,3},{8,12},{12,8},{9,1... | collective-permute-start | bytes 2949128 | tf_op jit(solution)/shard_map/ppermute | solution.py:65
  452.4 24.2 %collective-permute-start.25 = (bf16[2,2,32,2560]{3,2,1,0:T(8,128)(2,1)}, bf16[2,2,32,2560]{3,2,1,0:T(8,128)(2,1)}, u32[]{:S(2)}, u32[]{:S(2)}) collective-permute-start(bf16[2,2,32,2560]{3,2,1,0:T(8,128)(2,1)} %dynamic-slice_bitcast_fusion.6), channel_id=1, source_target_pairs={{0,8},{8,0},{1,9},{9,1},{2,10},{10,2},{3,11},{11,3},{4,12},{12,4},... | collective-permute-start | bytes 1966088 | tf_op jit(solution)/shard_map/ppermute | solution.py:65
  478.5 14.9 %collective-permute-start.29 = (bf16[2,48,2560]{2,1,0:T(8,128)(2,1)S(1)}, bf16[2,48,2560]{2,1,0:T(8,128)(2,1)}, u32[]{:S(2)}, u32[]{:S(2)}) collective-permute-start(bf16[2,48,2560]{2,1,0:T(8,128)(2,1)S(1)} %dynamic-slice_bitcast_fusion.10), channel_id=1, source_target_pairs={{0,8},{8,0},{1,9},{9,1},{2,10},{10,2},{3,11},{11,3},{4,12},{12,4},... | collective-permute-start | bytes 1474568 | tf_op jit(solution)/shard_map/ppermute | solution.py:65
  482.7 12.2 %collective-permute-start.30 = (bf16[2,48,2560]{2,1,0:T(8,128)(2,1)}, bf16[2,48,2560]{2,1,0:T(8,128)(2,1)}, u32[]{:S(2)}, u32[]{:S(2)}) collective-permute-start(bf16[2,48,2560]{2,1,0:T(8,128)(2,1)} %dynamic-slice_bitcast_fusion.9), channel_id=1, source_target_pairs={{0,1},{1,0},{2,3},{3,2},{4,5},{5,4},{6,7},{7,6},{8,9},{9,8},{10,11... | collective-permute-start | bytes 1474568 | tf_op jit(solution)/shard_map/ppermute | solution.py:65
  514.7 18.5 %collective-permute-start.36 = (bf16[1024,2560]{1,0:T(8,128)(2,1)}, bf16[1024,2560]{1,0:T(8,128)(2,1)}, u32[]{:S(2)}, u32[]{:S(2)}) collective-permute-start(bf16[1024,2560]{1,0:T(8,128)(2,1)} %shard_map.261), channel_id=1, source_target_pairs={{0,2},{2,0},{1,3},{3,1},{4,6},{6,4},{5,7},{7,5},{8,10},{10,8},{9,1... | collective-permute-start | bytes 15728648 | tf_op jit(solution)/shard_map/ppermute | solution.py:65
  514.7 17.3 %collective-permute-start.37 = (bf16[128,2560]{1,0:T(8,128)(2,1)S(1)}, bf16[128,2560]{1,0:T(8,128)(2,1)}, u32[]{:S(2)}, u32[]{:S(2)}) collective-permute-start(bf16[128,2560]{1,0:T(8,128)(2,1)S(1)} %convert_element_type.496), channel_id=1, source_target_pairs={{0,1},{1,0},{2,3},{3,2},{4,5},{5,4},{6,7},{7,6},{8,9},{9,8},{10,11... | collective-permute-start | bytes 1966088 | tf_op jit(solution)/shard_map/ppermute | solution.py:65
  519.0 21.4 %collective-permute-start.41 = (f32[2,2048]{1,0:T(2,128)S(1)}, f32[2,2048]{1,0:T(2,128)S(1)}, u32[]{:S(2)}, u32[]{:S(2)}) collective-permute-start(f32[2,2048]{1,0:T(2,128)S(1)} %pad_maximum_fusion.27), channel_id=1, source_target_pairs={{0,8},{8,0},{1,9},{9,1},{2,10},{10,2},{3,11},{11,3},{4,12},{12,4},... | collective-permute-start | bytes 49160 | tf_op jit(solution)/shard_map/ppermute | solution.py:65
  540.1 38.4 %collective-permute-start.38 = (bf16[2,2,32,2560]{3,2,1,0:T(8,128)(2,1)}, bf16[2,2,32,2560]{3,2,1,0:T(8,128)(2,1)S(1)}, u32[]{:S(2)}, u32[]{:S(2)}) collective-permute-start(bf16[2,2,32,2560]{3,2,1,0:T(8,128)(2,1)} %dynamic-slice_bitcast_fusion.5), channel_id=1, source_target_pairs={{0,8},{8,0},{1,9},{9,1},{2,10},{10,2},{3,11},{11,3},{4,12},{12,4},... | collective-permute-start | bytes 1966088 | tf_op jit(solution)/shard_map/ppermute | solution.py:65
  556.4 9.5 %collective-permute-start.42 = (bf16[512,512]{1,0:T(8,128)(2,1)S(1)}, bf16[512,512]{1,0:T(8,128)(2,1)S(1)}, u32[]{:S(2)}, u32[]{:S(2)}) collective-permute-start(bf16[512,512]{1,0:T(8,128)(2,1)S(1)} %slice.244), channel_id=1, source_target_pairs={{0,2},{2,0},{1,3},{3,1},{4,6},{6,4},{5,7},{7,5},{8,10},{10,8},{9,1... | collective-permute-start | bytes 1572872 | tf_op jit(solution)/shard_map/ppermute | solution.py:65
  557.5 31.5 %collective-permute-start.39 = (bf16[2,2,48,2560]{3,2,1,0:T(8,128)(2,1)}, bf16[2,2,48,2560]{3,2,1,0:T(8,128)(2,1)S(1)}, u32[]{:S(2)}, u32[]{:S(2)}) collective-permute-start(bf16[2,2,48,2560]{3,2,1,0:T(8,128)(2,1)} %dynamic-slice_bitcast_fusion), channel_id=1, source_target_pairs={{0,1},{1,0},{2,3},{3,2},{4,5},{5,4},{6,7},{7,6},{8,9},{9,8},{10,11... | collective-permute-start | bytes 2949128 | tf_op jit(solution)/shard_map/ppermute | solution.py:65
  559.5 29.6 %collective-permute-start.40 = (bf16[2,2,48,2560]{3,2,0,1:T(8,128)(2,1)S(1)}, bf16[2,2,48,2560]{3,2,0,1:T(8,128)(2,1)}, u32[]{:S(2)}, u32[]{:S(2)}) collective-permute-start(bf16[2,2,48,2560]{3,2,0,1:T(8,128)(2,1)S(1)} %bitcast.399), channel_id=1, source_target_pairs={{0,4},{4,0},{1,5},{5,1},{2,6},{6,2},{3,7},{7,3},{8,12},{12,8},{9,1... | collective-permute-start | bytes 2949128 | tf_op jit(solution)/shard_map/ppermute | solution.py:65
  566.1 22.9 %collective-permute-start.43 = (bf16[256,512]{1,0:T(8,128)(2,1)S(1)}, bf16[256,512]{1,0:T(8,128)(2,1)S(1)}, u32[]{:S(2)}, u32[]{:S(2)}) collective-permute-start(bf16[256,512]{1,0:T(8,128)(2,1)S(1)} %slice.245), channel_id=1, source_target_pairs={{0,4},{4,0},{1,5},{5,1},{2,6},{6,2},{3,7},{7,3},{8,12},{12,8},{9,1... | collective-permute-start | bytes 786440 | tf_op jit(solution)/shard_map/ppermute | solution.py:65
  572.7 22.7 %collective-permute-start.47 = (bf16[2,2,2,1,160,1280]{5,4,0,1,2,3:T(8,128)(2,1)}, bf16[2,2,2,1,160,1280]{5,4,0,1,2,3:T(8,128)(2,1)}, u32[]{:S(2)}, u32[]{:S(2)}) collective-permute-start(bf16[2,2,2,1,160,1280]{5,4,0,1,2,3:T(8,128)(2,1)} %copy.150), channel_id=1, source_target_pairs={{0,2},{2,0},{1,3},{3,1},{4,6},{6,4},{5,7},{7,5},{8,10},{10,8},{9,1... | collective-permute-start | bytes 9830408 | tf_op jit(solution)/shard_map/ppermute | solution.py:65
  590.0 25.9 %collective-permute-start.44 = (bf16[2,32,2560]{2,1,0:T(8,128)(2,1)S(1)}, bf16[2,32,2560]{2,1,0:T(8,128)(2,1)S(1)}, u32[]{:S(2)}, u32[]{:S(2)}) collective-permute-start(bf16[2,32,2560]{2,1,0:T(8,128)(2,1)S(1)} %dynamic-slice_bitcast_fusion.11), channel_id=1, source_target_pairs={{0,4},{4,0},{1,5},{5,1},{2,6},{6,2},{3,7},{7,3},{8,12},{12,8},{9,1... | collective-permute-start | bytes 983048 | tf_op jit(solution)/shard_map/ppermute | solution.py:65
  592.8 23.1 %collective-permute-start.45 = (bf16[2,48,2560]{2,1,0:T(8,128)(2,1)S(1)}, bf16[2,48,2560]{2,1,0:T(8,128)(2,1)S(1)}, u32[]{:S(2)}, u32[]{:S(2)}) collective-permute-start(bf16[2,48,2560]{2,1,0:T(8,128)(2,1)S(1)} %dynamic-slice_bitcast_fusion.8), channel_id=1, source_target_pairs={{0,8},{8,0},{1,9},{9,1},{2,10},{10,2},{3,11},{11,3},{4,12},{12,4},... | collective-permute-start | bytes 1474568 | tf_op jit(solution)/shard_map/ppermute | solution.py:65
  595.9 20.0 %collective-permute-start.46 = (bf16[2,48,2560]{2,1,0:T(8,128)(2,1)S(1)}, bf16[2,48,2560]{2,1,0:T(8,128)(2,1)S(1)}, u32[]{:S(2)}, u32[]{:S(2)}) collective-permute-start(bf16[2,48,2560]{2,1,0:T(8,128)(2,1)S(1)} %dynamic-slice_bitcast_fusion.7), channel_id=1, source_target_pairs={{0,1},{1,0},{2,3},{3,2},{4,5},{5,4},{6,7},{7,6},{8,9},{9,8},{10,11... | collective-permute-start | bytes 1474568 | tf_op jit(solution)/shard_map/ppermute | solution.py:65
  608.3 16.2 %collective-permute-start.49 = (bf16[128,2560]{1,0:T(8,128)(2,1)S(1)}, bf16[128,2560]{1,0:T(8,128)(2,1)S(1)}, u32[]{:S(2)}, u32[]{:S(2)}) collective-permute-start(bf16[128,2560]{1,0:T(8,128)(2,1)S(1)} %dynamic-slice_convert_fusion), channel_id=1, source_target_pairs={{0,1},{1,0},{2,3},{3,2},{4,5},{5,4},{6,7},{7,6},{8,9},{9,8},{10,11... | collective-permute-start | bytes 1966088 | tf_op jit(solution)/shard_map/ppermute | solution.py:65
  613.5 40.3 %collective-permute-start.53 = (bf16[2,2,1,160,1280]{4,3,0,1,2:T(8,128)(2,1)}, bf16[2,2,1,160,1280]{4,3,0,1,2:T(8,128)(2,1)}, u32[]{:S(2)}, u32[]{:S(2)}) collective-permute-start(bf16[2,2,1,160,1280]{4,3,0,1,2:T(8,128)(2,1)} %constant_dynamic-slice_fusion.12), channel_id=1, source_target_pairs={{0,4},{4,0},{1,5},{5,1},{2,6},{6,2},{3,7},{7,3},{8,12},{12,8},{9,1... | collective-permute-start | bytes 4915208 | tf_op jit(solution)/shard_map/ppermute | solution.py:65
  625.9 27.9 %collective-permute-start.51 = (bf16[48,2560]{1,0:T(8,128)(2,1)S(1)}, bf16[48,2560]{1,0:T(8,128)(2,1)}, u32[]{:S(2)}, u32[]{:S(2)}) collective-permute-start(bf16[48,2560]{1,0:T(8,128)(2,1)S(1)} %dynamic-slice_bitcast_fusion.14), channel_id=1, source_target_pairs={{0,4},{4,0},{1,5},{5,1},{2,6},{6,2},{3,7},{7,3},{8,12},{12,8},{9,1... | collective-permute-start | bytes 737288 | tf_op jit(solution)/shard_map/ppermute | solution.py:65
  627.5 26.3 %collective-permute-start.52 = (bf16[48,2560]{1,0:T(8,128)(2,1)}, bf16[48,2560]{1,0:T(8,128)(2,1)}, u32[]{:S(2)}, u32[]{:S(2)}) collective-permute-start(bf16[48,2560]{1,0:T(8,128)(2,1)} %dynamic-slice_bitcast_fusion.13), channel_id=1, source_target_pairs={{0,8},{8,0},{1,9},{9,1},{2,10},{10,2},{3,11},{11,3},{4,12},{12,4},... | collective-permute-start | bytes 737288 | tf_op jit(solution)/shard_map/ppermute | solution.py:65
  657.5 11.4 %collective-permute-start.54 = (bf16[2,2,2,1,160,1280]{5,4,0,1,2,3:T(8,128)(2,1)S(1)}, bf16[2,2,2,1,160,1280]{5,4,0,1,2,3:T(8,128)(2,1)S(1)}, u32[]{:S(2)}, u32[]{:S(2)}) collective-permute-start(bf16[2,2,2,1,160,1280]{5,4,0,1,2,3:T(8,128)(2,1)S(1)} %copy.153), channel_id=1, source_target_pairs={{0,2},{2,0},{1,3},{3,1},{4,6},{6,4},{5,7},{7,5},{8,10},{10,8},{9,1... | collective-permute-start | bytes 9830408 | tf_op jit(solution)/shard_map/ppermute | solution.py:65
  659.2 12.5 %collective-permute-start.57 = (bf16[2,2,2,1,160,384]{5,4,0,1,2,3:T(8,128)(2,1)S(1)}, bf16[2,2,2,1,160,384]{5,4,0,1,2,3:T(8,128)(2,1)}, u32[]{:S(2)}, u32[]{:S(2)}) collective-permute-start(bf16[2,2,2,1,160,384]{5,4,0,1,2,3:T(8,128)(2,1)S(1)} %copy.155), channel_id=1, source_target_pairs={{0,2},{2,0},{1,3},{3,1},{4,6},{6,4},{5,7},{7,5},{8,10},{10,8},{9,1... | collective-permute-start | bytes 2949128 | tf_op jit(solution)/shard_map/ppermute | solution.py:65
  668.3 41.8 %collective-permute-start.59 = (bf16[2,1,160,1280]{3,2,0,1:T(8,128)(2,1)}, bf16[2,1,160,1280]{3,2,0,1:T(8,128)(2,1)}, u32[]{:S(2)}, u32[]{:S(2)}) collective-permute-start(bf16[2,1,160,1280]{3,2,0,1:T(8,128)(2,1)} %constant_dynamic-slice_fusion.5), channel_id=1, source_target_pairs={{0,8},{8,0},{1,9},{9,1},{2,10},{10,2},{3,11},{11,3},{4,12},{12,4},... | collective-permute-start | bytes 2457608 | tf_op jit(solution)/shard_map/ppermute | solution.py:65
  671.1 48.0 %collective-permute-start.55 = (bf16[2,2,1,160,1280]{4,3,0,1,2:T(8,128)(2,1)}, bf16[2,2,1,160,1280]{4,3,0,1,2:T(8,128)(2,1)}, u32[]{:S(2)}, u32[]{:S(2)}) collective-permute-start(bf16[2,2,1,160,1280]{4,3,0,1,2:T(8,128)(2,1)} %constant_dynamic-slice_fusion.9), channel_id=1, source_target_pairs={{0,4},{4,0},{1,5},{5,1},{2,6},{6,2},{3,7},{7,3},{8,12},{12,8},{9,1... | collective-permute-start | bytes 4915208 | tf_op jit(solution)/shard_map/ppermute | solution.py:65
  699.5 19.6 %collective-permute-start.58 = (bf16[2,2,1,160,384]{4,3,0,1,2:T(8,128)(2,1)S(1)}, bf16[2,2,1,160,384]{4,3,0,1,2:T(8,128)(2,1)S(1)}, u32[]{:S(2)}, u32[]{:S(2)}) collective-permute-start(bf16[2,2,1,160,384]{4,3,0,1,2:T(8,128)(2,1)S(1)} %constant_dynamic-slice_fusion.6), channel_id=1, source_target_pairs={{0,4},{4,0},{1,5},{5,1},{2,6},{6,2},{3,7},{7,3},{8,12},{12,8},{9,1... | collective-permute-start | bytes 1474568 | tf_op jit(solution)/shard_map/ppermute | solution.py:65
  722.6 31.4 %collective-permute-start.66 = (bf16[2,160,1024]{2,1,0:T(8,128)(2,1)S(1)}, bf16[2,160,1024]{2,1,0:T(8,128)(2,1)S(1)}, u32[]{:S(2)}, u32[]{:S(2)}) collective-permute-start(bf16[2,160,1024]{2,1,0:T(8,128)(2,1)S(1)} %fusion.62), channel_id=1, source_target_pairs={{0,8},{8,0},{1,9},{9,1},{2,10},{10,2},{3,11},{11,3},{4,12},{12,4},... | collective-permute-start | bytes 1966088 | tf_op jit(solution)/shard_map/ppermute | solution.py:65
  724.3 29.8 %collective-permute-start.67 = (bf16[2,160,1024]{2,1,0:T(8,128)(2,1)S(1)}, bf16[2,160,1024]{2,1,0:T(8,128)(2,1)S(1)}, u32[]{:S(2)}, u32[]{:S(2)}) collective-permute-start(bf16[2,160,1024]{2,1,0:T(8,128)(2,1)S(1)} %fusion.58), channel_id=1, source_target_pairs={{0,4},{4,0},{1,5},{5,1},{2,6},{6,2},{3,7},{7,3},{8,12},{12,8},{9,1... | collective-permute-start | bytes 1966088 | tf_op jit(solution)/shard_map/ppermute | solution.py:65
  725.2 28.2 %collective-permute-start.68 = (bf16[2,160,1024]{2,1,0:T(8,128)(2,1)S(1)}, bf16[2,160,1024]{2,1,0:T(8,128)(2,1)S(1)}, u32[]{:S(2)}, u32[]{:S(2)}) collective-permute-start(bf16[2,160,1024]{2,1,0:T(8,128)(2,1)S(1)} %fusion.54), channel_id=1, source_target_pairs={{0,4},{4,0},{1,5},{5,1},{2,6},{6,2},{3,7},{7,3},{8,12},{12,8},{9,1... | collective-permute-start | bytes 1966088 | tf_op jit(solution)/shard_map/ppermute | solution.py:65
  726.6 27.4 %collective-permute-start.65 = (bf16[1,160,1280]{2,1,0:T(8,128)(2,1)S(1)}, bf16[1,160,1280]{2,1,0:T(8,128)(2,1)S(1)}, u32[]{:S(2)}, u32[]{:S(2)}) collective-permute-start(bf16[1,160,1280]{2,1,0:T(8,128)(2,1)S(1)} %constant_dynamic-slice_fusion.2), channel_id=1, source_target_pairs={{0,16},{16,0},{1,17},{17,1},{2,18},{18,2},{3,19},{19,3},{4,20},{20... | collective-permute-start | bytes 1228808 | tf_op jit(solution)/shard_map/ppermute | solution.py:65
  727.2 26.8 %collective-permute-start.64 = (bf16[2,1,160,384]{3,2,0,1:T(8,128)(2,1)S(1)}, bf16[2,1,160,384]{3,2,0,1:T(8,128)(2,1)S(1)}, u32[]{:S(2)}, u32[]{:S(2)}) collective-permute-start(bf16[2,1,160,384]{3,2,0,1:T(8,128)(2,1)S(1)} %constant_dynamic-slice_fusion.3), channel_id=1, source_target_pairs={{0,8},{8,0},{1,9},{9,1},{2,10},{10,2},{3,11},{11,3},{4,12},{12,4},... | collective-permute-start | bytes 737288 | tf_op jit(solution)/shard_map/ppermute | solution.py:65
  753.4 23.1 %collective-permute-start.63 = (bf16[2,1,160,1280]{3,2,0,1:T(8,128)(2,1)S(1)}, bf16[2,1,160,1280]{3,2,0,1:T(8,128)(2,1)S(1)}, u32[]{:S(2)}, u32[]{:S(2)}) collective-permute-start(bf16[2,1,160,1280]{3,2,0,1:T(8,128)(2,1)S(1)} %constant_dynamic-slice_fusion.4), channel_id=1, source_target_pairs={{0,8},{8,0},{1,9},{9,1},{2,10},{10,2},{3,11},{11,3},{4,12},{12,4},... | collective-permute-start | bytes 2457608 | tf_op jit(solution)/shard_map/ppermute | solution.py:65
  754.2 56.3 %collective-permute-start.70 = (bf16[1,160,384]{2,1,0:T(8,128)(2,1)S(1)}, bf16[1,160,384]{2,1,0:T(8,128)(2,1)S(1)}, u32[]{:S(2)}, u32[]{:S(2)}) collective-permute-start(bf16[1,160,384]{2,1,0:T(8,128)(2,1)S(1)} %constant_dynamic-slice_fusion), channel_id=1, source_target_pairs={{0,16},{16,0},{1,17},{17,1},{2,18},{18,2},{3,19},{19,3},{4,20},{20... | collective-permute-start | bytes 368648 | tf_op jit(solution)/shard_map/ppermute | solution.py:65
  755.7 54.8 %collective-permute-start.71 = (bf16[160,2048]{1,0:T(8,128)(2,1)S(1)}, bf16[160,2048]{1,0:T(8,128)(2,1)S(1)}, u32[]{:S(2)}, u32[]{:S(2)}) collective-permute-start(bf16[160,2048]{1,0:T(8,128)(2,1)S(1)} %fusion.50), channel_id=1, source_target_pairs={{0,4},{4,0},{1,5},{5,1},{2,6},{6,2},{3,7},{7,3},{8,12},{12,8},{9,1... | collective-permute-start | bytes 1966088 | tf_op jit(solution)/shard_map/ppermute | solution.py:65
  756.8 53.7 %collective-permute-start.72 = (bf16[160,2048]{1,0:T(8,128)(2,1)S(1)}, bf16[160,2048]{1,0:T(8,128)(2,1)S(1)}, u32[]{:S(2)}, u32[]{:S(2)}) collective-permute-start(bf16[160,2048]{1,0:T(8,128)(2,1)S(1)} %fusion.46), channel_id=1, source_target_pairs={{0,8},{8,0},{1,9},{9,1},{2,10},{10,2},{3,11},{11,3},{4,12},{12,4},... | collective-permute-start | bytes 1966088 | tf_op jit(solution)/shard_map/ppermute | solution.py:65
  757.9 52.6 %collective-permute-start.73 = (bf16[160,2048]{1,0:T(8,128)(2,1)S(1)}, bf16[160,2048]{1,0:T(8,128)(2,1)S(1)}, u32[]{:S(2)}, u32[]{:S(2)}) collective-permute-start(bf16[160,2048]{1,0:T(8,128)(2,1)S(1)} %fusion.42), channel_id=1, source_target_pairs={{0,8},{8,0},{1,9},{9,1},{2,10},{10,2},{3,11},{11,3},{4,12},{12,4},... | collective-permute-start | bytes 1966088 | tf_op jit(solution)/shard_map/ppermute | solution.py:65
  776.7 35.3 %collective-permute-start.69 = (bf16[1,160,1280]{2,1,0:T(8,128)(2,1)S(1)}, bf16[1,160,1280]{2,1,0:T(8,128)(2,1)S(1)}, u32[]{:S(2)}, u32[]{:S(2)}) collective-permute-start(bf16[1,160,1280]{2,1,0:T(8,128)(2,1)S(1)} %constant_dynamic-slice_fusion.1), channel_id=1, source_target_pairs={{0,16},{16,0},{1,17},{17,1},{2,18},{18,2},{3,19},{19,3},{4,20},{20... | collective-permute-start | bytes 1228808 | tf_op jit(solution)/shard_map/ppermute | solution.py:65
  (112 other events, 720.5 us)
Sparse Core Ops, SparseCore 0:
  12.2 105.2 all-gather.4
  119.7 106.6 all-gather.6
  228.0 124.0 all-gather.8
  517.8 176.5 reduce-scatter.1

commit v5 on v4

--- a/solution.py
+++ b/solution.py
@@ -751,7 +751,7 @@
     input_grad = backs[2].step(input_grad)
     input_grad = query_sum.step(input_grad)
     input_grad = keyvalue_sum.step(input_grad)
-    input_grad = finish_all([output_sum, *backs, query_sum, keyvalue_sum], input_grad)
+    input_grad = finish_all([output_sum, query_sum, *backs, keyvalue_sum], input_grad)
     proj_out = output_sum.result[0]
     query_out = query_sum.result[0]
     keyvalue_out = keyvalue_sum.result[0][:, :keyvalue_columns]

time: 844 us -> 843 us (level)
  transfers between devices with their start and end apart: 81 -> 81, of which waited for: 38 -> 38; matrix products, arithmetic and copies ran while one was open for 12% -> 13% of each run, Pallas kernels for 11% -> 11%
where the time goes in v5:
time: 843 us; the launch traced here: 835 us
  waiting for transfers between devices  445 us (53%)
  Pallas kernels  123 us (15%)
  starting transfers between devices  87.2 us (10%)
  other arithmetic  83.3 us (10%)
  local copies, waits for them, and re-layouts  77.9 us (9%)
  between operations  15.8 us (2%)
    ppermute x74, waiting for transfers between devices, swap(): lax.ppermute(values, axis, [(i, i ^ mask) for i in range(lax.axis_size(ax...  347 us
    all_to_all x3, waiting for transfers between devices, by_block(): lax.all_to_all(jnp.pad(item, ((0, 0), (0, ff_pad))), ('near',) + CTX, spl...  74 us
    ppermute x74, starting transfers between devices, swap(): lax.ppermute(values, axis, [(i, i ^ mask) for i in range(lax.axis_size(ax...  74 us
    pallas_call x6, Pallas kernels, rows_out(): pl.pallas_call(rows_kernel, grid=(count // tile,), in_specs=[pl.BlockSpec...  39.6 us
    pallas_call x4, Pallas kernels, weight_out(): pl.pallas_call(partial(weight_kernel, groups), grid_spec=pltpu.PrefetchSc...  33.1 us
    unnamed x195, local copies, waits for them, and re-layouts  26.5 us
    pallas_call x2, Pallas kernels, hidden_units(): pl.pallas_call(hidden_kernel, grid_spec=pltpu.PrefetchScalarGridSpec(num_...  25.7 us
    reduce_scatter x1, waiting for transfers between devices, local(): ff_sum = lax.psum_scatter(ff_wgrad, 'far', scatter_dimension=0, tiled=True)  22.7 us
  transfers between devices with their start and end apart: 81, of which 38 were waited for; matrix products, arithmetic and copies ran while one was open for 13% of the time, Pallas kernels for 11%

profile of v5, /device:TPU:0, one launch (start us, length us, event | category | flops | bytes accessed | tf_op | source)
XLA Modules:
  0.0 834.7 jit_solution(2913005083812169934)
XLA Ops:
  14.1 5.4 all-to-all-start
  20.8 30.1 %all-to-all-done = bf16[160,8,512]{2,0,1:T(8,128)(2,1)S(1)} async-done(((bf16[160,8,512]{2,0,1:T(8,128)(2,1)}), bf16[160,8,512]{2,0,1:T(8,128)(2,1)S(1)}, u32[]{:S(2)}, u32[]{:S(2)}) %all-to-all-start) | async-done | bytes 1310752 | tf_op jit(solution)/shard_map/all_to_all | solution.py:586
  50.9 4.1 all-to-all-start.1
  57.6 34.6 %all-to-all-done.1 = bf16[160,8,512]{2,0,1:T(8,128)(2,1)S(1)} async-done(((bf16[160,8,512]{2,0,1:T(8,128)(2,1)}), bf16[160,8,512]{2,0,1:T(8,128)(2,1)S(1)}, u32[]{:S(2)}, u32[]{:S(2)}) %all-to-all-start.1) | async-done | bytes 1310752 | tf_op jit(solution)/shard_map/all_to_all | solution.py:586
  93.3 3.6 all-to-all-start.2
  98.5 2.1 collective-permute-start.2
  102.4 5.3 collective-permute-done.2
  109.8 4.3 collective-permute-done
  114.1 9.3 %all-to-all-done.2 = bf16[160,8,512]{2,0,1:T(8,128)(2,1)S(1)} async-done(((bf16[160,8,512]{2,0,1:T(8,128)(2,1)}), bf16[160,8,512]{2,0,1:T(8,128)(2,1)S(1)}, u32[]{:S(2)}, u32[]{:S(2)}) %all-to-all-start.2) | async-done | bytes 1310752 | tf_op jit(solution)/shard_map/all_to_all | solution.py:586
  125.0 2.7 slice_reduce_fusion
  129.7 2.3 fusion.26
  135.1 3.6 collective-permute-start.1
  141.7 5.7 collective-permute-done.5
  147.5 33.8 %collective-permute-done.1 = bf16[640,512]{1,0:T(8,128)(2,1)S(1)} collective-permute-done((bf16[640,512]{1,0:T(8,128)(2,1)S(1)}, bf16[640,512]{1,0:T(8,128)(2,1)S(1)}, u32[]{:S(2)}, u32[]{:S(2)}) %collective-permute-start.1) | collective-permute-done | bytes 655392 | tf_op jit(solution)/shard_map/ppermute | solution.py:65
  184.2 45.0 %collective-permute-done.6 = bf16[640,512]{1,0:T(8,128)(2,1)S(1)} collective-permute-done((bf16[640,512]{1,0:T(8,128)(2,1)S(1)}, bf16[640,512]{1,0:T(8,128)(2,1)S(1)}, u32[]{:S(2)}, u32[]{:S(2)}) %collective-permute-start.6) | collective-permute-done | bytes 655392 | tf_op jit(solution)/shard_map/ppermute | solution.py:65
  231.6 10.9 %shard_map.254 = (bf16[256,1280]{1,0:T(8,128)(2,1)S(1)}, bf16[256,1280]{1,0:T(8,128)(2,1)S(1)}, f32[256,640]{1,0:T(8,128)S(1)}) custom-call(bf16[256,2560]{1,0:T(8,128)(2,1)S(1)} %fusion.7.rows_ref.refs_0_, bf16[2560,1664]{1,0:T(8,128)(2,1)} %all-gather.5.cloned.1.call-done.weight_ref.refs_2_.refs_3_, ...), custom_call_target="tpu_custom_call" | custom-call | tf_op jit(solution)/shard_map/pallas_call | solution.py:410
  243.4 5.3 shard_map.255
  248.7 10.9 %collective-permute-done.8 = bf16[640,512]{1,0:T(8,128)(2,1)} collective-permute-done((bf16[640,512]{1,0:T(8,128)(2,1)}, bf16[640,512]{1,0:T(8,128)(2,1)}, u32[]{:S(2)}, u32[]{:S(2)}) %collective-permute-start.8) | collective-permute-done | bytes 655392 | tf_op jit(solution)/shard_map/ppermute | solution.py:65
  264.5 25.3 %collective-permute-done.10 = bf16[128,2560]{1,0:T(8,128)(2,1)S(1)} collective-permute-done((bf16[128,2560]{1,0:T(8,128)(2,1)S(1)}, bf16[128,2560]{1,0:T(8,128)(2,1)S(1)}, u32[]{:S(2)}, u32[]{:S(2)}) %collective-permute-start.10) | collective-permute-done | bytes 655392 | tf_op jit(solution)/shard_map/ppermute | solution.py:65
  296.0 2.8 collective-permute-start.17
  300.4 2.4 collective-permute-done.11
  302.8 18.8 %collective-permute-done.13 = bf16[48,2560]{1,0:T(8,128)(2,1)S(1)} collective-permute-done((bf16[48,2560]{1,0:T(8,128)(2,1)S(1)}, bf16[48,2560]{1,0:T(8,128)(2,1)S(1)}, u32[]{:S(2)}, u32[]{:S(2)}) %collective-permute-start.13) | collective-permute-done | bytes 245792 | tf_op jit(solution)/shard_map/ppermute | solution.py:65
  323.1 3.2 collective-permute-done.17
  326.3 3.4 collective-permute-start.21
  330.9 22.6 %collective-permute-done.15 = bf16[2,48,2560]{2,1,0:T(8,128)(2,1)S(1)} collective-permute-done((bf16[2,48,2560]{2,1,0:T(8,128)(2,1)S(1)}, bf16[2,48,2560]{2,1,0:T(8,128)(2,1)S(1)}, u32[]{:S(2)}, u32[]{:S(2)}) %collective-permute-start.15) | collective-permute-done | bytes 491552 | tf_op jit(solution)/shard_map/ppermute | solution.py:65
  354.1 3.2 collective-permute-start.20
  359.4 11.4 %collective-permute-done.18 = bf16[2,2,32,2560]{3,2,1,0:T(8,128)(2,1)S(1)} collective-permute-done((bf16[2,2,32,2560]{3,2,1,0:T(8,128)(2,1)S(1)}, bf16[2,2,32,2560]{3,2,1,0:T(8,128)(2,1)S(1)}, u32[]{:S(2)}, u32[]{:S(2)}) %collective-permute-start.18) | collective-permute-done | bytes 655392 | tf_op jit(solution)/shard_map/ppermute | solution.py:65
  370.8 6.6 collective-permute-done.19
  379.8 2.8 copy.124
  382.7 12.9 %shard_map.256 = (bf16[1024,512]{1,0:T(8,128)(2,1)S(1)}, bf16[1024,512]{1,0:T(8,128)(2,1)S(1)}, bf16[1024,512]{1,0:T(8,128)(2,1)S(1)}, f32[2,512]{1,0:T(2,128)S(1)}) custom-call(s32[1]{0:T(128)} %bitcast.44.half_ref, bf16[1024,2560]{1,0:T(8,128)(2,1)} %bitcast.43.rows_ref.refs_4_, bf16[2048,2560]{1,0:T(8,128)(2,1)} %bitcast.355, ...), custom_call_target="tpu_custom_call" | custom-call | tf_op jit(solution)/shard_map/pallas_call | solution.py:332
  398.6 12.8 %shard_map.257 = (bf16[1024,512]{1,0:T(8,128)(2,1)S(1)}, bf16[1024,512]{1,0:T(8,128)(2,1)S(1)}, bf16[1024,512]{1,0:T(8,128)(2,1)S(1)}, f32[2,512]{1,0:T(2,128)S(1)}) custom-call(s32[1]{0:T(128)} %bitcast.46.half_ref, bf16[1024,2560]{1,0:T(8,128)(2,1)} %collective-permute-done.22.rows_ref.refs_5_, bf16[2048,2560]{1,0:T(8,128)(2,1)} %bitcast.356, ...), custom_call_target="tpu_custom_call" | custom-call | tf_op jit(solution)/shard_map/pallas_call | solution.py:332
  412.4 9.8 %shard_map.258 = bf16[1024,2560]{1,0:T(8,128)(2,1)} custom-call(bf16[1024,512]{1,0:T(8,128)(2,1)S(1)} %get-tuple-element.262.refs_0_.refs_7_, bf16[1024,512]{1,0:T(8,128)(2,1)S(1)} %get-tuple-element.264.refs_1_.refs_9_, bf16[2560,512]{1,0:T(8,128)(2,1)S(1)} %bitcast.353, bf16[2560,512]{1,0:T(8,128)(2,1)} %bitcast.361), custom_call_target="tpu_custom_call" | custom-call | tf_op jit(solution)/shard_map/pallas_call | solution.py:369
  422.7 4.8 collective-permute-start.23
  430.0 9.1 %shard_map.259 = bf16[1024,2560]{1,0:T(8,128)(2,1)} custom-call(bf16[1024,512]{1,0:T(8,128)(2,1)S(1)} %copy-done.14, bf16[1024,512]{1,0:T(8,128)(2,1)S(1)} %copy-done.17, bf16[2560,512]{1,0:T(8,128)(2,1)S(1)} %bitcast.354, bf16[2560,512]{1,0:T(8,128)(2,1)} %bitcast.362), custom_call_target="tpu_custom_call" | custom-call | tf_op jit(solution)/shard_map/pallas_call | solution.py:369
  439.1 5.4 add_convert_fusion.1
  455.2 21.4 %shard_map.260 = bf16[2560,1536]{1,0:T(8,128)(2,1)} custom-call(s32[1]{0:T(128)} %bitcast.44.half_ref, bf16[2048,2560]{1,0:T(8,128)(2,1)} %bitcast.357, bf16[2048,2560]{1,0:T(8,128)(2,1)} %bitcast.358, bf16[1024,512]{1,0:T(8,128)(2,1)S(1)} %copy-done.8, bf16[1024,512]{1,0:T(8,128)(2,1)S(1)} %copy-done.11, bf16[1024,2560]{1,0:T(8,128)(2,1)} %bitcast.43.rows_ref.refs_4_, ...), custom_call_target="tpu_custom_call" | custom-call | tf_op jit(solution)/shard_map/pallas_call | solution.py:522
  486.8 6.5 collective-permute-done.28
  501.2 2.6 collective-permute-done.35
  510.0 4.8 shard_map.261
  520.5 5.2 shard_map.262
  527.5 4.5 collective-permute-done.37
  533.3 5.4 add_convert_fusion
  541.1 14.0 %shard_map.263 = (bf16[256,1280]{1,0:T(8,128)(2,1)S(1)}, f32[1024,512]{1,0:T(8,128)}) custom-call(bf16[256,2560]{1,0:T(8,128)(2,1)S(1)} %pad_maximum_fusion.11.rows_ref.refs_0_, bf16[2560,1280]{1,0:T(8,128)(2,1)} %all-gather.7.cloned.1.call-done.refs_1_.weight_ref, bf16[256,1280]{1,0:T(8,128)(2,1)S(1)} %copy-done.25, f32[256,640]{1,0:T(8,128)S(1)} %copy-done.27, ...), custom_call_target="tpu_custom_call" | custom-call | tf_op jit(solution)/shard_map/pallas_call | solution.py:456
  560.9 5.0 shard_map.264
  567.3 3.4 constant_dynamic-slice_fusion.13
  573.4 5.0 shard_map.265
  578.5 10.6 %collective-permute-done.43 = bf16[256,512]{1,0:T(8,128)(2,1)S(1)} collective-permute-done((bf16[256,512]{1,0:T(8,128)(2,1)S(1)}, bf16[256,512]{1,0:T(8,128)(2,1)S(1)}, u32[]{:S(2)}, u32[]{:S(2)}) %collective-permute-start.43) | collective-permute-done | bytes 262176 | tf_op jit(solution)/shard_map/ppermute | solution.py:65
  597.7 4.3 collective-permute-done.48
  602.8 5.4 shard_map.266
  608.6 2.7 fusion.1
  615.9 8.6 %collective-permute-done.49 = bf16[128,2560]{1,0:T(8,128)(2,1)S(1)} collective-permute-done((bf16[128,2560]{1,0:T(8,128)(2,1)S(1)}, bf16[128,2560]{1,0:T(8,128)(2,1)S(1)}, u32[]{:S(2)}, u32[]{:S(2)}) %collective-permute-start.49) | collective-permute-done | bytes 655392 | tf_op jit(solution)/shard_map/ppermute | solution.py:65
  633.7 20.1 %collective-permute-done.51 = bf16[48,2560]{1,0:T(8,128)(2,1)} collective-permute-done((bf16[48,2560]{1,0:T(8,128)(2,1)S(1)}, bf16[48,2560]{1,0:T(8,128)(2,1)}, u32[]{:S(2)}, u32[]{:S(2)}) %collective-permute-start.51) | collective-permute-done | bytes 245792 | tf_op jit(solution)/shard_map/ppermute | solution.py:65
  653.8 3.5 constant_dynamic-slice_fusion.11
  671.7 22.7 %reduce-scatter.2.cloned.1.call-done = bf16[1280,1536]{1,0:T(8,128)(2,1)} async-done(((bf16[2560,1536]{1,0:T(8,128)(2,1)}), bf16[1280,1536]{1,0:T(8,128)(2,1)}) %reduce-scatter.2.cloned.1.call-update) | async-done | bytes 3932176 | tf_op jit(solution)/shard_map/reduce_scatter | solution.py:677
  694.4 2.4 fusion.92
  704.2 5.8 collective-permute-done.59
  710.0 9.1 %collective-permute-done.58 = bf16[2,2,1,160,384]{4,3,0,1,2:T(8,128)(2,1)S(1)} collective-permute-done((bf16[2,2,1,160,384]{4,3,0,1,2:T(8,128)(2,1)S(1)}, bf16[2,2,1,160,384]{4,3,0,1,2:T(8,128)(2,1)S(1)}, u32[]{:S(2)}, u32[]{:S(2)}) %collective-permute-start.58) | collective-permute-done | bytes 491552 | tf_op jit(solution)/shard_map/ppermute | solution.py:65
  728.7 33.0 %collective-permute-done.68 = bf16[1,160,1280]{2,1,0:T(8,128)(2,1)S(1)} collective-permute-done((bf16[1,160,1280]{2,1,0:T(8,128)(2,1)S(1)}, bf16[1,160,1280]{2,1,0:T(8,128)(2,1)S(1)}, u32[]{:S(2)}, u32[]{:S(2)}) %collective-permute-start.68) | collective-permute-done | bytes 409632 | tf_op jit(solution)/shard_map/ppermute | solution.py:65
  761.6 2.2 collective-permute-start.64
  764.8 3.2 collective-permute-done.64
  768.1 4.1 collective-permute-start.70
  776.7 33.1 %collective-permute-done.73 = bf16[160,2048]{1,0:T(8,128)(2,1)S(1)} collective-permute-done((bf16[160,2048]{1,0:T(8,128)(2,1)S(1)}, bf16[160,2048]{1,0:T(8,128)(2,1)S(1)}, u32[]{:S(2)}, u32[]{:S(2)}) %collective-permute-start.73) | collective-permute-done | bytes 655392 | tf_op jit(solution)/shard_map/ppermute | solution.py:65
  816.6 2.2 copy.136
  820.7 2.9 slice_convert_fusion
  (527 shorter events, 188.6 us)
Async XLA Ops:
  7.2 116.2 %all-gather.5.cloned.1.call-start = ((), (), s32[]{:S(2)}) async-start(), calls=%async_computation.4 | async-start | bytes 9052160 | tf_op jit(solution)/shard_map/all_gather | solution.py:602
  12.0 231.3 %all-gather.7.cloned.1.call-start = ((), (), s32[]{:S(2)}) async-start(), calls=%async_computation.5 | async-start | bytes 6963200 | tf_op jit(solution)/shard_map/all_gather | solution.py:608
  14.1 36.8 %all-to-all-start = ((bf16[160,8,512]{2,0,1:T(8,128)(2,1)}), bf16[160,8,512]{2,0,1:T(8,128)(2,1)S(1)}, u32[]{:S(2)}, u32[]{:S(2)}) async-start(bf16[160,8,512]{2,0,1:T(8,128)(2,1)} %bitcast.344), calls=%async_computation | async-start | bytes 2621440 | tf_op jit(solution)/shard_map/all_to_all | solution.py:586
  50.9 41.3 %all-to-all-start.1 = ((bf16[160,8,512]{2,0,1:T(8,128)(2,1)}), bf16[160,8,512]{2,0,1:T(8,128)(2,1)S(1)}, u32[]{:S(2)}, u32[]{:S(2)}) async-start(bf16[160,8,512]{2,0,1:T(8,128)(2,1)} %bitcast.382), calls=%async_computation.1 | async-start | bytes 2621440 | tf_op jit(solution)/shard_map/all_to_all | solution.py:586
  93.3 30.1 %all-to-all-start.2 = ((bf16[160,8,512]{2,0,1:T(8,128)(2,1)}), bf16[160,8,512]{2,0,1:T(8,128)(2,1)S(1)}, u32[]{:S(2)}, u32[]{:S(2)}) async-start(bf16[160,8,512]{2,0,1:T(8,128)(2,1)} %bitcast.381), calls=%async_computation.2 | async-start | bytes 2621440 | tf_op jit(solution)/shard_map/all_to_all | solution.py:586
  96.9 285.9 %all-gather.9.cloned.1.call-start = ((), (), s32[]{:S(2)}) async-start(), calls=%async_computation.7 | async-start | bytes 11141120 | tf_op jit(solution)/shard_map/all_gather | solution.py:638
  96.9 17.2 %collective-permute-start = (bf16[128,2560]{1,0:T(8,128)(2,1)S(1)}, bf16[128,2560]{1,0:T(8,128)(2,1)}, u32[]{:S(2)}, u32[]{:S(2)}) collective-permute-start(bf16[128,2560]{1,0:T(8,128)(2,1)S(1)} %bitcast.369), channel_id=1, source_target_pairs={{0,1},{1,0},{2,3},{3,2},{4,5},{5,4},{6,7},{7,6},{8,9},{9,8},{10,11... | collective-permute-start | bytes 1966088 | tf_op jit(solution)/shard_map/ppermute | solution.py:65
  98.5 9.3 %collective-permute-start.2 = (s32[256]{0:T(256)S(1)}, s32[256]{0:T(256)S(1)}, u32[]{:S(2)}, u32[]{:S(2)}) collective-permute-start(s32[256]{0:T(256)S(1)} %bitcast.407), channel_id=1, source_target_pairs={{0,4},{4,0},{1,5},{5,1},{2,6},{6,2},{3,7},{7,3},{8,12},{12,8},{9,1... | collective-permute-start | bytes 3080 | tf_op jit(solution)/shard_map/ppermute | solution.py:65
  100.7 593.7 %reduce-scatter.2.cloned.1.call-start = ((), (), s32[]{:S(2)}) async-start(), calls=%async_computation.6 | async-start | bytes 11796480 | tf_op jit(solution)/shard_map/reduce_scatter | solution.py:677
  135.1 46.2 %collective-permute-start.1 = (bf16[640,512]{1,0:T(8,128)(2,1)S(1)}, bf16[640,512]{1,0:T(8,128)(2,1)S(1)}, u32[]{:S(2)}, u32[]{:S(2)}) collective-permute-start(bf16[640,512]{1,0:T(8,128)(2,1)S(1)} %slice.141), channel_id=1, source_target_pairs={{0,16},{16,0},{1,17},{17,1},{2,18},{18,2},{3,19},{19,3},{4,20},{20... | collective-permute-start | bytes 1966088 | tf_op jit(solution)/shard_map/ppermute | solution.py:65
  181.4 47.7 %collective-permute-start.6 = (bf16[640,512]{1,0:T(8,128)(2,1)S(1)}, bf16[640,512]{1,0:T(8,128)(2,1)S(1)}, u32[]{:S(2)}, u32[]{:S(2)}) collective-permute-start(bf16[640,512]{1,0:T(8,128)(2,1)S(1)} %get-tuple-element.201), channel_id=1, source_target_pairs={{0,16},{16,0},{1,17},{17,1},{2,18},{18,2},{3,19},{19,3},{4,20},{20... | collective-permute-start | bytes 1966088 | tf_op jit(solution)/shard_map/ppermute | solution.py:65
  229.2 30.5 %collective-permute-start.8 = (bf16[640,512]{1,0:T(8,128)(2,1)}, bf16[640,512]{1,0:T(8,128)(2,1)}, u32[]{:S(2)}, u32[]{:S(2)}) collective-permute-start(bf16[640,512]{1,0:T(8,128)(2,1)} %get-tuple-element.204), channel_id=1, source_target_pairs={{0,16},{16,0},{1,17},{17,1},{2,18},{18,2},{3,19},{19,3},{4,20},{20... | collective-permute-start | bytes 1966088 | tf_op jit(solution)/shard_map/ppermute | solution.py:65
  259.8 30.1 %collective-permute-start.10 = (bf16[128,2560]{1,0:T(8,128)(2,1)S(1)}, bf16[128,2560]{1,0:T(8,128)(2,1)S(1)}, u32[]{:S(2)}, u32[]{:S(2)}) collective-permute-start(bf16[128,2560]{1,0:T(8,128)(2,1)S(1)} %dynamic-slice_convert_fusion.1), channel_id=1, source_target_pairs={{0,1},{1,0},{2,3},{3,2},{4,5},{5,4},{6,7},{7,6},{8,9},{9,8},{10,11... | collective-permute-start | bytes 1966088 | tf_op jit(solution)/shard_map/ppermute | solution.py:65
  261.4 31.1 %collective-permute-start.9 = (bf16[640,512]{1,0:T(8,128)(2,1)S(1)}, bf16[640,512]{1,0:T(8,128)(2,1)S(1)}, u32[]{:S(2)}, u32[]{:S(2)}) collective-permute-start(bf16[640,512]{1,0:T(8,128)(2,1)S(1)} %copy-done.52), channel_id=1, source_target_pairs={{0,16},{16,0},{1,17},{17,1},{2,18},{18,2},{3,19},{19,3},{4,20},{20... | collective-permute-start | bytes 1966088 | tf_op jit(solution)/shard_map/ppermute | solution.py:65
  292.9 9.8 %collective-permute-start.11 = (bf16[32,2560]{1,0:T(8,128)(2,1)S(1)}, bf16[32,2560]{1,0:T(8,128)(2,1)S(1)}, u32[]{:S(2)}, u32[]{:S(2)}) collective-permute-start(bf16[32,2560]{1,0:T(8,128)(2,1)S(1)} %slice.188), channel_id=1, source_target_pairs={{0,1},{1,0},{2,3},{3,2},{4,5},{5,4},{6,7},{7,6},{8,9},{9,8},{10,11... | collective-permute-start | bytes 491528 | tf_op jit(solution)/shard_map/ppermute | solution.py:65
  295.9 25.6 %collective-permute-start.13 = (bf16[48,2560]{1,0:T(8,128)(2,1)S(1)}, bf16[48,2560]{1,0:T(8,128)(2,1)S(1)}, u32[]{:S(2)}, u32[]{:S(2)}) collective-permute-start(bf16[48,2560]{1,0:T(8,128)(2,1)S(1)} %get-tuple-element.471), channel_id=1, source_target_pairs={{0,8},{8,0},{1,9},{9,1},{2,10},{10,2},{3,11},{11,3},{4,12},{12,4},... | collective-permute-start | bytes 737288 | tf_op jit(solution)/shard_map/ppermute | solution.py:65
  296.0 30.3 %collective-permute-start.17 = (bf16[640,512]{1,0:T(8,128)(2,1)S(1)}, bf16[640,512]{1,0:T(8,128)(2,1)S(1)}, u32[]{:S(2)}, u32[]{:S(2)}) collective-permute-start(bf16[640,512]{1,0:T(8,128)(2,1)S(1)} %copy-done.51), channel_id=1, source_target_pairs={{0,16},{16,0},{1,17},{17,1},{2,18},{18,2},{3,19},{19,3},{4,20},{20... | collective-permute-start | bytes 1966088 | tf_op jit(solution)/shard_map/ppermute | solution.py:65
  321.7 31.8 %collective-permute-start.15 = (bf16[2,48,2560]{2,1,0:T(8,128)(2,1)S(1)}, bf16[2,48,2560]{2,1,0:T(8,128)(2,1)S(1)}, u32[]{:S(2)}, u32[]{:S(2)}) collective-permute-start(bf16[2,48,2560]{2,1,0:T(8,128)(2,1)S(1)} %pad_maximum_fusion.20), channel_id=1, source_target_pairs={{0,8},{8,0},{1,9},{9,1},{2,10},{10,2},{3,11},{11,3},{4,12},{12,4},... | collective-permute-start | bytes 1474568 | tf_op jit(solution)/shard_map/ppermute | solution.py:65
  321.8 31.7 %collective-permute-start.16 = (bf16[2,48,2560]{2,1,0:T(8,128)(2,1)S(1)}, bf16[2,48,2560]{2,1,0:T(8,128)(2,1)S(1)}, u32[]{:S(2)}, u32[]{:S(2)}) collective-permute-start(bf16[2,48,2560]{2,1,0:T(8,128)(2,1)S(1)} %pad_maximum_fusion.21), channel_id=1, source_target_pairs={{0,1},{1,0},{2,3},{3,2},{4,5},{5,4},{6,7},{7,6},{8,9},{9,8},{10,11... | collective-permute-start | bytes 1474568 | tf_op jit(solution)/shard_map/ppermute | solution.py:65
  322.0 8.9 %collective-permute-start.14 = (bf16[2,32,2560]{2,1,0:T(8,128)(2,1)S(1)}, bf16[2,32,2560]{2,1,0:T(8,128)(2,1)S(1)}, u32[]{:S(2)}, u32[]{:S(2)}) collective-permute-start(bf16[2,32,2560]{2,1,0:T(8,128)(2,1)S(1)} %pad_maximum_fusion.22), channel_id=1, source_target_pairs={{0,4},{4,0},{1,5},{5,1},{2,6},{6,2},{3,7},{7,3},{8,12},{12,8},{9,1... | collective-permute-start | bytes 983048 | tf_op jit(solution)/shard_map/ppermute | solution.py:65
  326.3 31.1 %collective-permute-start.21 = (bf16[640,512]{1,0:T(8,128)(2,1)S(1)}, bf16[640,512]{1,0:T(8,128)(2,1)S(1)}, u32[]{:S(2)}, u32[]{:S(2)}) collective-permute-start(bf16[640,512]{1,0:T(8,128)(2,1)S(1)} %copy-done.50), channel_id=1, source_target_pairs={{0,16},{16,0},{1,17},{17,1},{2,18},{18,2},{3,19},{19,3},{4,20},{20... | collective-permute-start | bytes 1966088 | tf_op jit(solution)/shard_map/ppermute | solution.py:65
  353.6 17.2 %collective-permute-start.18 = (bf16[2,2,32,2560]{3,2,1,0:T(8,128)(2,1)S(1)}, bf16[2,2,32,2560]{3,2,1,0:T(8,128)(2,1)S(1)}, u32[]{:S(2)}, u32[]{:S(2)}) collective-permute-start(bf16[2,2,32,2560]{3,2,1,0:T(8,128)(2,1)S(1)} %pad_maximum_fusion.18), channel_id=1, source_target_pairs={{0,8},{8,0},{1,9},{9,1},{2,10},{10,2},{3,11},{11,3},{4,12},{12,4},... | collective-permute-start | bytes 1966088 | tf_op jit(solution)/shard_map/ppermute | solution.py:65
  353.9 23.6 %collective-permute-start.19 = (bf16[2,2,48,2560]{3,2,0,1:T(8,128)(2,1)S(1)}, bf16[2,2,48,2560]{3,2,0,1:T(8,128)(2,1)S(1)}, u32[]{:S(2)}, u32[]{:S(2)}) collective-permute-start(bf16[2,2,48,2560]{3,2,0,1:T(8,128)(2,1)S(1)} %pad_maximum_fusion.16), channel_id=1, source_target_pairs={{0,1},{1,0},{2,3},{3,2},{4,5},{5,4},{6,7},{7,6},{8,9},{9,8},{10,11... | collective-permute-start | bytes 2949128 | tf_op jit(solution)/shard_map/ppermute | solution.py:65
  354.1 24.5 %collective-permute-start.20 = (bf16[2,2,48,2560]{3,2,0,1:T(8,128)(2,1)S(1)}, bf16[2,2,48,2560]{3,2,0,1:T(8,128)(2,1)S(1)}, u32[]{:S(2)}, u32[]{:S(2)}) collective-permute-start(bf16[2,2,48,2560]{3,2,0,1:T(8,128)(2,1)S(1)} %pad_maximum_fusion.17), channel_id=1, source_target_pairs={{0,4},{4,0},{1,5},{5,1},{2,6},{6,2},{3,7},{7,3},{8,12},{12,8},{9,1... | collective-permute-start | bytes 2949128 | tf_op jit(solution)/shard_map/ppermute | solution.py:65
  382.6 16.0 %collective-permute-start.22 = (bf16[1024,2560]{1,0:T(8,128)(2,1)}, bf16[1024,2560]{1,0:T(8,128)(2,1)}, u32[]{:S(2)}, u32[]{:S(2)}) collective-permute-start(bf16[1024,2560]{1,0:T(8,128)(2,1)} %bitcast.43.rows_ref.refs_4_), channel_id=1, source_target_pairs={{0,2},{2,0},{1,3},{3,1},{4,6},{6,4},{5,7},{7,5},{8,10},{10,8},{9,1... | collective-permute-start | bytes 15728648 | tf_op jit(solution)/shard_map/ppermute | solution.py:65
  422.2 16.9 %collective-permute-start.24 = (bf16[1024,2560]{1,0:T(8,128)(2,1)}, bf16[1024,2560]{1,0:T(8,128)(2,1)}, u32[]{:S(2)}, u32[]{:S(2)}) collective-permute-start(bf16[1024,2560]{1,0:T(8,128)(2,1)} %shard_map.258), channel_id=1, source_target_pairs={{0,2},{2,0},{1,3},{3,1},{4,6},{6,4},{5,7},{7,5},{8,10},{10,8},{9,1... | collective-permute-start | bytes 15728648 | tf_op jit(solution)/shard_map/ppermute | solution.py:65
  422.7 16.4 %collective-permute-start.23 = (f32[2,512]{1,0:T(2,128)S(1)}, f32[2,512]{1,0:T(2,128)S(1)}, u32[]{:S(2)}, u32[]{:S(2)}) collective-permute-start(f32[2,512]{1,0:T(2,128)S(1)} %add.477), channel_id=1, source_target_pairs={{0,16},{16,0},{1,17},{17,1},{2,18},{18,2},{3,19},{19,3},{4,20},{20... | collective-permute-start | bytes 12296 | tf_op jit(solution)/shard_map/ppermute | solution.py:65
  446.2 30.4 %collective-permute-start.26 = (bf16[2,2,48,2560]{3,2,1,0:T(8,128)(2,1)}, bf16[2,2,48,2560]{3,2,1,0:T(8,128)(2,1)}, u32[]{:S(2)}, u32[]{:S(2)}) collective-permute-start(bf16[2,2,48,2560]{3,2,1,0:T(8,128)(2,1)} %dynamic-slice_bitcast_fusion.1), channel_id=1, source_target_pairs={{0,1},{1,0},{2,3},{3,2},{4,5},{5,4},{6,7},{7,6},{8,9},{9,8},{10,11... | collective-permute-start | bytes 2949128 | tf_op jit(solution)/shard_map/ppermute | solution.py:65
  450.2 26.4 %collective-permute-start.27 = (bf16[2,2,48,2560]{3,2,0,1:T(8,128)(2,1)}, bf16[2,2,48,2560]{3,2,0,1:T(8,128)(2,1)}, u32[]{:S(2)}, u32[]{:S(2)}) collective-permute-start(bf16[2,2,48,2560]{3,2,0,1:T(8,128)(2,1)} %bitcast.346), channel_id=1, source_target_pairs={{0,4},{4,0},{1,5},{5,1},{2,6},{6,2},{3,7},{7,3},{8,12},{12,8},{9,1... | collective-permute-start | bytes 2949128 | tf_op jit(solution)/shard_map/ppermute | solution.py:65
  452.4 24.2 %collective-permute-start.25 = (bf16[2,2,32,2560]{3,2,1,0:T(8,128)(2,1)}, bf16[2,2,32,2560]{3,2,1,0:T(8,128)(2,1)}, u32[]{:S(2)}, u32[]{:S(2)}) collective-permute-start(bf16[2,2,32,2560]{3,2,1,0:T(8,128)(2,1)} %dynamic-slice_bitcast_fusion.6), channel_id=1, source_target_pairs={{0,8},{8,0},{1,9},{9,1},{2,10},{10,2},{3,11},{11,3},{4,12},{12,4},... | collective-permute-start | bytes 1966088 | tf_op jit(solution)/shard_map/ppermute | solution.py:65
  478.5 14.9 %collective-permute-start.29 = (bf16[2,48,2560]{2,1,0:T(8,128)(2,1)S(1)}, bf16[2,48,2560]{2,1,0:T(8,128)(2,1)}, u32[]{:S(2)}, u32[]{:S(2)}) collective-permute-start(bf16[2,48,2560]{2,1,0:T(8,128)(2,1)S(1)} %dynamic-slice_bitcast_fusion.10), channel_id=1, source_target_pairs={{0,8},{8,0},{1,9},{9,1},{2,10},{10,2},{3,11},{11,3},{4,12},{12,4},... | collective-permute-start | bytes 1474568 | tf_op jit(solution)/shard_map/ppermute | solution.py:65
  482.7 12.2 %collective-permute-start.30 = (bf16[2,48,2560]{2,1,0:T(8,128)(2,1)}, bf16[2,48,2560]{2,1,0:T(8,128)(2,1)}, u32[]{:S(2)}, u32[]{:S(2)}) collective-permute-start(bf16[2,48,2560]{2,1,0:T(8,128)(2,1)} %dynamic-slice_bitcast_fusion.9), channel_id=1, source_target_pairs={{0,1},{1,0},{2,3},{3,2},{4,5},{5,4},{6,7},{7,6},{8,9},{9,8},{10,11... | collective-permute-start | bytes 1474568 | tf_op jit(solution)/shard_map/ppermute | solution.py:65
  514.7 18.5 %collective-permute-start.36 = (bf16[1024,2560]{1,0:T(8,128)(2,1)}, bf16[1024,2560]{1,0:T(8,128)(2,1)}, u32[]{:S(2)}, u32[]{:S(2)}) collective-permute-start(bf16[1024,2560]{1,0:T(8,128)(2,1)} %shard_map.261), channel_id=1, source_target_pairs={{0,2},{2,0},{1,3},{3,1},{4,6},{6,4},{5,7},{7,5},{8,10},{10,8},{9,1... | collective-permute-start | bytes 15728648 | tf_op jit(solution)/shard_map/ppermute | solution.py:65
  514.7 17.3 %collective-permute-start.37 = (bf16[128,2560]{1,0:T(8,128)(2,1)S(1)}, bf16[128,2560]{1,0:T(8,128)(2,1)}, u32[]{:S(2)}, u32[]{:S(2)}) collective-permute-start(bf16[128,2560]{1,0:T(8,128)(2,1)S(1)} %convert_element_type.496), channel_id=1, source_target_pairs={{0,1},{1,0},{2,3},{3,2},{4,5},{5,4},{6,7},{7,6},{8,9},{9,8},{10,11... | collective-permute-start | bytes 1966088 | tf_op jit(solution)/shard_map/ppermute | solution.py:65
  519.0 21.4 %collective-permute-start.41 = (f32[2,2048]{1,0:T(2,128)S(1)}, f32[2,2048]{1,0:T(2,128)S(1)}, u32[]{:S(2)}, u32[]{:S(2)}) collective-permute-start(f32[2,2048]{1,0:T(2,128)S(1)} %pad_maximum_fusion.27), channel_id=1, source_target_pairs={{0,8},{8,0},{1,9},{9,1},{2,10},{10,2},{3,11},{11,3},{4,12},{12,4},... | collective-permute-start | bytes 49160 | tf_op jit(solution)/shard_map/ppermute | solution.py:65
  540.1 38.4 %collective-permute-start.38 = (bf16[2,2,32,2560]{3,2,1,0:T(8,128)(2,1)}, bf16[2,2,32,2560]{3,2,1,0:T(8,128)(2,1)S(1)}, u32[]{:S(2)}, u32[]{:S(2)}) collective-permute-start(bf16[2,2,32,2560]{3,2,1,0:T(8,128)(2,1)} %dynamic-slice_bitcast_fusion.5), channel_id=1, source_target_pairs={{0,8},{8,0},{1,9},{9,1},{2,10},{10,2},{3,11},{11,3},{4,12},{12,4},... | collective-permute-start | bytes 1966088 | tf_op jit(solution)/shard_map/ppermute | solution.py:65
  556.4 9.5 %collective-permute-start.42 = (bf16[512,512]{1,0:T(8,128)(2,1)S(1)}, bf16[512,512]{1,0:T(8,128)(2,1)S(1)}, u32[]{:S(2)}, u32[]{:S(2)}) collective-permute-start(bf16[512,512]{1,0:T(8,128)(2,1)S(1)} %slice.244), channel_id=1, source_target_pairs={{0,2},{2,0},{1,3},{3,1},{4,6},{6,4},{5,7},{7,5},{8,10},{10,8},{9,1... | collective-permute-start | bytes 1572872 | tf_op jit(solution)/shard_map/ppermute | solution.py:65
  557.5 31.5 %collective-permute-start.39 = (bf16[2,2,48,2560]{3,2,1,0:T(8,128)(2,1)}, bf16[2,2,48,2560]{3,2,1,0:T(8,128)(2,1)S(1)}, u32[]{:S(2)}, u32[]{:S(2)}) collective-permute-start(bf16[2,2,48,2560]{3,2,1,0:T(8,128)(2,1)} %dynamic-slice_bitcast_fusion), channel_id=1, source_target_pairs={{0,1},{1,0},{2,3},{3,2},{4,5},{5,4},{6,7},{7,6},{8,9},{9,8},{10,11... | collective-permute-start | bytes 2949128 | tf_op jit(solution)/shard_map/ppermute | solution.py:65
  559.5 29.6 %collective-permute-start.40 = (bf16[2,2,48,2560]{3,2,0,1:T(8,128)(2,1)S(1)}, bf16[2,2,48,2560]{3,2,0,1:T(8,128)(2,1)}, u32[]{:S(2)}, u32[]{:S(2)}) collective-permute-start(bf16[2,2,48,2560]{3,2,0,1:T(8,128)(2,1)S(1)} %bitcast.399), channel_id=1, source_target_pairs={{0,4},{4,0},{1,5},{5,1},{2,6},{6,2},{3,7},{7,3},{8,12},{12,8},{9,1... | collective-permute-start | bytes 2949128 | tf_op jit(solution)/shard_map/ppermute | solution.py:65
  566.1 22.9 %collective-permute-start.43 = (bf16[256,512]{1,0:T(8,128)(2,1)S(1)}, bf16[256,512]{1,0:T(8,128)(2,1)S(1)}, u32[]{:S(2)}, u32[]{:S(2)}) collective-permute-start(bf16[256,512]{1,0:T(8,128)(2,1)S(1)} %slice.245), channel_id=1, source_target_pairs={{0,4},{4,0},{1,5},{5,1},{2,6},{6,2},{3,7},{7,3},{8,12},{12,8},{9,1... | collective-permute-start | bytes 786440 | tf_op jit(solution)/shard_map/ppermute | solution.py:65
  572.7 22.7 %collective-permute-start.47 = (bf16[2,2,2,1,160,1280]{5,4,0,1,2,3:T(8,128)(2,1)}, bf16[2,2,2,1,160,1280]{5,4,0,1,2,3:T(8,128)(2,1)}, u32[]{:S(2)}, u32[]{:S(2)}) collective-permute-start(bf16[2,2,2,1,160,1280]{5,4,0,1,2,3:T(8,128)(2,1)} %copy.150), channel_id=1, source_target_pairs={{0,2},{2,0},{1,3},{3,1},{4,6},{6,4},{5,7},{7,5},{8,10},{10,8},{9,1... | collective-permute-start | bytes 9830408 | tf_op jit(solution)/shard_map/ppermute | solution.py:65
  590.0 25.9 %collective-permute-start.44 = (bf16[2,32,2560]{2,1,0:T(8,128)(2,1)S(1)}, bf16[2,32,2560]{2,1,0:T(8,128)(2,1)S(1)}, u32[]{:S(2)}, u32[]{:S(2)}) collective-permute-start(bf16[2,32,2560]{2,1,0:T(8,128)(2,1)S(1)} %dynamic-slice_bitcast_fusion.11), channel_id=1, source_target_pairs={{0,4},{4,0},{1,5},{5,1},{2,6},{6,2},{3,7},{7,3},{8,12},{12,8},{9,1... | collective-permute-start | bytes 983048 | tf_op jit(solution)/shard_map/ppermute | solution.py:65
  592.8 23.1 %collective-permute-start.45 = (bf16[2,48,2560]{2,1,0:T(8,128)(2,1)S(1)}, bf16[2,48,2560]{2,1,0:T(8,128)(2,1)S(1)}, u32[]{:S(2)}, u32[]{:S(2)}) collective-permute-start(bf16[2,48,2560]{2,1,0:T(8,128)(2,1)S(1)} %dynamic-slice_bitcast_fusion.8), channel_id=1, source_target_pairs={{0,8},{8,0},{1,9},{9,1},{2,10},{10,2},{3,11},{11,3},{4,12},{12,4},... | collective-permute-start | bytes 1474568 | tf_op jit(solution)/shard_map/ppermute | solution.py:65
  595.9 20.0 %collective-permute-start.46 = (bf16[2,48,2560]{2,1,0:T(8,128)(2,1)S(1)}, bf16[2,48,2560]{2,1,0:T(8,128)(2,1)S(1)}, u32[]{:S(2)}, u32[]{:S(2)}) collective-permute-start(bf16[2,48,2560]{2,1,0:T(8,128)(2,1)S(1)} %dynamic-slice_bitcast_fusion.7), channel_id=1, source_target_pairs={{0,1},{1,0},{2,3},{3,2},{4,5},{5,4},{6,7},{7,6},{8,9},{9,8},{10,11... | collective-permute-start | bytes 1474568 | tf_op jit(solution)/shard_map/ppermute | solution.py:65
  608.3 16.2 %collective-permute-start.49 = (bf16[128,2560]{1,0:T(8,128)(2,1)S(1)}, bf16[128,2560]{1,0:T(8,128)(2,1)S(1)}, u32[]{:S(2)}, u32[]{:S(2)}) collective-permute-start(bf16[128,2560]{1,0:T(8,128)(2,1)S(1)} %dynamic-slice_convert_fusion), channel_id=1, source_target_pairs={{0,1},{1,0},{2,3},{3,2},{4,5},{5,4},{6,7},{7,6},{8,9},{9,8},{10,11... | collective-permute-start | bytes 1966088 | tf_op jit(solution)/shard_map/ppermute | solution.py:65
  613.5 40.3 %collective-permute-start.53 = (bf16[2,2,1,160,1280]{4,3,0,1,2:T(8,128)(2,1)}, bf16[2,2,1,160,1280]{4,3,0,1,2:T(8,128)(2,1)}, u32[]{:S(2)}, u32[]{:S(2)}) collective-permute-start(bf16[2,2,1,160,1280]{4,3,0,1,2:T(8,128)(2,1)} %constant_dynamic-slice_fusion.12), channel_id=1, source_target_pairs={{0,4},{4,0},{1,5},{5,1},{2,6},{6,2},{3,7},{7,3},{8,12},{12,8},{9,1... | collective-permute-start | bytes 4915208 | tf_op jit(solution)/shard_map/ppermute | solution.py:65
  625.3 8.4 %collective-permute-start.50 = (bf16[32,2560]{1,0:T(8,128)(2,1)}, bf16[32,2560]{1,0:T(8,128)(2,1)}, u32[]{:S(2)}, u32[]{:S(2)}) collective-permute-start(bf16[32,2560]{1,0:T(8,128)(2,1)} %dynamic-slice_bitcast_fusion.17), channel_id=1, source_target_pairs={{0,1},{1,0},{2,3},{3,2},{4,5},{5,4},{6,7},{7,6},{8,9},{9,8},{10,11... | collective-permute-start | bytes 491528 | tf_op jit(solution)/shard_map/ppermute | solution.py:65
  625.9 27.9 %collective-permute-start.51 = (bf16[48,2560]{1,0:T(8,128)(2,1)S(1)}, bf16[48,2560]{1,0:T(8,128)(2,1)}, u32[]{:S(2)}, u32[]{:S(2)}) collective-permute-start(bf16[48,2560]{1,0:T(8,128)(2,1)S(1)} %dynamic-slice_bitcast_fusion.14), channel_id=1, source_target_pairs={{0,4},{4,0},{1,5},{5,1},{2,6},{6,2},{3,7},{7,3},{8,12},{12,8},{9,1... | collective-permute-start | bytes 737288 | tf_op jit(solution)/shard_map/ppermute | solution.py:65
  627.5 26.3 %collective-permute-start.52 = (bf16[48,2560]{1,0:T(8,128)(2,1)}, bf16[48,2560]{1,0:T(8,128)(2,1)}, u32[]{:S(2)}, u32[]{:S(2)}) collective-permute-start(bf16[48,2560]{1,0:T(8,128)(2,1)} %dynamic-slice_bitcast_fusion.13), channel_id=1, source_target_pairs={{0,8},{8,0},{1,9},{9,1},{2,10},{10,2},{3,11},{11,3},{4,12},{12,4},... | collective-permute-start | bytes 737288 | tf_op jit(solution)/shard_map/ppermute | solution.py:65
  657.5 11.4 %collective-permute-start.54 = (bf16[2,2,2,1,160,1280]{5,4,0,1,2,3:T(8,128)(2,1)S(1)}, bf16[2,2,2,1,160,1280]{5,4,0,1,2,3:T(8,128)(2,1)S(1)}, u32[]{:S(2)}, u32[]{:S(2)}) collective-permute-start(bf16[2,2,2,1,160,1280]{5,4,0,1,2,3:T(8,128)(2,1)S(1)} %copy.153), channel_id=1, source_target_pairs={{0,2},{2,0},{1,3},{3,1},{4,6},{6,4},{5,7},{7,5},{8,10},{10,8},{9,1... | collective-permute-start | bytes 9830408 | tf_op jit(solution)/shard_map/ppermute | solution.py:65
  659.2 12.5 %collective-permute-start.57 = (bf16[2,2,2,1,160,384]{5,4,0,1,2,3:T(8,128)(2,1)S(1)}, bf16[2,2,2,1,160,384]{5,4,0,1,2,3:T(8,128)(2,1)}, u32[]{:S(2)}, u32[]{:S(2)}) collective-permute-start(bf16[2,2,2,1,160,384]{5,4,0,1,2,3:T(8,128)(2,1)S(1)} %copy.155), channel_id=1, source_target_pairs={{0,2},{2,0},{1,3},{3,1},{4,6},{6,4},{5,7},{7,5},{8,10},{10,8},{9,1... | collective-permute-start | bytes 2949128 | tf_op jit(solution)/shard_map/ppermute | solution.py:65
  668.3 41.8 %collective-permute-start.59 = (bf16[2,1,160,1280]{3,2,0,1:T(8,128)(2,1)}, bf16[2,1,160,1280]{3,2,0,1:T(8,128)(2,1)}, u32[]{:S(2)}, u32[]{:S(2)}) collective-permute-start(bf16[2,1,160,1280]{3,2,0,1:T(8,128)(2,1)} %constant_dynamic-slice_fusion.5), channel_id=1, source_target_pairs={{0,8},{8,0},{1,9},{9,1},{2,10},{10,2},{3,11},{11,3},{4,12},{12,4},... | collective-permute-start | bytes 2457608 | tf_op jit(solution)/shard_map/ppermute | solution.py:65
  671.1 48.0 %collective-permute-start.55 = (bf16[2,2,1,160,1280]{4,3,0,1,2:T(8,128)(2,1)}, bf16[2,2,1,160,1280]{4,3,0,1,2:T(8,128)(2,1)}, u32[]{:S(2)}, u32[]{:S(2)}) collective-permute-start(bf16[2,2,1,160,1280]{4,3,0,1,2:T(8,128)(2,1)} %constant_dynamic-slice_fusion.9), channel_id=1, source_target_pairs={{0,4},{4,0},{1,5},{5,1},{2,6},{6,2},{3,7},{7,3},{8,12},{12,8},{9,1... | collective-permute-start | bytes 4915208 | tf_op jit(solution)/shard_map/ppermute | solution.py:65
  699.5 19.6 %collective-permute-start.58 = (bf16[2,2,1,160,384]{4,3,0,1,2:T(8,128)(2,1)S(1)}, bf16[2,2,1,160,384]{4,3,0,1,2:T(8,128)(2,1)S(1)}, u32[]{:S(2)}, u32[]{:S(2)}) collective-permute-start(bf16[2,2,1,160,384]{4,3,0,1,2:T(8,128)(2,1)S(1)} %constant_dynamic-slice_fusion.6), channel_id=1, source_target_pairs={{0,4},{4,0},{1,5},{5,1},{2,6},{6,2},{3,7},{7,3},{8,12},{12,8},{9,1... | collective-permute-start | bytes 1474568 | tf_op jit(solution)/shard_map/ppermute | solution.py:65
  721.0 55.3 %collective-permute-start.63 = (bf16[2,1,160,1280]{3,2,0,1:T(8,128)(2,1)S(1)}, bf16[2,1,160,1280]{3,2,0,1:T(8,128)(2,1)S(1)}, u32[]{:S(2)}, u32[]{:S(2)}) collective-permute-start(bf16[2,1,160,1280]{3,2,0,1:T(8,128)(2,1)S(1)} %constant_dynamic-slice_fusion.4), channel_id=1, source_target_pairs={{0,8},{8,0},{1,9},{9,1},{2,10},{10,2},{3,11},{11,3},{4,12},{12,4},... | collective-permute-start | bytes 2457608 | tf_op jit(solution)/shard_map/ppermute | solution.py:65
  722.7 42.2 %collective-permute-start.65 = (bf16[2,160,1024]{2,1,0:T(8,128)(2,1)S(1)}, bf16[2,160,1024]{2,1,0:T(8,128)(2,1)S(1)}, u32[]{:S(2)}, u32[]{:S(2)}) collective-permute-start(bf16[2,160,1024]{2,1,0:T(8,128)(2,1)S(1)} %fusion.62), channel_id=1, source_target_pairs={{0,8},{8,0},{1,9},{9,1},{2,10},{10,2},{3,11},{11,3},{4,12},{12,4},... | collective-permute-start | bytes 1966088 | tf_op jit(solution)/shard_map/ppermute | solution.py:65
  723.5 41.3 %collective-permute-start.66 = (bf16[2,160,1024]{2,1,0:T(8,128)(2,1)S(1)}, bf16[2,160,1024]{2,1,0:T(8,128)(2,1)S(1)}, u32[]{:S(2)}, u32[]{:S(2)}) collective-permute-start(bf16[2,160,1024]{2,1,0:T(8,128)(2,1)S(1)} %fusion.58), channel_id=1, source_target_pairs={{0,4},{4,0},{1,5},{5,1},{2,6},{6,2},{3,7},{7,3},{8,12},{12,8},{9,1... | collective-permute-start | bytes 1966088 | tf_op jit(solution)/shard_map/ppermute | solution.py:65
  726.4 35.2 %collective-permute-start.68 = (bf16[1,160,1280]{2,1,0:T(8,128)(2,1)S(1)}, bf16[1,160,1280]{2,1,0:T(8,128)(2,1)S(1)}, u32[]{:S(2)}, u32[]{:S(2)}) collective-permute-start(bf16[1,160,1280]{2,1,0:T(8,128)(2,1)S(1)} %constant_dynamic-slice_fusion.2), channel_id=1, source_target_pairs={{0,16},{16,0},{1,17},{17,1},{2,18},{18,2},{3,19},{19,3},{4,20},{20... | collective-permute-start | bytes 1228808 | tf_op jit(solution)/shard_map/ppermute | solution.py:65
  727.6 37.2 %collective-permute-start.67 = (bf16[2,160,1024]{2,1,0:T(8,128)(2,1)S(1)}, bf16[2,160,1024]{2,1,0:T(8,128)(2,1)S(1)}, u32[]{:S(2)}, u32[]{:S(2)}) collective-permute-start(bf16[2,160,1024]{2,1,0:T(8,128)(2,1)S(1)} %fusion.54), channel_id=1, source_target_pairs={{0,4},{4,0},{1,5},{5,1},{2,6},{6,2},{3,7},{7,3},{8,12},{12,8},{9,1... | collective-permute-start | bytes 1966088 | tf_op jit(solution)/shard_map/ppermute | solution.py:65
  768.1 41.6 %collective-permute-start.70 = (bf16[1,160,384]{2,1,0:T(8,128)(2,1)S(1)}, bf16[1,160,384]{2,1,0:T(8,128)(2,1)S(1)}, u32[]{:S(2)}, u32[]{:S(2)}) collective-permute-start(bf16[1,160,384]{2,1,0:T(8,128)(2,1)S(1)} %constant_dynamic-slice_fusion), channel_id=1, source_target_pairs={{0,16},{16,0},{1,17},{17,1},{2,18},{18,2},{3,19},{19,3},{4,20},{20... | collective-permute-start | bytes 368648 | tf_op jit(solution)/shard_map/ppermute | solution.py:65
  772.6 37.1 %collective-permute-start.71 = (bf16[160,2048]{1,0:T(8,128)(2,1)S(1)}, bf16[160,2048]{1,0:T(8,128)(2,1)S(1)}, u32[]{:S(2)}, u32[]{:S(2)}) collective-permute-start(bf16[160,2048]{1,0:T(8,128)(2,1)S(1)} %fusion.50), channel_id=1, source_target_pairs={{0,4},{4,0},{1,5},{5,1},{2,6},{6,2},{3,7},{7,3},{8,12},{12,8},{9,1... | collective-permute-start | bytes 1966088 | tf_op jit(solution)/shard_map/ppermute | solution.py:65
  773.8 36.0 %collective-permute-start.72 = (bf16[160,2048]{1,0:T(8,128)(2,1)S(1)}, bf16[160,2048]{1,0:T(8,128)(2,1)S(1)}, u32[]{:S(2)}, u32[]{:S(2)}) collective-permute-start(bf16[160,2048]{1,0:T(8,128)(2,1)S(1)} %fusion.46), channel_id=1, source_target_pairs={{0,8},{8,0},{1,9},{9,1},{2,10},{10,2},{3,11},{11,3},{4,12},{12,4},... | collective-permute-start | bytes 1966088 | tf_op jit(solution)/shard_map/ppermute | solution.py:65
  774.2 35.5 %collective-permute-start.73 = (bf16[160,2048]{1,0:T(8,128)(2,1)S(1)}, bf16[160,2048]{1,0:T(8,128)(2,1)S(1)}, u32[]{:S(2)}, u32[]{:S(2)}) collective-permute-start(bf16[160,2048]{1,0:T(8,128)(2,1)S(1)} %fusion.42), channel_id=1, source_target_pairs={{0,8},{8,0},{1,9},{9,1},{2,10},{10,2},{3,11},{11,3},{4,12},{12,4},... | collective-permute-start | bytes 1966088 | tf_op jit(solution)/shard_map/ppermute | solution.py:65
  776.6 34.7 %collective-permute-start.69 = (bf16[1,160,1280]{2,1,0:T(8,128)(2,1)S(1)}, bf16[1,160,1280]{2,1,0:T(8,128)(2,1)S(1)}, u32[]{:S(2)}, u32[]{:S(2)}) collective-permute-start(bf16[1,160,1280]{2,1,0:T(8,128)(2,1)S(1)} %constant_dynamic-slice_fusion.1), channel_id=1, source_target_pairs={{0,16},{16,0},{1,17},{17,1},{2,18},{18,2},{3,19},{19,3},{4,20},{20... | collective-permute-start | bytes 1228808 | tf_op jit(solution)/shard_map/ppermute | solution.py:65
  (112 other events, 717.9 us)
Sparse Core Ops, SparseCore 0:
  12.2 105.2 all-gather.4
  119.7 106.6 all-gather.6
  228.0 124.0 all-gather.8
  517.8 176.5 reduce-scatter.1
